TPU v7x, 32 devices: a whole 2x2x4 slice. The times are simulated.
32 devices in a mesh: groups: 2 (over y), shard: 8 (over z, x), sub: 2 (over core).
Axes of the slice: x: 2, y: 2, z: 4, core: 2. Of those that a mesh axis runs over, the one named last changes fastest.
Arguments:
- embeddings: bfloat16 [4096, 1024], P(('groups', 'shard', 'sub')), parts along dimension 0, may hold values from -24 to 24
- cluster_id: int32 [4096], P(('groups', 'shard', 'sub')), parts along dimension 0, may hold values from 0 to 255, as said below
- item_order: int32 [4096], P(('groups', 'shard', 'sub')), parts along dimension 0, may hold values from 0 to 2047, each once
- owner_map: int32 [512], P('groups'), parts along dimension 0, may hold values from 0 to 7, as said below
Outputs:
- max_cosine: float32 [4096], P(('groups', 'shard', 'sub')), parts along dimension 0
- centroid_dist: float32 [4096], P(('groups', 'shard', 'sub')), parts along dimension 0
- cluster_cohesion: float32 [512], P(('groups', 'shard')), parts along dimension 0
There are 2 independent parts, one for each index of `groups`. A program takes and returns all parts, laid end to end along the dimension named above; each array names one. Nothing has to cross between parts.
Inputs may be any that keep to these rules, and one draw needn't show every extreme that they name: `cluster_id`: among the rows of one device, at most 32 name clusters of one owner index (owner_map of the cluster); in every draw some owner index gets exactly 32 rows from every device. `owner_map`: every owner index holds exactly 32 clusters.
All inputs are finite; a program needn't handle non-finite values.
Results may differ from a plain program's by a relative error of at most 0.0015.
Values may be sent and summed in bfloat16 or wider, within the bound.
No kernel may reach another device: no remote copies, remote signals or barrier semaphores. Data moves between devices by JAX's collectives and lax.ppermute only.
A program may use at most 64 MiB of HBM per device.

v0:
```python
import math

import jax
import jax.numpy as jnp
from jax import lax
from jax.sharding import PartitionSpec as P


def normalize(embeddings):
    values = embeddings.astype(jnp.float32)
    mean_sq = jnp.mean(values * values, axis=1, keepdims=True)
    return (values * lax.rsqrt(embeddings.shape[1] * (mean_sq + 1e-06))).astype(jnp.bfloat16)


def local(embeddings, cluster_id, item_order, owner_map):
    owners = lax.axis_size("shard")
    core_count = lax.axis_size("sub")
    local_rows = embeddings.shape[0]
    width = embeddings.shape[1]
    rows_all = local_rows * owners * core_count
    clus_dev = owner_map.shape[0] // owners
    capacity = 2 * local_rows // owners
    query_count = owners * capacity
    block_rows = math.gcd(query_count, 512)
    block_count = query_count // block_rows
    owner_index = lax.axis_index("shard")
    unit_rows = normalize(embeddings)
    sort_key = cluster_id * rows_all + item_order
    owner_of = owner_map[cluster_id]
    owner_hot = (owner_of[:, None] == jnp.arange(owners, dtype=jnp.int32)[None, :]).astype(
        jnp.int32
    )
    rank_within = jnp.sum(owner_hot * (jnp.cumsum(owner_hot, axis=0) - 1), axis=1)
    slot_index = owner_of * capacity + rank_within
    own_clusters = jnp.nonzero(owner_map == owner_index, size=clus_dev)[0].astype(jnp.int32)

    def key_pass(query_rows, query_keys):
        query_blocks = query_rows.reshape(block_count, block_rows, width)
        query_key_blocks = query_keys.reshape(block_count, block_rows)

        def fold_step(state_now, piece, offset):
            best_cos, cluster_sums, counts = state_now
            key_rows, key_ids = piece
            key_cluster = key_ids // rows_all

            def per_block(inputs):
                block_query, block_keys, block_best = inputs
                scores = jnp.einsum(
                    "qd,kd->qk", block_query, key_rows, preferred_element_type=jnp.float32
                )
                earlier = (key_cluster[None, :] == (block_keys // rows_all)[:, None]) & (
                    key_ids[None, :] < block_keys[:, None]
                )
                return jnp.maximum(block_best, jnp.max(jnp.where(earlier, scores, -3.0), axis=1))

            best_cos = lax.map(
                per_block,
                (query_blocks, query_key_blocks, best_cos.reshape(block_count, block_rows)),
            ).reshape(query_count)
            member = (key_cluster[:, None] == own_clusters[None, :]).astype(jnp.bfloat16)
            cluster_sums = cluster_sums + jnp.einsum(
                "kc,kd->cd", member, key_rows, preferred_element_type=jnp.float32
            )
            counts = counts + jnp.sum(member.astype(jnp.float32), axis=0)
            return (best_cos, cluster_sums, counts)

        initial = (
            jnp.full((query_count,), -3.0, jnp.float32),
            jnp.zeros((clus_dev, width), jnp.float32),
            jnp.zeros((clus_dev,), jnp.float32),
        )
        return (fold_step, initial)

    pair_units, pair_keys, pair_slots = (
        lax.all_gather(unit_rows, "sub", axis=0, tiled=True),
        lax.all_gather(sort_key, "sub", axis=0, tiled=True),
        lax.all_gather(slot_index, "sub", axis=0, tiled=True),
    )
    anchor = jnp.arange(core_count * local_rows, dtype=jnp.int32) // local_rows
    chip_slot = (
        pair_slots // capacity * (core_count * capacity) + anchor * capacity + pair_slots % capacity
    )
    row_buffer = (
        jnp.zeros((owners * core_count * capacity, width), jnp.bfloat16)
        .at[chip_slot]
        .set(pair_units)
    )
    key_buffer = (
        jnp.full((owners * core_count * capacity,), -1, jnp.int32).at[chip_slot].set(pair_keys)
    )
    got_rows, got_keys = (
        lax.all_to_all(
            row_buffer.reshape(owners, core_count * capacity, width),
            "shard",
            split_axis=0,
            concat_axis=0,
            tiled=True,
        ),
        lax.all_to_all(
            key_buffer.reshape(owners, core_count * capacity),
            "shard",
            split_axis=0,
            concat_axis=0,
            tiled=True,
        ),
    )
    core_index = lax.axis_index("sub")
    query_rows = lax.dynamic_index_in_dim(
        got_rows.reshape(owners, core_count, capacity, width), core_index, axis=1, keepdims=False
    ).reshape(query_count, width)
    query_keys = lax.dynamic_index_in_dim(
        got_keys.reshape(owners, core_count, capacity), core_index, axis=1, keepdims=False
    ).reshape(query_count)
    fold_step, initial = key_pass(query_rows, query_keys)
    best_cos, cluster_sums, counts = fold_step(
        initial,
        (
            got_rows.reshape(owners * core_count * capacity, width),
            got_keys.reshape(owners * core_count * capacity),
        ),
        0,
    )
    centroid = cluster_sums / jnp.maximum(counts, 1.0)[:, None]
    cluster_cohesion = jnp.sum(centroid * centroid, axis=1)
    best_cos = jnp.where(best_cos > -2.0, best_cos, 0.0)
    query_member = ((query_keys // rows_all)[:, None] == own_clusters[None, :]).astype(jnp.float32)

    def centre_distance(inputs):
        block_query, block_member = inputs
        centre_rows = jnp.dot(block_member, centroid, precision=lax.Precision.HIGHEST)
        offset_rows = block_query.astype(jnp.float32) - centre_rows
        return jnp.sum(offset_rows * offset_rows, axis=1)

    distance = lax.map(
        centre_distance,
        (
            query_rows.reshape(block_count, block_rows, width),
            query_member.reshape(block_count, block_rows, clus_dev),
        ),
    ).reshape(query_count)
    results = jnp.stack([best_cos.reshape(owners, capacity), distance.reshape(owners, capacity)])
    returned = lax.all_to_all(results, "shard", split_axis=1, concat_axis=1, tiled=True)
    flat_results = returned.reshape(2, query_count)
    return (flat_results[0][slot_index], flat_results[1][slot_index], cluster_cohesion)


def solution(mesh):
    in_specs = (
        P(("groups", "shard", "sub"), None),
        P(("groups", "shard", "sub")),
        P(("groups", "shard", "sub")),
        P("groups"),
    )
    out_specs = (
        P(("groups", "shard", "sub")),
        P(("groups", "shard", "sub")),
        P(("groups", "shard")),
    )
    return jax.shard_map(local, mesh=mesh, in_specs=in_specs, out_specs=out_specs, check_vma=False)
```

profile of v0, /device:TPU:0, one launch (start us, length us, event | category | flops | bytes accessed | tf_op | source)
XLA Modules:
  0.0 71.2 jit_solution(13437715776109748898)
XLA Ops:
  0.6 0.7 add_bitcast_fusion
  1.3 0.0 copy-start
  1.3 0.7 copy-done
  2.0 1.3 %gather_fusion = s32[128]{0:T(128)S(1)} fusion(s32[256]{0:T(256)S(1)} %copy-done, s32[1024]{0:T(1024)S(1)} %pad_clamp_fusion.1), kind=kCustom, calls=%fused_computation | custom fusion | bytes 1536 | tf_op jit(solution)/shard_map/gather | solution.py:29
  3.3 0.0 copy-start.1
  3.3 0.1 fusion.10
  3.4 0.2 reduce_window_sum.40
  3.5 0.2 select_reduce_fusion
  3.7 1.9 %all-gather = s32[2,1,128]{2,1,0:T(1,128)S(1)} all-gather(s32[1,1,128]{2,1,0:T(1,128)S(1)} %fusion.27), channel_id=1, replica_groups=mesh['groups'=2,'shard'=8,'sub'=2] {'sub'}, dimensions={0}, use_global_device_ids=true | all-gather | bytes 1536 | tf_op jit(solution)/shard_map/all_gather | solution.py:77
  5.7 1.8 %all-gather.1 = s32[2,1,128]{2,1,0:T(1,128)S(1)} all-gather(s32[1,1,128]{2,1,0:T(1,128)S(1)} %get-tuple-element.31), channel_id=1, replica_groups=mesh['groups'=2,'shard'=8,'sub'=2] {'sub'}, dimensions={0}, use_global_device_ids=true | all-gather | bytes 1536 | tf_op jit(solution)/shard_map/all_gather | solution.py:76
  7.4 1.4 %scatter_custom_fusion = s32[512]{0:T(512)S(1)} fusion(s32[256]{0:T(256)S(1)} %compare_select_fusion.2, s32[256]{0:T(256)S(1)} %bitcast.34, s32[]{:T(128)} %constant.157.clone.1), kind=kCustom, calls=%fused_computation.70 | custom fusion | bytes 2052 | tf_op jit(solution)/shard_map/scatter | solution.py:89
  8.8 0.7 all_to_all.12
  9.5 7.1 %all-to-all-start = ((s32[8,1,64]{2,1,0:T(1,128)}), s32[8,1,64]{2,1,0:T(1,128)S(1)}, u32[]{:S(2)}, u32[]{:S(2)}) async-start(s32[8,1,64]{2,1,0:T(1,128)} %all_to_all.12), calls=%async_computation | async-start | bytes 8192 | tf_op jit(solution)/shard_map/all_to_all | solution.py:99
  16.6 0.0 copy-done.1
  16.6 0.1 fusion.3
  16.7 0.1 fusion.4
  16.9 2.2 %all_gather.11 = bf16[256,1024]{1,0:T(8,128)(2,1)S(1)} all-gather(bf16[128,1024]{1,0:T(8,128)(2,1)S(1)} %fusion.4), channel_id=1, replica_groups=mesh['groups'=2,'shard'=8,'sub'=2] {'sub'}, dimensions={0}, use_global_device_ids=true | all-gather | bytes 786432 | tf_op jit(solution)/shard_map/all_gather | solution.py:75
  19.1 0.3 reduce-window.19
  19.4 0.1 slice.15
  19.5 2.7 %scatter_custom_fusion.1 = bf16[512,1024]{1,0:T(8,128)(2,1)} fusion(s32[256]{0:T(256)S(1)} %compare_select_fusion.2, bf16[256,1024]{1,0:T(8,128)(2,1)S(1)} %all_gather.11, bf16[]{:T(256)} %constant.173.clone.1), kind=kCustom, calls=%fused_computation.16 | custom fusion | bytes 1048578 | tf_op jit(solution)/shard_map/scatter | solution.py:86
  22.2 0.9 %all-to-all-done = s32[8,1,64]{2,1,0:T(1,128)S(1)} async-done(((s32[8,1,64]{2,1,0:T(1,128)}), s32[8,1,64]{2,1,0:T(1,128)S(1)}, u32[]{:S(2)}, u32[]{:S(2)}) %all-to-all-start) | async-done | bytes 2080 | tf_op jit(solution)/shard_map/all_to_all | solution.py:99
  23.1 5.1 %all-to-all-start.1 = ((bf16[8,64,1024]{2,1,0:T(8,128)(2,1)}), bf16[8,64,1024]{2,1,0:T(8,128)(2,1)S(1)}, u32[]{:S(2)}, u32[]{:S(2)}) async-start(bf16[8,64,1024]{2,1,0:T(8,128)(2,1)} %bitcast.4), calls=%async_computation.1 | async-start | bytes 2097152 | tf_op jit(solution)/shard_map/all_to_all | solution.py:92
  28.2 0.1 slice_reduce_fusion.2
  28.3 0.1 broadcast_add_fusion
  28.3 2.3 %scatter_custom_fusion.2 = s32[32]{0:T(128)S(1)} fusion(s32[256]{0:T(256)S(1)} %bitcast.31, s32[256]{0:T(256)S(1)} %ne.110, s32[]{:T(128)} %constant.158.clone.1), kind=kCustom, calls=%fused_computation.83 | custom fusion | flops 256 | bytes 132 | tf_op jit(solution)/shard_map/scatter-add | solution.py:35
  30.7 0.1 copy.10
  30.8 0.1 reduce-window.21
  30.8 0.1 reduce.4
  30.9 0.6 fusion.22
  31.6 0.7 compare_select_fusion.7
  32.2 0.1 reshape.281
  32.3 0.1 squeeze.31
  32.4 0.5 broadcast.337
  32.9 0.7 reduce.20
  33.6 0.1 reshape.280
  33.7 0.2 convert_reduce_fusion
  33.9 20.3 %all-to-all-done.1 = bf16[8,64,1024]{2,1,0:T(8,128)(2,1)S(1)} async-done(((bf16[8,64,1024]{2,1,0:T(8,128)(2,1)}), bf16[8,64,1024]{2,1,0:T(8,128)(2,1)S(1)}, u32[]{:S(2)}, u32[]{:S(2)}) %all-to-all-start.1) | async-done | bytes 1048608 | tf_op jit(solution)/shard_map/all_to_all | solution.py:92
  54.3 0.6 fusion.2
  54.8 0.1 max.26
  54.9 0.9 %multiply_reduce_fusion = (f32[32]{0:T(128)}, f32[32,1024]{1,0:T(8,128)S(1)}) fusion(f32[32]{0:T(128)S(1)} %broadcast_maximum_fusion.1, bf16[512,1024]{1,0:T(8,128)(2,1)S(1)} %bitcast.26, s32[512]{0:T(512)S(1)} %add_select_fusion, s32[32]{0:T(128)S(1)} %compare_select_fusion.7), kind=kOutput, calls=%fused_computation.18 | convolution fusion | flops 33669088 | bytes 1182080 | tf_op jit(solution)/shard_map/kc,kd->cd/dot_general | solution.py:61
  55.9 0.7 %fusion.1 = f32[256]{0:T(256)S(1)} fusion(f32[32,1024]{1,0:T(8,128)S(1)} %get-tuple-element.39, bf16[256,1024]{1,0:T(8,128)(2,1)S(1)} %bitcast.28, s32[32]{0:T(128)S(1)} %compare_select_fusion.7, s32[256]{0:T(256)S(1)} %and_select_fusion.1), kind=kOutput, calls=%fused_computation.8 | convolution fusion | flops 101719808 | bytes 657536 | tf_op jit(solution)/shard_map/while/body/eval_jaxpr/dot_general | solution.py:130
  56.6 0.1 stack_reshape_reshape.3
  56.7 0.6 pad_maximum_fusion
  57.3 3.6 %all-to-all-start.2 = ((f32[2,8,32]{2,0,1:T(2,128)}), f32[2,8,32]{2,0,1:T(2,128)S(1)}, u32[]{:S(2)}, u32[]{:S(2)}) async-start(f32[2,8,32]{2,0,1:T(2,128)} %pad_maximum_fusion), calls=%async_computation.2 | async-start | bytes 16384 | tf_op jit(solution)/shard_map/all_to_all | solution.py:142
  61.0 6.5 %all-to-all-done.2 = f32[2,8,32]{2,0,1:T(2,128)S(1)} async-done(((f32[2,8,32]{2,0,1:T(2,128)}), f32[2,8,32]{2,0,1:T(2,128)S(1)}, u32[]{:S(2)}, u32[]{:S(2)}) %all-to-all-start.2) | async-done | bytes 2080 | tf_op jit(solution)/shard_map/all_to_all | solution.py:142
  67.5 0.1 squeeze.34
  67.6 0.1 squeeze.33
  67.7 1.8 %gather_fusion.2 = f32[128]{0:T(128)} fusion(f32[256]{0:T(256)S(1)} %squeeze.34, s32[1024]{0:T(1024)S(1)} %pad_clamp_fusion), kind=kCustom, calls=%fused_computation.2 | custom fusion | bytes 1536 | tf_op jit(solution)/shard_map/gather | solution.py:144
  69.4 1.8 %gather_fusion.1 = f32[128]{0:T(128)} fusion(f32[256]{0:T(256)S(1)} %squeeze.33, s32[1024]{0:T(1024)S(1)} %pad_clamp_fusion), kind=kCustom, calls=%fused_computation.1 | custom fusion | bytes 1536 | tf_op jit(solution)/shard_map/gather | solution.py:144
  (18 shorter events, 0.2 us)
Async XLA Ops:
  1.3 0.7 copy-start
  3.3 13.3 %copy-start.1 = (bf16[128,1024]{1,0:T(8,128)(2,1)S(1)}, bf16[128,1024]{1,0:T(8,128)(2,1)}, u32[]{:S(2)}) copy-start(bf16[128,1024]{1,0:T(8,128)(2,1)} %param.4) | copy-start | bytes 786436
  9.5 13.6 %all-to-all-start = ((s32[8,1,64]{2,1,0:T(1,128)}), s32[8,1,64]{2,1,0:T(1,128)S(1)}, u32[]{:S(2)}, u32[]{:S(2)}) async-start(s32[8,1,64]{2,1,0:T(1,128)} %all_to_all.12), calls=%async_computation | async-start | bytes 8192 | tf_op jit(solution)/shard_map/all_to_all | solution.py:99
  23.1 31.2 %all-to-all-start.1 = ((bf16[8,64,1024]{2,1,0:T(8,128)(2,1)}), bf16[8,64,1024]{2,1,0:T(8,128)(2,1)S(1)}, u32[]{:S(2)}, u32[]{:S(2)}) async-start(bf16[8,64,1024]{2,1,0:T(8,128)(2,1)} %bitcast.4), calls=%async_computation.1 | async-start | bytes 2097152 | tf_op jit(solution)/shard_map/all_to_all | solution.py:92
  57.3 10.2 %all-to-all-start.2 = ((f32[2,8,32]{2,0,1:T(2,128)}), f32[2,8,32]{2,0,1:T(2,128)S(1)}, u32[]{:S(2)}, u32[]{:S(2)}) async-start(f32[2,8,32]{2,0,1:T(2,128)} %pad_maximum_fusion), calls=%async_computation.2 | async-start | bytes 16384 | tf_op jit(solution)/shard_map/all_to_all | solution.py:142
where the time goes:
time: 71.6 us; the launch traced here: 71.2 us
  waiting for transfers between devices  27.7 us (39%)
  starting transfers between devices  15.8 us (22%)
  local copies, waits for them, and re-layouts  11.6 us (16%)
  other arithmetic  7.11 us (10%)
  blocking collectives  5.87 us (8%)
  matrix products  2.26 us (3%)
  between operations  0.77 us (1%)
    all_to_all x1, waiting for transfers between devices, local(): lax.all_to_all(row_buffer.reshape(owners, core_count * capacity, width),...  20.3 us
    all_to_all x1, starting transfers between devices, local(): lax.all_to_all(key_buffer.reshape(owners, core_count * capacity), 'shard'...  7.1 us
    all_to_all x1, waiting for transfers between devices, local(): lax.all_to_all(results, 'shard', split_axis=1, concat_axis=1, tiled=True)  6.51 us
    all_to_all x1, starting transfers between devices, local(): lax.all_to_all(row_buffer.reshape(owners, core_count * capacity, width),...  5.09 us
    all_to_all x1, starting transfers between devices, local(): lax.all_to_all(results, 'shard', split_axis=1, concat_axis=1, tiled=True)  3.65 us
    scatter x1, local copies, waits for them, and re-layouts, local(): row_buffer = jnp.zeros((owners * core_count * capacity, width), jnp.bfloa...  2.66 us
    scatter-add x1, other arithmetic, local(): jnp.nonzero(owner_map == owner_index, size=clus_dev)[0].astype(jnp.int32)  2.32 us
    all_gather x1, blocking collectives, local(): lax.all_gather(unit_rows, 'sub', axis=0, tiled=True)  2.18 us
  transfers between devices with their start and end apart: 3, of which 3 were waited for; matrix products, arithmetic and copies ran while one was open for 13% of the time, Pallas kernels for 0%

commit v1 on v0

v1 whole, which is shorter than its diff:
```python
import functools

import jax
import jax.numpy as jnp
from jax import lax
from jax.experimental import pallas as pl
from jax.experimental.pallas import tpu as pltpu
from jax.sharding import PartitionSpec as P

VMEM = pltpu.VMEM
GATHER_BYTES = 8 << 20


def normalize(embeddings):
    values = embeddings.astype(jnp.float32)
    mean_sq = jnp.mean(values * values, axis=1, keepdims=True)
    return (values * lax.rsqrt(embeddings.shape[1] * (mean_sq + 1e-06))).astype(jnp.bfloat16)


def as_column(row):
    return jnp.transpose(jnp.broadcast_to(row, (128, row.shape[1])))[:, :1]


def ranked(hot):
    at = [lax.broadcasted_iota(jnp.int32, (128, 128), d) for d in (0, 1)]
    upto = (at[0] <= at[1]).astype(jnp.bfloat16)
    before, parts = jnp.zeros((1, 1), jnp.float32), []
    for start in range(0, hot.shape[1], 128):
        piece = hot[:, start : start + 128]
        count = jnp.dot(
            jnp.broadcast_to(piece, (16, 128)).astype(jnp.bfloat16),
            upto,
            preferred_element_type=jnp.float32,
        )[:1]
        parts.append(count + before)
        before = before + jnp.sum(piece, axis=1, keepdims=True)
    return jnp.concatenate(parts, axis=1)


def window_kernel(
    rows_all, clus_dev, owner_ref, map_ref, qkey_ref, qlow_ref, key_ref, query_ref, rows_ref,
    best_ref, dist_ref, cohesion_ref,
):
    queries = query_ref.shape[0]
    keys = key_ref[...]
    query = query_ref[...]
    rows = rows_ref[...]
    hot = (map_ref[...] == owner_ref[0]).astype(jnp.float32)
    rank = ranked(hot)
    width = hot.shape[1]
    kth = lax.broadcasted_iota(jnp.int32, (clus_dev, width), 0).astype(jnp.float32) + 1.0
    name = lax.broadcasted_iota(jnp.int32, (clus_dev, width), 1).astype(jnp.float32)
    own = jnp.sum(jnp.where((rank == kth) & (hot > 0.0), name, 0.0), axis=1, keepdims=True)
    low = as_column(qlow_ref[...])
    lows = jnp.concatenate([low, own.astype(jnp.int32) * rows_all], axis=0)
    above = keys >= lows
    member = (above & (keys < lows + rows_all)).astype(jnp.float32)
    counts = jnp.sum(member, axis=1, keepdims=True)
    sums = jnp.dot(member.astype(jnp.bfloat16), rows, preferred_element_type=jnp.float32)
    centroid = sums * (1.0 / jnp.maximum(counts, 1.0))
    scores = lax.dot_general(
        query, rows, (((1,), (1,)), ((), ())), preferred_element_type=jnp.float32
    )
    earlier = above[:queries] & (keys < as_column(qkey_ref[...]))
    best = jnp.max(jnp.where(earlier, scores, -3.0), axis=1, keepdims=True)
    best = jnp.where(best > -2.0, best, 0.0)
    offset = query.astype(jnp.float32) - centroid[:queries]
    distance = jnp.sum(offset * offset, axis=1, keepdims=True)
    centre = centroid[queries:]
    cohesion = jnp.sum(centre * centre, axis=1, keepdims=True)
    best_ref[...] = jnp.transpose(jnp.broadcast_to(best, (queries, 128)))[:1]
    dist_ref[...] = jnp.transpose(jnp.broadcast_to(distance, (queries, 128)))[:1]
    cohesion_ref[...] = jnp.transpose(jnp.broadcast_to(cohesion, (clus_dev, 128)))[:1]


def window(owner_index, owner_map, query_keys, query_lows, keys, query, rows, rows_all, clus_dev):
    queries, count, width = query.shape[0], rows.shape[0], rows.shape[1]
    best, distance, cohesion = pl.pallas_call(
        functools.partial(window_kernel, rows_all, clus_dev),
        out_shape=(
            jax.ShapeDtypeStruct((1, queries), jnp.float32),
            jax.ShapeDtypeStruct((1, queries), jnp.float32),
            jax.ShapeDtypeStruct((1, clus_dev), jnp.float32),
        ),
        in_specs=[pl.BlockSpec(memory_space=pltpu.SMEM)]
        + [pl.BlockSpec(memory_space=VMEM)] * 6,
        out_specs=[pl.BlockSpec(memory_space=VMEM)] * 3,
        compiler_params=pltpu.CompilerParams(vmem_limit_bytes=32 << 20),
        cost_estimate=pl.CostEstimate(
            flops=4 * queries * count * width, bytes_accessed=2 * count * width, transcendentals=0
        ),
        name="window",
    )(
        owner_index.reshape(1).astype(jnp.int32),
        owner_map.reshape(1, -1),
        query_keys.reshape(1, -1),
        query_lows.reshape(1, -1),
        keys.reshape(1, -1),
        query,
        rows,
    )
    return best.reshape(queries), distance.reshape(queries), cohesion.reshape(clus_dev)


def gathered(embeddings, cluster_id, item_order, owner_map, rows_all, clus_dev):
    axes = ("shard", "sub")
    low = cluster_id * rows_all
    sort_key = low + item_order
    unit_rows = normalize(embeddings)
    rows = lax.all_gather(unit_rows, axes, axis=0, tiled=True)
    keys = lax.all_gather(sort_key, axes, axis=0, tiled=True)
    return window(
        lax.axis_index("shard"), owner_map, sort_key, low, keys, unit_rows, rows, rows_all, clus_dev
    )


def routed(embeddings, cluster_id, item_order, owner_map, rows_all, clus_dev):
    owners = lax.axis_size("shard")
    local_rows, width = embeddings.shape
    capacity = 2 * local_rows // owners
    slots = owners * capacity
    unit_rows = normalize(embeddings)
    sort_key = cluster_id * rows_all + item_order
    owner_of = owner_map[cluster_id]
    owner_hot = (owner_of[:, None] == jnp.arange(owners, dtype=jnp.int32)[None, :]).astype(jnp.int32)
    rank_within = jnp.sum(owner_hot * (jnp.cumsum(owner_hot, axis=0) - 1), axis=1)
    slot_index = owner_of * capacity + rank_within
    row_buffer = jnp.zeros((slots, width), jnp.bfloat16).at[slot_index].set(unit_rows)
    key_buffer = jnp.full((slots,), -1, jnp.int32).at[slot_index].set(sort_key)
    query = lax.all_to_all(
        row_buffer.reshape(owners, capacity, width), "shard", 0, 0, tiled=True
    ).reshape(slots, width)
    query_keys = lax.all_to_all(
        key_buffer.reshape(owners, capacity), "shard", 0, 0, tiled=True
    ).reshape(slots)
    rows = lax.all_gather(query, "sub", axis=0, tiled=True)
    keys = lax.all_gather(query_keys, "sub", axis=0, tiled=True)
    query_lows = query_keys // rows_all * rows_all
    best, distance, cohesion = window(
        lax.axis_index("shard"), owner_map, query_keys, query_lows, keys, query, rows, rows_all, clus_dev
    )
    results = jnp.stack([best.reshape(owners, capacity), distance.reshape(owners, capacity)])
    returned = lax.all_to_all(results, "shard", 1, 1, tiled=True).reshape(2, slots)
    return returned[0][slot_index], returned[1][slot_index], cohesion


def local(embeddings, cluster_id, item_order, owner_map):
    owners = lax.axis_size("shard")
    local_rows, width = embeddings.shape
    rows_all = local_rows * owners * lax.axis_size("sub")
    clus_dev = owner_map.shape[0] // owners
    plan = gathered if rows_all * width * embeddings.dtype.itemsize <= GATHER_BYTES else routed
    return plan(embeddings, cluster_id, item_order, owner_map, rows_all, clus_dev)


def solution(mesh):
    in_specs = (
        P(("groups", "shard", "sub"), None),
        P(("groups", "shard", "sub")),
        P(("groups", "shard", "sub")),
        P("groups"),
    )
    out_specs = (
        P(("groups", "shard", "sub")),
        P(("groups", "shard", "sub")),
        P(("groups", "shard")),
    )
    return jax.shard_map(local, mesh=mesh, in_specs=in_specs, out_specs=out_specs, check_vma=False)
```

time: 71.6 us -> 77.7 us (1.085)
  blocking collectives: 5.87 us -> 23 us
  starting transfers between devices: 15.8 us -> 0.04 us
  between operations: 0.77 us -> 14 us
  local copies, waits for them, and re-layouts: 11.6 us -> 3.82 us
  other arithmetic: 7.11 us -> 3.53 us
  Pallas kernels: 0 us -> 3.29 us
  matrix products: 2.26 us -> 0 us
  waiting for transfers between devices: 27.7 us -> 29.8 us
    all_gather x0 -> x1, waiting for transfers between devices: none -> 29.8 us  [gathered(): rows = lax.all_gather(unit_rows, axes, axis=0, tiled=True)]
    all_to_all x3 -> x0, waiting for transfers between devices: 27.7 us -> none  [the longest x1 20.3 us: local(): lax.all_to_all(row_buffer.reshape(owners, core_count * capacity, width),...]
    all_gather x3 -> x1, blocking collectives: 5.87 us -> 23 us  [gathered(): keys = lax.all_gather(sort_key, axes, axis=0, tiled=True)]
    all_to_all x3 -> x0, starting transfers between devices: 15.8 us -> none  [the longest x1 7.1 us: local(): lax.all_to_all(key_buffer.reshape(owners, core_count * capacity), 'shard'...]
    gather x3 -> x0, local copies, waits for them, and re-layouts: 4.79 us -> none  [the longest x1 1.76 us: local(): flat_results[1][slot_index]]
    scatter x2 -> x0, local copies, waits for them, and re-layouts: 4.06 us -> none  [the longest x1 2.66 us: local(): row_buffer = jnp.zeros((owners * core_count * capacity, width), jnp.bfloa...]
    pallas_call x0 -> x1, Pallas kernels: none -> 3.29 us  [window(): pl.pallas_call(functools.partial(window_kernel, rows_all, clus_dev), out_...]
    unnamed x4 -> x6, local copies, waits for them, and re-layouts: 0.68 us -> 3.82 us
  transfers between devices with their start and end apart: 3 -> 1, of which waited for: 3 -> 1; matrix products, arithmetic and copies ran while one was open for 13% -> 1% of each run, Pallas kernels for 0% -> 0%
where the time goes in v1:
time: 77.7 us; the launch traced here: 77.5 us
  waiting for transfers between devices  29.8 us (38%)
  blocking collectives  23 us (30%)
  between operations  14 us (18%)
  local copies, waits for them, and re-layouts  3.82 us (5%)
  other arithmetic  3.53 us (5%)
  Pallas kernels  3.29 us (4%)
    all_gather x1, waiting for transfers between devices, gathered(): rows = lax.all_gather(unit_rows, axes, axis=0, tiled=True)  29.8 us
    all_gather x1, blocking collectives, gathered(): keys = lax.all_gather(sort_key, axes, axis=0, tiled=True)  23 us
    unnamed x6, local copies, waits for them, and re-layouts  3.82 us
    pallas_call x1, Pallas kernels, window(): pl.pallas_call(functools.partial(window_kernel, rows_all, clus_dev), out_...  3.29 us
    convert_element_type x1, other arithmetic, normalize(): (values * lax.rsqrt(embeddings.shape[1] * (mean_sq + 1e-06))).astype(jnp....  1.76 us
  transfers between devices with their start and end apart: 1, of which 1 were waited for; matrix products, arithmetic and copies ran while one was open for 1% of the time, Pallas kernels for 0%

profile of v1, /device:TPU:0, one launch (start us, length us, event | category | flops | bytes accessed | tf_op | source)
XLA Modules:
  0.0 77.5 jit_solution(5821815781785064269)
XLA Ops:
  7.2 0.0 all-gather.3.cloned.1.call-start
  7.2 1.1 %fusion = f32[128]{0:T(128)S(1)} fusion(bf16[128,1024]{1,0:T(8,128)(2,1)} %param.4), kind=kLoop, calls=%fused_computation.2 | loop fusion | flops 393088 | bytes 262656 | tf_op jit(solution)/shard_map/reduce_sum | solution.py:16
  8.3 1.8 %fusion.1.query_ref = bf16[128,1024]{1,0:T(8,128)(2,1)} fusion(bf16[128,1024]{1,0:T(8,128)(2,1)} %param.4, f32[128]{0:T(128)S(1)} %multiply_rsqrt_fusion), kind=kLoop, calls=%fused_computation.3 | loop fusion | flops 393216 | bytes 524800 | tf_op jit(solution)/shard_map/convert_element_type | solution.py:17
  10.1 0.0 all-gather.3.cloned.1.call-update
  10.1 0.7 fusion.2
  10.8 23.0 %all-gather = s32[16,1,128]{2,1,0:T(1,128)S(1)} all-gather(s32[1,1,128]{2,1,0:T(1,128)S(1)} %get-tuple-element.9), channel_id=1, replica_groups=mesh['groups'=2,'shard'=8,'sub'=2] {'shard','sub'}, dimensions={0}, use_global_device_ids=true | all-gather | bytes 8704 | tf_op jit(solution)/shard_map/all_gather | solution.py:111
  33.7 29.8 %all-gather.3.cloned.1.call-done.rows_ref = bf16[2048,1024]{1,0:T(8,128)(2,1)} async-done(((bf16[128,1024]{1,0:T(8,128)(2,1)}), bf16[2048,1024]{1,0:T(8,128)(2,1)}) %all-gather.3.cloned.1.call-update) | async-done | bytes 4194320 | tf_op jit(solution)/shard_map/all_gather | solution.py:110
  63.5 0.0 copy-start
  63.5 2.2 %copy-done = bf16[2048,1024]{1,0:T(8,128)(2,1)S(1)} copy-done((bf16[2048,1024]{1,0:T(8,128)(2,1)S(1)}, bf16[2048,1024]{1,0:T(8,128)(2,1)}, u32[]{:S(2)}) %copy-start) | copy-done | bytes 4194328
  65.7 0.0 copy-start.1
  65.7 0.9 %copy-done.1 = bf16[128,1024]{1,0:T(8,128)(2,1)S(1)} copy-done((bf16[128,1024]{1,0:T(8,128)(2,1)S(1)}, bf16[128,1024]{1,0:T(8,128)(2,1)}, u32[]{:S(2)}) %copy-start.1) | copy-done | bytes 262168
  66.6 0.0 copy-start.2
  66.6 0.7 copy-done.2
  67.3 3.3 %window.1 = (f32[1,128]{1,0:T(1,128)}, f32[1,128]{1,0:T(1,128)}, f32[1,32]{1,0:T(1,128)}) custom-call(s32[1]{0:T(128)} %bitcast.owner_ref, s32[1,256]{1,0:T(1,128)S(1)} %bitcast.13, s32[1,128]{1,0:T(1,128)S(1)} %get-tuple-element.10.qkey_ref, s32[1,128]{1,0:T(1,128)S(1)} %get-tuple-element.11.qlow_ref, s32[1,2048]{1,0:T(1,128)S(1)} %bitcast.12, ...), custom_call_target="tpu_custom_call" | custom-call | flops 1073741824 | bytes 4194304 | tf_op jit(solution)/shard_map/window/pallas_call | solution.py:78
  (1 shorter events, 0.0 us)
Async XLA Ops:
  7.2 56.3 %all-gather.3.cloned.1.call-start = ((), (), s32[]{:S(2)}) async-start(), calls=%async_computation | async-start | bytes 4456448 | tf_op jit(solution)/shard_map/all_gather | solution.py:110
  63.5 2.2 %copy-start = (bf16[2048,1024]{1,0:T(8,128)(2,1)S(1)}, bf16[2048,1024]{1,0:T(8,128)(2,1)}, u32[]{:S(2)}) copy-start(bf16[2048,1024]{1,0:T(8,128)(2,1)} %all-gather.3.cloned.1.call-done.rows_ref) | copy-start | bytes 12582916
  65.7 0.9 %copy-start.1 = (bf16[128,1024]{1,0:T(8,128)(2,1)S(1)}, bf16[128,1024]{1,0:T(8,128)(2,1)}, u32[]{:S(2)}) copy-start(bf16[128,1024]{1,0:T(8,128)(2,1)} %fusion.1.query_ref) | copy-start | bytes 786436
  66.6 0.7 copy-start.2
Sparse Core Ops, SparseCore 0:
  10.2 53.2 all-gather.2

commit v2 on v1

v2 whole, which is shorter than its diff:
```python
import functools

import jax
import jax.numpy as jnp
from jax import lax
from jax.experimental import pallas as pl
from jax.experimental.pallas import tpu as pltpu
from jax.sharding import PartitionSpec as P

LANES = 128
DIGITS = 3
MOST_PERMUTES = 16
WHOLE = pl.BlockSpec(memory_space=pltpu.VMEM)
SCALAR = pl.BlockSpec(memory_space=pltpu.SMEM)


def iota(shape, dim):
    return lax.broadcasted_iota(jnp.int32, shape, dim)


def as_column(row):
    return jnp.transpose(jnp.broadcast_to(row, (LANES, row.shape[1])))[:, :1]


def as_row(column):
    return jnp.transpose(jnp.broadcast_to(column, (column.shape[0], LANES)))[:1]


def matmul(a, b):
    return jnp.dot(a, b, preferred_element_type=jnp.float32)


def ranked(hot):
    upto = (iota((LANES, LANES), 0) <= iota((LANES, LANES), 1)).astype(jnp.bfloat16)
    before, parts = jnp.zeros((1, 1), jnp.float32), []
    for start in range(0, hot.shape[1], LANES):
        piece = hot[:, start : start + LANES]
        spread = jnp.broadcast_to(piece, (16, LANES)).astype(jnp.bfloat16)
        parts.append(matmul(spread, upto)[:1] + before)
        before = before + jnp.sum(piece, axis=1, keepdims=True)
    return jnp.concatenate(parts, axis=1)


def pack_kernel(
    rows_all, owners, capacity, me_ref, map_ref, cluster_ref, order_ref, embed_ref, slot_ref, *out_refs
):
    rows, width = embed_ref.shape
    values = embed_ref[...].astype(jnp.float32)
    mean_sq = jnp.sum(values * values, axis=1, keepdims=True) * (1.0 / width)
    unit = (values * lax.rsqrt(width * (mean_sq + 1e-06))).astype(jnp.bfloat16)

    cluster = as_column(cluster_ref[...])
    clusters = map_ref.shape[1]
    named = cluster == iota((rows, clusters), 1)
    owner = jnp.sum(jnp.where(named, map_ref[...], 0).astype(jnp.float32), axis=1, keepdims=True)
    owner = owner.astype(jnp.int32)
    hot = (owner == iota((rows, max(owners, LANES)), 1)).astype(jnp.float32)
    upto = (iota((rows, rows), 1) <= iota((rows, rows), 0)).astype(jnp.bfloat16)
    rank = jnp.sum(hot * matmul(upto, hot.astype(jnp.bfloat16)), axis=1, keepdims=True) - 1.0
    slot = as_row((owner ^ me_ref[0]) * capacity + rank.astype(jnp.int32))
    slot_ref[...] = slot

    lane = iota((rows, LANES), 1)
    digit = jnp.zeros((rows, LANES), jnp.int32)
    for first, number in ((0, cluster + 1), (DIGITS, as_column(order_ref[...]))):
        for place in range(DIGITS):
            digit = jnp.where(lane == first + place, (number >> (8 * place)) & 255, digit)
    digit = digit.astype(jnp.float32).astype(jnp.bfloat16)

    slots = owners * capacity
    move = (iota((slots, rows), 0) == slot).astype(jnp.float32).astype(jnp.bfloat16)
    moved = matmul(move, unit).astype(jnp.bfloat16)
    moved_digit = matmul(move, digit).astype(jnp.bfloat16)
    each = slots // len(out_refs)
    for index, out_ref in enumerate(out_refs):
        part = slice(index * each, (index + 1) * each)
        out_ref[:, :width] = moved[part]
        out_ref[:, width:] = moved_digit[part]


def window_kernel(rows_all, clus_dev, me_ref, map_ref, query_ref, rows_ref, result_ref, cohesion_ref):
    queries = query_ref.shape[0]
    width = query_ref.shape[1] - LANES
    query = query_ref[:, :width]
    rows = rows_ref[:, :width]
    digit = query_ref[:, width:].astype(jnp.float32)
    low, order = (
        sum(digit[:, i + place : i + place + 1] * (256.0**place) for place in range(DIGITS))
        for i in (0, DIGITS)
    )
    low = (low.astype(jnp.int32) - 1) * rows_all
    query_key = low + order.astype(jnp.int32)
    digit = jnp.transpose(rows_ref[:, width:].astype(jnp.float32))
    keys, order = (
        sum(digit[i + place : i + place + 1] * (256.0**place) for place in range(DIGITS))
        for i in (0, DIGITS)
    )
    keys = (keys.astype(jnp.int32) - 1) * rows_all + order.astype(jnp.int32)

    hot = (map_ref[...] == me_ref[0]).astype(jnp.float32)
    rank = ranked(hot)
    shape = (clus_dev, hot.shape[1])
    kth = (rank == iota(shape, 0).astype(jnp.float32) + 1.0) & (hot > 0.0)
    own = jnp.sum(jnp.where(kth, iota(shape, 1).astype(jnp.float32), 0.0), axis=1, keepdims=True)
    lows = jnp.concatenate([low, own.astype(jnp.int32) * rows_all], axis=0)
    above = keys >= lows
    member = (above & (keys < lows + rows_all)).astype(jnp.float32)
    counts = jnp.sum(member, axis=1, keepdims=True)
    centroid = matmul(member.astype(jnp.bfloat16), rows) * (1.0 / jnp.maximum(counts, 1.0))
    scores = lax.dot_general(
        query, rows, (((1,), (1,)), ((), ())), preferred_element_type=jnp.float32
    )
    earlier = above[:queries] & (keys < query_key)
    best = jnp.max(jnp.where(earlier, scores, -3.0), axis=1, keepdims=True)
    best = jnp.where(best > -2.0, best, 0.0)
    offset = query.astype(jnp.float32) - centroid[:queries]
    distance = jnp.sum(offset * offset, axis=1, keepdims=True)
    lane = iota((queries, LANES), 1)
    result_ref[...] = jnp.transpose(jnp.where(lane == 0, best, distance))[: result_ref.shape[0]]
    centre = centroid[queries:]
    cohesion_ref[...] = as_row(jnp.sum(centre * centre, axis=1, keepdims=True))


def pick_kernel(slot_ref, *refs):
    *result_refs, best_ref, distance_ref = refs
    rows = slot_ref.shape[1]
    slots = result_refs[0].shape[1]
    each = slots // len(result_refs)
    part = iota((1, slots), 1) // each
    at = as_column(slot_ref[...]) == iota((rows, slots), 1)
    for line, out_ref in enumerate((best_ref, distance_ref)):
        values = result_refs[0][line : line + 1]
        for index, result_ref in enumerate(result_refs[1:]):
            values = jnp.where(part == index + 1, result_ref[line : line + 1], values)
        out_ref[...] = as_row(jnp.sum(jnp.where(at, values, 0.0), axis=1, keepdims=True))


def local(embeddings, cluster_id, item_order, owner_map):
    owners = lax.axis_size("shard")
    local_rows, width = embeddings.shape
    rows_all = local_rows * owners * lax.axis_size("sub")
    clus_dev = owner_map.shape[0] // owners
    capacity = 2 * local_rows // owners
    slots = owners * capacity
    wide = width + LANES
    params = pltpu.CompilerParams(vmem_limit_bytes=32 << 20)
    direct = owners <= MOST_PERMUTES and owners & (owners - 1) == 0
    me = lax.axis_index("shard").astype(jnp.int32).reshape(1)
    owner_row = owner_map.reshape(1, -1)

    def from_partner(value, k):
        pairs = [(i, i ^ k) for i in range(owners)]
        return lax.ppermute(value, "shard", pairs) if k else value

    parts = owners if direct else 1
    slot, *packed = pl.pallas_call(
        functools.partial(pack_kernel, rows_all, owners, capacity),
        out_shape=[jax.ShapeDtypeStruct((1, local_rows), jnp.int32)]
        + [jax.ShapeDtypeStruct((slots // parts, wide), jnp.bfloat16)] * parts,
        in_specs=[SCALAR] + [WHOLE] * 4,
        out_specs=[WHOLE] * (1 + parts),
        compiler_params=params,
        name="pack",
    )(
        me if direct else jnp.zeros_like(me),
        owner_row,
        cluster_id.reshape(1, -1),
        item_order.reshape(1, -1),
        embeddings,
    )
    if direct:
        query = jnp.concatenate([from_partner(block, k) for k, block in enumerate(packed)])
    else:
        query = lax.all_to_all(
            packed[0].reshape(owners, capacity, wide), "shard", 0, 0, tiled=True
        ).reshape(slots, wide)
    rows = lax.all_gather(query, "sub", axis=0, tiled=True)

    results, cohesion = pl.pallas_call(
        functools.partial(window_kernel, rows_all, clus_dev),
        out_shape=[
            jax.ShapeDtypeStruct((2, slots), jnp.float32),
            jax.ShapeDtypeStruct((1, clus_dev), jnp.float32),
        ],
        in_specs=[SCALAR] + [WHOLE] * 3,
        out_specs=[WHOLE] * 2,
        compiler_params=params,
        name="window",
    )(me, owner_row, query, rows)

    if direct:
        returned = [from_partner(results, k) for k in range(owners)]
    else:
        returned = [
            lax.all_to_all(
                results.reshape(2, owners, capacity), "shard", 1, 1, tiled=True
            ).reshape(2, slots)
        ]
    best, distance = pl.pallas_call(
        pick_kernel,
        out_shape=[jax.ShapeDtypeStruct((1, local_rows), jnp.float32)] * 2,
        in_specs=[WHOLE] * (1 + len(returned)),
        out_specs=[WHOLE] * 2,
        compiler_params=params,
        name="pick",
    )(slot, *returned)
    return best.reshape(local_rows), distance.reshape(local_rows), cohesion.reshape(clus_dev)


def solution(mesh):
    in_specs = (
        P(("groups", "shard", "sub"), None),
        P(("groups", "shard", "sub")),
        P(("groups", "shard", "sub")),
        P("groups"),
    )
    out_specs = (
        P(("groups", "shard", "sub")),
        P(("groups", "shard", "sub")),
        P(("groups", "shard")),
    )
    return jax.shard_map(local, mesh=mesh, in_specs=in_specs, out_specs=out_specs, check_vma=False)
```

time: 77.7 us -> 68.1 us (0.88)
  starting transfers between devices: 0.04 us -> 23.8 us
  blocking collectives: 23 us -> 0 us
  waiting for transfers between devices: 29.8 us -> 20.3 us
  other arithmetic: 3.53 us -> 0 us
  local copies, waits for them, and re-layouts: 3.82 us -> 6.18 us
    ppermute x0 -> x14, starting transfers between devices: none -> 23.7 us  [from_partner(): return lax.ppermute(value, 'shard', pairs) if k else value]
    all_gather x1 -> x0, blocking collectives: 23 us -> none  [gathered(): keys = lax.all_gather(sort_key, axes, axis=0, tiled=True)]
    all_gather x1, waiting for transfers between devices: 29.8 us -> 10 us  [local(): rows = lax.all_gather(query, 'sub', axis=0, tiled=True)]
    ppermute x0 -> x14, waiting for transfers between devices: none -> 10.3 us  [from_partner(): return lax.ppermute(value, 'shard', pairs) if k else value]
    unnamed x6 -> x23, local copies, waits for them, and re-layouts: 3.82 us -> 6.17 us
    convert_element_type x1 -> x0, other arithmetic: 1.76 us -> none  [normalize(): (values * lax.rsqrt(embeddings.shape[1] * (mean_sq + 1e-06))).astype(jnp....]
    reduce_sum x1 -> x0, other arithmetic: 1.08 us -> none  [normalize(): mean_sq = jnp.mean(values * values, axis=1, keepdims=True)]
    pallas_call x1 -> x3, Pallas kernels: 3.29 us -> 3.44 us  [the longest x1 1.79 us: local(): pl.pallas_call(functools.partial(window_kernel, rows_all, clus_dev), out_...]
  transfers between devices with their start and end apart: 1 -> 15, of which waited for: 1 -> 6; matrix products, arithmetic and copies ran while one was open for 1% -> 0% of each run, Pallas kernels for 0% -> 0%
where the time goes in v2:
time: 68.1 us; the launch traced here: 67.9 us
  starting transfers between devices  23.8 us (35%)
  waiting for transfers between devices  20.3 us (30%)
  between operations  14.1 us (21%)
  local copies, waits for them, and re-layouts  6.18 us (9%)
  Pallas kernels  3.44 us (5%)
    ppermute x14, starting transfers between devices, from_partner(): return lax.ppermute(value, 'shard', pairs) if k else value  23.7 us
    ppermute x14, waiting for transfers between devices, from_partner(): return lax.ppermute(value, 'shard', pairs) if k else value  10.3 us
    all_gather x1, waiting for transfers between devices, local(): rows = lax.all_gather(query, 'sub', axis=0, tiled=True)  10 us
    unnamed x23, local copies, waits for them, and re-layouts  6.17 us
    pallas_call x1, Pallas kernels, local(): pl.pallas_call(functools.partial(window_kernel, rows_all, clus_dev), out_...  1.79 us
  transfers between devices with their start and end apart: 15, of which 6 were waited for; matrix products, arithmetic and copies ran while one was open for 0% of the time, Pallas kernels for 0%

profile of v2, /device:TPU:0, one launch (start us, length us, event | category | flops | bytes accessed | tf_op | source)
XLA Modules:
  0.0 67.9 jit_solution(14508100723149549510)
XLA Ops:
  7.2 0.0 copy-start.5
  7.2 0.0 all-gather.2.cloned.1.call-start
  7.2 0.0 copy-start.3
  7.2 0.9 %copy-done.3 = bf16[128,1024]{1,0:T(8,128)(2,1)S(1)} copy-done((bf16[128,1024]{1,0:T(8,128)(2,1)S(1)}, bf16[128,1024]{1,0:T(8,128)(2,1)}, u32[]{:S(2)}) %copy-start.3) | copy-done | bytes 262168
  8.2 0.0 copy-start.4
  8.2 0.7 copy-done.4
  8.9 0.0 copy-start.6
  8.9 0.7 copy-done.6
  9.5 0.0 copy-start.7
  9.5 0.7 copy-done.7
  10.2 0.8 %pack.1 = (s32[1,128]{1,0:T(1,128)S(1)}, bf16[32,1152]{1,0:T(8,128)(2,1)S(1)}, bf16[32,1152]{1,0:T(8,128)(2,1)S(1)}, bf16[32,1152]{1,0:T(8,128)(2,1)S(1)}, bf16[...) custom-call(s32[1]{0:T(128)} %bitcast.me_ref, ...), custom_call_target="tpu_custom_call" | custom-call | tf_op jit(solution)/shard_map/pack/pallas_call | solution.py:156
  11.0 3.0 %collective-permute-start = (bf16[32,1152]{1,0:T(8,128)(2,1)S(1)}, bf16[32,1152]{1,0:T(8,128)(2,1)S(1)}, u32[]{:S(2)}, u32[]{:S(2)}) collective-permute-start(bf16[32,1152]{1,0:T(8,128)(2,1)S(1)} %get-tuple-element.18), channel_id=1, source_target_pairs={{0,2},{2,0},{4,6},{6,4},{8,10},{10,8},{12,14},{14,12},{1,3},{3,1},... | collective-permute-start | bytes 221192 | tf_op jit(solution)/shard_map/ppermute | solution.py:153
  14.0 1.6 %collective-permute-start.1 = (bf16[32,1152]{1,0:T(8,128)(2,1)S(1)}, bf16[32,1152]{1,0:T(8,128)(2,1)S(1)}, u32[]{:S(2)}, u32[]{:S(2)}) collective-permute-start(bf16[32,1152]{1,0:T(8,128)(2,1)S(1)} %get-tuple-element.19), channel_id=1, source_target_pairs={{0,4},{2,6},{4,0},{6,2},{8,12},{10,14},{12,8},{14,10},{1,5},{3,7},... | collective-permute-start | bytes 221192 | tf_op jit(solution)/shard_map/ppermute | solution.py:153
  15.6 0.0 collective-permute-start.2
  15.6 3.0 %collective-permute-start.3 = (bf16[32,1152]{1,0:T(8,128)(2,1)S(1)}, bf16[32,1152]{1,0:T(8,128)(2,1)S(1)}, u32[]{:S(2)}, u32[]{:S(2)}) collective-permute-start(bf16[32,1152]{1,0:T(8,128)(2,1)S(1)} %get-tuple-element.21), channel_id=1, source_target_pairs={{0,8},{2,10},{4,12},{6,14},{8,0},{10,2},{12,4},{14,6},{1,9},{3,11}... | collective-permute-start | bytes 221192 | tf_op jit(solution)/shard_map/ppermute | solution.py:153
  18.6 1.3 %collective-permute-start.4 = (bf16[32,1152]{1,0:T(8,128)(2,1)S(1)}, bf16[32,1152]{1,0:T(8,128)(2,1)S(1)}, u32[]{:S(2)}, u32[]{:S(2)}) collective-permute-start(bf16[32,1152]{1,0:T(8,128)(2,1)S(1)} %get-tuple-element.22), channel_id=1, source_target_pairs={{0,10},{2,8},{4,14},{6,12},{8,2},{10,0},{12,6},{14,4},{1,11},{3,9}... | collective-permute-start | bytes 221192 | tf_op jit(solution)/shard_map/ppermute | solution.py:153
  19.9 0.0 collective-permute-done
  19.9 3.7 %collective-permute-start.5 = (bf16[32,1152]{1,0:T(8,128)(2,1)S(1)}, bf16[32,1152]{1,0:T(8,128)(2,1)S(1)}, u32[]{:S(2)}, u32[]{:S(2)}) collective-permute-start(bf16[32,1152]{1,0:T(8,128)(2,1)S(1)} %get-tuple-element.23), channel_id=1, source_target_pairs={{0,12},{2,14},{4,8},{6,10},{8,4},{10,6},{12,0},{14,2},{1,13},{3,15... | collective-permute-start | bytes 221192 | tf_op jit(solution)/shard_map/ppermute | solution.py:153
  23.6 0.0 collective-permute-done.1
  23.6 0.1 collective-permute-start.6
  23.7 0.0 collective-permute-done.2
  23.7 0.0 collective-permute-done.3
  23.7 6.1 %collective-permute-done.4 = bf16[32,1152]{1,0:T(8,128)(2,1)S(1)} collective-permute-done((bf16[32,1152]{1,0:T(8,128)(2,1)S(1)}, bf16[32,1152]{1,0:T(8,128)(2,1)S(1)}, u32[]{:S(2)}, u32[]{:S(2)}) %collective-permute-start.4) | collective-permute-done | bytes 73760 | tf_op jit(solution)/shard_map/ppermute | solution.py:153
  29.8 0.0 collective-permute-done.5
  29.9 0.9 %collective-permute-done.6 = bf16[32,1152]{1,0:T(8,128)(2,1)S(1)} collective-permute-done((bf16[32,1152]{1,0:T(8,128)(2,1)S(1)}, bf16[32,1152]{1,0:T(8,128)(2,1)S(1)}, u32[]{:S(2)}, u32[]{:S(2)}) %collective-permute-start.6) | collective-permute-done | bytes 73760 | tf_op jit(solution)/shard_map/ppermute | solution.py:153
  30.8 0.0 copy-start
  30.8 0.8 %copy-done = bf16[256,1152]{1,0:T(8,128)(2,1)} copy-done((bf16[256,1152]{1,0:T(8,128)(2,1)}, bf16[256,1152]{1,0:T(8,128)(2,1)S(1)}, u32[]{:S(2)}) %copy-start) | copy-done | bytes 589848
  31.6 0.0 all-gather.2.cloned.1.call-update
  31.7 10.0 %all-gather.2.cloned.1.call-done.rows_ref = bf16[512,1152]{1,0:T(8,128)(2,1)} async-done(((bf16[256,1152]{1,0:T(8,128)(2,1)}), bf16[512,1152]{1,0:T(8,128)(2,1)}) %all-gather.2.cloned.1.call-update) | async-done | bytes 1179664 | tf_op jit(solution)/shard_map/all_gather | solution.py:177
  41.7 0.0 copy-done.5
  41.7 0.0 copy-start.1
  41.7 1.1 %copy-done.1 = bf16[256,1152]{1,0:T(8,128)(2,1)S(1)} copy-done((bf16[256,1152]{1,0:T(8,128)(2,1)S(1)}, bf16[256,1152]{1,0:T(8,128)(2,1)}, u32[]{:S(2)}) %copy-start.1) | copy-done | bytes 589848
  42.7 0.0 copy-start.2
  42.7 1.3 %copy-done.2 = bf16[512,1152]{1,0:T(8,128)(2,1)S(1)} copy-done((bf16[512,1152]{1,0:T(8,128)(2,1)S(1)}, bf16[512,1152]{1,0:T(8,128)(2,1)}, u32[]{:S(2)}) %copy-start.2) | copy-done | bytes 1179672
  44.0 1.8 %window.1 = (f32[2,256]{1,0:T(2,128)S(1)}, f32[1,32]{1,0:T(1,128)}) custom-call(s32[1]{0:T(128)} %bitcast.me_ref, s32[1,256]{1,0:T(1,128)S(1)} %bitcast.8, bf16[256,1152]{1,0:T(8,128)(2,1)S(1)} %copy-done.1, bf16[512,1152]{1,0:T(8,128)(2,1)S(1)} %copy-done.2), custom_call_target="tpu_custom_call" | custom-call | tf_op jit(solution)/shard_map/window/pallas_call | solution.py:179
  45.8 4.5 %collective-permute-start.13 = (f32[2,256]{1,0:T(2,128)S(1)}, f32[2,256]{1,0:T(2,128)S(1)}, u32[]{:S(2)}, u32[]{:S(2)}) collective-permute-start(f32[2,256]{1,0:T(2,128)S(1)} %get-tuple-element.25.refs_0_), channel_id=1, source_target_pairs={{0,14},{2,12},{4,10},{6,8},{8,6},{10,4},{12,2},{14,0},{1,15},{3,13... | collective-permute-start | bytes 6152 | tf_op jit(solution)/shard_map/ppermute | solution.py:153
  50.3 0.5 collective-permute-start.12
  50.8 0.6 collective-permute-start.11
  51.4 2.1 %collective-permute-start.10 = (f32[2,256]{1,0:T(2,128)S(1)}, f32[2,256]{1,0:T(2,128)S(1)}, u32[]{:S(2)}, u32[]{:S(2)}) collective-permute-start(f32[2,256]{1,0:T(2,128)S(1)} %get-tuple-element.25.refs_0_), channel_id=1, source_target_pairs={{0,8},{2,10},{4,12},{6,14},{8,0},{10,2},{12,4},{14,6},{1,9},{3,11}... | collective-permute-start | bytes 6152 | tf_op jit(solution)/shard_map/ppermute | solution.py:153
  53.4 2.1 %collective-permute-start.9 = (f32[2,256]{1,0:T(2,128)S(1)}, f32[2,256]{1,0:T(2,128)S(1)}, u32[]{:S(2)}, u32[]{:S(2)}) collective-permute-start(f32[2,256]{1,0:T(2,128)S(1)} %get-tuple-element.25.refs_0_), channel_id=1, source_target_pairs={{0,6},{2,4},{4,2},{6,0},{8,14},{10,12},{12,10},{14,8},{1,7},{3,5},... | collective-permute-start | bytes 6152 | tf_op jit(solution)/shard_map/ppermute | solution.py:153
  55.6 0.0 collective-permute-done.13.refs_7_
  55.6 1.1 %collective-permute-start.8 = (f32[2,256]{1,0:T(2,128)S(1)}, f32[2,256]{1,0:T(2,128)S(1)}, u32[]{:S(2)}, u32[]{:S(2)}) collective-permute-start(f32[2,256]{1,0:T(2,128)S(1)} %get-tuple-element.25.refs_0_), channel_id=1, source_target_pairs={{0,4},{2,6},{4,0},{6,2},{8,12},{10,14},{12,8},{14,10},{1,5},{3,7},... | collective-permute-start | bytes 6152 | tf_op jit(solution)/shard_map/ppermute | solution.py:153
  56.6 0.0 collective-permute-done.12.refs_6_
  56.6 0.3 collective-permute-start.7
  56.9 0.0 collective-permute-done.11.refs_5_
  56.9 0.0 collective-permute-done.10.refs_4_
  56.9 1.0 %collective-permute-done.9.refs_3_ = f32[2,256]{1,0:T(2,128)S(1)} collective-permute-done((f32[2,256]{1,0:T(2,128)S(1)}, f32[2,256]{1,0:T(2,128)S(1)}, u32[]{:S(2)}, u32[]{:S(2)}) %collective-permute-start.9) | collective-permute-done | bytes 2080 | tf_op jit(solution)/shard_map/ppermute | solution.py:153
  57.9 1.2 %collective-permute-done.8.refs_2_ = f32[2,256]{1,0:T(2,128)S(1)} collective-permute-done((f32[2,256]{1,0:T(2,128)S(1)}, f32[2,256]{1,0:T(2,128)S(1)}, u32[]{:S(2)}, u32[]{:S(2)}) %collective-permute-start.8) | collective-permute-done | bytes 2080 | tf_op jit(solution)/shard_map/ppermute | solution.py:153
  59.2 1.1 %collective-permute-done.7.refs_1_ = f32[2,256]{1,0:T(2,128)S(1)} collective-permute-done((f32[2,256]{1,0:T(2,128)S(1)}, f32[2,256]{1,0:T(2,128)S(1)}, u32[]{:S(2)}, u32[]{:S(2)}) %collective-permute-start.7) | collective-permute-done | bytes 2080 | tf_op jit(solution)/shard_map/ppermute | solution.py:153
  60.2 0.8 %pick.1 = (f32[1,128]{1,0:T(1,128)}, f32[1,128]{1,0:T(1,128)}) custom-call(s32[1,128]{1,0:T(1,128)S(1)} %get-tuple-element.16.slot_ref, f32[2,256]{1,0:T(2,128)S(1)} %get-tuple-element.25.refs_0_, f32[2,256]{1,0:T(2,128)S(1)} %collective-permute-done.7.refs_1_, f32[2,256]{1,0:T(2,128)S(1)} %collective-permute-done.8.refs_2_, ...), custom_call_target="tpu_custom_call" | custom-call | tf_op jit(solution)/shard_map/pick/pallas_call | solution.py:199
  (8 shorter events, 0.1 us)
Async XLA Ops:
  7.2 34.5 %copy-start.5 = (s32[256]{0:T(256)S(1)}, s32[256]{0:T(256)}, u32[]{:S(2)}) copy-start(s32[256]{0:T(256)} %param.7) | copy-start | bytes 3076
  7.2 34.5 %all-gather.2.cloned.1.call-start = ((), (), s32[]{:S(2)}) async-start(), calls=%async_computation | async-start | bytes 1769472 | tf_op jit(solution)/shard_map/all_gather | solution.py:177
  7.2 1.0 %copy-start.3 = (bf16[128,1024]{1,0:T(8,128)(2,1)S(1)}, bf16[128,1024]{1,0:T(8,128)(2,1)}, u32[]{:S(2)}) copy-start(bf16[128,1024]{1,0:T(8,128)(2,1)} %embed_ref.1) | copy-start | bytes 786436
  8.2 0.7 %copy-start.4 = (s32[256]{0:T(256)S(1)}, s32[256]{0:T(256)}, u32[]{:S(2)}) copy-start(s32[256]{0:T(256)} %param.7) | copy-start | bytes 3076
  8.9 0.7 copy-start.6
  9.5 0.7 copy-start.7
  11.0 8.9 %collective-permute-start = (bf16[32,1152]{1,0:T(8,128)(2,1)S(1)}, bf16[32,1152]{1,0:T(8,128)(2,1)S(1)}, u32[]{:S(2)}, u32[]{:S(2)}) collective-permute-start(bf16[32,1152]{1,0:T(8,128)(2,1)S(1)} %get-tuple-element.18), channel_id=1, source_target_pairs={{0,2},{2,0},{4,6},{6,4},{8,10},{10,8},{12,14},{14,12},{1,3},{3,1},... | collective-permute-start | bytes 221192 | tf_op jit(solution)/shard_map/ppermute | solution.py:153
  14.0 9.6 %collective-permute-start.1 = (bf16[32,1152]{1,0:T(8,128)(2,1)S(1)}, bf16[32,1152]{1,0:T(8,128)(2,1)S(1)}, u32[]{:S(2)}, u32[]{:S(2)}) collective-permute-start(bf16[32,1152]{1,0:T(8,128)(2,1)S(1)} %get-tuple-element.19), channel_id=1, source_target_pairs={{0,4},{2,6},{4,0},{6,2},{8,12},{10,14},{12,8},{14,10},{1,5},{3,7},... | collective-permute-start | bytes 221192 | tf_op jit(solution)/shard_map/ppermute | solution.py:153
  15.6 8.1 %collective-permute-start.2 = (bf16[32,1152]{1,0:T(8,128)(2,1)S(1)}, bf16[32,1152]{1,0:T(8,128)(2,1)S(1)}, u32[]{:S(2)}, u32[]{:S(2)}) collective-permute-start(bf16[32,1152]{1,0:T(8,128)(2,1)S(1)} %get-tuple-element.20), channel_id=1, source_target_pairs={{0,6},{2,4},{4,2},{6,0},{8,14},{10,12},{12,10},{14,8},{1,7},{3,5},... | collective-permute-start | bytes 221192 | tf_op jit(solution)/shard_map/ppermute | solution.py:153
  15.6 8.1 %collective-permute-start.3 = (bf16[32,1152]{1,0:T(8,128)(2,1)S(1)}, bf16[32,1152]{1,0:T(8,128)(2,1)S(1)}, u32[]{:S(2)}, u32[]{:S(2)}) collective-permute-start(bf16[32,1152]{1,0:T(8,128)(2,1)S(1)} %get-tuple-element.21), channel_id=1, source_target_pairs={{0,8},{2,10},{4,12},{6,14},{8,0},{10,2},{12,4},{14,6},{1,9},{3,11}... | collective-permute-start | bytes 221192 | tf_op jit(solution)/shard_map/ppermute | solution.py:153
  18.6 11.2 %collective-permute-start.4 = (bf16[32,1152]{1,0:T(8,128)(2,1)S(1)}, bf16[32,1152]{1,0:T(8,128)(2,1)S(1)}, u32[]{:S(2)}, u32[]{:S(2)}) collective-permute-start(bf16[32,1152]{1,0:T(8,128)(2,1)S(1)} %get-tuple-element.22), channel_id=1, source_target_pairs={{0,10},{2,8},{4,14},{6,12},{8,2},{10,0},{12,6},{14,4},{1,11},{3,9}... | collective-permute-start | bytes 221192 | tf_op jit(solution)/shard_map/ppermute | solution.py:153
  19.9 10.0 %collective-permute-start.5 = (bf16[32,1152]{1,0:T(8,128)(2,1)S(1)}, bf16[32,1152]{1,0:T(8,128)(2,1)S(1)}, u32[]{:S(2)}, u32[]{:S(2)}) collective-permute-start(bf16[32,1152]{1,0:T(8,128)(2,1)S(1)} %get-tuple-element.23), channel_id=1, source_target_pairs={{0,12},{2,14},{4,8},{6,10},{8,4},{10,6},{12,0},{14,2},{1,13},{3,15... | collective-permute-start | bytes 221192 | tf_op jit(solution)/shard_map/ppermute | solution.py:153
  23.6 7.2 %collective-permute-start.6 = (bf16[32,1152]{1,0:T(8,128)(2,1)S(1)}, bf16[32,1152]{1,0:T(8,128)(2,1)S(1)}, u32[]{:S(2)}, u32[]{:S(2)}) collective-permute-start(bf16[32,1152]{1,0:T(8,128)(2,1)S(1)} %get-tuple-element.24), channel_id=1, source_target_pairs={{0,14},{2,12},{4,10},{6,8},{8,6},{10,4},{12,2},{14,0},{1,15},{3,13... | collective-permute-start | bytes 221192 | tf_op jit(solution)/shard_map/ppermute | solution.py:153
  30.8 0.8 %copy-start = (bf16[256,1152]{1,0:T(8,128)(2,1)}, bf16[256,1152]{1,0:T(8,128)(2,1)S(1)}, u32[]{:S(2)}) copy-start(bf16[256,1152]{1,0:T(8,128)(2,1)S(1)} %constant_dynamic-update-slice_fusion.query_ref) | copy-start | bytes 1769476
  41.7 1.1 %copy-start.1 = (bf16[256,1152]{1,0:T(8,128)(2,1)S(1)}, bf16[256,1152]{1,0:T(8,128)(2,1)}, u32[]{:S(2)}) copy-start(bf16[256,1152]{1,0:T(8,128)(2,1)} %copy-done) | copy-start | bytes 1769476
  42.7 1.3 %copy-start.2 = (bf16[512,1152]{1,0:T(8,128)(2,1)S(1)}, bf16[512,1152]{1,0:T(8,128)(2,1)}, u32[]{:S(2)}) copy-start(bf16[512,1152]{1,0:T(8,128)(2,1)} %all-gather.2.cloned.1.call-done.rows_ref) | copy-start | bytes 3538948
  45.8 9.8 %collective-permute-start.13 = (f32[2,256]{1,0:T(2,128)S(1)}, f32[2,256]{1,0:T(2,128)S(1)}, u32[]{:S(2)}, u32[]{:S(2)}) collective-permute-start(f32[2,256]{1,0:T(2,128)S(1)} %get-tuple-element.25.refs_0_), channel_id=1, source_target_pairs={{0,14},{2,12},{4,10},{6,8},{8,6},{10,4},{12,2},{14,0},{1,15},{3,13... | collective-permute-start | bytes 6152 | tf_op jit(solution)/shard_map/ppermute | solution.py:153
  50.3 6.4 %collective-permute-start.12 = (f32[2,256]{1,0:T(2,128)S(1)}, f32[2,256]{1,0:T(2,128)S(1)}, u32[]{:S(2)}, u32[]{:S(2)}) collective-permute-start(f32[2,256]{1,0:T(2,128)S(1)} %get-tuple-element.25.refs_0_), channel_id=1, source_target_pairs={{0,12},{2,14},{4,8},{6,10},{8,4},{10,6},{12,0},{14,2},{1,13},{3,15... | collective-permute-start | bytes 6152 | tf_op jit(solution)/shard_map/ppermute | solution.py:153
  50.8 6.2 %collective-permute-start.11 = (f32[2,256]{1,0:T(2,128)S(1)}, f32[2,256]{1,0:T(2,128)S(1)}, u32[]{:S(2)}, u32[]{:S(2)}) collective-permute-start(f32[2,256]{1,0:T(2,128)S(1)} %get-tuple-element.25.refs_0_), channel_id=1, source_target_pairs={{0,10},{2,8},{4,14},{6,12},{8,2},{10,0},{12,6},{14,4},{1,11},{3,9}... | collective-permute-start | bytes 6152 | tf_op jit(solution)/shard_map/ppermute | solution.py:153
  51.4 5.6 %collective-permute-start.10 = (f32[2,256]{1,0:T(2,128)S(1)}, f32[2,256]{1,0:T(2,128)S(1)}, u32[]{:S(2)}, u32[]{:S(2)}) collective-permute-start(f32[2,256]{1,0:T(2,128)S(1)} %get-tuple-element.25.refs_0_), channel_id=1, source_target_pairs={{0,8},{2,10},{4,12},{6,14},{8,0},{10,2},{12,4},{14,6},{1,9},{3,11}... | collective-permute-start | bytes 6152 | tf_op jit(solution)/shard_map/ppermute | solution.py:153
  53.4 4.5 %collective-permute-start.9 = (f32[2,256]{1,0:T(2,128)S(1)}, f32[2,256]{1,0:T(2,128)S(1)}, u32[]{:S(2)}, u32[]{:S(2)}) collective-permute-start(f32[2,256]{1,0:T(2,128)S(1)} %get-tuple-element.25.refs_0_), channel_id=1, source_target_pairs={{0,6},{2,4},{4,2},{6,0},{8,14},{10,12},{12,10},{14,8},{1,7},{3,5},... | collective-permute-start | bytes 6152 | tf_op jit(solution)/shard_map/ppermute | solution.py:153
  55.6 3.6 %collective-permute-start.8 = (f32[2,256]{1,0:T(2,128)S(1)}, f32[2,256]{1,0:T(2,128)S(1)}, u32[]{:S(2)}, u32[]{:S(2)}) collective-permute-start(f32[2,256]{1,0:T(2,128)S(1)} %get-tuple-element.25.refs_0_), channel_id=1, source_target_pairs={{0,4},{2,6},{4,0},{6,2},{8,12},{10,14},{12,8},{14,10},{1,5},{3,7},... | collective-permute-start | bytes 6152 | tf_op jit(solution)/shard_map/ppermute | solution.py:153
  56.6 3.6 %collective-permute-start.7 = (f32[2,256]{1,0:T(2,128)S(1)}, f32[2,256]{1,0:T(2,128)S(1)}, u32[]{:S(2)}, u32[]{:S(2)}) collective-permute-start(f32[2,256]{1,0:T(2,128)S(1)} %get-tuple-element.25.refs_0_), channel_id=1, source_target_pairs={{0,2},{2,0},{4,6},{6,4},{8,10},{10,8},{12,14},{14,12},{1,3},{3,1},... | collective-permute-start | bytes 6152 | tf_op jit(solution)/shard_map/ppermute | solution.py:153
Sparse Core Ops, SparseCore 0:
  31.8 9.8 all-gather.1

commit v3 on v2

v3 whole, which is shorter than its diff:
```python
import functools

import jax
import jax.numpy as jnp
from jax import lax
from jax.experimental import pallas as pl
from jax.experimental.pallas import tpu as pltpu
from jax.sharding import PartitionSpec as P

LANES = 128
DIGITS = 3
SCALAR = pl.BlockSpec(memory_space=pltpu.SMEM)


def iota(shape, dim):
    return lax.broadcasted_iota(jnp.int32, shape, dim)


def as_column(row):
    return jnp.transpose(jnp.broadcast_to(row, (LANES, row.shape[1])))[:, :1]


def as_row(column):
    return jnp.transpose(jnp.broadcast_to(column, (column.shape[0], LANES)))[:1]


def matmul(a, b):
    return jnp.dot(a, b, preferred_element_type=jnp.float32)


def ranked(hot):
    upto = (iota((LANES, LANES), 0) <= iota((LANES, LANES), 1)).astype(jnp.bfloat16)
    before, parts = jnp.zeros((1, 1), jnp.float32), []
    for start in range(0, hot.shape[1], LANES):
        piece = hot[:, start : start + LANES]
        spread = jnp.broadcast_to(piece, (16, LANES)).astype(jnp.bfloat16)
        parts.append(matmul(spread, upto)[:1] + before)
        before = before + jnp.sum(piece, axis=1, keepdims=True)
    return jnp.concatenate(parts, axis=1)


def call(kernel, out_shape, name, *operands):
    def whole(x):
        return pl.BlockSpec(x.shape, lambda i: (0,) * len(x.shape))

    return pl.pallas_call(
        kernel,
        grid=(1,),
        out_shape=out_shape,
        in_specs=[SCALAR] + [whole(x) for x in operands[1:]],
        out_specs=[whole(x) for x in out_shape],
        compiler_params=pltpu.CompilerParams(vmem_limit_bytes=32 << 20),
        name=name,
    )(*operands)


def pack_kernel(
    rows_all, owners, capacity, me_ref, map_ref, cluster_ref, order_ref, embed_ref, slot_ref, packed_ref
):
    rows, width = embed_ref.shape
    values = embed_ref[...].astype(jnp.float32)
    mean_sq = jnp.sum(values * values, axis=1, keepdims=True) * (1.0 / width)
    unit = (values * lax.rsqrt(width * (mean_sq + 1e-06))).astype(jnp.bfloat16)

    cluster = as_column(cluster_ref[...])
    clusters = map_ref.shape[1]
    named = cluster == iota((rows, clusters), 1)
    owner = jnp.sum(jnp.where(named, map_ref[...], 0).astype(jnp.float32), axis=1, keepdims=True)
    owner = owner.astype(jnp.int32)
    hot = (owner == iota((rows, max(owners, LANES)), 1)).astype(jnp.float32)
    upto = (iota((rows, rows), 1) <= iota((rows, rows), 0)).astype(jnp.bfloat16)
    rank = jnp.sum(hot * matmul(upto, hot.astype(jnp.bfloat16)), axis=1, keepdims=True) - 1.0
    slot = as_row(owner * capacity + rank.astype(jnp.int32))
    slot_ref[...] = slot

    lane = iota((rows, LANES), 1)
    digit = jnp.zeros((rows, LANES), jnp.int32)
    for first, number in ((0, cluster + 1), (DIGITS, as_column(order_ref[...]))):
        for place in range(DIGITS):
            digit = jnp.where(lane == first + place, (number >> (8 * place)) & 255, digit)
    digit = digit.astype(jnp.float32).astype(jnp.bfloat16)

    slots = owners * capacity
    move = (iota((slots, rows), 0) == slot).astype(jnp.float32).astype(jnp.bfloat16)
    packed_ref[:, :width] = matmul(move, unit).astype(jnp.bfloat16)
    packed_ref[:, width:] = matmul(move, digit).astype(jnp.bfloat16)


def window_kernel(rows_all, clus_dev, me_ref, map_ref, query_ref, other_ref, result_ref, cohesion_ref):
    queries = query_ref.shape[0]
    width = query_ref.shape[1] - LANES
    query = query_ref[:, :width]

    def numbers(take):
        return (
            sum(take(i + place) * (256.0**place) for place in range(DIGITS)).astype(jnp.int32)
            for i in (0, DIGITS)
        )

    hot = (map_ref[...] == me_ref[0]).astype(jnp.float32)
    rank = ranked(hot)
    shape = (clus_dev, hot.shape[1])
    kth = (rank == iota(shape, 0).astype(jnp.float32) + 1.0) & (hot > 0.0)
    own = jnp.sum(jnp.where(kth, iota(shape, 1).astype(jnp.float32), 0.0), axis=1, keepdims=True)
    digit = query_ref[:, width:].astype(jnp.float32)
    name, order = numbers(lambda i: digit[:, i : i + 1])
    low = (name - 1) * rows_all
    query_key = low + order
    lows = jnp.concatenate([low, own.astype(jnp.int32) * rows_all], axis=0)

    best, counts, sums = None, None, None
    for rows_ref in (query_ref, other_ref):
        rows = rows_ref[:, :width]
        across = jnp.transpose(rows_ref[:, width:].astype(jnp.float32))
        name, order = numbers(lambda i: across[i : i + 1])
        keys = (name - 1) * rows_all + order
        above = keys >= lows
        member = (above & (keys < lows + rows_all)).astype(jnp.float32)
        count = jnp.sum(member, axis=1, keepdims=True)
        total = matmul(member.astype(jnp.bfloat16), rows)
        scores = lax.dot_general(
            query, rows, (((1,), (1,)), ((), ())), preferred_element_type=jnp.float32
        )
        earlier = above[:queries] & (keys < query_key)
        most = jnp.max(jnp.where(earlier, scores, -3.0), axis=1, keepdims=True)
        best = most if best is None else jnp.maximum(best, most)
        counts = count if counts is None else counts + count
        sums = total if sums is None else sums + total
    centroid = sums * (1.0 / jnp.maximum(counts, 1.0))
    best = jnp.where(best > -2.0, best, 0.0)
    offset = query.astype(jnp.float32) - centroid[:queries]
    distance = jnp.sum(offset * offset, axis=1, keepdims=True)
    lane = iota((queries, LANES), 1)
    result = jnp.transpose(jnp.where(lane == 0, best, distance))[: result_ref.shape[1]]
    for owner in range(result_ref.shape[0]):
        result_ref[owner] = result
    centre = centroid[queries:]
    cohesion_ref[...] = as_row(jnp.sum(centre * centre, axis=1, keepdims=True))


def pick_kernel(capacity, me_ref, slot_ref, result_ref, best_ref, distance_ref):
    rows = slot_ref.shape[1]
    owners, _, slots = result_ref.shape
    slot = as_column(slot_ref[...])
    best = jnp.zeros((rows, slots), jnp.float32)
    distance = jnp.zeros((rows, slots), jnp.float32)
    for owner in range(owners):
        shift = (me_ref[0] - owner) * capacity
        first = owner * capacity
        lane = jnp.where((slot >= first) & (slot < first + capacity), slot + shift, -1)
        at = lane == iota((rows, slots), 1)
        best = jnp.where(at, result_ref[owner, 0:1], best)
        distance = jnp.where(at, result_ref[owner, 1:2], distance)
    best_ref[...] = as_row(jnp.sum(best, axis=1, keepdims=True))
    distance_ref[...] = as_row(jnp.sum(distance, axis=1, keepdims=True))


def local(embeddings, cluster_id, item_order, owner_map):
    owners = lax.axis_size("shard")
    local_rows, width = embeddings.shape
    rows_all = local_rows * owners * lax.axis_size("sub")
    clus_dev = owner_map.shape[0] // owners
    capacity = 2 * local_rows // owners
    slots = owners * capacity
    wide = width + LANES
    me = lax.axis_index("shard").astype(jnp.int32).reshape(1)
    owner_row = owner_map.reshape(1, -1)

    slot, packed = call(
        functools.partial(pack_kernel, rows_all, owners, capacity),
        [
            jax.ShapeDtypeStruct((1, local_rows), jnp.int32),
            jax.ShapeDtypeStruct((slots, wide), jnp.bfloat16),
        ],
        "pack",
        me,
        owner_row,
        cluster_id.reshape(1, -1),
        item_order.reshape(1, -1),
        embeddings,
    )
    query = lax.all_to_all(
        packed.reshape(owners, capacity, wide), "shard", 0, 0, tiled=True
    ).reshape(slots, wide)
    other = lax.ppermute(query, "sub", [(0, 1), (1, 0)])
    results, cohesion = call(
        functools.partial(window_kernel, rows_all, clus_dev),
        [
            jax.ShapeDtypeStruct((owners, 2, slots), jnp.float32),
            jax.ShapeDtypeStruct((1, clus_dev), jnp.float32),
        ],
        "window",
        me,
        owner_row,
        query,
        other,
    )
    returned = lax.all_to_all(results, "shard", 0, 0, tiled=True)
    best, distance = call(
        functools.partial(pick_kernel, capacity),
        [jax.ShapeDtypeStruct((1, local_rows), jnp.float32)] * 2,
        "pick",
        me,
        slot,
        returned,
    )
    return best.reshape(local_rows), distance.reshape(local_rows), cohesion.reshape(clus_dev)


def solution(mesh):
    in_specs = (
        P(("groups", "shard", "sub"), None),
        P(("groups", "shard", "sub")),
        P(("groups", "shard", "sub")),
        P("groups"),
    )
    out_specs = (
        P(("groups", "shard", "sub")),
        P(("groups", "shard", "sub")),
        P(("groups", "shard")),
    )
    return jax.shard_map(local, mesh=mesh, in_specs=in_specs, out_specs=out_specs, check_vma=False)
```

time: 68.1 us -> 41 us (0.60)
  blocking collectives: 0 us -> 32.9 us
  starting transfers between devices: 23.8 us -> 0.01 us
  waiting for transfers between devices: 20.3 us -> 2 us
  between operations: 14.1 us -> 0.67 us
  local copies, waits for them, and re-layouts: 6.18 us -> 1.62 us
    all_to_all x0 -> x2, blocking collectives: none -> 32.9 us  [the longest x1 23.6 us: local(): lax.all_to_all(packed.reshape(owners, capacity, wide), 'shard', 0, 0, til...]
    ppermute x14 -> x1, starting transfers between devices: 23.7 us -> 0.01 us  [local(): other = lax.ppermute(query, 'sub', [(0, 1), (1, 0)])]
    all_gather x1 -> x0, waiting for transfers between devices: 10 us -> none  [local(): rows = lax.all_gather(query, 'sub', axis=0, tiled=True)]
    ppermute x14 -> x1, waiting for transfers between devices: 10.3 us -> 2 us  [local(): other = lax.ppermute(query, 'sub', [(0, 1), (1, 0)])]
    unnamed x23 -> x8, local copies, waits for them, and re-layouts: 6.17 us -> 1.62 us
  transfers between devices with their start and end apart: 15 -> 1, of which waited for: 6 -> 1; matrix products, arithmetic and copies ran while one was open for 0% -> 0% of each run, Pallas kernels for 0% -> 0%
where the time goes in v3:
time: 41 us; the launch traced here: 40.8 us
  blocking collectives  32.9 us (80%)
  Pallas kernels  3.57 us (9%)
  waiting for transfers between devices  2 us (5%)
  local copies, waits for them, and re-layouts  1.62 us (4%)
  between operations  0.67 us (2%)
    all_to_all x1, blocking collectives, local(): lax.all_to_all(packed.reshape(owners, capacity, wide), 'shard', 0, 0, til...  23.6 us
    all_to_all x1, blocking collectives, local(): returned = lax.all_to_all(results, 'shard', 0, 0, tiled=True)  9.32 us
    pallas_call x3, Pallas kernels, call(): pl.pallas_call(kernel, grid=(1,), out_shape=out_shape, in_specs=[SCALAR]...  3.57 us
    ppermute x1, waiting for transfers between devices, local(): other = lax.ppermute(query, 'sub', [(0, 1), (1, 0)])  2 us
    unnamed x8, local copies, waits for them, and re-layouts  1.62 us
  transfers between devices with their start and end apart: 1, of which 1 were waited for; matrix products, arithmetic and copies ran while one was open for 0% of the time, Pallas kernels for 0%

profile of v3, /device:TPU:0, one launch (start us, length us, event | category | flops | bytes accessed | tf_op | source)
XLA Modules:
  0.0 40.8 jit_solution(11615817600765361937)
XLA Ops:
  0.6 0.0 copy-start.3
  0.6 0.0 copy-start.1
  0.7 0.0 copy-start.2
  0.7 0.6 %copy-done.3 = s32[128]{0:T(128)S(1)} copy-done((s32[128]{0:T(128)S(1)}, s32[128]{0:T(128)}, u32[]{:S(2)}) %copy-start.3) | copy-done | bytes 536
  1.3 0.0 copy-done.1
  1.3 0.0 copy-done.2
  1.3 0.0 copy-start
  1.3 0.9 %copy-done = bf16[128,1024]{1,0:T(8,128)(2,1)S(1)} copy-done((bf16[128,1024]{1,0:T(8,128)(2,1)S(1)}, bf16[128,1024]{1,0:T(8,128)(2,1)}, u32[]{:S(2)}) %copy-start) | copy-done | bytes 262168
  2.3 0.8 %pack.1 = (s32[1,128]{1,0:T(1,128)S(1)}, bf16[256,1152]{1,0:T(8,128)(2,1)S(1)}) custom-call(s32[1]{0:T(128)} %bitcast.me_ref, s32[1,256]{1,0:T(1,128)S(1)} %bitcast.12, s32[1,128]{1,0:T(1,128)S(1)} %bitcast.14, s32[1,128]{1,0:T(1,128)S(1)} %bitcast.15, bf16[128,1024]{1,0:T(8,128)(2,1)S(1)} %copy-done), custom_call_target="tpu_custom_call" | custom-call | tf_op jit(solution)/shard_map/pack/pallas_call | solution.py:46
  3.1 23.6 %all_to_all.10 = bf16[8,32,1152]{2,1,0:T(8,128)(2,1)S(1)} all-to-all(bf16[8,32,1152]{2,1,0:T(8,128)(2,1)S(1)} %bitcast.11), channel_id=1, replica_groups=mesh['groups'=2,'shard'=8,'sub'=2] {'shard'}, dimensions={0} | all-to-all | bytes 1179648 | tf_op jit(solution)/shard_map/all_to_all | solution.py:182
  26.7 0.0 collective-permute-start
  26.7 2.0 %collective-permute-done.other_ref = bf16[256,1152]{1,0:T(8,128)(2,1)S(1)} collective-permute-done((bf16[256,1152]{1,0:T(8,128)(2,1)S(1)}, bf16[256,1152]{1,0:T(8,128)(2,1)S(1)}, u32[]{:S(2)}, u32[]{:S(2)}) %collective-permute-start) | collective-permute-done | bytes 589856 | tf_op jit(solution)/shard_map/ppermute | solution.py:185
  28.8 1.7 %window.1 = (f32[8,2,256]{2,1,0:T(2,128)S(1)}, f32[1,32]{1,0:T(1,128)}) custom-call(s32[1]{0:T(128)} %bitcast.me_ref, s32[1,256]{1,0:T(1,128)S(1)} %bitcast.13, bf16[256,1152]{1,0:T(8,128)(2,1)S(1)} %bitcast.10, bf16[256,1152]{1,0:T(8,128)(2,1)S(1)} %collective-permute-done.other_ref), custom_call_target="tpu_custom_call" | custom-call | tf_op jit(solution)/shard_map/window/pallas_call | solution.py:46
  30.5 9.3 %all_to_all.11.result_ref = f32[8,2,256]{2,1,0:T(2,128)S(1)} all-to-all(f32[8,2,256]{2,1,0:T(2,128)S(1)} %get-tuple-element.11), channel_id=1, replica_groups=mesh['groups'=2,'shard'=8,'sub'=2] {'shard'}, dimensions={0} | all-to-all | bytes 32768 | tf_op jit(solution)/shard_map/all_to_all | solution.py:198
  39.8 1.0 %pick.1 = (f32[1,128]{1,0:T(1,128)}, f32[1,128]{1,0:T(1,128)}) custom-call(s32[1]{0:T(128)} %bitcast.me_ref, s32[1,128]{1,0:T(1,128)S(1)} %get-tuple-element.9.slot_ref, f32[8,2,256]{2,1,0:T(2,128)S(1)} %all_to_all.11.result_ref), custom_call_target="tpu_custom_call" | custom-call | tf_op jit(solution)/shard_map/pick/pallas_call | solution.py:46
Async XLA Ops:
  0.6 0.7 %copy-start.3 = (s32[128]{0:T(128)S(1)}, s32[128]{0:T(128)}, u32[]{:S(2)}) copy-start(s32[128]{0:T(128)} %param.6) | copy-start | bytes 1540
  0.6 0.7 %copy-start.1 = (s32[256]{0:T(256)S(1)}, s32[256]{0:T(256)}, u32[]{:S(2)}) copy-start(s32[256]{0:T(256)} %param.7) | copy-start | bytes 3076
  0.7 0.7 %copy-start.2 = (s32[128]{0:T(128)S(1)}, s32[128]{0:T(128)}, u32[]{:S(2)}) copy-start(s32[128]{0:T(128)} %param.5) | copy-start | bytes 1540
  1.3 1.0 %copy-start = (bf16[128,1024]{1,0:T(8,128)(2,1)S(1)}, bf16[128,1024]{1,0:T(8,128)(2,1)}, u32[]{:S(2)}) copy-start(bf16[128,1024]{1,0:T(8,128)(2,1)} %embed_ref.1) | copy-start | bytes 786436
  26.7 2.0 %collective-permute-start = (bf16[256,1152]{1,0:T(8,128)(2,1)S(1)}, bf16[256,1152]{1,0:T(8,128)(2,1)S(1)}, u32[]{:S(2)}, u32[]{:S(2)}) collective-permute-start(bf16[256,1152]{1,0:T(8,128)(2,1)S(1)} %bitcast.9), channel_id=1, source_target_pairs={{0,1},{1,0},{2,3},{3,2},{4,5},{5,4},{6,7},{7,6},{8,9},{9,8},{10,11... | collective-permute-start | bytes 1769480 | tf_op jit(solution)/shard_map/ppermute | solution.py:185

commit v4 on v3

--- a/solution.py
+++ b/solution.py
@@ -9,7 +9,10 @@
 
 LANES = 128
 DIGITS = 3
+MOST_PERMUTES = 16
+WHOLE = pl.BlockSpec(memory_space=pltpu.VMEM)
 SCALAR = pl.BlockSpec(memory_space=pltpu.SMEM)
+HBM = pl.BlockSpec(memory_space=pltpu.HBM)
 
 
 def iota(shape, dim):
@@ -39,28 +42,20 @@
     return jnp.concatenate(parts, axis=1)
 
 
-def call(kernel, out_shape, name, *operands):
-    def whole(x):
-        return pl.BlockSpec(x.shape, lambda i: (0,) * len(x.shape))
-
-    return pl.pallas_call(
-        kernel,
-        grid=(1,),
-        out_shape=out_shape,
-        in_specs=[SCALAR] + [whole(x) for x in operands[1:]],
-        out_specs=[whole(x) for x in out_shape],
-        compiler_params=pltpu.CompilerParams(vmem_limit_bytes=32 << 20),
-        name=name,
-    )(*operands)
-
-
-def pack_kernel(
-    rows_all, owners, capacity, me_ref, map_ref, cluster_ref, order_ref, embed_ref, slot_ref, packed_ref
-):
+def pack_kernel(rows_all, owners, capacity, order, *refs):
+    me_ref, *sources = refs[:5]
+    slot_ref, *out_refs = refs[5:-5]
+    *held, sems = refs[-5:]
+    copies = [
+        pltpu.make_async_copy(source, target, sems.at[i])
+        for i, (source, target) in enumerate(zip(sources, held))
+    ]
+    for copy in copies:
+        copy.start()
+    map_ref, cluster_ref, order_ref, embed_ref = held
     rows, width = embed_ref.shape
-    values = embed_ref[...].astype(jnp.float32)
-    mean_sq = jnp.sum(values * values, axis=1, keepdims=True) * (1.0 / width)
-    unit = (values * lax.rsqrt(width * (mean_sq + 1e-06))).astype(jnp.bfloat16)
+    for copy in copies[:3]:
+        copy.wait()
 
     cluster = as_column(cluster_ref[...])
     clusters = map_ref.shape[1]
@@ -70,8 +65,14 @@
     hot = (owner == iota((rows, max(owners, LANES)), 1)).astype(jnp.float32)
     upto = (iota((rows, rows), 1) <= iota((rows, rows), 0)).astype(jnp.bfloat16)
     rank = jnp.sum(hot * matmul(upto, hot.astype(jnp.bfloat16)), axis=1, keepdims=True) - 1.0
-    slot = as_row(owner * capacity + rank.astype(jnp.int32))
+    partner = owner ^ me_ref[0]
+    place = partner
+    for index, k in enumerate(order):
+        place = jnp.where(partner == k, index, place)
+    slot = as_row(place * capacity + rank.astype(jnp.int32))
     slot_ref[...] = slot
+    slots = owners * capacity
+    move = (iota((slots, rows), 0) == slot).astype(jnp.float32).astype(jnp.bfloat16)
 
     lane = iota((rows, LANES), 1)
     digit = jnp.zeros((rows, LANES), jnp.int32)
@@ -79,11 +80,18 @@
         for place in range(DIGITS):
             digit = jnp.where(lane == first + place, (number >> (8 * place)) & 255, digit)
     digit = digit.astype(jnp.float32).astype(jnp.bfloat16)
-
-    slots = owners * capacity
-    move = (iota((slots, rows), 0) == slot).astype(jnp.float32).astype(jnp.bfloat16)
-    packed_ref[:, :width] = matmul(move, unit).astype(jnp.bfloat16)
-    packed_ref[:, width:] = matmul(move, digit).astype(jnp.bfloat16)
+    moved_digit = matmul(move, digit).astype(jnp.bfloat16)
+
+    copies[3].wait()
+    values = embed_ref[...].astype(jnp.float32)
+    mean_sq = jnp.sum(values * values, axis=1, keepdims=True) * (1.0 / width)
+    unit = (values * lax.rsqrt(width * (mean_sq + 1e-06))).astype(jnp.bfloat16)
+    moved = matmul(move, unit).astype(jnp.bfloat16)
+    each = slots // len(out_refs)
+    for index, out_ref in enumerate(out_refs):
+        part = slice(index * each, (index + 1) * each)
+        out_ref[:, :width] = moved[part]
+        out_ref[:, width:] = moved_digit[part]
 
 
 def window_kernel(rows_all, clus_dev, me_ref, map_ref, query_ref, other_ref, result_ref, cohesion_ref):
@@ -131,28 +139,44 @@
     offset = query.astype(jnp.float32) - centroid[:queries]
     distance = jnp.sum(offset * offset, axis=1, keepdims=True)
     lane = iota((queries, LANES), 1)
-    result = jnp.transpose(jnp.where(lane == 0, best, distance))[: result_ref.shape[1]]
-    for owner in range(result_ref.shape[0]):
-        result_ref[owner] = result
+    result_ref[0] = jnp.transpose(jnp.where(lane == 0, best, distance))[: result_ref.shape[1]]
     centre = centroid[queries:]
     cohesion_ref[...] = as_row(jnp.sum(centre * centre, axis=1, keepdims=True))
 
 
-def pick_kernel(capacity, me_ref, slot_ref, result_ref, best_ref, distance_ref):
+def pick_kernel(order, slot_ref, result_ref, best_ref, distance_ref):
     rows = slot_ref.shape[1]
     owners, _, slots = result_ref.shape
-    slot = as_column(slot_ref[...])
-    best = jnp.zeros((rows, slots), jnp.float32)
-    distance = jnp.zeros((rows, slots), jnp.float32)
-    for owner in range(owners):
-        shift = (me_ref[0] - owner) * capacity
-        first = owner * capacity
-        lane = jnp.where((slot >= first) & (slot < first + capacity), slot + shift, -1)
-        at = lane == iota((rows, slots), 1)
-        best = jnp.where(at, result_ref[owner, 0:1], best)
-        distance = jnp.where(at, result_ref[owner, 1:2], distance)
-    best_ref[...] = as_row(jnp.sum(best, axis=1, keepdims=True))
-    distance_ref[...] = as_row(jnp.sum(distance, axis=1, keepdims=True))
+    place = iota((1, slots), 1) // (slots // owners)
+    at = as_column(slot_ref[...]) == iota((rows, slots), 1)
+    for line, out_ref in enumerate((best_ref, distance_ref)):
+        values = result_ref[0, line : line + 1]
+        for k in range(1, owners):
+            values = jnp.where(place == order.index(k), result_ref[k, line : line + 1], values)
+        out_ref[...] = as_row(jnp.sum(jnp.where(at, values, 0.0), axis=1, keepdims=True))
+
+
+def from_partner(value, k, axis):
+    return lax.ppermute(value, axis, [(i, i ^ k) for i in range(lax.axis_size(axis))])
+
+
+def exchange(blocks, order, me):
+    if len(blocks) > 1:
+        return jnp.concatenate(
+            [from_partner(block, k, "shard") if k else block for k, block in zip(order, blocks)]
+        )
+    owners = lax.axis_size("shard")
+    partner = me ^ jnp.array(order, jnp.int32)
+    place = jnp.argsort(partner)
+    parted = blocks[0].reshape(owners, -1, blocks[0].shape[1])
+    got = lax.all_to_all(parted[place], "shard", 0, 0, tiled=True)
+    return got[partner].reshape(blocks[0].shape)
+
+
+def partner_order(owners):
+    half = owners // 2
+    near, far = list(range(1, half)), list(range(half, owners))
+    return [0] + far[:1] + near[:1] + far[1:] + near[1:]
 
 
 def local(embeddings, cluster_id, item_order, owner_map):
@@ -163,47 +187,49 @@
     capacity = 2 * local_rows // owners
     slots = owners * capacity
     wide = width + LANES
+    params = pltpu.CompilerParams(vmem_limit_bytes=32 << 20)
     me = lax.axis_index("shard").astype(jnp.int32).reshape(1)
     owner_row = owner_map.reshape(1, -1)
 
-    slot, packed = call(
-        functools.partial(pack_kernel, rows_all, owners, capacity),
-        [
-            jax.ShapeDtypeStruct((1, local_rows), jnp.int32),
-            jax.ShapeDtypeStruct((slots, wide), jnp.bfloat16),
-        ],
-        "pack",
-        me,
-        owner_row,
-        cluster_id.reshape(1, -1),
-        item_order.reshape(1, -1),
-        embeddings,
-    )
-    query = lax.all_to_all(
-        packed.reshape(owners, capacity, wide), "shard", 0, 0, tiled=True
-    ).reshape(slots, wide)
-    other = lax.ppermute(query, "sub", [(0, 1), (1, 0)])
-    results, cohesion = call(
+    order = partner_order(owners)
+    parts = owners if owners <= MOST_PERMUTES else 1
+    sources = (owner_row, cluster_id.reshape(1, -1), item_order.reshape(1, -1), embeddings)
+    slot, *packed = pl.pallas_call(
+        functools.partial(pack_kernel, rows_all, owners, capacity, order),
+        out_shape=[jax.ShapeDtypeStruct((1, local_rows), jnp.int32)]
+        + [jax.ShapeDtypeStruct((slots // parts, wide), jnp.bfloat16)] * parts,
+        in_specs=[SCALAR] + [HBM] * 4,
+        out_specs=[WHOLE] * (1 + parts),
+        scratch_shapes=[pltpu.VMEM(x.shape, x.dtype) for x in sources]
+        + [pltpu.SemaphoreType.DMA((4,))],
+        compiler_params=params,
+        name="pack",
+    )(me, *sources)
+    query = exchange(packed, order, me)
+    other = from_partner(query, 1, "sub")
+    results, cohesion = pl.pallas_call(
         functools.partial(window_kernel, rows_all, clus_dev),
-        [
-            jax.ShapeDtypeStruct((owners, 2, slots), jnp.float32),
+        out_shape=[
+            jax.ShapeDtypeStruct((1, 2, slots), jnp.float32),
             jax.ShapeDtypeStruct((1, clus_dev), jnp.float32),
         ],
-        "window",
-        me,
-        owner_row,
-        query,
-        other,
-    )
-    returned = lax.all_to_all(results, "shard", 0, 0, tiled=True)
-    best, distance = call(
-        functools.partial(pick_kernel, capacity),
-        [jax.ShapeDtypeStruct((1, local_rows), jnp.float32)] * 2,
-        "pick",
-        me,
-        slot,
-        returned,
-    )
+        in_specs=[SCALAR] + [WHOLE] * 3,
+        out_specs=[WHOLE] * 2,
+        compiler_params=params,
+        name="window",
+    )(me, owner_row, query, other)
+    k = 1
+    while k < owners:
+        results = jnp.concatenate([results, from_partner(results, k, "shard")])
+        k *= 2
+    best, distance = pl.pallas_call(
+        functools.partial(pick_kernel, order),
+        out_shape=[jax.ShapeDtypeStruct((1, local_rows), jnp.float32)] * 2,
+        in_specs=[WHOLE] * 2,
+        out_specs=[WHOLE] * 2,
+        compiler_params=params,
+        name="pick",
+    )(slot, results)
     return best.reshape(local_rows), distance.reshape(local_rows), cohesion.reshape(clus_dev)
 
 

time: 41 us -> 39 us (0.951)
  blocking collectives: 32.9 us -> 0 us
  starting transfers between devices: 0.01 us -> 19.1 us
  waiting for transfers between devices: 2 us -> 13.5 us
    all_to_all x2 -> x0, blocking collectives: 32.9 us -> none  [the longest x1 23.6 us: local(): lax.all_to_all(packed.reshape(owners, capacity, wide), 'shard', 0, 0, til...]
    ppermute x1 -> x11, starting transfers between devices: 0.01 us -> 19.1 us  [from_partner(): lax.ppermute(value, axis, [(i, i ^ k) for i in range(lax.axis_size(axis))])]
    ppermute x1 -> x11, waiting for transfers between devices: 2 us -> 13.5 us  [from_partner(): lax.ppermute(value, axis, [(i, i ^ k) for i in range(lax.axis_size(axis))])]
    unnamed x8 -> x15, local copies, waits for them, and re-layouts: 1.62 us -> 1.71 us
  transfers between devices with their start and end apart: 1 -> 11, of which waited for: 1 -> 8; matrix products, arithmetic and copies ran while one was open for 0% -> 0% of each run, Pallas kernels for 0% -> 0%
where the time goes in v4:
time: 39 us; the launch traced here: 38.8 us
  starting transfers between devices  19.1 us (49%)
  waiting for transfers between devices  13.5 us (35%)
  Pallas kernels  3.74 us (10%)
  local copies, waits for them, and re-layouts  1.72 us (4%)
  between operations  0.72 us (2%)
    ppermute x11, starting transfers between devices, from_partner(): lax.ppermute(value, axis, [(i, i ^ k) for i in range(lax.axis_size(axis))])  19.1 us
    ppermute x11, waiting for transfers between devices, from_partner(): lax.ppermute(value, axis, [(i, i ^ k) for i in range(lax.axis_size(axis))])  13.5 us
    pallas_call x1, Pallas kernels, local(): pl.pallas_call(functools.partial(window_kernel, rows_all, clus_dev), out_...  1.74 us
    unnamed x15, local copies, waits for them, and re-layouts  1.71 us
    pallas_call x1, Pallas kernels, local(): pl.pallas_call(functools.partial(pack_kernel, rows_all, owners, capacity,...  1.19 us
    pallas_call x1, Pallas kernels, local(): pl.pallas_call(functools.partial(pick_kernel, order), out_shape=[jax.Shap...  0.81 us
  transfers between devices with their start and end apart: 11, of which 8 were waited for; matrix products, arithmetic and copies ran while one was open for 0% of the time, Pallas kernels for 0%

profile of v4, /device:TPU:0, one launch (start us, length us, event | category | flops | bytes accessed | tf_op | source)
XLA Modules:
  0.0 38.8 jit_solution(5439736745766373542)
XLA Ops:
  0.6 0.0 copy-start.3
  0.6 0.0 copy-start.1
  0.7 0.0 copy-start.2
  0.7 0.6 %copy-done.3 = s32[128]{0:T(128)S(1)} copy-done((s32[128]{0:T(128)S(1)}, s32[128]{0:T(128)}, u32[]{:S(2)}) %copy-start.3) | copy-done | bytes 536
  1.3 0.0 copy-done.1
  1.3 0.0 copy-done.2
  1.3 0.0 copy-start
  1.3 0.9 %copy-done = bf16[128,1024]{1,0:T(8,128)(2,1)S(1)} copy-done((bf16[128,1024]{1,0:T(8,128)(2,1)S(1)}, bf16[128,1024]{1,0:T(8,128)(2,1)}, u32[]{:S(2)}) %copy-start) | copy-done | bytes 262168
  2.3 1.2 %pack.1 = (s32[1,128]{1,0:T(1,128)S(1)}, bf16[32,1152]{1,0:T(8,128)(2,1)S(1)}, bf16[32,1152]{1,0:T(8,128)(2,1)S(1)}, bf16[32,1152]{1,0:T(8,128)(2,1)S(1)}, bf16[...) custom-call(s32[1]{0:T(128)} %bitcast.refs_0_.me_ref, ...), custom_call_target="tpu_custom_call" | custom-call | tf_op jit(solution)/shard_map/pack/pallas_call | solution.py:197
  3.5 4.1 %collective-permute-start = (bf16[32,1152]{1,0:T(8,128)(2,1)S(1)}, bf16[32,1152]{1,0:T(8,128)(2,1)S(1)}, u32[]{:S(2)}, u32[]{:S(2)}) collective-permute-start(bf16[32,1152]{1,0:T(8,128)(2,1)S(1)} %get-tuple-element.18), channel_id=1, source_target_pairs={{0,8},{2,10},{4,12},{6,14},{8,0},{10,2},{12,4},{14,6},{1,9},{3,11}... | collective-permute-start | bytes 221192 | tf_op jit(solution)/shard_map/ppermute | solution.py:160
  7.6 1.5 %collective-permute-start.1 = (bf16[32,1152]{1,0:T(8,128)(2,1)S(1)}, bf16[32,1152]{1,0:T(8,128)(2,1)S(1)}, u32[]{:S(2)}, u32[]{:S(2)}) collective-permute-start(bf16[32,1152]{1,0:T(8,128)(2,1)S(1)} %get-tuple-element.19), channel_id=1, source_target_pairs={{0,2},{2,0},{4,6},{6,4},{8,10},{10,8},{12,14},{14,12},{1,3},{3,1},... | collective-permute-start | bytes 221192 | tf_op jit(solution)/shard_map/ppermute | solution.py:160
  9.1 0.1 collective-permute-start.2
  9.1 3.9 %collective-permute-start.3 = (bf16[32,1152]{1,0:T(8,128)(2,1)S(1)}, bf16[32,1152]{1,0:T(8,128)(2,1)S(1)}, u32[]{:S(2)}, u32[]{:S(2)}) collective-permute-start(bf16[32,1152]{1,0:T(8,128)(2,1)S(1)} %get-tuple-element.21), channel_id=1, source_target_pairs={{0,12},{2,14},{4,8},{6,10},{8,4},{10,6},{12,0},{14,2},{1,13},{3,15... | collective-permute-start | bytes 221192 | tf_op jit(solution)/shard_map/ppermute | solution.py:160
  13.0 1.1 %collective-permute-start.4 = (bf16[32,1152]{1,0:T(8,128)(2,1)S(1)}, bf16[32,1152]{1,0:T(8,128)(2,1)S(1)}, u32[]{:S(2)}, u32[]{:S(2)}) collective-permute-start(bf16[32,1152]{1,0:T(8,128)(2,1)S(1)} %get-tuple-element.22), channel_id=1, source_target_pairs={{0,14},{2,12},{4,10},{6,8},{8,6},{10,4},{12,2},{14,0},{1,15},{3,13... | collective-permute-start | bytes 221192 | tf_op jit(solution)/shard_map/ppermute | solution.py:160
  14.1 0.0 collective-permute-done
  14.2 1.4 %collective-permute-start.5 = (bf16[32,1152]{1,0:T(8,128)(2,1)S(1)}, bf16[32,1152]{1,0:T(8,128)(2,1)S(1)}, u32[]{:S(2)}, u32[]{:S(2)}) collective-permute-start(bf16[32,1152]{1,0:T(8,128)(2,1)S(1)} %get-tuple-element.23), channel_id=1, source_target_pairs={{0,4},{2,6},{4,0},{6,2},{8,12},{10,14},{12,8},{14,10},{1,5},{3,7},... | collective-permute-start | bytes 221192 | tf_op jit(solution)/shard_map/ppermute | solution.py:160
  15.5 0.0 collective-permute-done.1
  15.5 1.0 %collective-permute-start.6 = (bf16[32,1152]{1,0:T(8,128)(2,1)S(1)}, bf16[32,1152]{1,0:T(8,128)(2,1)S(1)}, u32[]{:S(2)}, u32[]{:S(2)}) collective-permute-start(bf16[32,1152]{1,0:T(8,128)(2,1)S(1)} %get-tuple-element.24), channel_id=1, source_target_pairs={{0,6},{2,4},{4,2},{6,0},{8,14},{10,12},{12,10},{14,8},{1,7},{3,5},... | collective-permute-start | bytes 221192 | tf_op jit(solution)/shard_map/ppermute | solution.py:160
  16.5 3.4 %collective-permute-done.2 = bf16[32,1152]{1,0:T(8,128)(2,1)S(1)} collective-permute-done((bf16[32,1152]{1,0:T(8,128)(2,1)S(1)}, bf16[32,1152]{1,0:T(8,128)(2,1)S(1)}, u32[]{:S(2)}, u32[]{:S(2)}) %collective-permute-start.2) | collective-permute-done | bytes 73760 | tf_op jit(solution)/shard_map/ppermute | solution.py:160
  19.9 0.0 collective-permute-done.3
  20.0 0.6 %collective-permute-done.4 = bf16[32,1152]{1,0:T(8,128)(2,1)S(1)} collective-permute-done((bf16[32,1152]{1,0:T(8,128)(2,1)S(1)}, bf16[32,1152]{1,0:T(8,128)(2,1)S(1)}, u32[]{:S(2)}, u32[]{:S(2)}) %collective-permute-start.4) | collective-permute-done | bytes 73760 | tf_op jit(solution)/shard_map/ppermute | solution.py:160
  20.6 0.2 collective-permute-done.5
  20.7 1.1 %collective-permute-done.6 = bf16[32,1152]{1,0:T(8,128)(2,1)S(1)} collective-permute-done((bf16[32,1152]{1,0:T(8,128)(2,1)S(1)}, bf16[32,1152]{1,0:T(8,128)(2,1)S(1)}, u32[]{:S(2)}, u32[]{:S(2)}) %collective-permute-start.6) | collective-permute-done | bytes 73760 | tf_op jit(solution)/shard_map/ppermute | solution.py:160
  21.8 0.1 collective-permute-start.7
  21.9 2.0 %collective-permute-done.7.other_ref = bf16[256,1152]{1,0:T(8,128)(2,1)S(1)} collective-permute-done((bf16[256,1152]{1,0:T(8,128)(2,1)S(1)}, bf16[256,1152]{1,0:T(8,128)(2,1)S(1)}, u32[]{:S(2)}, u32[]{:S(2)}) %collective-permute-start.7) | collective-permute-done | bytes 589856 | tf_op jit(solution)/shard_map/ppermute | solution.py:160
  23.9 1.7 %window.1 = (f32[1,2,256]{2,1,0:T(2,128)S(1)}, f32[1,32]{1,0:T(1,128)}) custom-call(s32[1]{0:T(128)} %bitcast.refs_0_.me_ref, s32[1,256]{1,0:T(1,128)S(1)} %bitcast.8, bf16[256,1152]{1,0:T(8,128)(2,1)S(1)} %constant_dynamic-update-slice_fusion.query_ref, bf16[256,1152]{1,0:T(8,128)(2,1)S(1)} %collective-permute-done.7.other_ref), custom_call_target="tpu_custom_call" | custom-call | tf_op jit(solution)/shard_map/window/pallas_call | solution.py:210
  25.6 1.3 %collective-permute-start.8 = (f32[1,2,256]{2,1,0:T(2,128)S(1)}, f32[1,2,256]{2,1,0:T(2,128)S(1)}, u32[]{:S(2)}, u32[]{:S(2)}) collective-permute-start(f32[1,2,256]{2,1,0:T(2,128)S(1)} %get-tuple-element.25), channel_id=1, source_target_pairs={{0,2},{2,0},{4,6},{6,4},{8,10},{10,8},{12,14},{14,12},{1,3},{3,1},... | collective-permute-start | bytes 6152 | tf_op jit(solution)/shard_map/ppermute | solution.py:160
  26.9 2.3 %collective-permute-done.8 = f32[1,2,256]{2,1,0:T(2,128)S(1)} collective-permute-done((f32[1,2,256]{2,1,0:T(2,128)S(1)}, f32[1,2,256]{2,1,0:T(2,128)S(1)}, u32[]{:S(2)}, u32[]{:S(2)}) %collective-permute-start.8) | collective-permute-done | bytes 2080 | tf_op jit(solution)/shard_map/ppermute | solution.py:160
  29.2 1.2 %collective-permute-start.9 = (f32[2,2,256]{2,1,0:T(2,128)S(1)}, f32[2,2,256]{2,1,0:T(2,128)S(1)}, u32[]{:S(2)}, u32[]{:S(2)}) collective-permute-start(f32[2,2,256]{2,1,0:T(2,128)S(1)} %pad_maximum_fusion.2), channel_id=1, source_target_pairs={{0,4},{2,6},{4,0},{6,2},{8,12},{10,14},{12,8},{14,10},{1,5},{3,7},... | collective-permute-start | bytes 12296 | tf_op jit(solution)/shard_map/ppermute | solution.py:160
  30.4 2.4 %collective-permute-done.9 = f32[2,2,256]{2,1,0:T(2,128)S(1)} collective-permute-done((f32[2,2,256]{2,1,0:T(2,128)S(1)}, f32[2,2,256]{2,1,0:T(2,128)S(1)}, u32[]{:S(2)}, u32[]{:S(2)}) %collective-permute-start.9) | collective-permute-done | bytes 4128 | tf_op jit(solution)/shard_map/ppermute | solution.py:160
  32.8 3.5 %collective-permute-start.10 = (f32[4,2,256]{2,1,0:T(2,128)S(1)}, f32[4,2,256]{2,1,0:T(2,128)S(1)}, u32[]{:S(2)}, u32[]{:S(2)}) collective-permute-start(f32[4,2,256]{2,1,0:T(2,128)S(1)} %pad_maximum_fusion.1), channel_id=1, source_target_pairs={{0,8},{2,10},{4,12},{6,14},{8,0},{10,2},{12,4},{14,6},{1,9},{3,11}... | collective-permute-start | bytes 24584 | tf_op jit(solution)/shard_map/ppermute | solution.py:160
  36.3 1.6 %collective-permute-done.10 = f32[4,2,256]{2,1,0:T(2,128)S(1)} collective-permute-done((f32[4,2,256]{2,1,0:T(2,128)S(1)}, f32[4,2,256]{2,1,0:T(2,128)S(1)}, u32[]{:S(2)}, u32[]{:S(2)}) %collective-permute-start.10) | collective-permute-done | bytes 8224 | tf_op jit(solution)/shard_map/ppermute | solution.py:160
  38.0 0.8 %pick.1 = (f32[1,128]{1,0:T(1,128)}, f32[1,128]{1,0:T(1,128)}) custom-call(s32[1,128]{1,0:T(1,128)S(1)} %get-tuple-element.16.slot_ref, f32[8,2,256]{2,1,0:T(2,128)S(1)} %pad_maximum_fusion.result_ref), custom_call_target="tpu_custom_call" | custom-call | tf_op jit(solution)/shard_map/pick/pallas_call | solution.py:225
  (11 shorter events, 0.1 us)
Async XLA Ops:
  0.6 0.7 %copy-start.3 = (s32[128]{0:T(128)S(1)}, s32[128]{0:T(128)}, u32[]{:S(2)}) copy-start(s32[128]{0:T(128)} %param.6) | copy-start | bytes 1540
  0.6 0.7 %copy-start.1 = (s32[256]{0:T(256)S(1)}, s32[256]{0:T(256)}, u32[]{:S(2)}) copy-start(s32[256]{0:T(256)} %param.7) | copy-start | bytes 3076
  0.7 0.7 %copy-start.2 = (s32[128]{0:T(128)S(1)}, s32[128]{0:T(128)}, u32[]{:S(2)}) copy-start(s32[128]{0:T(128)} %param.5) | copy-start | bytes 1540
  1.3 1.0 %copy-start = (bf16[128,1024]{1,0:T(8,128)(2,1)S(1)}, bf16[128,1024]{1,0:T(8,128)(2,1)}, u32[]{:S(2)}) copy-start(bf16[128,1024]{1,0:T(8,128)(2,1)} %refs_4_.1) | copy-start | bytes 786436
  3.5 10.7 %collective-permute-start = (bf16[32,1152]{1,0:T(8,128)(2,1)S(1)}, bf16[32,1152]{1,0:T(8,128)(2,1)S(1)}, u32[]{:S(2)}, u32[]{:S(2)}) collective-permute-start(bf16[32,1152]{1,0:T(8,128)(2,1)S(1)} %get-tuple-element.18), channel_id=1, source_target_pairs={{0,8},{2,10},{4,12},{6,14},{8,0},{10,2},{12,4},{14,6},{1,9},{3,11}... | collective-permute-start | bytes 221192 | tf_op jit(solution)/shard_map/ppermute | solution.py:160
  7.6 7.9 %collective-permute-start.1 = (bf16[32,1152]{1,0:T(8,128)(2,1)S(1)}, bf16[32,1152]{1,0:T(8,128)(2,1)S(1)}, u32[]{:S(2)}, u32[]{:S(2)}) collective-permute-start(bf16[32,1152]{1,0:T(8,128)(2,1)S(1)} %get-tuple-element.19), channel_id=1, source_target_pairs={{0,2},{2,0},{4,6},{6,4},{8,10},{10,8},{12,14},{14,12},{1,3},{3,1},... | collective-permute-start | bytes 221192 | tf_op jit(solution)/shard_map/ppermute | solution.py:160
  9.1 10.9 %collective-permute-start.2 = (bf16[32,1152]{1,0:T(8,128)(2,1)S(1)}, bf16[32,1152]{1,0:T(8,128)(2,1)S(1)}, u32[]{:S(2)}, u32[]{:S(2)}) collective-permute-start(bf16[32,1152]{1,0:T(8,128)(2,1)S(1)} %get-tuple-element.20), channel_id=1, source_target_pairs={{0,10},{2,8},{4,14},{6,12},{8,2},{10,0},{12,6},{14,4},{1,11},{3,9}... | collective-permute-start | bytes 221192 | tf_op jit(solution)/shard_map/ppermute | solution.py:160
  9.1 10.8 %collective-permute-start.3 = (bf16[32,1152]{1,0:T(8,128)(2,1)S(1)}, bf16[32,1152]{1,0:T(8,128)(2,1)S(1)}, u32[]{:S(2)}, u32[]{:S(2)}) collective-permute-start(bf16[32,1152]{1,0:T(8,128)(2,1)S(1)} %get-tuple-element.21), channel_id=1, source_target_pairs={{0,12},{2,14},{4,8},{6,10},{8,4},{10,6},{12,0},{14,2},{1,13},{3,15... | collective-permute-start | bytes 221192 | tf_op jit(solution)/shard_map/ppermute | solution.py:160
  13.0 7.6 %collective-permute-start.4 = (bf16[32,1152]{1,0:T(8,128)(2,1)S(1)}, bf16[32,1152]{1,0:T(8,128)(2,1)S(1)}, u32[]{:S(2)}, u32[]{:S(2)}) collective-permute-start(bf16[32,1152]{1,0:T(8,128)(2,1)S(1)} %get-tuple-element.22), channel_id=1, source_target_pairs={{0,14},{2,12},{4,10},{6,8},{8,6},{10,4},{12,2},{14,0},{1,15},{3,13... | collective-permute-start | bytes 221192 | tf_op jit(solution)/shard_map/ppermute | solution.py:160
  14.2 6.6 %collective-permute-start.5 = (bf16[32,1152]{1,0:T(8,128)(2,1)S(1)}, bf16[32,1152]{1,0:T(8,128)(2,1)S(1)}, u32[]{:S(2)}, u32[]{:S(2)}) collective-permute-start(bf16[32,1152]{1,0:T(8,128)(2,1)S(1)} %get-tuple-element.23), channel_id=1, source_target_pairs={{0,4},{2,6},{4,0},{6,2},{8,12},{10,14},{12,8},{14,10},{1,5},{3,7},... | collective-permute-start | bytes 221192 | tf_op jit(solution)/shard_map/ppermute | solution.py:160
  15.5 6.2 %collective-permute-start.6 = (bf16[32,1152]{1,0:T(8,128)(2,1)S(1)}, bf16[32,1152]{1,0:T(8,128)(2,1)S(1)}, u32[]{:S(2)}, u32[]{:S(2)}) collective-permute-start(bf16[32,1152]{1,0:T(8,128)(2,1)S(1)} %get-tuple-element.24), channel_id=1, source_target_pairs={{0,6},{2,4},{4,2},{6,0},{8,14},{10,12},{12,10},{14,8},{1,7},{3,5},... | collective-permute-start | bytes 221192 | tf_op jit(solution)/shard_map/ppermute | solution.py:160
  21.8 2.1 %collective-permute-start.7 = (bf16[256,1152]{1,0:T(8,128)(2,1)S(1)}, bf16[256,1152]{1,0:T(8,128)(2,1)S(1)}, u32[]{:S(2)}, u32[]{:S(2)}) collective-permute-start(bf16[256,1152]{1,0:T(8,128)(2,1)S(1)} %constant_dynamic-update-slice_fusion.query_ref), channel_id=1, source_target_pairs={{0,1},{1,0},{2,3},{3,2},{4,5},{5,4},{6,7},{7,6},{8,9},{9,8},{10,11... | collective-permute-start | bytes 1769480 | tf_op jit(solution)/shard_map/ppermute | solution.py:160
  25.6 3.6 %collective-permute-start.8 = (f32[1,2,256]{2,1,0:T(2,128)S(1)}, f32[1,2,256]{2,1,0:T(2,128)S(1)}, u32[]{:S(2)}, u32[]{:S(2)}) collective-permute-start(f32[1,2,256]{2,1,0:T(2,128)S(1)} %get-tuple-element.25), channel_id=1, source_target_pairs={{0,2},{2,0},{4,6},{6,4},{8,10},{10,8},{12,14},{14,12},{1,3},{3,1},... | collective-permute-start | bytes 6152 | tf_op jit(solution)/shard_map/ppermute | solution.py:160
  29.2 3.6 %collective-permute-start.9 = (f32[2,2,256]{2,1,0:T(2,128)S(1)}, f32[2,2,256]{2,1,0:T(2,128)S(1)}, u32[]{:S(2)}, u32[]{:S(2)}) collective-permute-start(f32[2,2,256]{2,1,0:T(2,128)S(1)} %pad_maximum_fusion.2), channel_id=1, source_target_pairs={{0,4},{2,6},{4,0},{6,2},{8,12},{10,14},{12,8},{14,10},{1,5},{3,7},... | collective-permute-start | bytes 12296 | tf_op jit(solution)/shard_map/ppermute | solution.py:160
  32.8 5.2 %collective-permute-start.10 = (f32[4,2,256]{2,1,0:T(2,128)S(1)}, f32[4,2,256]{2,1,0:T(2,128)S(1)}, u32[]{:S(2)}, u32[]{:S(2)}) collective-permute-start(f32[4,2,256]{2,1,0:T(2,128)S(1)} %pad_maximum_fusion.1), channel_id=1, source_target_pairs={{0,8},{2,10},{4,12},{6,14},{8,0},{10,2},{12,4},{14,6},{1,9},{3,11}... | collective-permute-start | bytes 24584 | tf_op jit(solution)/shard_map/ppermute | solution.py:160

commit v5 on v4

--- a/solution.py
+++ b/solution.py
@@ -12,7 +12,6 @@
 MOST_PERMUTES = 16
 WHOLE = pl.BlockSpec(memory_space=pltpu.VMEM)
 SCALAR = pl.BlockSpec(memory_space=pltpu.SMEM)
-HBM = pl.BlockSpec(memory_space=pltpu.HBM)
 
 
 def iota(shape, dim):
@@ -42,24 +41,12 @@
     return jnp.concatenate(parts, axis=1)
 
 
-def pack_kernel(rows_all, owners, capacity, order, *refs):
-    me_ref, *sources = refs[:5]
-    slot_ref, *out_refs = refs[5:-5]
-    *held, sems = refs[-5:]
-    copies = [
-        pltpu.make_async_copy(source, target, sems.at[i])
-        for i, (source, target) in enumerate(zip(sources, held))
-    ]
-    for copy in copies:
-        copy.start()
-    map_ref, cluster_ref, order_ref, embed_ref = held
-    rows, width = embed_ref.shape
-    for copy in copies[:3]:
-        copy.wait()
-
+def slot_kernel(
+    owners, capacity, order, me_ref, map_ref, cluster_ref, order_ref, slot_ref, digit_ref
+):
+    rows = cluster_ref.shape[1]
     cluster = as_column(cluster_ref[...])
-    clusters = map_ref.shape[1]
-    named = cluster == iota((rows, clusters), 1)
+    named = cluster == iota((rows, map_ref.shape[1]), 1)
     owner = jnp.sum(jnp.where(named, map_ref[...], 0).astype(jnp.float32), axis=1, keepdims=True)
     owner = owner.astype(jnp.int32)
     hot = (owner == iota((rows, max(owners, LANES)), 1)).astype(jnp.float32)
@@ -69,25 +56,26 @@
     place = partner
     for index, k in enumerate(order):
         place = jnp.where(partner == k, index, place)
-    slot = as_row(place * capacity + rank.astype(jnp.int32))
-    slot_ref[...] = slot
-    slots = owners * capacity
-    move = (iota((slots, rows), 0) == slot).astype(jnp.float32).astype(jnp.bfloat16)
+    slot_ref[...] = as_row(place * capacity + rank.astype(jnp.int32))
 
     lane = iota((rows, LANES), 1)
     digit = jnp.zeros((rows, LANES), jnp.int32)
     for first, number in ((0, cluster + 1), (DIGITS, as_column(order_ref[...]))):
-        for place in range(DIGITS):
-            digit = jnp.where(lane == first + place, (number >> (8 * place)) & 255, digit)
-    digit = digit.astype(jnp.float32).astype(jnp.bfloat16)
-    moved_digit = matmul(move, digit).astype(jnp.bfloat16)
-
-    copies[3].wait()
+        for at in range(DIGITS):
+            digit = jnp.where(lane == first + at, (number >> (8 * at)) & 255, digit)
+    digit_ref[...] = digit.astype(jnp.float32).astype(jnp.bfloat16)
+
+
+def pack_kernel(slot_ref, digit_ref, embed_ref, *out_refs):
+    rows, width = embed_ref.shape
+    each = out_refs[0].shape[0]
     values = embed_ref[...].astype(jnp.float32)
     mean_sq = jnp.sum(values * values, axis=1, keepdims=True) * (1.0 / width)
     unit = (values * lax.rsqrt(width * (mean_sq + 1e-06))).astype(jnp.bfloat16)
+    slots = each * len(out_refs)
+    move = (iota((slots, rows), 0) == slot_ref[...]).astype(jnp.float32).astype(jnp.bfloat16)
     moved = matmul(move, unit).astype(jnp.bfloat16)
-    each = slots // len(out_refs)
+    moved_digit = matmul(move, digit_ref[...]).astype(jnp.bfloat16)
     for index, out_ref in enumerate(out_refs):
         part = slice(index * each, (index + 1) * each)
         out_ref[:, :width] = moved[part]
@@ -144,15 +132,16 @@
     cohesion_ref[...] = as_row(jnp.sum(centre * centre, axis=1, keepdims=True))
 
 
-def pick_kernel(order, slot_ref, result_ref, best_ref, distance_ref):
+def pick_kernel(order, me_ref, slot_ref, result_ref, best_ref, distance_ref):
     rows = slot_ref.shape[1]
     owners, _, slots = result_ref.shape
     place = iota((1, slots), 1) // (slots // owners)
     at = as_column(slot_ref[...]) == iota((rows, slots), 1)
     for line, out_ref in enumerate((best_ref, distance_ref)):
-        values = result_ref[0, line : line + 1]
-        for k in range(1, owners):
-            values = jnp.where(place == order.index(k), result_ref[k, line : line + 1], values)
+        values = result_ref[me_ref[0], line : line + 1]
+        for index in range(1, owners):
+            given = result_ref[me_ref[0] ^ order[index], line : line + 1]
+            values = jnp.where(place == index, given, values)
         out_ref[...] = as_row(jnp.sum(jnp.where(at, values, 0.0), axis=1, keepdims=True))
 
 
@@ -193,18 +182,25 @@
 
     order = partner_order(owners)
     parts = owners if owners <= MOST_PERMUTES else 1
-    sources = (owner_row, cluster_id.reshape(1, -1), item_order.reshape(1, -1), embeddings)
-    slot, *packed = pl.pallas_call(
-        functools.partial(pack_kernel, rows_all, owners, capacity, order),
-        out_shape=[jax.ShapeDtypeStruct((1, local_rows), jnp.int32)]
-        + [jax.ShapeDtypeStruct((slots // parts, wide), jnp.bfloat16)] * parts,
-        in_specs=[SCALAR] + [HBM] * 4,
-        out_specs=[WHOLE] * (1 + parts),
-        scratch_shapes=[pltpu.VMEM(x.shape, x.dtype) for x in sources]
-        + [pltpu.SemaphoreType.DMA((4,))],
+    slot, digit = pl.pallas_call(
+        functools.partial(slot_kernel, owners, capacity, order),
+        out_shape=[
+            jax.ShapeDtypeStruct((1, local_rows), jnp.int32),
+            jax.ShapeDtypeStruct((local_rows, LANES), jnp.bfloat16),
+        ],
+        in_specs=[SCALAR] + [WHOLE] * 3,
+        out_specs=[WHOLE] * 2,
+        compiler_params=params,
+        name="slots",
+    )(me, owner_row, cluster_id.reshape(1, -1), item_order.reshape(1, -1))
+    packed = pl.pallas_call(
+        pack_kernel,
+        out_shape=[jax.ShapeDtypeStruct((slots // parts, wide), jnp.bfloat16)] * parts,
+        in_specs=[WHOLE] * 3,
+        out_specs=[WHOLE] * parts,
         compiler_params=params,
         name="pack",
-    )(me, *sources)
+    )(slot, digit, embeddings)
     query = exchange(packed, order, me)
     other = from_partner(query, 1, "sub")
     results, cohesion = pl.pallas_call(
@@ -218,18 +214,15 @@
         compiler_params=params,
         name="window",
     )(me, owner_row, query, other)
-    k = 1
-    while k < owners:
-        results = jnp.concatenate([results, from_partner(results, k, "shard")])
-        k *= 2
+    results = lax.all_gather(results, "shard", axis=0, tiled=True)
     best, distance = pl.pallas_call(
         functools.partial(pick_kernel, order),
         out_shape=[jax.ShapeDtypeStruct((1, local_rows), jnp.float32)] * 2,
-        in_specs=[WHOLE] * 2,
+        in_specs=[SCALAR] + [WHOLE] * 2,
         out_specs=[WHOLE] * 2,
         compiler_params=params,
         name="pick",
-    )(slot, results)
+    )(me, slot, results)
     return best.reshape(local_rows), distance.reshape(local_rows), cohesion.reshape(clus_dev)
 
 

time: 39 us -> 52.7 us (1.35)
  blocking collectives: 0 us -> 26.3 us
  waiting for transfers between devices: 13.5 us -> 7.14 us
  starting transfers between devices: 19.1 us -> 13.1 us
    all_gather x0 -> x1, blocking collectives: none -> 26.3 us  [local(): results = lax.all_gather(results, 'shard', axis=0, tiled=True)]
    ppermute x11 -> x8, waiting for transfers between devices: 13.5 us -> 7.14 us  [from_partner(): lax.ppermute(value, axis, [(i, i ^ k) for i in range(lax.axis_size(axis))])]
    ppermute x11 -> x8, starting transfers between devices: 19.1 us -> 13.1 us  [from_partner(): lax.ppermute(value, axis, [(i, i ^ k) for i in range(lax.axis_size(axis))])]
    pallas_call x1 -> x2, Pallas kernels: 1.19 us -> 1 us  [the longest x1 0.57 us: local(): pl.pallas_call(functools.partial(slot_kernel, owners, capacity, order), o...]
  transfers between devices with their start and end apart: 11 -> 8, of which waited for: 8 -> 5; matrix products, arithmetic and copies ran while one was open for 0% -> 0% of each run, Pallas kernels for 0% -> 0%
where the time goes in v5:
time: 52.7 us; the launch traced here: 52.6 us
  blocking collectives  26.3 us (50%)
  starting transfers between devices  13.1 us (25%)
  waiting for transfers between devices  7.14 us (14%)
  Pallas kernels  3.55 us (7%)
  local copies, waits for them, and re-layouts  1.73 us (3%)
  between operations  0.71 us (1%)
    all_gather x1, blocking collectives, local(): results = lax.all_gather(results, 'shard', axis=0, tiled=True)  26.3 us
    ppermute x8, starting transfers between devices, from_partner(): lax.ppermute(value, axis, [(i, i ^ k) for i in range(lax.axis_size(axis))])  13.1 us
    ppermute x8, waiting for transfers between devices, from_partner(): lax.ppermute(value, axis, [(i, i ^ k) for i in range(lax.axis_size(axis))])  7.14 us
    pallas_call x1, Pallas kernels, local(): pl.pallas_call(functools.partial(window_kernel, rows_all, clus_dev), out_...  1.74 us
    unnamed x15, local copies, waits for them, and re-layouts  1.72 us
  transfers between devices with their start and end apart: 8, of which 5 were waited for; matrix products, arithmetic and copies ran while one was open for 0% of the time, Pallas kernels for 0%

profile of v5, /device:TPU:0, one launch (start us, length us, event | category | flops | bytes accessed | tf_op | source)
XLA Modules:
  0.0 52.6 jit_solution(16225915900424968706)
XLA Ops:
  0.6 0.0 copy-start.3
  0.6 0.0 copy-start.1
  0.7 0.0 copy-start.2
  0.7 0.6 %copy-done.3 = s32[128]{0:T(128)S(1)} copy-done((s32[128]{0:T(128)S(1)}, s32[128]{0:T(128)}, u32[]{:S(2)}) %copy-start.3) | copy-done | bytes 536
  1.3 0.0 copy-done.1
  1.3 0.0 copy-done.2
  1.3 0.6 %slots.1 = (s32[1,128]{1,0:T(1,128)S(1)}, bf16[128,128]{1,0:T(8,128)(2,1)S(1)}) custom-call(s32[1]{0:T(128)} %bitcast.me_ref, s32[1,256]{1,0:T(1,128)S(1)} %bitcast.7, s32[1,128]{1,0:T(1,128)S(1)} %bitcast.9, s32[1,128]{1,0:T(1,128)S(1)} %bitcast.10), custom_call_target="tpu_custom_call" | custom-call | tf_op jit(solution)/shard_map/slots/pallas_call | solution.py:185
  1.9 0.0 copy-start
  1.9 1.0 %copy-done = bf16[128,1024]{1,0:T(8,128)(2,1)S(1)} copy-done((bf16[128,1024]{1,0:T(8,128)(2,1)S(1)}, bf16[128,1024]{1,0:T(8,128)(2,1)}, u32[]{:S(2)}) %copy-start) | copy-done | bytes 262168
  2.9 0.4 pack.1
  3.3 4.1 %collective-permute-start = (bf16[32,1152]{1,0:T(8,128)(2,1)S(1)}, bf16[32,1152]{1,0:T(8,128)(2,1)S(1)}, u32[]{:S(2)}, u32[]{:S(2)}) collective-permute-start(bf16[32,1152]{1,0:T(8,128)(2,1)S(1)} %get-tuple-element.20), channel_id=1, source_target_pairs={{0,8},{2,10},{4,12},{6,14},{8,0},{10,2},{12,4},{14,6},{1,9},{3,11}... | collective-permute-start | bytes 221192 | tf_op jit(solution)/shard_map/ppermute | solution.py:149
  7.4 1.5 %collective-permute-start.1 = (bf16[32,1152]{1,0:T(8,128)(2,1)S(1)}, bf16[32,1152]{1,0:T(8,128)(2,1)S(1)}, u32[]{:S(2)}, u32[]{:S(2)}) collective-permute-start(bf16[32,1152]{1,0:T(8,128)(2,1)S(1)} %get-tuple-element.21), channel_id=1, source_target_pairs={{0,2},{2,0},{4,6},{6,4},{8,10},{10,8},{12,14},{14,12},{1,3},{3,1},... | collective-permute-start | bytes 221192 | tf_op jit(solution)/shard_map/ppermute | solution.py:149
  8.9 0.0 collective-permute-start.2
  9.0 3.9 %collective-permute-start.3 = (bf16[32,1152]{1,0:T(8,128)(2,1)S(1)}, bf16[32,1152]{1,0:T(8,128)(2,1)S(1)}, u32[]{:S(2)}, u32[]{:S(2)}) collective-permute-start(bf16[32,1152]{1,0:T(8,128)(2,1)S(1)} %get-tuple-element.23), channel_id=1, source_target_pairs={{0,12},{2,14},{4,8},{6,10},{8,4},{10,6},{12,0},{14,2},{1,13},{3,15... | collective-permute-start | bytes 221192 | tf_op jit(solution)/shard_map/ppermute | solution.py:149
  12.8 1.2 %collective-permute-start.4 = (bf16[32,1152]{1,0:T(8,128)(2,1)S(1)}, bf16[32,1152]{1,0:T(8,128)(2,1)S(1)}, u32[]{:S(2)}, u32[]{:S(2)}) collective-permute-start(bf16[32,1152]{1,0:T(8,128)(2,1)S(1)} %get-tuple-element.24), channel_id=1, source_target_pairs={{0,14},{2,12},{4,10},{6,8},{8,6},{10,4},{12,2},{14,0},{1,15},{3,13... | collective-permute-start | bytes 221192 | tf_op jit(solution)/shard_map/ppermute | solution.py:149
  14.0 0.0 collective-permute-done
  14.0 1.4 %collective-permute-start.5 = (bf16[32,1152]{1,0:T(8,128)(2,1)S(1)}, bf16[32,1152]{1,0:T(8,128)(2,1)S(1)}, u32[]{:S(2)}, u32[]{:S(2)}) collective-permute-start(bf16[32,1152]{1,0:T(8,128)(2,1)S(1)} %get-tuple-element.25), channel_id=1, source_target_pairs={{0,4},{2,6},{4,0},{6,2},{8,12},{10,14},{12,8},{14,10},{1,5},{3,7},... | collective-permute-start | bytes 221192 | tf_op jit(solution)/shard_map/ppermute | solution.py:149
  15.3 0.0 collective-permute-done.1
  15.4 1.0 %collective-permute-start.6 = (bf16[32,1152]{1,0:T(8,128)(2,1)S(1)}, bf16[32,1152]{1,0:T(8,128)(2,1)S(1)}, u32[]{:S(2)}, u32[]{:S(2)}) collective-permute-start(bf16[32,1152]{1,0:T(8,128)(2,1)S(1)} %get-tuple-element.26), channel_id=1, source_target_pairs={{0,6},{2,4},{4,2},{6,0},{8,14},{10,12},{12,10},{14,8},{1,7},{3,5},... | collective-permute-start | bytes 221192 | tf_op jit(solution)/shard_map/ppermute | solution.py:149
  16.4 3.4 %collective-permute-done.2 = bf16[32,1152]{1,0:T(8,128)(2,1)S(1)} collective-permute-done((bf16[32,1152]{1,0:T(8,128)(2,1)S(1)}, bf16[32,1152]{1,0:T(8,128)(2,1)S(1)}, u32[]{:S(2)}, u32[]{:S(2)}) %collective-permute-start.2) | collective-permute-done | bytes 73760 | tf_op jit(solution)/shard_map/ppermute | solution.py:149
  19.8 0.0 collective-permute-done.3
  19.8 0.5 %collective-permute-done.4 = bf16[32,1152]{1,0:T(8,128)(2,1)S(1)} collective-permute-done((bf16[32,1152]{1,0:T(8,128)(2,1)S(1)}, bf16[32,1152]{1,0:T(8,128)(2,1)S(1)}, u32[]{:S(2)}, u32[]{:S(2)}) %collective-permute-start.4) | collective-permute-done | bytes 73760 | tf_op jit(solution)/shard_map/ppermute | solution.py:149
  20.4 0.2 collective-permute-done.5
  20.5 1.1 %collective-permute-done.6 = bf16[32,1152]{1,0:T(8,128)(2,1)S(1)} collective-permute-done((bf16[32,1152]{1,0:T(8,128)(2,1)S(1)}, bf16[32,1152]{1,0:T(8,128)(2,1)S(1)}, u32[]{:S(2)}, u32[]{:S(2)}) %collective-permute-start.6) | collective-permute-done | bytes 73760 | tf_op jit(solution)/shard_map/ppermute | solution.py:149
  21.6 0.1 collective-permute-start.7
  21.7 2.0 %collective-permute-done.7.other_ref = bf16[256,1152]{1,0:T(8,128)(2,1)S(1)} collective-permute-done((bf16[256,1152]{1,0:T(8,128)(2,1)S(1)}, bf16[256,1152]{1,0:T(8,128)(2,1)S(1)}, u32[]{:S(2)}, u32[]{:S(2)}) %collective-permute-start.7) | collective-permute-done | bytes 589856 | tf_op jit(solution)/shard_map/ppermute | solution.py:149
  23.7 1.7 %window.1 = (f32[1,2,256]{2,1,0:T(2,128)S(1)}, f32[1,32]{1,0:T(1,128)}) custom-call(s32[1]{0:T(128)} %bitcast.me_ref, s32[1,256]{1,0:T(1,128)S(1)} %bitcast.8, bf16[256,1152]{1,0:T(8,128)(2,1)S(1)} %constant_dynamic-update-slice_fusion.query_ref, bf16[256,1152]{1,0:T(8,128)(2,1)S(1)} %collective-permute-done.7.other_ref), custom_call_target="tpu_custom_call" | custom-call | tf_op jit(solution)/shard_map/window/pallas_call | solution.py:206
  25.4 26.3 %all_gather.3.result_ref = f32[8,2,256]{2,1,0:T(2,128)S(1)} all-gather(f32[1,2,256]{2,1,0:T(2,128)S(1)} %get-tuple-element.27), channel_id=1, replica_groups=mesh['groups'=2,'shard'=8,'sub'=2] {'shard'}, dimensions={0}, use_global_device_ids=true | all-gather | bytes 18432 | tf_op jit(solution)/shard_map/all_gather | solution.py:217
  51.8 0.8 %pick.1 = (f32[1,128]{1,0:T(1,128)}, f32[1,128]{1,0:T(1,128)}) custom-call(s32[1]{0:T(128)} %bitcast.me_ref, s32[1,128]{1,0:T(1,128)S(1)} %get-tuple-element.17.slot_ref, f32[8,2,256]{2,1,0:T(2,128)S(1)} %all_gather.3.result_ref), custom_call_target="tpu_custom_call" | custom-call | tf_op jit(solution)/shard_map/pick/pallas_call | solution.py:218
  (8 shorter events, 0.1 us)
Async XLA Ops:
  0.6 0.7 %copy-start.3 = (s32[128]{0:T(128)S(1)}, s32[128]{0:T(128)}, u32[]{:S(2)}) copy-start(s32[128]{0:T(128)} %param.6) | copy-start | bytes 1540
  0.6 0.7 %copy-start.1 = (s32[256]{0:T(256)S(1)}, s32[256]{0:T(256)}, u32[]{:S(2)}) copy-start(s32[256]{0:T(256)} %param.7) | copy-start | bytes 3076
  0.7 0.7 %copy-start.2 = (s32[128]{0:T(128)S(1)}, s32[128]{0:T(128)}, u32[]{:S(2)}) copy-start(s32[128]{0:T(128)} %param.5) | copy-start | bytes 1540
  1.9 1.0 %copy-start = (bf16[128,1024]{1,0:T(8,128)(2,1)S(1)}, bf16[128,1024]{1,0:T(8,128)(2,1)}, u32[]{:S(2)}) copy-start(bf16[128,1024]{1,0:T(8,128)(2,1)} %embed_ref.1) | copy-start | bytes 786436
  3.3 10.7 %collective-permute-start = (bf16[32,1152]{1,0:T(8,128)(2,1)S(1)}, bf16[32,1152]{1,0:T(8,128)(2,1)S(1)}, u32[]{:S(2)}, u32[]{:S(2)}) collective-permute-start(bf16[32,1152]{1,0:T(8,128)(2,1)S(1)} %get-tuple-element.20), channel_id=1, source_target_pairs={{0,8},{2,10},{4,12},{6,14},{8,0},{10,2},{12,4},{14,6},{1,9},{3,11}... | collective-permute-start | bytes 221192 | tf_op jit(solution)/shard_map/ppermute | solution.py:149
  7.4 7.9 %collective-permute-start.1 = (bf16[32,1152]{1,0:T(8,128)(2,1)S(1)}, bf16[32,1152]{1,0:T(8,128)(2,1)S(1)}, u32[]{:S(2)}, u32[]{:S(2)}) collective-permute-start(bf16[32,1152]{1,0:T(8,128)(2,1)S(1)} %get-tuple-element.21), channel_id=1, source_target_pairs={{0,2},{2,0},{4,6},{6,4},{8,10},{10,8},{12,14},{14,12},{1,3},{3,1},... | collective-permute-start | bytes 221192 | tf_op jit(solution)/shard_map/ppermute | solution.py:149
  8.9 10.9 %collective-permute-start.2 = (bf16[32,1152]{1,0:T(8,128)(2,1)S(1)}, bf16[32,1152]{1,0:T(8,128)(2,1)S(1)}, u32[]{:S(2)}, u32[]{:S(2)}) collective-permute-start(bf16[32,1152]{1,0:T(8,128)(2,1)S(1)} %get-tuple-element.22), channel_id=1, source_target_pairs={{0,10},{2,8},{4,14},{6,12},{8,2},{10,0},{12,6},{14,4},{1,11},{3,9}... | collective-permute-start | bytes 221192 | tf_op jit(solution)/shard_map/ppermute | solution.py:149
  9.0 10.8 %collective-permute-start.3 = (bf16[32,1152]{1,0:T(8,128)(2,1)S(1)}, bf16[32,1152]{1,0:T(8,128)(2,1)S(1)}, u32[]{:S(2)}, u32[]{:S(2)}) collective-permute-start(bf16[32,1152]{1,0:T(8,128)(2,1)S(1)} %get-tuple-element.23), channel_id=1, source_target_pairs={{0,12},{2,14},{4,8},{6,10},{8,4},{10,6},{12,0},{14,2},{1,13},{3,15... | collective-permute-start | bytes 221192 | tf_op jit(solution)/shard_map/ppermute | solution.py:149
  12.8 7.5 %collective-permute-start.4 = (bf16[32,1152]{1,0:T(8,128)(2,1)S(1)}, bf16[32,1152]{1,0:T(8,128)(2,1)S(1)}, u32[]{:S(2)}, u32[]{:S(2)}) collective-permute-start(bf16[32,1152]{1,0:T(8,128)(2,1)S(1)} %get-tuple-element.24), channel_id=1, source_target_pairs={{0,14},{2,12},{4,10},{6,8},{8,6},{10,4},{12,2},{14,0},{1,15},{3,13... | collective-permute-start | bytes 221192 | tf_op jit(solution)/shard_map/ppermute | solution.py:149
  14.0 6.6 %collective-permute-start.5 = (bf16[32,1152]{1,0:T(8,128)(2,1)S(1)}, bf16[32,1152]{1,0:T(8,128)(2,1)S(1)}, u32[]{:S(2)}, u32[]{:S(2)}) collective-permute-start(bf16[32,1152]{1,0:T(8,128)(2,1)S(1)} %get-tuple-element.25), channel_id=1, source_target_pairs={{0,4},{2,6},{4,0},{6,2},{8,12},{10,14},{12,8},{14,10},{1,5},{3,7},... | collective-permute-start | bytes 221192 | tf_op jit(solution)/shard_map/ppermute | solution.py:149
  15.4 6.2 %collective-permute-start.6 = (bf16[32,1152]{1,0:T(8,128)(2,1)S(1)}, bf16[32,1152]{1,0:T(8,128)(2,1)S(1)}, u32[]{:S(2)}, u32[]{:S(2)}) collective-permute-start(bf16[32,1152]{1,0:T(8,128)(2,1)S(1)} %get-tuple-element.26), channel_id=1, source_target_pairs={{0,6},{2,4},{4,2},{6,0},{8,14},{10,12},{12,10},{14,8},{1,7},{3,5},... | collective-permute-start | bytes 221192 | tf_op jit(solution)/shard_map/ppermute | solution.py:149
  21.6 2.1 %collective-permute-start.7 = (bf16[256,1152]{1,0:T(8,128)(2,1)S(1)}, bf16[256,1152]{1,0:T(8,128)(2,1)S(1)}, u32[]{:S(2)}, u32[]{:S(2)}) collective-permute-start(bf16[256,1152]{1,0:T(8,128)(2,1)S(1)} %constant_dynamic-update-slice_fusion.query_ref), channel_id=1, source_target_pairs={{0,1},{1,0},{2,3},{3,2},{4,5},{5,4},{6,7},{7,6},{8,9},{9,8},{10,11... | collective-permute-start | bytes 1769480 | tf_op jit(solution)/shard_map/ppermute | solution.py:149

commit v6 on v5

--- a/solution.py
+++ b/solution.py
@@ -42,12 +42,12 @@
 
 
 def slot_kernel(
-    owners, capacity, order, me_ref, map_ref, cluster_ref, order_ref, slot_ref, digit_ref
+    owners, capacity, order, rows, me_ref, ints_ref, slot_ref, digit_ref
 ):
-    rows = cluster_ref.shape[1]
-    cluster = as_column(cluster_ref[...])
-    named = cluster == iota((rows, map_ref.shape[1]), 1)
-    owner = jnp.sum(jnp.where(named, map_ref[...], 0).astype(jnp.float32), axis=1, keepdims=True)
+    clusters = ints_ref.shape[1] - 2 * rows
+    cluster = as_column(ints_ref[:, clusters : clusters + rows])
+    named = cluster == iota((rows, clusters), 1)
+    owner = jnp.sum(jnp.where(named, ints_ref[:, :clusters], 0).astype(jnp.float32), axis=1, keepdims=True)
     owner = owner.astype(jnp.int32)
     hot = (owner == iota((rows, max(owners, LANES)), 1)).astype(jnp.float32)
     upto = (iota((rows, rows), 1) <= iota((rows, rows), 0)).astype(jnp.bfloat16)
@@ -60,7 +60,7 @@
 
     lane = iota((rows, LANES), 1)
     digit = jnp.zeros((rows, LANES), jnp.int32)
-    for first, number in ((0, cluster + 1), (DIGITS, as_column(order_ref[...]))):
+    for first, number in ((0, cluster + 1), (DIGITS, as_column(ints_ref[:, clusters + rows :]))):
         for at in range(DIGITS):
             digit = jnp.where(lane == first + at, (number >> (8 * at)) & 255, digit)
     digit_ref[...] = digit.astype(jnp.float32).astype(jnp.bfloat16)
@@ -82,52 +82,75 @@
         out_ref[:, width:] = moved_digit[part]
 
 
-def window_kernel(rows_all, clus_dev, me_ref, map_ref, query_ref, other_ref, result_ref, cohesion_ref):
+def key_numbers(take):
+    name, order = (
+        sum(take(i + at) * (256.0**at) for at in range(DIGITS)).astype(jnp.int32)
+        for i in (0, DIGITS)
+    )
+    return name - 1, order
+
+
+def compare(rows_all, query, query_key, lows, rows_ref):
+    queries, width = query.shape
+    rows = rows_ref[:, :width]
+    across = jnp.transpose(rows_ref[:, width:].astype(jnp.float32))
+    name, order = key_numbers(lambda i: across[i : i + 1])
+    keys = name * rows_all + order
+    above = keys >= lows
+    member = (above & (keys < lows + rows_all)).astype(jnp.float32)
+    counts = jnp.sum(member, axis=1, keepdims=True)
+    sums = matmul(member.astype(jnp.bfloat16), rows)
+    scores = lax.dot_general(
+        query, rows, (((1,), (1,)), ((), ())), preferred_element_type=jnp.float32
+    )
+    earlier = above[:queries] & (keys < query_key)
+    best = jnp.max(jnp.where(earlier, scores, -3.0), axis=1, keepdims=True)
+    return best, counts, sums
+
+
+def near_kernel(
+    rows_all, clusters, clus_dev, me_ref, ints_ref, query_ref, column_ref, number_ref, sums_ref
+):
     queries = query_ref.shape[0]
     width = query_ref.shape[1] - LANES
-    query = query_ref[:, :width]
-
-    def numbers(take):
-        return (
-            sum(take(i + place) * (256.0**place) for place in range(DIGITS)).astype(jnp.int32)
-            for i in (0, DIGITS)
-        )
-
-    hot = (map_ref[...] == me_ref[0]).astype(jnp.float32)
+    hot = (ints_ref[:, :clusters] == me_ref[0]).astype(jnp.float32)
     rank = ranked(hot)
     shape = (clus_dev, hot.shape[1])
     kth = (rank == iota(shape, 0).astype(jnp.float32) + 1.0) & (hot > 0.0)
     own = jnp.sum(jnp.where(kth, iota(shape, 1).astype(jnp.float32), 0.0), axis=1, keepdims=True)
     digit = query_ref[:, width:].astype(jnp.float32)
-    name, order = numbers(lambda i: digit[:, i : i + 1])
-    low = (name - 1) * rows_all
-    query_key = low + order
+    name, order = key_numbers(lambda i: digit[:, i : i + 1])
+    low = name * rows_all
     lows = jnp.concatenate([low, own.astype(jnp.int32) * rows_all], axis=0)
-
-    best, counts, sums = None, None, None
-    for rows_ref in (query_ref, other_ref):
-        rows = rows_ref[:, :width]
-        across = jnp.transpose(rows_ref[:, width:].astype(jnp.float32))
-        name, order = numbers(lambda i: across[i : i + 1])
-        keys = (name - 1) * rows_all + order
-        above = keys >= lows
-        member = (above & (keys < lows + rows_all)).astype(jnp.float32)
-        count = jnp.sum(member, axis=1, keepdims=True)
-        total = matmul(member.astype(jnp.bfloat16), rows)
-        scores = lax.dot_general(
-            query, rows, (((1,), (1,)), ((), ())), preferred_element_type=jnp.float32
-        )
-        earlier = above[:queries] & (keys < query_key)
-        most = jnp.max(jnp.where(earlier, scores, -3.0), axis=1, keepdims=True)
-        best = most if best is None else jnp.maximum(best, most)
-        counts = count if counts is None else counts + count
-        sums = total if sums is None else sums + total
-    centroid = sums * (1.0 / jnp.maximum(counts, 1.0))
+    best, counts, sums = compare(rows_all, query_ref[:, :width], low + order, lows, query_ref)
+    count = counts.shape[0]
+    lane = iota((count, LANES), 1)
+    best = jnp.concatenate([best, jnp.zeros((clus_dev, 1), jnp.float32)], axis=0)
+    order = jnp.concatenate([order, jnp.zeros((clus_dev, 1), jnp.int32)], axis=0)
+    column_ref[...] = jnp.where(lane == 0, best, counts)
+    number_ref[...] = jnp.where(lane == 0, lows, order)
+    sums_ref[...] = sums
+
+
+def far_kernel(
+    rows_all, query_ref, other_ref, column_ref, number_ref, sums_ref, result_ref, cohesion_ref
+):
+    queries = query_ref.shape[0]
+    width = query_ref.shape[1] - LANES
+    query = query_ref[:, :width]
+    lows = number_ref[:, 0:1]
+    query_key = lows[:queries] + number_ref[:queries, 1:2]
+    best, counts, sums = compare(rows_all, query, query_key, lows, other_ref)
+    best = jnp.maximum(best, column_ref[:queries, 0:1])
+    counts = counts + column_ref[:, 1:2]
+    centroid = (sums + sums_ref[...]) * (1.0 / jnp.maximum(counts, 1.0))
     best = jnp.where(best > -2.0, best, 0.0)
     offset = query.astype(jnp.float32) - centroid[:queries]
     distance = jnp.sum(offset * offset, axis=1, keepdims=True)
     lane = iota((queries, LANES), 1)
-    result_ref[0] = jnp.transpose(jnp.where(lane == 0, best, distance))[: result_ref.shape[1]]
+    result = jnp.transpose(jnp.where(lane == 0, best, distance))[: result_ref.shape[1]]
+    for owner in range(result_ref.shape[0]):
+        result_ref[owner] = result
     centre = centroid[queries:]
     cohesion_ref[...] = as_row(jnp.sum(centre * centre, axis=1, keepdims=True))
 
@@ -177,22 +200,26 @@
     slots = owners * capacity
     wide = width + LANES
     params = pltpu.CompilerParams(vmem_limit_bytes=32 << 20)
+    compare_cost = pl.CostEstimate(
+        flops=4 * slots * slots * width, bytes_accessed=4 * slots * wide, transcendentals=0
+    )
     me = lax.axis_index("shard").astype(jnp.int32).reshape(1)
-    owner_row = owner_map.reshape(1, -1)
+    ints = jnp.concatenate([owner_map, cluster_id, item_order]).reshape(1, -1)
 
     order = partner_order(owners)
     parts = owners if owners <= MOST_PERMUTES else 1
     slot, digit = pl.pallas_call(
-        functools.partial(slot_kernel, owners, capacity, order),
+        functools.partial(slot_kernel, owners, capacity, order, local_rows),
         out_shape=[
             jax.ShapeDtypeStruct((1, local_rows), jnp.int32),
             jax.ShapeDtypeStruct((local_rows, LANES), jnp.bfloat16),
         ],
-        in_specs=[SCALAR] + [WHOLE] * 3,
+        in_specs=[SCALAR, WHOLE],
         out_specs=[WHOLE] * 2,
         compiler_params=params,
+        cost_estimate=pl.CostEstimate(flops=1 << 28, bytes_accessed=1 << 16, transcendentals=0),
         name="slots",
-    )(me, owner_row, cluster_id.reshape(1, -1), item_order.reshape(1, -1))
+    )(me, ints)
     packed = pl.pallas_call(
         pack_kernel,
         out_shape=[jax.ShapeDtypeStruct((slots // parts, wide), jnp.bfloat16)] * parts,
@@ -203,18 +230,33 @@
     )(slot, digit, embeddings)
     query = exchange(packed, order, me)
     other = from_partner(query, 1, "sub")
+    asked = slots + clus_dev
+    near = pl.pallas_call(
+        functools.partial(near_kernel, rows_all, owner_map.shape[0], clus_dev),
+        out_shape=[
+            jax.ShapeDtypeStruct((asked, LANES), jnp.float32),
+            jax.ShapeDtypeStruct((asked, LANES), jnp.int32),
+            jax.ShapeDtypeStruct((asked, width), jnp.float32),
+        ],
+        in_specs=[SCALAR] + [WHOLE] * 2,
+        out_specs=[WHOLE] * 3,
+        compiler_params=params,
+        cost_estimate=compare_cost,
+        name="near",
+    )(me, ints, query)
     results, cohesion = pl.pallas_call(
-        functools.partial(window_kernel, rows_all, clus_dev),
+        functools.partial(far_kernel, rows_all),
         out_shape=[
-            jax.ShapeDtypeStruct((1, 2, slots), jnp.float32),
+            jax.ShapeDtypeStruct((owners, 2, slots), jnp.float32),
             jax.ShapeDtypeStruct((1, clus_dev), jnp.float32),
         ],
-        in_specs=[SCALAR] + [WHOLE] * 3,
+        in_specs=[WHOLE] * 5,
         out_specs=[WHOLE] * 2,
         compiler_params=params,
-        name="window",
-    )(me, owner_row, query, other)
-    results = lax.all_gather(results, "shard", axis=0, tiled=True)
+        cost_estimate=compare_cost,
+        name="far",
+    )(query, other, *near)
+    results = lax.all_to_all(results, "shard", 0, 0, tiled=True)
     best, distance = pl.pallas_call(
         functools.partial(pick_kernel, order),
         out_shape=[jax.ShapeDtypeStruct((1, local_rows), jnp.float32)] * 2,

time: 52.7 us -> 36.6 us (0.69)
  blocking collectives: 26.3 us -> 11.2 us
  local copies, waits for them, and re-layouts: 1.73 us -> 0.1 us
  waiting for transfers between devices: 7.14 us -> 6.23 us
  Pallas kernels: 3.55 us -> 4.34 us
  other arithmetic: 0 us -> 0.76 us
    all_gather x1 -> x0, blocking collectives: 26.3 us -> none  [local(): results = lax.all_gather(results, 'shard', axis=0, tiled=True)]
    all_to_all x0 -> x1, blocking collectives: none -> 11.2 us  [local(): results = lax.all_to_all(results, 'shard', 0, 0, tiled=True)]
    unnamed x15 -> x9, local copies, waits for them, and re-layouts: 1.72 us -> 0.09 us
    ppermute x8, waiting for transfers between devices: 7.14 us -> 6.23 us  [from_partner(): lax.ppermute(value, axis, [(i, i ^ k) for i in range(lax.axis_size(axis))])]
    pallas_call x2 -> x3, Pallas kernels: 2.31 us -> 3.08 us  [the longest x1 1.59 us: local(): pl.pallas_call(functools.partial(far_kernel, rows_all), out_shape=[jax.Sh...]
    concatenate x0 -> x1, other arithmetic: none -> 0.76 us  [local(): ints = jnp.concatenate([owner_map, cluster_id, item_order]).reshape(1, -1)]
  transfers between devices with their start and end apart: 8 -> 8, of which waited for: 5 -> 5; matrix products, arithmetic and copies ran while one was open for 0% -> 0% of each run, Pallas kernels for 0% -> 3%
where the time goes in v6:
time: 36.6 us; the launch traced here: 36.5 us
  starting transfers between devices  13.1 us (36%)
  blocking collectives  11.2 us (31%)
  waiting for transfers between devices  6.23 us (17%)
  Pallas kernels  4.34 us (12%)
  other arithmetic  0.76 us (2%)
  between operations  0.7 us (2%)
    ppermute x8, starting transfers between devices, from_partner(): lax.ppermute(value, axis, [(i, i ^ k) for i in range(lax.axis_size(axis))])  13.1 us
    all_to_all x1, blocking collectives, local(): results = lax.all_to_all(results, 'shard', 0, 0, tiled=True)  11.2 us
    ppermute x8, waiting for transfers between devices, from_partner(): lax.ppermute(value, axis, [(i, i ^ k) for i in range(lax.axis_size(axis))])  6.23 us
    pallas_call x1, Pallas kernels, local(): pl.pallas_call(functools.partial(far_kernel, rows_all), out_shape=[jax.Sh...  1.59 us
    pallas_call x1, Pallas kernels, local(): pl.pallas_call(functools.partial(near_kernel, rows_all, owner_map.shape[0...  0.92 us
    pallas_call x1, Pallas kernels, local(): pl.pallas_call(functools.partial(pick_kernel, order), out_shape=[jax.Shap...  0.81 us
    concatenate x1, other arithmetic, local(): ints = jnp.concatenate([owner_map, cluster_id, item_order]).reshape(1, -1)  0.76 us
  transfers between devices with their start and end apart: 8, of which 5 were waited for; matrix products, arithmetic and copies ran while one was open for 0% of the time, Pallas kernels for 3%

profile of v6, /device:TPU:0, one launch (start us, length us, event | category | flops | bytes accessed | tf_op | source)
XLA Modules:
  0.0 36.5 jit_solution(5903923615676230236)
XLA Ops:
  0.6 0.0 copy-start
  0.6 0.8 %pad_add_fusion = s32[512]{0:T(512)S(1)} fusion(s32[128]{0:T(128)} %param.6, s32[128]{0:T(128)} %param.5, s32[256]{0:T(256)} %param.7), kind=kLoop, calls=%fused_computation.8 | loop fusion | flops 1024 | bytes 4096 | tf_op jit(solution)/shard_map/concatenate | solution.py:207
  1.4 0.6 %slots.1 = (s32[1,128]{1,0:T(1,128)S(1)}, bf16[128,128]{1,0:T(8,128)(2,1)S(1)}) custom-call(s32[1]{0:T(128)} %bitcast.me_ref, s32[1,512]{1,0:T(1,128)S(1)} %bitcast.5), custom_call_target="tpu_custom_call" | custom-call | flops 268435456 | bytes 65536 | tf_op jit(solution)/shard_map/slots/pallas_call | solution.py:211
  2.0 0.0 copy-done
  2.0 0.4 %pack.1 = (bf16[32,1152]{1,0:T(8,128)(2,1)S(1)}, bf16[32,1152]{1,0:T(8,128)(2,1)S(1)}, bf16[32,1152]{1,0:T(8,128)(2,1)S(1)}, bf16[32,1152]{1,0:T(8,128)(2,1)S(1)...) custom-call(s32[1,128]{1,0:T(1,128)S(1)} %get-tuple-element.20.slot_, ...), custom_call_target="tpu_custom_call" | custom-call | tf_op jit(solution)/shard_map/pack/pallas_call | solution.py:223
  2.4 4.1 %collective-permute-start = (bf16[32,1152]{1,0:T(8,128)(2,1)S(1)}, bf16[32,1152]{1,0:T(8,128)(2,1)S(1)}, u32[]{:S(2)}, u32[]{:S(2)}) collective-permute-start(bf16[32,1152]{1,0:T(8,128)(2,1)S(1)} %get-tuple-element.23), channel_id=1, source_target_pairs={{0,8},{2,10},{4,12},{6,14},{8,0},{10,2},{12,4},{14,6},{1,9},{3,11}... | collective-permute-start | bytes 221192 | tf_op jit(solution)/shard_map/ppermute | solution.py:172
  6.5 1.5 %collective-permute-start.1 = (bf16[32,1152]{1,0:T(8,128)(2,1)S(1)}, bf16[32,1152]{1,0:T(8,128)(2,1)S(1)}, u32[]{:S(2)}, u32[]{:S(2)}) collective-permute-start(bf16[32,1152]{1,0:T(8,128)(2,1)S(1)} %get-tuple-element.24), channel_id=1, source_target_pairs={{0,2},{2,0},{4,6},{6,4},{8,10},{10,8},{12,14},{14,12},{1,3},{3,1},... | collective-permute-start | bytes 221192 | tf_op jit(solution)/shard_map/ppermute | solution.py:172
  8.0 0.1 collective-permute-start.2
  8.1 3.9 %collective-permute-start.3 = (bf16[32,1152]{1,0:T(8,128)(2,1)S(1)}, bf16[32,1152]{1,0:T(8,128)(2,1)S(1)}, u32[]{:S(2)}, u32[]{:S(2)}) collective-permute-start(bf16[32,1152]{1,0:T(8,128)(2,1)S(1)} %get-tuple-element.26), channel_id=1, source_target_pairs={{0,12},{2,14},{4,8},{6,10},{8,4},{10,6},{12,0},{14,2},{1,13},{3,15... | collective-permute-start | bytes 221192 | tf_op jit(solution)/shard_map/ppermute | solution.py:172
  11.9 1.1 %collective-permute-start.4 = (bf16[32,1152]{1,0:T(8,128)(2,1)S(1)}, bf16[32,1152]{1,0:T(8,128)(2,1)S(1)}, u32[]{:S(2)}, u32[]{:S(2)}) collective-permute-start(bf16[32,1152]{1,0:T(8,128)(2,1)S(1)} %get-tuple-element.27), channel_id=1, source_target_pairs={{0,14},{2,12},{4,10},{6,8},{8,6},{10,4},{12,2},{14,0},{1,15},{3,13... | collective-permute-start | bytes 221192 | tf_op jit(solution)/shard_map/ppermute | solution.py:172
  13.1 0.0 collective-permute-done
  13.1 1.4 %collective-permute-start.5 = (bf16[32,1152]{1,0:T(8,128)(2,1)S(1)}, bf16[32,1152]{1,0:T(8,128)(2,1)S(1)}, u32[]{:S(2)}, u32[]{:S(2)}) collective-permute-start(bf16[32,1152]{1,0:T(8,128)(2,1)S(1)} %get-tuple-element.28), channel_id=1, source_target_pairs={{0,4},{2,6},{4,0},{6,2},{8,12},{10,14},{12,8},{14,10},{1,5},{3,7},... | collective-permute-start | bytes 221192 | tf_op jit(solution)/shard_map/ppermute | solution.py:172
  14.5 0.0 collective-permute-done.1
  14.5 1.0 %collective-permute-start.6 = (bf16[32,1152]{1,0:T(8,128)(2,1)S(1)}, bf16[32,1152]{1,0:T(8,128)(2,1)S(1)}, u32[]{:S(2)}, u32[]{:S(2)}) collective-permute-start(bf16[32,1152]{1,0:T(8,128)(2,1)S(1)} %get-tuple-element.29), channel_id=1, source_target_pairs={{0,6},{2,4},{4,2},{6,0},{8,14},{10,12},{12,10},{14,8},{1,7},{3,5},... | collective-permute-start | bytes 221192 | tf_op jit(solution)/shard_map/ppermute | solution.py:172
  15.5 3.4 %collective-permute-done.2 = bf16[32,1152]{1,0:T(8,128)(2,1)S(1)} collective-permute-done((bf16[32,1152]{1,0:T(8,128)(2,1)S(1)}, bf16[32,1152]{1,0:T(8,128)(2,1)S(1)}, u32[]{:S(2)}, u32[]{:S(2)}) %collective-permute-start.2) | collective-permute-done | bytes 73760 | tf_op jit(solution)/shard_map/ppermute | solution.py:172
  18.9 0.0 collective-permute-done.3
  18.9 0.6 %collective-permute-done.4 = bf16[32,1152]{1,0:T(8,128)(2,1)S(1)} collective-permute-done((bf16[32,1152]{1,0:T(8,128)(2,1)S(1)}, bf16[32,1152]{1,0:T(8,128)(2,1)S(1)}, u32[]{:S(2)}, u32[]{:S(2)}) %collective-permute-start.4) | collective-permute-done | bytes 73760 | tf_op jit(solution)/shard_map/ppermute | solution.py:172
  19.5 0.2 collective-permute-done.5
  19.7 1.1 %collective-permute-done.6 = bf16[32,1152]{1,0:T(8,128)(2,1)S(1)} collective-permute-done((bf16[32,1152]{1,0:T(8,128)(2,1)S(1)}, bf16[32,1152]{1,0:T(8,128)(2,1)S(1)}, u32[]{:S(2)}, u32[]{:S(2)}) %collective-permute-start.6) | collective-permute-done | bytes 73760 | tf_op jit(solution)/shard_map/ppermute | solution.py:172
  20.7 0.1 collective-permute-start.7
  20.8 0.9 %near.1 = (f32[288,128]{1,0:T(8,128)S(1)}, s32[288,128]{1,0:T(8,128)S(1)}, f32[288,1024]{1,0:T(8,128)S(1)}) custom-call(s32[1]{0:T(128)} %bitcast.me_ref, s32[1,512]{1,0:T(1,128)S(1)} %bitcast.6, bf16[256,1152]{1,0:T(8,128)(2,1)S(1)} %constant_dynamic-update-slice_fusion.query_ref), custom_call_target="tpu_custom_call" | custom-call | flops 268435456 | bytes 1179648 | tf_op jit(solution)/shard_map/near/pallas_call | solution.py:234
  21.7 1.1 %collective-permute-done.7.other_ref = bf16[256,1152]{1,0:T(8,128)(2,1)S(1)} collective-permute-done((bf16[256,1152]{1,0:T(8,128)(2,1)S(1)}, bf16[256,1152]{1,0:T(8,128)(2,1)S(1)}, u32[]{:S(2)}, u32[]{:S(2)}) %collective-permute-start.7) | collective-permute-done | bytes 589856 | tf_op jit(solution)/shard_map/ppermute | solution.py:172
  22.8 1.6 %far.1 = (f32[8,2,256]{2,1,0:T(2,128)S(1)}, f32[1,32]{1,0:T(1,128)}) custom-call(bf16[256,1152]{1,0:T(8,128)(2,1)S(1)} %constant_dynamic-update-slice_fusion.query_ref, bf16[256,1152]{1,0:T(8,128)(2,1)S(1)} %collective-permute-done.7.other_ref, f32[288,128]{1,0:T(8,128)S(1)} %get-tuple-element.30.column_ref, s32[288,128]{1,0:T(8,128)S(1)} %get-tuple-element.31.number_ref, ...), custom_call_target="tpu_custom_call" | custom-call | flops 268435456 | bytes 1179648 | tf_op jit(solution)/shard_map/far/pallas_call | solution.py:247
  24.4 11.2 %all_to_all.5.result_ref = f32[8,2,256]{2,1,0:T(2,128)S(1)} all-to-all(f32[8,2,256]{2,1,0:T(2,128)S(1)} %get-tuple-element.33), channel_id=1, replica_groups=mesh['groups'=2,'shard'=8,'sub'=2] {'shard'}, dimensions={0} | all-to-all | bytes 32768 | tf_op jit(solution)/shard_map/all_to_all | solution.py:259
  35.6 0.8 %pick.1 = (f32[1,128]{1,0:T(1,128)}, f32[1,128]{1,0:T(1,128)}) custom-call(s32[1]{0:T(128)} %bitcast.me_ref, s32[1,128]{1,0:T(1,128)S(1)} %get-tuple-element.20.slot_ref, f32[8,2,256]{2,1,0:T(2,128)S(1)} %all_to_all.5.result_ref), custom_call_target="tpu_custom_call" | custom-call | tf_op jit(solution)/shard_map/pick/pallas_call | solution.py:260
  (8 shorter events, 0.1 us)
Async XLA Ops:
  0.6 1.4 %copy-start = (bf16[128,1024]{1,0:T(8,128)(2,1)S(1)}, bf16[128,1024]{1,0:T(8,128)(2,1)}, u32[]{:S(2)}) copy-start(bf16[128,1024]{1,0:T(8,128)(2,1)} %embed_ref.1) | copy-start | bytes 786436
  2.4 10.7 %collective-permute-start = (bf16[32,1152]{1,0:T(8,128)(2,1)S(1)}, bf16[32,1152]{1,0:T(8,128)(2,1)S(1)}, u32[]{:S(2)}, u32[]{:S(2)}) collective-permute-start(bf16[32,1152]{1,0:T(8,128)(2,1)S(1)} %get-tuple-element.23), channel_id=1, source_target_pairs={{0,8},{2,10},{4,12},{6,14},{8,0},{10,2},{12,4},{14,6},{1,9},{3,11}... | collective-permute-start | bytes 221192 | tf_op jit(solution)/shard_map/ppermute | solution.py:172
  6.5 7.9 %collective-permute-start.1 = (bf16[32,1152]{1,0:T(8,128)(2,1)S(1)}, bf16[32,1152]{1,0:T(8,128)(2,1)S(1)}, u32[]{:S(2)}, u32[]{:S(2)}) collective-permute-start(bf16[32,1152]{1,0:T(8,128)(2,1)S(1)} %get-tuple-element.24), channel_id=1, source_target_pairs={{0,2},{2,0},{4,6},{6,4},{8,10},{10,8},{12,14},{14,12},{1,3},{3,1},... | collective-permute-start | bytes 221192 | tf_op jit(solution)/shard_map/ppermute | solution.py:172
  8.0 10.9 %collective-permute-start.2 = (bf16[32,1152]{1,0:T(8,128)(2,1)S(1)}, bf16[32,1152]{1,0:T(8,128)(2,1)S(1)}, u32[]{:S(2)}, u32[]{:S(2)}) collective-permute-start(bf16[32,1152]{1,0:T(8,128)(2,1)S(1)} %get-tuple-element.25), channel_id=1, source_target_pairs={{0,10},{2,8},{4,14},{6,12},{8,2},{10,0},{12,6},{14,4},{1,11},{3,9}... | collective-permute-start | bytes 221192 | tf_op jit(solution)/shard_map/ppermute | solution.py:172
  8.1 10.8 %collective-permute-start.3 = (bf16[32,1152]{1,0:T(8,128)(2,1)S(1)}, bf16[32,1152]{1,0:T(8,128)(2,1)S(1)}, u32[]{:S(2)}, u32[]{:S(2)}) collective-permute-start(bf16[32,1152]{1,0:T(8,128)(2,1)S(1)} %get-tuple-element.26), channel_id=1, source_target_pairs={{0,12},{2,14},{4,8},{6,10},{8,4},{10,6},{12,0},{14,2},{1,13},{3,15... | collective-permute-start | bytes 221192 | tf_op jit(solution)/shard_map/ppermute | solution.py:172
  11.9 7.6 %collective-permute-start.4 = (bf16[32,1152]{1,0:T(8,128)(2,1)S(1)}, bf16[32,1152]{1,0:T(8,128)(2,1)S(1)}, u32[]{:S(2)}, u32[]{:S(2)}) collective-permute-start(bf16[32,1152]{1,0:T(8,128)(2,1)S(1)} %get-tuple-element.27), channel_id=1, source_target_pairs={{0,14},{2,12},{4,10},{6,8},{8,6},{10,4},{12,2},{14,0},{1,15},{3,13... | collective-permute-start | bytes 221192 | tf_op jit(solution)/shard_map/ppermute | solution.py:172
  13.1 6.6 %collective-permute-start.5 = (bf16[32,1152]{1,0:T(8,128)(2,1)S(1)}, bf16[32,1152]{1,0:T(8,128)(2,1)S(1)}, u32[]{:S(2)}, u32[]{:S(2)}) collective-permute-start(bf16[32,1152]{1,0:T(8,128)(2,1)S(1)} %get-tuple-element.28), channel_id=1, source_target_pairs={{0,4},{2,6},{4,0},{6,2},{8,12},{10,14},{12,8},{14,10},{1,5},{3,7},... | collective-permute-start | bytes 221192 | tf_op jit(solution)/shard_map/ppermute | solution.py:172
  14.5 6.2 %collective-permute-start.6 = (bf16[32,1152]{1,0:T(8,128)(2,1)S(1)}, bf16[32,1152]{1,0:T(8,128)(2,1)S(1)}, u32[]{:S(2)}, u32[]{:S(2)}) collective-permute-start(bf16[32,1152]{1,0:T(8,128)(2,1)S(1)} %get-tuple-element.29), channel_id=1, source_target_pairs={{0,6},{2,4},{4,2},{6,0},{8,14},{10,12},{12,10},{14,8},{1,7},{3,5},... | collective-permute-start | bytes 221192 | tf_op jit(solution)/shard_map/ppermute | solution.py:172
  20.7 2.1 %collective-permute-start.7 = (bf16[256,1152]{1,0:T(8,128)(2,1)S(1)}, bf16[256,1152]{1,0:T(8,128)(2,1)S(1)}, u32[]{:S(2)}, u32[]{:S(2)}) collective-permute-start(bf16[256,1152]{1,0:T(8,128)(2,1)S(1)} %constant_dynamic-update-slice_fusion.query_ref), channel_id=1, source_target_pairs={{0,1},{1,0},{2,3},{3,2},{4,5},{5,4},{6,7},{7,6},{8,9},{9,8},{10,11... | collective-permute-start | bytes 1769480 | tf_op jit(solution)/shard_map/ppermute | solution.py:172

commit v7 on v6

--- a/solution.py
+++ b/solution.py
@@ -9,7 +9,7 @@
 
 LANES = 128
 DIGITS = 3
-MOST_PERMUTES = 16
+MOST_PERMUTES = 8
 WHOLE = pl.BlockSpec(memory_space=pltpu.VMEM)
 SCALAR = pl.BlockSpec(memory_space=pltpu.SMEM)
 
@@ -68,18 +68,19 @@
 
 def pack_kernel(slot_ref, digit_ref, embed_ref, *out_refs):
     rows, width = embed_ref.shape
-    each = out_refs[0].shape[0]
     values = embed_ref[...].astype(jnp.float32)
     mean_sq = jnp.sum(values * values, axis=1, keepdims=True) * (1.0 / width)
     unit = (values * lax.rsqrt(width * (mean_sq + 1e-06))).astype(jnp.bfloat16)
-    slots = each * len(out_refs)
+    slots = sum(out_ref.shape[0] for out_ref in out_refs)
     move = (iota((slots, rows), 0) == slot_ref[...]).astype(jnp.float32).astype(jnp.bfloat16)
     moved = matmul(move, unit).astype(jnp.bfloat16)
     moved_digit = matmul(move, digit_ref[...]).astype(jnp.bfloat16)
-    for index, out_ref in enumerate(out_refs):
-        part = slice(index * each, (index + 1) * each)
+    first = 0
+    for out_ref in out_refs:
+        part = slice(first, first + out_ref.shape[0])
         out_ref[:, :width] = moved[part]
         out_ref[:, width:] = moved_digit[part]
+        first = part.stop
 
 
 def key_numbers(take):
@@ -161,9 +162,9 @@
     place = iota((1, slots), 1) // (slots // owners)
     at = as_column(slot_ref[...]) == iota((rows, slots), 1)
     for line, out_ref in enumerate((best_ref, distance_ref)):
-        values = result_ref[me_ref[0], line : line + 1]
-        for index in range(1, owners):
-            given = result_ref[me_ref[0] ^ order[index], line : line + 1]
+        values = jnp.zeros((1, slots), jnp.float32)
+        for index, k in enumerate(order):
+            given = result_ref[me_ref[0] ^ k, line : line + 1]
             values = jnp.where(place == index, given, values)
         out_ref[...] = as_row(jnp.sum(jnp.where(at, values, 0.0), axis=1, keepdims=True))
 
@@ -172,23 +173,41 @@
     return lax.ppermute(value, axis, [(i, i ^ k) for i in range(lax.axis_size(axis))])
 
 
-def exchange(blocks, order, me):
-    if len(blocks) > 1:
-        return jnp.concatenate(
-            [from_partner(block, k, "shard") if k else block for k, block in zip(order, blocks)]
-        )
+def partner_groups(owners):
+    half = owners // 2
+    odd = [list(range(1, half, 2))] if half > 1 else []
+    return [[k] for k in range(0, half, 2)] + odd + [[k] for k in range(half, owners)]
+
+
+def exchange(packed, groups):
+    owners = lax.axis_size("shard")
+    half = owners // 2
+    rows = packed[0].shape[0]
+    blocks = {}
+    for group, block in zip(groups, packed):
+        if len(group) > 1:
+            near = from_partner(block, 1, "shard")
+            for i, k in enumerate(group):
+                blocks[k] = near[i * rows : (i + 1) * rows]
+        else:
+            k = group[0]
+            blocks[k] = from_partner(block, k, "shard") if k >= half else block
+    step = 2
+    while step < half:
+        sent = [k for k in range(half) if k & step]
+        near = from_partner(jnp.concatenate([blocks[k] for k in sent]), step, "shard")
+        for i, k in enumerate(sent):
+            blocks[k] = near[i * rows : (i + 1) * rows]
+        step *= 2
+    return jnp.concatenate([blocks[k] for group in groups for k in group])
+
+
+def exchange_all(packed, order, me):
     owners = lax.axis_size("shard")
     partner = me ^ jnp.array(order, jnp.int32)
-    place = jnp.argsort(partner)
-    parted = blocks[0].reshape(owners, -1, blocks[0].shape[1])
-    got = lax.all_to_all(parted[place], "shard", 0, 0, tiled=True)
-    return got[partner].reshape(blocks[0].shape)
-
-
-def partner_order(owners):
-    half = owners // 2
-    near, far = list(range(1, half)), list(range(half, owners))
-    return [0] + far[:1] + near[:1] + far[1:] + near[1:]
+    parted = packed.reshape(owners, -1, packed.shape[1])
+    got = lax.all_to_all(parted[jnp.argsort(partner)], "shard", 0, 0, tiled=True)
+    return got[partner].reshape(packed.shape)
 
 
 def local(embeddings, cluster_id, item_order, owner_map):
@@ -206,8 +225,9 @@
     me = lax.axis_index("shard").astype(jnp.int32).reshape(1)
     ints = jnp.concatenate([owner_map, cluster_id, item_order]).reshape(1, -1)
 
-    order = partner_order(owners)
-    parts = owners if owners <= MOST_PERMUTES else 1
+    direct = owners <= MOST_PERMUTES
+    groups = partner_groups(owners) if direct else [list(range(owners))]
+    order = [k for group in groups for k in group]
     slot, digit = pl.pallas_call(
         functools.partial(slot_kernel, owners, capacity, order, local_rows),
         out_shape=[
@@ -222,13 +242,13 @@
     )(me, ints)
     packed = pl.pallas_call(
         pack_kernel,
-        out_shape=[jax.ShapeDtypeStruct((slots // parts, wide), jnp.bfloat16)] * parts,
+        out_shape=[jax.ShapeDtypeStruct((len(g) * capacity, wide), jnp.bfloat16) for g in groups],
         in_specs=[WHOLE] * 3,
-        out_specs=[WHOLE] * parts,
+        out_specs=[WHOLE] * len(groups),
         compiler_params=params,
         name="pack",
     )(slot, digit, embeddings)
-    query = exchange(packed, order, me)
+    query = exchange(packed, groups) if direct else exchange_all(packed[0], order, me)
     other = from_partner(query, 1, "sub")
     asked = slots + clus_dev
     near = pl.pallas_call(

time: 36.6 us -> 37.1 us (1.014)
  waiting for transfers between devices: 6.23 us -> 9.21 us
  starting transfers between devices: 13.1 us -> 10.8 us
    ppermute x8 -> x7, waiting for transfers between devices: 6.23 us -> 9.21 us  [from_partner(): lax.ppermute(value, axis, [(i, i ^ k) for i in range(lax.axis_size(axis))])]
    ppermute x8 -> x7, starting transfers between devices: 13.1 us -> 10.8 us  [from_partner(): lax.ppermute(value, axis, [(i, i ^ k) for i in range(lax.axis_size(axis))])]
  transfers between devices with their start and end apart: 8 -> 7, of which waited for: 5 -> 2; matrix products, arithmetic and copies ran while one was open for 0% -> 0% of each run, Pallas kernels for 3% -> 2%
where the time goes in v7:
time: 37.1 us; the launch traced here: 36.9 us
  blocking collectives  10.9 us (29%)
  starting transfers between devices  10.8 us (29%)
  waiting for transfers between devices  9.21 us (25%)
  Pallas kernels  4.33 us (12%)
  other arithmetic  0.77 us (2%)
  between operations  0.75 us (2%)
    all_to_all x1, blocking collectives, local(): results = lax.all_to_all(results, 'shard', 0, 0, tiled=True)  10.9 us
    ppermute x7, starting transfers between devices, from_partner(): lax.ppermute(value, axis, [(i, i ^ k) for i in range(lax.axis_size(axis))])  10.8 us
    ppermute x7, waiting for transfers between devices, from_partner(): lax.ppermute(value, axis, [(i, i ^ k) for i in range(lax.axis_size(axis))])  9.21 us
    pallas_call x1, Pallas kernels, local(): pl.pallas_call(functools.partial(far_kernel, rows_all), out_shape=[jax.Sh...  1.59 us
    pallas_call x1, Pallas kernels, local(): pl.pallas_call(functools.partial(near_kernel, rows_all, owner_map.shape[0...  0.92 us
    pallas_call x1, Pallas kernels, local(): pl.pallas_call(functools.partial(pick_kernel, order), out_shape=[jax.Shap...  0.81 us
    concatenate x1, other arithmetic, local(): ints = jnp.concatenate([owner_map, cluster_id, item_order]).reshape(1, -1)  0.76 us
  transfers between devices with their start and end apart: 7, of which 2 were waited for; matrix products, arithmetic and copies ran while one was open for 0% of the time, Pallas kernels for 2%

profile of v7, /device:TPU:0, one launch (start us, length us, event | category | flops | bytes accessed | tf_op | source)
XLA Modules:
  0.0 36.9 jit_solution(12016030343426171810)
XLA Ops:
  0.6 0.0 copy-start
  0.6 0.8 %pad_add_fusion = s32[512]{0:T(512)S(1)} fusion(s32[128]{0:T(128)} %param.6, s32[128]{0:T(128)} %param.5, s32[256]{0:T(256)} %param.7), kind=kLoop, calls=%fused_computation.9 | loop fusion | flops 1024 | bytes 4096 | tf_op jit(solution)/shard_map/concatenate | solution.py:226
  1.4 0.6 %slots.1 = (s32[1,128]{1,0:T(1,128)S(1)}, bf16[128,128]{1,0:T(8,128)(2,1)S(1)}) custom-call(s32[1]{0:T(128)} %bitcast.me_ref, s32[1,512]{1,0:T(1,128)S(1)} %bitcast.5), custom_call_target="tpu_custom_call" | custom-call | flops 268435456 | bytes 65536 | tf_op jit(solution)/shard_map/slots/pallas_call | solution.py:231
  2.0 0.0 copy-done
  2.0 0.4 %pack.1 = (bf16[32,1152]{1,0:T(8,128)(2,1)S(1)}, bf16[32,1152]{1,0:T(8,128)(2,1)S(1)}, bf16[64,1152]{1,0:T(8,128)(2,1)S(1)}, bf16[32,1152]{1,0:T(8,128)(2,1)S(1)...) custom-call(s32[1,128]{1,0:T(1,128)S(1)} %get-tuple-element.19.slot_ref, ...), custom_call_target="tpu_custom_call" | custom-call | tf_op jit(solution)/shard_map/pack/pallas_call | solution.py:243
  2.4 3.0 %collective-permute-start = (bf16[64,1152]{1,0:T(8,128)(2,1)S(1)}, bf16[64,1152]{1,0:T(8,128)(2,1)S(1)}, u32[]{:S(2)}, u32[]{:S(2)}) collective-permute-start(bf16[64,1152]{1,0:T(8,128)(2,1)S(1)} %get-tuple-element.23), channel_id=1, source_target_pairs={{0,2},{2,0},{4,6},{6,4},{8,10},{10,8},{12,14},{14,12},{1,3},{3,1},... | collective-permute-start | bytes 442376 | tf_op jit(solution)/shard_map/ppermute | solution.py:173
  5.4 2.6 %collective-permute-start.2 = (bf16[32,1152]{1,0:T(8,128)(2,1)S(1)}, bf16[32,1152]{1,0:T(8,128)(2,1)S(1)}, u32[]{:S(2)}, u32[]{:S(2)}) collective-permute-start(bf16[32,1152]{1,0:T(8,128)(2,1)S(1)} %get-tuple-element.24), channel_id=1, source_target_pairs={{0,8},{2,10},{4,12},{6,14},{8,0},{10,2},{12,4},{14,6},{1,9},{3,11}... | collective-permute-start | bytes 221192 | tf_op jit(solution)/shard_map/ppermute | solution.py:173
  8.0 0.0 collective-permute-start.3
  8.0 3.9 %collective-permute-start.4 = (bf16[32,1152]{1,0:T(8,128)(2,1)S(1)}, bf16[32,1152]{1,0:T(8,128)(2,1)S(1)}, u32[]{:S(2)}, u32[]{:S(2)}) collective-permute-start(bf16[32,1152]{1,0:T(8,128)(2,1)S(1)} %get-tuple-element.26), channel_id=1, source_target_pairs={{0,12},{2,14},{4,8},{6,10},{8,4},{10,6},{12,0},{14,2},{1,13},{3,15... | collective-permute-start | bytes 221192 | tf_op jit(solution)/shard_map/ppermute | solution.py:173
  11.9 1.1 %collective-permute-start.5 = (bf16[32,1152]{1,0:T(8,128)(2,1)S(1)}, bf16[32,1152]{1,0:T(8,128)(2,1)S(1)}, u32[]{:S(2)}, u32[]{:S(2)}) collective-permute-start(bf16[32,1152]{1,0:T(8,128)(2,1)S(1)} %get-tuple-element.27), channel_id=1, source_target_pairs={{0,14},{2,12},{4,10},{6,8},{8,6},{10,4},{12,2},{14,0},{1,15},{3,13... | collective-permute-start | bytes 221192 | tf_op jit(solution)/shard_map/ppermute | solution.py:173
  13.1 0.0 collective-permute-done
  13.1 0.1 collective-permute-start.1
  13.2 8.1 %collective-permute-done.1 = bf16[64,1152]{1,0:T(8,128)(2,1)S(1)} collective-permute-done((bf16[64,1152]{1,0:T(8,128)(2,1)S(1)}, bf16[64,1152]{1,0:T(8,128)(2,1)S(1)}, u32[]{:S(2)}, u32[]{:S(2)}) %collective-permute-start.1) | collective-permute-done | bytes 147488 | tf_op jit(solution)/shard_map/ppermute | solution.py:173
  21.4 0.0 collective-permute-done.2
  21.4 0.0 collective-permute-done.3
  21.5 0.0 collective-permute-done.4
  21.5 0.0 collective-permute-done.5
  21.5 0.1 collective-permute-start.6
  21.6 0.9 %near.1 = (f32[288,128]{1,0:T(8,128)S(1)}, s32[288,128]{1,0:T(8,128)S(1)}, f32[288,1024]{1,0:T(8,128)S(1)}) custom-call(s32[1]{0:T(128)} %bitcast.me_ref, s32[1,512]{1,0:T(1,128)S(1)} %bitcast.6, bf16[256,1152]{1,0:T(8,128)(2,1)S(1)} %constant_dynamic-update-slice_fusion.query_ref), custom_call_target="tpu_custom_call" | custom-call | flops 268435456 | bytes 1179648 | tf_op jit(solution)/shard_map/near/pallas_call | solution.py:254
  22.5 1.1 %collective-permute-done.6.other_ref = bf16[256,1152]{1,0:T(8,128)(2,1)S(1)} collective-permute-done((bf16[256,1152]{1,0:T(8,128)(2,1)S(1)}, bf16[256,1152]{1,0:T(8,128)(2,1)S(1)}, u32[]{:S(2)}, u32[]{:S(2)}) %collective-permute-start.6) | collective-permute-done | bytes 589856 | tf_op jit(solution)/shard_map/ppermute | solution.py:173
  23.6 1.6 %far.1 = (f32[8,2,256]{2,1,0:T(2,128)S(1)}, f32[1,32]{1,0:T(1,128)}) custom-call(bf16[256,1152]{1,0:T(8,128)(2,1)S(1)} %constant_dynamic-update-slice_fusion.query_ref, bf16[256,1152]{1,0:T(8,128)(2,1)S(1)} %collective-permute-done.6.other_ref, f32[288,128]{1,0:T(8,128)S(1)} %get-tuple-element.28.column_ref, s32[288,128]{1,0:T(8,128)S(1)} %get-tuple-element.29.number_ref, ...), custom_call_target="tpu_custom_call" | custom-call | flops 268435456 | bytes 1179648 | tf_op jit(solution)/shard_map/far/pallas_call | solution.py:267
  25.2 10.9 %all_to_all.5.result_ref = f32[8,2,256]{2,1,0:T(2,128)S(1)} all-to-all(f32[8,2,256]{2,1,0:T(2,128)S(1)} %get-tuple-element.31), channel_id=1, replica_groups=mesh['groups'=2,'shard'=8,'sub'=2] {'shard'}, dimensions={0} | all-to-all | bytes 32768 | tf_op jit(solution)/shard_map/all_to_all | solution.py:279
  36.1 0.8 %pick.1 = (f32[1,128]{1,0:T(1,128)}, f32[1,128]{1,0:T(1,128)}) custom-call(s32[1]{0:T(128)} %bitcast.me_ref, s32[1,128]{1,0:T(1,128)S(1)} %get-tuple-element.19.slot_ref, f32[8,2,256]{2,1,0:T(2,128)S(1)} %all_to_all.5.result_ref), custom_call_target="tpu_custom_call" | custom-call | tf_op jit(solution)/shard_map/pick/pallas_call | solution.py:280
  (10 shorter events, 0.1 us)
Async XLA Ops:
  0.6 1.4 %copy-start = (bf16[128,1024]{1,0:T(8,128)(2,1)S(1)}, bf16[128,1024]{1,0:T(8,128)(2,1)}, u32[]{:S(2)}) copy-start(bf16[128,1024]{1,0:T(8,128)(2,1)} %embed_ref.1) | copy-start | bytes 786436
  2.4 10.7 %collective-permute-start = (bf16[64,1152]{1,0:T(8,128)(2,1)S(1)}, bf16[64,1152]{1,0:T(8,128)(2,1)S(1)}, u32[]{:S(2)}, u32[]{:S(2)}) collective-permute-start(bf16[64,1152]{1,0:T(8,128)(2,1)S(1)} %get-tuple-element.23), channel_id=1, source_target_pairs={{0,2},{2,0},{4,6},{6,4},{8,10},{10,8},{12,14},{14,12},{1,3},{3,1},... | collective-permute-start | bytes 442376 | tf_op jit(solution)/shard_map/ppermute | solution.py:173
  5.4 16.0 %collective-permute-start.2 = (bf16[32,1152]{1,0:T(8,128)(2,1)S(1)}, bf16[32,1152]{1,0:T(8,128)(2,1)S(1)}, u32[]{:S(2)}, u32[]{:S(2)}) collective-permute-start(bf16[32,1152]{1,0:T(8,128)(2,1)S(1)} %get-tuple-element.24), channel_id=1, source_target_pairs={{0,8},{2,10},{4,12},{6,14},{8,0},{10,2},{12,4},{14,6},{1,9},{3,11}... | collective-permute-start | bytes 221192 | tf_op jit(solution)/shard_map/ppermute | solution.py:173
  8.0 13.4 %collective-permute-start.3 = (bf16[32,1152]{1,0:T(8,128)(2,1)S(1)}, bf16[32,1152]{1,0:T(8,128)(2,1)S(1)}, u32[]{:S(2)}, u32[]{:S(2)}) collective-permute-start(bf16[32,1152]{1,0:T(8,128)(2,1)S(1)} %get-tuple-element.25), channel_id=1, source_target_pairs={{0,10},{2,8},{4,14},{6,12},{8,2},{10,0},{12,6},{14,4},{1,11},{3,9}... | collective-permute-start | bytes 221192 | tf_op jit(solution)/shard_map/ppermute | solution.py:173
  8.0 13.4 %collective-permute-start.4 = (bf16[32,1152]{1,0:T(8,128)(2,1)S(1)}, bf16[32,1152]{1,0:T(8,128)(2,1)S(1)}, u32[]{:S(2)}, u32[]{:S(2)}) collective-permute-start(bf16[32,1152]{1,0:T(8,128)(2,1)S(1)} %get-tuple-element.26), channel_id=1, source_target_pairs={{0,12},{2,14},{4,8},{6,10},{8,4},{10,6},{12,0},{14,2},{1,13},{3,15... | collective-permute-start | bytes 221192 | tf_op jit(solution)/shard_map/ppermute | solution.py:173
  11.9 9.5 %collective-permute-start.5 = (bf16[32,1152]{1,0:T(8,128)(2,1)S(1)}, bf16[32,1152]{1,0:T(8,128)(2,1)S(1)}, u32[]{:S(2)}, u32[]{:S(2)}) collective-permute-start(bf16[32,1152]{1,0:T(8,128)(2,1)S(1)} %get-tuple-element.27), channel_id=1, source_target_pairs={{0,14},{2,12},{4,10},{6,8},{8,6},{10,4},{12,2},{14,0},{1,15},{3,13... | collective-permute-start | bytes 221192 | tf_op jit(solution)/shard_map/ppermute | solution.py:173
  13.1 8.2 %collective-permute-start.1 = (bf16[64,1152]{1,0:T(8,128)(2,1)S(1)}, bf16[64,1152]{1,0:T(8,128)(2,1)S(1)}, u32[]{:S(2)}, u32[]{:S(2)}) collective-permute-start(bf16[64,1152]{1,0:T(8,128)(2,1)S(1)} %pad_maximum_fusion), channel_id=1, source_target_pairs={{0,4},{2,6},{4,0},{6,2},{8,12},{10,14},{12,8},{14,10},{1,5},{3,7},... | collective-permute-start | bytes 442376 | tf_op jit(solution)/shard_map/ppermute | solution.py:173
  21.5 2.1 %collective-permute-start.6 = (bf16[256,1152]{1,0:T(8,128)(2,1)S(1)}, bf16[256,1152]{1,0:T(8,128)(2,1)S(1)}, u32[]{:S(2)}, u32[]{:S(2)}) collective-permute-start(bf16[256,1152]{1,0:T(8,128)(2,1)S(1)} %constant_dynamic-update-slice_fusion.query_ref), channel_id=1, source_target_pairs={{0,1},{1,0},{2,3},{3,2},{4,5},{5,4},{6,7},{7,6},{8,9},{9,8},{10,11... | collective-permute-start | bytes 1769480 | tf_op jit(solution)/shard_map/ppermute | solution.py:173

commit v8 on v7

--- a/solution.py
+++ b/solution.py
@@ -173,33 +173,16 @@
     return lax.ppermute(value, axis, [(i, i ^ k) for i in range(lax.axis_size(axis))])
 
 
-def partner_groups(owners):
+def partner_order(owners):
     half = owners // 2
-    odd = [list(range(1, half, 2))] if half > 1 else []
-    return [[k] for k in range(0, half, 2)] + odd + [[k] for k in range(half, owners)]
-
-
-def exchange(packed, groups):
-    owners = lax.axis_size("shard")
-    half = owners // 2
-    rows = packed[0].shape[0]
-    blocks = {}
-    for group, block in zip(groups, packed):
-        if len(group) > 1:
-            near = from_partner(block, 1, "shard")
-            for i, k in enumerate(group):
-                blocks[k] = near[i * rows : (i + 1) * rows]
-        else:
-            k = group[0]
-            blocks[k] = from_partner(block, k, "shard") if k >= half else block
-    step = 2
-    while step < half:
-        sent = [k for k in range(half) if k & step]
-        near = from_partner(jnp.concatenate([blocks[k] for k in sent]), step, "shard")
-        for i, k in enumerate(sent):
-            blocks[k] = near[i * rows : (i + 1) * rows]
-        step *= 2
-    return jnp.concatenate([blocks[k] for group in groups for k in group])
+    far, near = list(range(half, owners)), list(range(2, half))
+    return far[:1] + near + far[1:] + list(range(1, min(half, 2))) + [0]
+
+
+def exchange(packed, order):
+    return jnp.concatenate(
+        [from_partner(block, k, "shard") if k else block for k, block in zip(order, packed)]
+    )
 
 
 def exchange_all(packed, order, me):
@@ -226,8 +209,8 @@
     ints = jnp.concatenate([owner_map, cluster_id, item_order]).reshape(1, -1)
 
     direct = owners <= MOST_PERMUTES
-    groups = partner_groups(owners) if direct else [list(range(owners))]
-    order = [k for group in groups for k in group]
+    order = partner_order(owners)
+    parts = owners if direct else 1
     slot, digit = pl.pallas_call(
         functools.partial(slot_kernel, owners, capacity, order, local_rows),
         out_shape=[
@@ -242,13 +225,13 @@
     )(me, ints)
     packed = pl.pallas_call(
         pack_kernel,
-        out_shape=[jax.ShapeDtypeStruct((len(g) * capacity, wide), jnp.bfloat16) for g in groups],
+        out_shape=[jax.ShapeDtypeStruct((slots // parts, wide), jnp.bfloat16)] * parts,
         in_specs=[WHOLE] * 3,
-        out_specs=[WHOLE] * len(groups),
+        out_specs=[WHOLE] * parts,
         compiler_params=params,
         name="pack",
     )(slot, digit, embeddings)
-    query = exchange(packed, groups) if direct else exchange_all(packed[0], order, me)
+    query = exchange(packed, order) if direct else exchange_all(packed[0], order, me)
     other = from_partner(query, 1, "sub")
     asked = slots + clus_dev
     near = pl.pallas_call(

time: 37.1 us -> 35.8 us (0.965)
  waiting for transfers between devices: 9.21 us -> 6.04 us
  starting transfers between devices: 10.8 us -> 13.4 us
  blocking collectives: 10.9 us -> 10.2 us
    ppermute x7 -> x8, waiting for transfers between devices: 9.21 us -> 6.04 us  [from_partner(): lax.ppermute(value, axis, [(i, i ^ k) for i in range(lax.axis_size(axis))])]
    ppermute x7 -> x8, starting transfers between devices: 10.8 us -> 13.4 us  [from_partner(): lax.ppermute(value, axis, [(i, i ^ k) for i in range(lax.axis_size(axis))])]
    all_to_all x1, blocking collectives: 10.9 us -> 10.2 us  [local(): results = lax.all_to_all(results, 'shard', 0, 0, tiled=True)]
  transfers between devices with their start and end apart: 7 -> 8, of which waited for: 2 -> 4; matrix products, arithmetic and copies ran while one was open for 0% -> 0% of each run, Pallas kernels for 2% -> 3%
where the time goes in v8:
time: 35.8 us; the launch traced here: 35.6 us
  starting transfers between devices  13.4 us (37%)
  blocking collectives  10.2 us (28%)
  waiting for transfers between devices  6.04 us (17%)
  Pallas kernels  4.34 us (12%)
  other arithmetic  0.76 us (2%)
  between operations  0.71 us (2%)
    ppermute x8, starting transfers between devices, from_partner(): lax.ppermute(value, axis, [(i, i ^ k) for i in range(lax.axis_size(axis))])  13.4 us
    all_to_all x1, blocking collectives, local(): results = lax.all_to_all(results, 'shard', 0, 0, tiled=True)  10.2 us
    ppermute x8, waiting for transfers between devices, from_partner(): lax.ppermute(value, axis, [(i, i ^ k) for i in range(lax.axis_size(axis))])  6.04 us
    pallas_call x1, Pallas kernels, local(): pl.pallas_call(functools.partial(far_kernel, rows_all), out_shape=[jax.Sh...  1.59 us
    pallas_call x1, Pallas kernels, local(): pl.pallas_call(functools.partial(near_kernel, rows_all, owner_map.shape[0...  0.92 us
    pallas_call x1, Pallas kernels, local(): pl.pallas_call(functools.partial(pick_kernel, order), out_shape=[jax.Shap...  0.81 us
    concatenate x1, other arithmetic, local(): ints = jnp.concatenate([owner_map, cluster_id, item_order]).reshape(1, -1)  0.76 us
  transfers between devices with their start and end apart: 8, of which 4 were waited for; matrix products, arithmetic and copies ran while one was open for 0% of the time, Pallas kernels for 3%

profile of v8, /device:TPU:0, one launch (start us, length us, event | category | flops | bytes accessed | tf_op | source)
XLA Modules:
  0.0 35.6 jit_solution(18220432745194810674)
XLA Ops:
  0.6 0.0 copy-start
  0.6 0.8 %pad_add_fusion = s32[512]{0:T(512)S(1)} fusion(s32[128]{0:T(128)} %param.6, s32[128]{0:T(128)} %param.5, s32[256]{0:T(256)} %param.7), kind=kLoop, calls=%fused_computation.8 | loop fusion | flops 1024 | bytes 4096 | tf_op jit(solution)/shard_map/concatenate | solution.py:209
  1.4 0.6 %slots.1 = (s32[1,128]{1,0:T(1,128)S(1)}, bf16[128,128]{1,0:T(8,128)(2,1)S(1)}) custom-call(s32[1]{0:T(128)} %bitcast.me_ref, s32[1,512]{1,0:T(1,128)S(1)} %bitcast.5), custom_call_target="tpu_custom_call" | custom-call | flops 268435456 | bytes 65536 | tf_op jit(solution)/shard_map/slots/pallas_call | solution.py:214
  2.0 0.0 copy-done
  2.0 0.4 %pack.1 = (bf16[32,1152]{1,0:T(8,128)(2,1)S(1)}, bf16[32,1152]{1,0:T(8,128)(2,1)S(1)}, bf16[32,1152]{1,0:T(8,128)(2,1)S(1)}, bf16[32,1152]{1,0:T(8,128)(2,1)S(1)...) custom-call(s32[1,128]{1,0:T(1,128)S(1)} %get-tuple-element.20.slot_, ...), custom_call_target="tpu_custom_call" | custom-call | tf_op jit(solution)/shard_map/pack/pallas_call | solution.py:226
  2.4 4.1 %collective-permute-start = (bf16[32,1152]{1,0:T(8,128)(2,1)S(1)}, bf16[32,1152]{1,0:T(8,128)(2,1)S(1)}, u32[]{:S(2)}, u32[]{:S(2)}) collective-permute-start(bf16[32,1152]{1,0:T(8,128)(2,1)S(1)} %get-tuple-element.22), channel_id=1, source_target_pairs={{0,8},{2,10},{4,12},{6,14},{8,0},{10,2},{12,4},{14,6},{1,9},{3,11}... | collective-permute-start | bytes 221192 | tf_op jit(solution)/shard_map/ppermute | solution.py:173
  6.5 1.6 %collective-permute-start.1 = (bf16[32,1152]{1,0:T(8,128)(2,1)S(1)}, bf16[32,1152]{1,0:T(8,128)(2,1)S(1)}, u32[]{:S(2)}, u32[]{:S(2)}) collective-permute-start(bf16[32,1152]{1,0:T(8,128)(2,1)S(1)} %get-tuple-element.23), channel_id=1, source_target_pairs={{0,4},{2,6},{4,0},{6,2},{8,12},{10,14},{12,8},{14,10},{1,5},{3,7},... | collective-permute-start | bytes 221192 | tf_op jit(solution)/shard_map/ppermute | solution.py:173
  8.1 1.4 %collective-permute-start.2 = (bf16[32,1152]{1,0:T(8,128)(2,1)S(1)}, bf16[32,1152]{1,0:T(8,128)(2,1)S(1)}, u32[]{:S(2)}, u32[]{:S(2)}) collective-permute-start(bf16[32,1152]{1,0:T(8,128)(2,1)S(1)} %get-tuple-element.24), channel_id=1, source_target_pairs={{0,6},{2,4},{4,2},{6,0},{8,14},{10,12},{12,10},{14,8},{1,7},{3,5},... | collective-permute-start | bytes 221192 | tf_op jit(solution)/shard_map/ppermute | solution.py:173
  9.5 0.1 collective-permute-start.3
  9.5 3.9 %collective-permute-start.4 = (bf16[32,1152]{1,0:T(8,128)(2,1)S(1)}, bf16[32,1152]{1,0:T(8,128)(2,1)S(1)}, u32[]{:S(2)}, u32[]{:S(2)}) collective-permute-start(bf16[32,1152]{1,0:T(8,128)(2,1)S(1)} %get-tuple-element.26), channel_id=1, source_target_pairs={{0,12},{2,14},{4,8},{6,10},{8,4},{10,6},{12,0},{14,2},{1,13},{3,15... | collective-permute-start | bytes 221192 | tf_op jit(solution)/shard_map/ppermute | solution.py:173
  13.4 0.0 collective-permute-done
  13.4 1.8 %collective-permute-start.5 = (bf16[32,1152]{1,0:T(8,128)(2,1)S(1)}, bf16[32,1152]{1,0:T(8,128)(2,1)S(1)}, u32[]{:S(2)}, u32[]{:S(2)}) collective-permute-start(bf16[32,1152]{1,0:T(8,128)(2,1)S(1)} %get-tuple-element.27), channel_id=1, source_target_pairs={{0,14},{2,12},{4,10},{6,8},{8,6},{10,4},{12,2},{14,0},{1,15},{3,13... | collective-permute-start | bytes 221192 | tf_op jit(solution)/shard_map/ppermute | solution.py:173
  15.2 0.0 collective-permute-done.1
  15.3 0.6 %collective-permute-start.6 = (bf16[32,1152]{1,0:T(8,128)(2,1)S(1)}, bf16[32,1152]{1,0:T(8,128)(2,1)S(1)}, u32[]{:S(2)}, u32[]{:S(2)}) collective-permute-start(bf16[32,1152]{1,0:T(8,128)(2,1)S(1)} %get-tuple-element.28), channel_id=1, source_target_pairs={{0,2},{2,0},{4,6},{6,4},{8,10},{10,8},{12,14},{14,12},{1,3},{3,1},... | collective-permute-start | bytes 221192 | tf_op jit(solution)/shard_map/ppermute | solution.py:173
  15.8 0.0 collective-permute-done.2
  15.9 3.8 %collective-permute-done.3 = bf16[32,1152]{1,0:T(8,128)(2,1)S(1)} collective-permute-done((bf16[32,1152]{1,0:T(8,128)(2,1)S(1)}, bf16[32,1152]{1,0:T(8,128)(2,1)S(1)}, u32[]{:S(2)}, u32[]{:S(2)}) %collective-permute-start.3) | collective-permute-done | bytes 73760 | tf_op jit(solution)/shard_map/ppermute | solution.py:173
  19.7 0.0 collective-permute-done.4
  19.7 0.9 %collective-permute-done.5 = bf16[32,1152]{1,0:T(8,128)(2,1)S(1)} collective-permute-done((bf16[32,1152]{1,0:T(8,128)(2,1)S(1)}, bf16[32,1152]{1,0:T(8,128)(2,1)S(1)}, u32[]{:S(2)}, u32[]{:S(2)}) %collective-permute-start.5) | collective-permute-done | bytes 73760 | tf_op jit(solution)/shard_map/ppermute | solution.py:173
  20.6 0.2 collective-permute-done.6
  20.9 0.1 collective-permute-start.7
  21.0 0.9 %near.1 = (f32[288,128]{1,0:T(8,128)S(1)}, s32[288,128]{1,0:T(8,128)S(1)}, f32[288,1024]{1,0:T(8,128)S(1)}) custom-call(s32[1]{0:T(128)} %bitcast.me_ref, s32[1,512]{1,0:T(1,128)S(1)} %bitcast.6, bf16[256,1152]{1,0:T(8,128)(2,1)S(1)} %constant_dynamic-update-slice_fusion.query_ref), custom_call_target="tpu_custom_call" | custom-call | flops 268435456 | bytes 1179648 | tf_op jit(solution)/shard_map/near/pallas_call | solution.py:237
  21.9 1.1 %collective-permute-done.7.other_ref = bf16[256,1152]{1,0:T(8,128)(2,1)S(1)} collective-permute-done((bf16[256,1152]{1,0:T(8,128)(2,1)S(1)}, bf16[256,1152]{1,0:T(8,128)(2,1)S(1)}, u32[]{:S(2)}, u32[]{:S(2)}) %collective-permute-start.7) | collective-permute-done | bytes 589856 | tf_op jit(solution)/shard_map/ppermute | solution.py:173
  23.0 1.6 %far.1 = (f32[8,2,256]{2,1,0:T(2,128)S(1)}, f32[1,32]{1,0:T(1,128)}) custom-call(bf16[256,1152]{1,0:T(8,128)(2,1)S(1)} %constant_dynamic-update-slice_fusion.query_ref, bf16[256,1152]{1,0:T(8,128)(2,1)S(1)} %collective-permute-done.7.other_ref, f32[288,128]{1,0:T(8,128)S(1)} %get-tuple-element.30.column_ref, s32[288,128]{1,0:T(8,128)S(1)} %get-tuple-element.31.number_ref, ...), custom_call_target="tpu_custom_call" | custom-call | flops 268435456 | bytes 1179648 | tf_op jit(solution)/shard_map/far/pallas_call | solution.py:250
  24.6 10.2 %all_to_all.5.result_ref = f32[8,2,256]{2,1,0:T(2,128)S(1)} all-to-all(f32[8,2,256]{2,1,0:T(2,128)S(1)} %get-tuple-element.33), channel_id=1, replica_groups=mesh['groups'=2,'shard'=8,'sub'=2] {'shard'}, dimensions={0} | all-to-all | bytes 32768 | tf_op jit(solution)/shard_map/all_to_all | solution.py:262
  34.8 0.8 %pick.1 = (f32[1,128]{1,0:T(1,128)}, f32[1,128]{1,0:T(1,128)}) custom-call(s32[1]{0:T(128)} %bitcast.me_ref, s32[1,128]{1,0:T(1,128)S(1)} %get-tuple-element.20.slot_ref, f32[8,2,256]{2,1,0:T(2,128)S(1)} %all_to_all.5.result_ref), custom_call_target="tpu_custom_call" | custom-call | tf_op jit(solution)/shard_map/pick/pallas_call | solution.py:263
  (8 shorter events, 0.1 us)
Async XLA Ops:
  0.6 1.4 %copy-start = (bf16[128,1024]{1,0:T(8,128)(2,1)S(1)}, bf16[128,1024]{1,0:T(8,128)(2,1)}, u32[]{:S(2)}) copy-start(bf16[128,1024]{1,0:T(8,128)(2,1)} %embed_ref.1) | copy-start | bytes 786436
  2.4 11.0 %collective-permute-start = (bf16[32,1152]{1,0:T(8,128)(2,1)S(1)}, bf16[32,1152]{1,0:T(8,128)(2,1)S(1)}, u32[]{:S(2)}, u32[]{:S(2)}) collective-permute-start(bf16[32,1152]{1,0:T(8,128)(2,1)S(1)} %get-tuple-element.22), channel_id=1, source_target_pairs={{0,8},{2,10},{4,12},{6,14},{8,0},{10,2},{12,4},{14,6},{1,9},{3,11}... | collective-permute-start | bytes 221192 | tf_op jit(solution)/shard_map/ppermute | solution.py:173
  6.5 8.7 %collective-permute-start.1 = (bf16[32,1152]{1,0:T(8,128)(2,1)S(1)}, bf16[32,1152]{1,0:T(8,128)(2,1)S(1)}, u32[]{:S(2)}, u32[]{:S(2)}) collective-permute-start(bf16[32,1152]{1,0:T(8,128)(2,1)S(1)} %get-tuple-element.23), channel_id=1, source_target_pairs={{0,4},{2,6},{4,0},{6,2},{8,12},{10,14},{12,8},{14,10},{1,5},{3,7},... | collective-permute-start | bytes 221192 | tf_op jit(solution)/shard_map/ppermute | solution.py:173
  8.1 7.7 %collective-permute-start.2 = (bf16[32,1152]{1,0:T(8,128)(2,1)S(1)}, bf16[32,1152]{1,0:T(8,128)(2,1)S(1)}, u32[]{:S(2)}, u32[]{:S(2)}) collective-permute-start(bf16[32,1152]{1,0:T(8,128)(2,1)S(1)} %get-tuple-element.24), channel_id=1, source_target_pairs={{0,6},{2,4},{4,2},{6,0},{8,14},{10,12},{12,10},{14,8},{1,7},{3,5},... | collective-permute-start | bytes 221192 | tf_op jit(solution)/shard_map/ppermute | solution.py:173
  9.5 10.2 %collective-permute-start.3 = (bf16[32,1152]{1,0:T(8,128)(2,1)S(1)}, bf16[32,1152]{1,0:T(8,128)(2,1)S(1)}, u32[]{:S(2)}, u32[]{:S(2)}) collective-permute-start(bf16[32,1152]{1,0:T(8,128)(2,1)S(1)} %get-tuple-element.25), channel_id=1, source_target_pairs={{0,10},{2,8},{4,14},{6,12},{8,2},{10,0},{12,6},{14,4},{1,11},{3,9}... | collective-permute-start | bytes 221192 | tf_op jit(solution)/shard_map/ppermute | solution.py:173
  9.5 10.1 %collective-permute-start.4 = (bf16[32,1152]{1,0:T(8,128)(2,1)S(1)}, bf16[32,1152]{1,0:T(8,128)(2,1)S(1)}, u32[]{:S(2)}, u32[]{:S(2)}) collective-permute-start(bf16[32,1152]{1,0:T(8,128)(2,1)S(1)} %get-tuple-element.26), channel_id=1, source_target_pairs={{0,12},{2,14},{4,8},{6,10},{8,4},{10,6},{12,0},{14,2},{1,13},{3,15... | collective-permute-start | bytes 221192 | tf_op jit(solution)/shard_map/ppermute | solution.py:173
  13.4 7.2 %collective-permute-start.5 = (bf16[32,1152]{1,0:T(8,128)(2,1)S(1)}, bf16[32,1152]{1,0:T(8,128)(2,1)S(1)}, u32[]{:S(2)}, u32[]{:S(2)}) collective-permute-start(bf16[32,1152]{1,0:T(8,128)(2,1)S(1)} %get-tuple-element.27), channel_id=1, source_target_pairs={{0,14},{2,12},{4,10},{6,8},{8,6},{10,4},{12,2},{14,0},{1,15},{3,13... | collective-permute-start | bytes 221192 | tf_op jit(solution)/shard_map/ppermute | solution.py:173
  15.3 5.6 %collective-permute-start.6 = (bf16[32,1152]{1,0:T(8,128)(2,1)S(1)}, bf16[32,1152]{1,0:T(8,128)(2,1)S(1)}, u32[]{:S(2)}, u32[]{:S(2)}) collective-permute-start(bf16[32,1152]{1,0:T(8,128)(2,1)S(1)} %get-tuple-element.28), channel_id=1, source_target_pairs={{0,2},{2,0},{4,6},{6,4},{8,10},{10,8},{12,14},{14,12},{1,3},{3,1},... | collective-permute-start | bytes 221192 | tf_op jit(solution)/shard_map/ppermute | solution.py:173
  20.9 2.1 %collective-permute-start.7 = (bf16[256,1152]{1,0:T(8,128)(2,1)S(1)}, bf16[256,1152]{1,0:T(8,128)(2,1)S(1)}, u32[]{:S(2)}, u32[]{:S(2)}) collective-permute-start(bf16[256,1152]{1,0:T(8,128)(2,1)S(1)} %constant_dynamic-update-slice_fusion.query_ref), channel_id=1, source_target_pairs={{0,1},{1,0},{2,3},{3,2},{4,5},{5,4},{6,7},{7,6},{8,9},{9,8},{10,11... | collective-permute-start | bytes 1769480 | tf_op jit(solution)/shard_map/ppermute | solution.py:173

commit v9 on v8

--- a/solution.py
+++ b/solution.py
@@ -176,7 +176,7 @@
 def partner_order(owners):
     half = owners // 2
     far, near = list(range(half, owners)), list(range(2, half))
-    return far[:1] + near + far[1:] + list(range(1, min(half, 2))) + [0]
+    return far[:2] + near + far[2:] + list(range(1, min(half, 2))) + [0]
 
 
 def exchange(packed, order):

time: 35.8 us -> 37.1 us (1.036)
  starting transfers between devices: 13.4 us -> 15 us
  waiting for transfers between devices: 6.04 us -> 4.96 us
  blocking collectives: 10.2 us -> 11.1 us
    ppermute x8, starting transfers between devices: 13.4 us -> 15 us  [from_partner(): lax.ppermute(value, axis, [(i, i ^ k) for i in range(lax.axis_size(axis))])]
    ppermute x8, waiting for transfers between devices: 6.04 us -> 4.96 us  [from_partner(): lax.ppermute(value, axis, [(i, i ^ k) for i in range(lax.axis_size(axis))])]
    all_to_all x1, blocking collectives: 10.2 us -> 11.1 us  [local(): results = lax.all_to_all(results, 'shard', 0, 0, tiled=True)]
  transfers between devices with their start and end apart: 8 -> 8, of which waited for: 4 -> 4; matrix products, arithmetic and copies ran while one was open for 0% -> 0% of each run, Pallas kernels for 3% -> 2%
where the time goes in v9:
time: 37.1 us; the launch traced here: 37 us
  starting transfers between devices  15 us (40%)
  blocking collectives  11.1 us (30%)
  waiting for transfers between devices  4.96 us (13%)
  Pallas kernels  4.34 us (12%)
  other arithmetic  0.76 us (2%)
  between operations  0.71 us (2%)
    ppermute x8, starting transfers between devices, from_partner(): lax.ppermute(value, axis, [(i, i ^ k) for i in range(lax.axis_size(axis))])  15 us
    all_to_all x1, blocking collectives, local(): results = lax.all_to_all(results, 'shard', 0, 0, tiled=True)  11.1 us
    ppermute x8, waiting for transfers between devices, from_partner(): lax.ppermute(value, axis, [(i, i ^ k) for i in range(lax.axis_size(axis))])  4.96 us
    pallas_call x1, Pallas kernels, local(): pl.pallas_call(functools.partial(far_kernel, rows_all), out_shape=[jax.Sh...  1.59 us
    pallas_call x1, Pallas kernels, local(): pl.pallas_call(functools.partial(near_kernel, rows_all, owner_map.shape[0...  0.92 us
    pallas_call x1, Pallas kernels, local(): pl.pallas_call(functools.partial(pick_kernel, order), out_shape=[jax.Shap...  0.81 us
    concatenate x1, other arithmetic, local(): ints = jnp.concatenate([owner_map, cluster_id, item_order]).reshape(1, -1)  0.76 us
  transfers between devices with their start and end apart: 8, of which 4 were waited for; matrix products, arithmetic and copies ran while one was open for 0% of the time, Pallas kernels for 2%

profile of v9, /device:TPU:0, one launch (start us, length us, event | category | flops | bytes accessed | tf_op | source)
XLA Modules:
  0.0 37.0 jit_solution(1821048373885534514)
XLA Ops:
  0.6 0.0 copy-start
  0.6 0.8 %pad_add_fusion = s32[512]{0:T(512)S(1)} fusion(s32[128]{0:T(128)} %param.6, s32[128]{0:T(128)} %param.5, s32[256]{0:T(256)} %param.7), kind=kLoop, calls=%fused_computation.8 | loop fusion | flops 1024 | bytes 4096 | tf_op jit(solution)/shard_map/concatenate | solution.py:209
  1.4 0.6 %slots.1 = (s32[1,128]{1,0:T(1,128)S(1)}, bf16[128,128]{1,0:T(8,128)(2,1)S(1)}) custom-call(s32[1]{0:T(128)} %bitcast.me_ref, s32[1,512]{1,0:T(1,128)S(1)} %bitcast.5), custom_call_target="tpu_custom_call" | custom-call | flops 268435456 | bytes 65536 | tf_op jit(solution)/shard_map/slots/pallas_call | solution.py:214
  2.0 0.0 copy-done
  2.0 0.4 %pack.1 = (bf16[32,1152]{1,0:T(8,128)(2,1)S(1)}, bf16[32,1152]{1,0:T(8,128)(2,1)S(1)}, bf16[32,1152]{1,0:T(8,128)(2,1)S(1)}, bf16[32,1152]{1,0:T(8,128)(2,1)S(1)...) custom-call(s32[1,128]{1,0:T(1,128)S(1)} %get-tuple-element.20.slot_, ...), custom_call_target="tpu_custom_call" | custom-call | tf_op jit(solution)/shard_map/pack/pallas_call | solution.py:226
  2.4 4.1 %collective-permute-start = (bf16[32,1152]{1,0:T(8,128)(2,1)S(1)}, bf16[32,1152]{1,0:T(8,128)(2,1)S(1)}, u32[]{:S(2)}, u32[]{:S(2)}) collective-permute-start(bf16[32,1152]{1,0:T(8,128)(2,1)S(1)} %get-tuple-element.22), channel_id=1, source_target_pairs={{0,8},{2,10},{4,12},{6,14},{8,0},{10,2},{12,4},{14,6},{1,9},{3,11}... | collective-permute-start | bytes 221192 | tf_op jit(solution)/shard_map/ppermute | solution.py:173
  6.5 1.3 %collective-permute-start.1 = (bf16[32,1152]{1,0:T(8,128)(2,1)S(1)}, bf16[32,1152]{1,0:T(8,128)(2,1)S(1)}, u32[]{:S(2)}, u32[]{:S(2)}) collective-permute-start(bf16[32,1152]{1,0:T(8,128)(2,1)S(1)} %get-tuple-element.23), channel_id=1, source_target_pairs={{0,10},{2,8},{4,14},{6,12},{8,2},{10,0},{12,6},{14,4},{1,11},{3,9}... | collective-permute-start | bytes 221192 | tf_op jit(solution)/shard_map/ppermute | solution.py:173
  7.8 1.6 %collective-permute-start.2 = (bf16[32,1152]{1,0:T(8,128)(2,1)S(1)}, bf16[32,1152]{1,0:T(8,128)(2,1)S(1)}, u32[]{:S(2)}, u32[]{:S(2)}) collective-permute-start(bf16[32,1152]{1,0:T(8,128)(2,1)S(1)} %get-tuple-element.24), channel_id=1, source_target_pairs={{0,4},{2,6},{4,0},{6,2},{8,12},{10,14},{12,8},{14,10},{1,5},{3,7},... | collective-permute-start | bytes 221192 | tf_op jit(solution)/shard_map/ppermute | solution.py:173
  9.4 0.2 collective-permute-start.3
  9.5 3.9 %collective-permute-start.4 = (bf16[32,1152]{1,0:T(8,128)(2,1)S(1)}, bf16[32,1152]{1,0:T(8,128)(2,1)S(1)}, u32[]{:S(2)}, u32[]{:S(2)}) collective-permute-start(bf16[32,1152]{1,0:T(8,128)(2,1)S(1)} %get-tuple-element.26), channel_id=1, source_target_pairs={{0,12},{2,14},{4,8},{6,10},{8,4},{10,6},{12,0},{14,2},{1,13},{3,15... | collective-permute-start | bytes 221192 | tf_op jit(solution)/shard_map/ppermute | solution.py:173
  13.4 0.0 collective-permute-done
  13.4 3.2 %collective-permute-start.5 = (bf16[32,1152]{1,0:T(8,128)(2,1)S(1)}, bf16[32,1152]{1,0:T(8,128)(2,1)S(1)}, u32[]{:S(2)}, u32[]{:S(2)}) collective-permute-start(bf16[32,1152]{1,0:T(8,128)(2,1)S(1)} %get-tuple-element.27), channel_id=1, source_target_pairs={{0,14},{2,12},{4,10},{6,8},{8,6},{10,4},{12,2},{14,0},{1,15},{3,13... | collective-permute-start | bytes 221192 | tf_op jit(solution)/shard_map/ppermute | solution.py:173
  16.6 0.0 collective-permute-done.1
  16.6 0.7 %collective-permute-start.6 = (bf16[32,1152]{1,0:T(8,128)(2,1)S(1)}, bf16[32,1152]{1,0:T(8,128)(2,1)S(1)}, u32[]{:S(2)}, u32[]{:S(2)}) collective-permute-start(bf16[32,1152]{1,0:T(8,128)(2,1)S(1)} %get-tuple-element.28), channel_id=1, source_target_pairs={{0,2},{2,0},{4,6},{6,4},{8,10},{10,8},{12,14},{14,12},{1,3},{3,1},... | collective-permute-start | bytes 221192 | tf_op jit(solution)/shard_map/ppermute | solution.py:173
  17.4 0.0 collective-permute-done.2
  17.4 0.0 collective-permute-done.3
  17.4 1.1 %collective-permute-done.4 = bf16[32,1152]{1,0:T(8,128)(2,1)S(1)} collective-permute-done((bf16[32,1152]{1,0:T(8,128)(2,1)S(1)}, bf16[32,1152]{1,0:T(8,128)(2,1)S(1)}, u32[]{:S(2)}, u32[]{:S(2)}) %collective-permute-start.4) | collective-permute-done | bytes 73760 | tf_op jit(solution)/shard_map/ppermute | solution.py:173
  18.6 2.0 %collective-permute-done.5 = bf16[32,1152]{1,0:T(8,128)(2,1)S(1)} collective-permute-done((bf16[32,1152]{1,0:T(8,128)(2,1)S(1)}, bf16[32,1152]{1,0:T(8,128)(2,1)S(1)}, u32[]{:S(2)}, u32[]{:S(2)}) %collective-permute-start.5) | collective-permute-done | bytes 73760 | tf_op jit(solution)/shard_map/ppermute | solution.py:173
  20.6 0.7 %collective-permute-done.6 = bf16[32,1152]{1,0:T(8,128)(2,1)S(1)} collective-permute-done((bf16[32,1152]{1,0:T(8,128)(2,1)S(1)}, bf16[32,1152]{1,0:T(8,128)(2,1)S(1)}, u32[]{:S(2)}, u32[]{:S(2)}) %collective-permute-start.6) | collective-permute-done | bytes 73760 | tf_op jit(solution)/shard_map/ppermute | solution.py:173
  21.4 0.1 collective-permute-start.7
  21.5 0.9 %near.1 = (f32[288,128]{1,0:T(8,128)S(1)}, s32[288,128]{1,0:T(8,128)S(1)}, f32[288,1024]{1,0:T(8,128)S(1)}) custom-call(s32[1]{0:T(128)} %bitcast.me_ref, s32[1,512]{1,0:T(1,128)S(1)} %bitcast.6, bf16[256,1152]{1,0:T(8,128)(2,1)S(1)} %constant_dynamic-update-slice_fusion.query_ref), custom_call_target="tpu_custom_call" | custom-call | flops 268435456 | bytes 1179648 | tf_op jit(solution)/shard_map/near/pallas_call | solution.py:237
  22.4 1.1 %collective-permute-done.7.other_ref = bf16[256,1152]{1,0:T(8,128)(2,1)S(1)} collective-permute-done((bf16[256,1152]{1,0:T(8,128)(2,1)S(1)}, bf16[256,1152]{1,0:T(8,128)(2,1)S(1)}, u32[]{:S(2)}, u32[]{:S(2)}) %collective-permute-start.7) | collective-permute-done | bytes 589856 | tf_op jit(solution)/shard_map/ppermute | solution.py:173
  23.4 1.6 %far.1 = (f32[8,2,256]{2,1,0:T(2,128)S(1)}, f32[1,32]{1,0:T(1,128)}) custom-call(bf16[256,1152]{1,0:T(8,128)(2,1)S(1)} %constant_dynamic-update-slice_fusion.query_ref, bf16[256,1152]{1,0:T(8,128)(2,1)S(1)} %collective-permute-done.7.other_ref, f32[288,128]{1,0:T(8,128)S(1)} %get-tuple-element.30.column_ref, s32[288,128]{1,0:T(8,128)S(1)} %get-tuple-element.31.number_ref, ...), custom_call_target="tpu_custom_call" | custom-call | flops 268435456 | bytes 1179648 | tf_op jit(solution)/shard_map/far/pallas_call | solution.py:250
  25.0 11.1 %all_to_all.5.result_ref = f32[8,2,256]{2,1,0:T(2,128)S(1)} all-to-all(f32[8,2,256]{2,1,0:T(2,128)S(1)} %get-tuple-element.33), channel_id=1, replica_groups=mesh['groups'=2,'shard'=8,'sub'=2] {'shard'}, dimensions={0} | all-to-all | bytes 32768 | tf_op jit(solution)/shard_map/all_to_all | solution.py:262
  36.2 0.8 %pick.1 = (f32[1,128]{1,0:T(1,128)}, f32[1,128]{1,0:T(1,128)}) custom-call(s32[1]{0:T(128)} %bitcast.me_ref, s32[1,128]{1,0:T(1,128)S(1)} %get-tuple-element.20.slot_ref, f32[8,2,256]{2,1,0:T(2,128)S(1)} %all_to_all.5.result_ref), custom_call_target="tpu_custom_call" | custom-call | tf_op jit(solution)/shard_map/pick/pallas_call | solution.py:263
  (8 shorter events, 0.1 us)
Async XLA Ops:
  0.6 1.4 %copy-start = (bf16[128,1024]{1,0:T(8,128)(2,1)S(1)}, bf16[128,1024]{1,0:T(8,128)(2,1)}, u32[]{:S(2)}) copy-start(bf16[128,1024]{1,0:T(8,128)(2,1)} %embed_ref.1) | copy-start | bytes 786436
  2.4 11.0 %collective-permute-start = (bf16[32,1152]{1,0:T(8,128)(2,1)S(1)}, bf16[32,1152]{1,0:T(8,128)(2,1)S(1)}, u32[]{:S(2)}, u32[]{:S(2)}) collective-permute-start(bf16[32,1152]{1,0:T(8,128)(2,1)S(1)} %get-tuple-element.22), channel_id=1, source_target_pairs={{0,8},{2,10},{4,12},{6,14},{8,0},{10,2},{12,4},{14,6},{1,9},{3,11}... | collective-permute-start | bytes 221192 | tf_op jit(solution)/shard_map/ppermute | solution.py:173
  6.5 10.1 %collective-permute-start.1 = (bf16[32,1152]{1,0:T(8,128)(2,1)S(1)}, bf16[32,1152]{1,0:T(8,128)(2,1)S(1)}, u32[]{:S(2)}, u32[]{:S(2)}) collective-permute-start(bf16[32,1152]{1,0:T(8,128)(2,1)S(1)} %get-tuple-element.23), channel_id=1, source_target_pairs={{0,10},{2,8},{4,14},{6,12},{8,2},{10,0},{12,6},{14,4},{1,11},{3,9}... | collective-permute-start | bytes 221192 | tf_op jit(solution)/shard_map/ppermute | solution.py:173
  7.8 9.6 %collective-permute-start.2 = (bf16[32,1152]{1,0:T(8,128)(2,1)S(1)}, bf16[32,1152]{1,0:T(8,128)(2,1)S(1)}, u32[]{:S(2)}, u32[]{:S(2)}) collective-permute-start(bf16[32,1152]{1,0:T(8,128)(2,1)S(1)} %get-tuple-element.24), channel_id=1, source_target_pairs={{0,4},{2,6},{4,0},{6,2},{8,12},{10,14},{12,8},{14,10},{1,5},{3,7},... | collective-permute-start | bytes 221192 | tf_op jit(solution)/shard_map/ppermute | solution.py:173
  9.4 8.0 %collective-permute-start.3 = (bf16[32,1152]{1,0:T(8,128)(2,1)S(1)}, bf16[32,1152]{1,0:T(8,128)(2,1)S(1)}, u32[]{:S(2)}, u32[]{:S(2)}) collective-permute-start(bf16[32,1152]{1,0:T(8,128)(2,1)S(1)} %get-tuple-element.25), channel_id=1, source_target_pairs={{0,6},{2,4},{4,2},{6,0},{8,14},{10,12},{12,10},{14,8},{1,7},{3,5},... | collective-permute-start | bytes 221192 | tf_op jit(solution)/shard_map/ppermute | solution.py:173
  9.5 9.0 %collective-permute-start.4 = (bf16[32,1152]{1,0:T(8,128)(2,1)S(1)}, bf16[32,1152]{1,0:T(8,128)(2,1)S(1)}, u32[]{:S(2)}, u32[]{:S(2)}) collective-permute-start(bf16[32,1152]{1,0:T(8,128)(2,1)S(1)} %get-tuple-element.26), channel_id=1, source_target_pairs={{0,12},{2,14},{4,8},{6,10},{8,4},{10,6},{12,0},{14,2},{1,13},{3,15... | collective-permute-start | bytes 221192 | tf_op jit(solution)/shard_map/ppermute | solution.py:173
  13.4 7.2 %collective-permute-start.5 = (bf16[32,1152]{1,0:T(8,128)(2,1)S(1)}, bf16[32,1152]{1,0:T(8,128)(2,1)S(1)}, u32[]{:S(2)}, u32[]{:S(2)}) collective-permute-start(bf16[32,1152]{1,0:T(8,128)(2,1)S(1)} %get-tuple-element.27), channel_id=1, source_target_pairs={{0,14},{2,12},{4,10},{6,8},{8,6},{10,4},{12,2},{14,0},{1,15},{3,13... | collective-permute-start | bytes 221192 | tf_op jit(solution)/shard_map/ppermute | solution.py:173
  16.6 4.7 %collective-permute-start.6 = (bf16[32,1152]{1,0:T(8,128)(2,1)S(1)}, bf16[32,1152]{1,0:T(8,128)(2,1)S(1)}, u32[]{:S(2)}, u32[]{:S(2)}) collective-permute-start(bf16[32,1152]{1,0:T(8,128)(2,1)S(1)} %get-tuple-element.28), channel_id=1, source_target_pairs={{0,2},{2,0},{4,6},{6,4},{8,10},{10,8},{12,14},{14,12},{1,3},{3,1},... | collective-permute-start | bytes 221192 | tf_op jit(solution)/shard_map/ppermute | solution.py:173
  21.4 2.1 %collective-permute-start.7 = (bf16[256,1152]{1,0:T(8,128)(2,1)S(1)}, bf16[256,1152]{1,0:T(8,128)(2,1)S(1)}, u32[]{:S(2)}, u32[]{:S(2)}) collective-permute-start(bf16[256,1152]{1,0:T(8,128)(2,1)S(1)} %constant_dynamic-update-slice_fusion.query_ref), channel_id=1, source_target_pairs={{0,1},{1,0},{2,3},{3,2},{4,5},{5,4},{6,7},{7,6},{8,9},{9,8},{10,11... | collective-permute-start | bytes 1769480 | tf_op jit(solution)/shard_map/ppermute | solution.py:173

commit v10 on v8

v10 whole, which is shorter than its diff:
```python
import functools

import jax
import jax.numpy as jnp
from jax import lax
from jax.experimental import pallas as pl
from jax.experimental.pallas import tpu as pltpu
from jax.sharding import PartitionSpec as P

LANES = 128
DIGITS = 3
ONE = 2 * DIGITS
MOST_PERMUTES = 8
WHOLE = pl.BlockSpec(memory_space=pltpu.VMEM)
SCALAR = pl.BlockSpec(memory_space=pltpu.SMEM)


def iota(shape, dim):
    return lax.broadcasted_iota(jnp.int32, shape, dim)


def matmul(a, b):
    return jnp.dot(a, b, preferred_element_type=jnp.float32)


def matmul_t(a, b, precision=None):
    return lax.dot_general(
        a, b, (((1,), (1,)), ((), ())), precision=precision, preferred_element_type=jnp.float32
    )


def bf16(x):
    return x.astype(jnp.float32).astype(jnp.bfloat16)


def ranked(hot):
    upto = (iota((LANES, LANES), 0) <= iota((LANES, LANES), 1)).astype(jnp.bfloat16)
    before, parts = jnp.zeros((1, 1), jnp.float32), []
    for start in range(0, hot.shape[1], LANES):
        piece = hot[:, start : start + LANES]
        spread = jnp.broadcast_to(piece, (16, LANES)).astype(jnp.bfloat16)
        parts.append(matmul(spread, upto)[:1] + before)
        before = before + jnp.sum(piece, axis=1, keepdims=True)
    return jnp.concatenate(parts, axis=1)


def slot_kernel(
    owners, capacity, order, rows, me_ref, ints_ref, slot_ref, digit_ref
):
    clusters = ints_ref.shape[1] - 2 * rows
    cluster = ints_ref[:, clusters : clusters + rows]
    named = bf16(iota((clusters, rows), 0) == cluster)
    owner_map = bf16(jnp.broadcast_to(ints_ref[:, :clusters], (16, clusters)))
    owner = matmul(owner_map, named)[:1].astype(jnp.int32)
    hot = (iota((max(owners, 16), rows), 0) == owner).astype(jnp.float32)
    upto = bf16(iota((rows, rows), 0) <= iota((rows, rows), 1))
    rank = jnp.sum(hot * matmul(bf16(hot), upto), axis=0, keepdims=True) - 1.0
    partner = owner ^ me_ref[0]
    place = partner
    for index, k in enumerate(order):
        place = jnp.where(partner == k, index, place)
    slot_ref[...] = place * capacity + rank.astype(jnp.int32)

    line = iota((8, rows), 0)
    digit = (line == ONE).astype(jnp.int32)
    for first, number in ((0, cluster + 1), (DIGITS, ints_ref[:, clusters + rows :])):
        for at in range(DIGITS):
            digit = jnp.where(line == first + at, (number >> (8 * at)) & 255, digit)
    digit = jnp.concatenate([digit, jnp.zeros((LANES - 8, rows), jnp.int32)], axis=0)
    digit_ref[...] = bf16(digit)


def pack_kernel(slot_ref, digit_ref, embed_ref, *out_refs):
    rows, width = embed_ref.shape
    each = out_refs[0].shape[0]
    values = embed_ref[...].astype(jnp.float32)
    mean_sq = jnp.sum(values * values, axis=1, keepdims=True) * (1.0 / width)
    unit = (values * lax.rsqrt(width * (mean_sq + 1e-06))).astype(jnp.bfloat16)
    slots = each * len(out_refs)
    move = bf16(iota((slots, rows), 0) == slot_ref[...])
    moved = matmul(move, unit).astype(jnp.bfloat16)
    moved_digit = matmul_t(move, digit_ref[...]).astype(jnp.bfloat16)
    for index, out_ref in enumerate(out_refs):
        part = slice(index * each, (index + 1) * each)
        out_ref[:, :width] = moved[part]
        out_ref[:, width:] = moved_digit[part]


def weights(number, at):
    value = jnp.zeros(at.shape, jnp.float32)
    for place in range(DIGITS):
        for which in (0, 1):
            here = (at == which * DIGITS + place) & (number == which)
            value = jnp.where(here, 256.0**place, value)
    return value.astype(jnp.bfloat16)


def key_rows(rows_all, digit):
    numbers = matmul_t(weights(iota((16, LANES), 0), iota((16, LANES), 1)), digit)
    low = (numbers[0:1].astype(jnp.int32) - 1) * rows_all
    return low, low + numbers[1:2].astype(jnp.int32)


def key_columns(rows_all, digit):
    shape = (LANES, 2 * LANES)
    numbers = matmul(digit, weights(iota(shape, 1) // LANES, iota(shape, 0)))
    low = (numbers[:, :LANES].astype(jnp.int32) - 1) * rows_all
    return low, low + numbers[:, LANES:].astype(jnp.int32)


def across(column, count):
    return jnp.concatenate([column] * (count // LANES), axis=1)


def compare(rows_all, query, query_low, query_key, lows, rows_ref):
    count, width = query.shape
    digit = rows_ref[:, width:]
    _, key = key_rows(rows_all, digit)
    bound = across(lows, key.shape[1])
    member = bf16((key >= bound) & (key < bound + rows_all))
    sums = matmul(member, rows_ref[...])
    scores = matmul_t(rows_ref[:, :width], query)
    _, key = key_columns(rows_all, digit)
    key = across(key, count)
    earlier = (key >= query_low) & (key < query_key)
    best = jnp.max(jnp.where(earlier, scores, -3.0), axis=0, keepdims=True)
    return best, sums


def near_kernel(
    rows_all, clusters, clus_dev, me_ref, ints_ref, query_ref, lows_ref, key_ref, best_ref, sums_ref
):
    width = query_ref.shape[1] - LANES
    hot = (ints_ref[:, :clusters] == me_ref[0]).astype(jnp.float32)
    rank = ranked(hot)
    shape = (clus_dev, clusters)
    kth = (rank == iota(shape, 0).astype(jnp.float32) + 1.0) & (hot > 0.0)
    own = jnp.sum(jnp.where(kth, iota(shape, 1).astype(jnp.float32), 0.0), axis=1, keepdims=True)
    own = jnp.broadcast_to(own.astype(jnp.int32) * rows_all, (clus_dev, LANES))
    digit = query_ref[:, width:]
    low, _ = key_columns(rows_all, digit)
    lows = jnp.concatenate([low, own], axis=0)
    query_low, query_key = key_rows(rows_all, digit)
    best, sums = compare(rows_all, query_ref[:, :width], query_low, query_key, lows, query_ref)
    lows_ref[...] = lows
    key_ref[...] = jnp.concatenate([query_low, query_key], axis=0)
    best_ref[...] = best
    sums_ref[...] = sums


def far_kernel(
    rows_all, query_ref, other_ref, lows_ref, key_ref, best_ref, sums_ref, result_ref, cohesion_ref
):
    queries = query_ref.shape[0]
    width = query_ref.shape[1] - LANES
    query = query_ref[:, :width]
    best, sums = compare(
        rows_all, query, key_ref[0:1], key_ref[1:2], lows_ref[...], other_ref
    )
    best = jnp.maximum(best, best_ref[...])
    best = jnp.where(best > -2.0, best, 0.0)
    sums = sums + sums_ref[...]
    counts = sums[:, width + ONE : width + ONE + 1]
    centroid = sums[:, :width] * (1.0 / jnp.maximum(counts, 1.0))
    offset = jnp.concatenate(
        [query.astype(jnp.float32) - centroid[:queries], centroid[queries:]], axis=0
    )
    offset = offset * offset
    squares = offset[:, :LANES]
    for start in range(LANES, width, LANES):
        squares = squares + offset[:, start : start + LANES]
    ones = jnp.ones((8, LANES), jnp.float32)
    total = matmul_t(ones, squares, lax.Precision.HIGHEST)[:1]
    result = jnp.concatenate([best, total[:, :queries]], axis=0)
    for owner in range(result_ref.shape[0]):
        result_ref[owner] = result
    cohesion_ref[...] = total[:, queries:]


def pick_kernel(order, me_ref, slot_ref, result_ref, best_ref, distance_ref):
    rows = slot_ref.shape[1]
    owners, lines, slots = result_ref.shape
    place = iota((lines, slots), 1) // (slots // owners)
    values = jnp.zeros((lines, slots), jnp.float32)
    for index, k in enumerate(order):
        values = jnp.where(place == index, result_ref[me_ref[0] ^ k], values)
    values = jnp.concatenate([values, jnp.zeros((8 - lines, slots), jnp.float32)], axis=0)
    at = (iota((slots, rows), 0) == slot_ref[...]).astype(jnp.float32)
    picked = jnp.dot(
        values, at, precision=lax.Precision.HIGHEST, preferred_element_type=jnp.float32
    )
    best_ref[...] = picked[0:1]
    distance_ref[...] = picked[1:2]


def from_partner(value, k, axis):
    return lax.ppermute(value, axis, [(i, i ^ k) for i in range(lax.axis_size(axis))])


def partner_order(owners):
    half = owners // 2
    far, near = list(range(half, owners)), list(range(2, half))
    return far[:1] + near + far[1:] + list(range(1, min(half, 2))) + [0]


def exchange(packed, order):
    return jnp.concatenate(
        [from_partner(block, k, "shard") if k else block for k, block in zip(order, packed)]
    )


def exchange_all(packed, order, me):
    owners = lax.axis_size("shard")
    partner = me ^ jnp.array(order, jnp.int32)
    parted = packed.reshape(owners, -1, packed.shape[1])
    got = lax.all_to_all(parted[jnp.argsort(partner)], "shard", 0, 0, tiled=True)
    return got[partner].reshape(packed.shape)


def local(embeddings, cluster_id, item_order, owner_map):
    owners = lax.axis_size("shard")
    local_rows, width = embeddings.shape
    rows_all = local_rows * owners * lax.axis_size("sub")
    clus_dev = owner_map.shape[0] // owners
    capacity = 2 * local_rows // owners
    slots = owners * capacity
    wide = width + LANES
    params = pltpu.CompilerParams(vmem_limit_bytes=32 << 20)
    compare_cost = pl.CostEstimate(
        flops=4 * slots * slots * width, bytes_accessed=4 * slots * wide, transcendentals=0
    )
    me = lax.axis_index("shard").astype(jnp.int32).reshape(1)
    ints = jnp.concatenate([owner_map, cluster_id, item_order]).reshape(1, -1)

    direct = owners <= MOST_PERMUTES
    order = partner_order(owners)
    parts = owners if direct else 1
    slot, digit = pl.pallas_call(
        functools.partial(slot_kernel, owners, capacity, order, local_rows),
        out_shape=[
            jax.ShapeDtypeStruct((1, local_rows), jnp.int32),
            jax.ShapeDtypeStruct((LANES, local_rows), jnp.bfloat16),
        ],
        in_specs=[SCALAR, WHOLE],
        out_specs=[WHOLE] * 2,
        compiler_params=params,
        cost_estimate=pl.CostEstimate(flops=1 << 28, bytes_accessed=1 << 16, transcendentals=0),
        name="slots",
    )(me, ints)
    packed = pl.pallas_call(
        pack_kernel,
        out_shape=[jax.ShapeDtypeStruct((slots // parts, wide), jnp.bfloat16)] * parts,
        in_specs=[WHOLE] * 3,
        out_specs=[WHOLE] * parts,
        compiler_params=params,
        name="pack",
    )(slot, digit, embeddings)
    query = exchange(packed, order) if direct else exchange_all(packed[0], order, me)
    other = from_partner(query, 1, "sub")
    asked = slots + clus_dev
    near = pl.pallas_call(
        functools.partial(near_kernel, rows_all, owner_map.shape[0], clus_dev),
        out_shape=[
            jax.ShapeDtypeStruct((asked, LANES), jnp.int32),
            jax.ShapeDtypeStruct((2, slots), jnp.int32),
            jax.ShapeDtypeStruct((1, slots), jnp.float32),
            jax.ShapeDtypeStruct((asked, wide), jnp.float32),
        ],
        in_specs=[SCALAR] + [WHOLE] * 2,
        out_specs=[WHOLE] * 4,
        compiler_params=params,
        cost_estimate=compare_cost,
        name="near",
    )(me, ints, query)
    results, cohesion = pl.pallas_call(
        functools.partial(far_kernel, rows_all),
        out_shape=[
            jax.ShapeDtypeStruct((owners, 2, slots), jnp.float32),
            jax.ShapeDtypeStruct((1, clus_dev), jnp.float32),
        ],
        in_specs=[WHOLE] * 6,
        out_specs=[WHOLE] * 2,
        compiler_params=params,
        cost_estimate=compare_cost,
        name="far",
    )(query, other, *near)
    results = lax.all_to_all(results, "shard", 0, 0, tiled=True)
    best, distance = pl.pallas_call(
        functools.partial(pick_kernel, order),
        out_shape=[jax.ShapeDtypeStruct((1, local_rows), jnp.float32)] * 2,
        in_specs=[SCALAR] + [WHOLE] * 2,
        out_specs=[WHOLE] * 2,
        compiler_params=params,
        name="pick",
    )(me, slot, results)
    return best.reshape(local_rows), distance.reshape(local_rows), cohesion.reshape(clus_dev)


def solution(mesh):
    in_specs = (
        P(("groups", "shard", "sub"), None),
        P(("groups", "shard", "sub")),
        P(("groups", "shard", "sub")),
        P("groups"),
    )
    out_specs = (
        P(("groups", "shard", "sub")),
        P(("groups", "shard", "sub")),
        P(("groups", "shard")),
    )
    return jax.shard_map(local, mesh=mesh, in_specs=in_specs, out_specs=out_specs, check_vma=False)
```

time: 35.8 us -> 36.5 us (1.020)
  local copies, waits for them, and re-layouts: 0.1 us -> 1.05 us
  Pallas kernels: 4.34 us -> 3.88 us
    unnamed x9, local copies, waits for them, and re-layouts: 0.09 us -> 1.04 us
  transfers between devices with their start and end apart: 8 -> 8, of which waited for: 4 -> 4; matrix products, arithmetic and copies ran while one was open for 0% -> 0% of each run, Pallas kernels for 3% -> 2%
where the time goes in v10:
time: 36.5 us; the launch traced here: 36.3 us
  starting transfers between devices  13.4 us (37%)
  blocking collectives  10.2 us (28%)
  waiting for transfers between devices  6.26 us (17%)
  Pallas kernels  3.88 us (11%)
  local copies, waits for them, and re-layouts  1.05 us (3%)
  other arithmetic  0.72 us (2%)
  between operations  0.7 us (2%)
    ppermute x8, starting transfers between devices, from_partner(): lax.ppermute(value, axis, [(i, i ^ k) for i in range(lax.axis_size(axis))])  13.4 us
    all_to_all x1, blocking collectives, local(): results = lax.all_to_all(results, 'shard', 0, 0, tiled=True)  10.2 us
    ppermute x8, waiting for transfers between devices, from_partner(): lax.ppermute(value, axis, [(i, i ^ k) for i in range(lax.axis_size(axis))])  6.26 us
    pallas_call x1, Pallas kernels, local(): pl.pallas_call(functools.partial(far_kernel, rows_all), out_shape=[jax.Sh...  1.78 us
    unnamed x9, local copies, waits for them, and re-layouts  1.04 us
  transfers between devices with their start and end apart: 8, of which 4 were waited for; matrix products, arithmetic and copies ran while one was open for 0% of the time, Pallas kernels for 2%

profile of v10, /device:TPU:0, one launch (start us, length us, event | category | flops | bytes accessed | tf_op | source)
XLA Modules:
  0.0 36.3 jit_solution(6995375276171139347)
XLA Ops:
  0.6 0.7 %pad_add_fusion = s32[512]{0:T(512)S(1)} fusion(s32[128]{0:T(128)} %param.6, s32[128]{0:T(128)} %param.5, s32[256]{0:T(256)} %param.7), kind=kLoop, calls=%fused_computation.8 | loop fusion | flops 1024 | bytes 4096 | tf_op jit(solution)/shard_map/concatenate | solution.py:233
  1.4 0.3 slots.1
  1.6 0.0 copy-start
  1.6 1.0 %copy-done = bf16[128,1024]{1,0:T(8,128)(2,1)S(1)} copy-done((bf16[128,1024]{1,0:T(8,128)(2,1)S(1)}, bf16[128,1024]{1,0:T(8,128)(2,1)}, u32[]{:S(2)}) %copy-start) | copy-done | bytes 262168
  2.6 0.4 %pack.1 = (bf16[32,1152]{1,0:T(8,128)(2,1)S(1)}, bf16[32,1152]{1,0:T(8,128)(2,1)S(1)}, bf16[32,1152]{1,0:T(8,128)(2,1)S(1)}, bf16[32,1152]{1,0:T(8,128)(2,1)S(1)...) custom-call(s32[1,128]{1,0:T(1,128)S(1)} %get-tuple-element.21.slot_, ...), custom_call_target="tpu_custom_call" | custom-call | tf_op jit(solution)/shard_map/pack/pallas_call | solution.py:250
  3.0 4.1 %collective-permute-start = (bf16[32,1152]{1,0:T(8,128)(2,1)S(1)}, bf16[32,1152]{1,0:T(8,128)(2,1)S(1)}, u32[]{:S(2)}, u32[]{:S(2)}) collective-permute-start(bf16[32,1152]{1,0:T(8,128)(2,1)S(1)} %get-tuple-element.23), channel_id=1, source_target_pairs={{0,8},{2,10},{4,12},{6,14},{8,0},{10,2},{12,4},{14,6},{1,9},{3,11}... | collective-permute-start | bytes 221192 | tf_op jit(solution)/shard_map/ppermute | solution.py:197
  7.1 1.6 %collective-permute-start.1 = (bf16[32,1152]{1,0:T(8,128)(2,1)S(1)}, bf16[32,1152]{1,0:T(8,128)(2,1)S(1)}, u32[]{:S(2)}, u32[]{:S(2)}) collective-permute-start(bf16[32,1152]{1,0:T(8,128)(2,1)S(1)} %get-tuple-element.24), channel_id=1, source_target_pairs={{0,4},{2,6},{4,0},{6,2},{8,12},{10,14},{12,8},{14,10},{1,5},{3,7},... | collective-permute-start | bytes 221192 | tf_op jit(solution)/shard_map/ppermute | solution.py:197
  8.7 1.4 %collective-permute-start.2 = (bf16[32,1152]{1,0:T(8,128)(2,1)S(1)}, bf16[32,1152]{1,0:T(8,128)(2,1)S(1)}, u32[]{:S(2)}, u32[]{:S(2)}) collective-permute-start(bf16[32,1152]{1,0:T(8,128)(2,1)S(1)} %get-tuple-element.25), channel_id=1, source_target_pairs={{0,6},{2,4},{4,2},{6,0},{8,14},{10,12},{12,10},{14,8},{1,7},{3,5},... | collective-permute-start | bytes 221192 | tf_op jit(solution)/shard_map/ppermute | solution.py:197
  10.1 0.1 collective-permute-start.3
  10.1 3.9 %collective-permute-start.4 = (bf16[32,1152]{1,0:T(8,128)(2,1)S(1)}, bf16[32,1152]{1,0:T(8,128)(2,1)S(1)}, u32[]{:S(2)}, u32[]{:S(2)}) collective-permute-start(bf16[32,1152]{1,0:T(8,128)(2,1)S(1)} %get-tuple-element.27), channel_id=1, source_target_pairs={{0,12},{2,14},{4,8},{6,10},{8,4},{10,6},{12,0},{14,2},{1,13},{3,15... | collective-permute-start | bytes 221192 | tf_op jit(solution)/shard_map/ppermute | solution.py:197
  14.0 0.0 collective-permute-done
  14.0 1.8 %collective-permute-start.5 = (bf16[32,1152]{1,0:T(8,128)(2,1)S(1)}, bf16[32,1152]{1,0:T(8,128)(2,1)S(1)}, u32[]{:S(2)}, u32[]{:S(2)}) collective-permute-start(bf16[32,1152]{1,0:T(8,128)(2,1)S(1)} %get-tuple-element.28), channel_id=1, source_target_pairs={{0,14},{2,12},{4,10},{6,8},{8,6},{10,4},{12,2},{14,0},{1,15},{3,13... | collective-permute-start | bytes 221192 | tf_op jit(solution)/shard_map/ppermute | solution.py:197
  15.8 0.0 collective-permute-done.1
  15.8 0.6 %collective-permute-start.6 = (bf16[32,1152]{1,0:T(8,128)(2,1)S(1)}, bf16[32,1152]{1,0:T(8,128)(2,1)S(1)}, u32[]{:S(2)}, u32[]{:S(2)}) collective-permute-start(bf16[32,1152]{1,0:T(8,128)(2,1)S(1)} %get-tuple-element.29), channel_id=1, source_target_pairs={{0,2},{2,0},{4,6},{6,4},{8,10},{10,8},{12,14},{14,12},{1,3},{3,1},... | collective-permute-start | bytes 221192 | tf_op jit(solution)/shard_map/ppermute | solution.py:197
  16.4 0.0 collective-permute-done.2
  16.4 3.8 %collective-permute-done.3 = bf16[32,1152]{1,0:T(8,128)(2,1)S(1)} collective-permute-done((bf16[32,1152]{1,0:T(8,128)(2,1)S(1)}, bf16[32,1152]{1,0:T(8,128)(2,1)S(1)}, u32[]{:S(2)}, u32[]{:S(2)}) %collective-permute-start.3) | collective-permute-done | bytes 73760 | tf_op jit(solution)/shard_map/ppermute | solution.py:197
  20.2 0.0 collective-permute-done.4
  20.3 0.9 %collective-permute-done.5 = bf16[32,1152]{1,0:T(8,128)(2,1)S(1)} collective-permute-done((bf16[32,1152]{1,0:T(8,128)(2,1)S(1)}, bf16[32,1152]{1,0:T(8,128)(2,1)S(1)}, u32[]{:S(2)}, u32[]{:S(2)}) %collective-permute-start.5) | collective-permute-done | bytes 73760 | tf_op jit(solution)/shard_map/ppermute | solution.py:197
  21.2 0.2 collective-permute-done.6
  21.5 0.1 collective-permute-start.7
  21.6 0.7 %near.1 = (s32[288,128]{1,0:T(8,128)S(1)}, s32[2,256]{1,0:T(2,128)S(1)}, f32[1,256]{1,0:T(1,128)S(1)}, f32[288,1152]{1,0:T(8,128)S(1)}) custom-call(s32[1]{0:T(128)} %bitcast.me_ref, s32[1,512]{1,0:T(1,128)S(1)} %bitcast.6, bf16[256,1152]{1,0:T(8,128)(2,1)S(1)} %constant_dynamic-update-slice_fusion.query_ref), custom_call_target="tpu_custom_call" | custom-call | flops 268435456 | bytes 1179648 | tf_op jit(solution)/shard_map/near/pallas_call | solution.py:261
  22.3 1.3 %collective-permute-done.7.other_ref = bf16[256,1152]{1,0:T(8,128)(2,1)S(1)} collective-permute-done((bf16[256,1152]{1,0:T(8,128)(2,1)S(1)}, bf16[256,1152]{1,0:T(8,128)(2,1)S(1)}, u32[]{:S(2)}, u32[]{:S(2)}) %collective-permute-start.7) | collective-permute-done | bytes 589856 | tf_op jit(solution)/shard_map/ppermute | solution.py:197
  23.6 1.8 %far.1 = (f32[8,2,256]{2,1,0:T(2,128)S(1)}, f32[1,32]{1,0:T(1,128)}) custom-call(bf16[256,1152]{1,0:T(8,128)(2,1)S(1)} %constant_dynamic-update-slice_fusion.query_ref, bf16[256,1152]{1,0:T(8,128)(2,1)S(1)} %collective-permute-done.7.other_ref, s32[288,128]{1,0:T(8,128)S(1)} %get-tuple-element.31.lows_ref, s32[2,256]{1,0:T(2,128)S(1)} %get-tuple-element.32.key_ref, ...), custom_call_target="tpu_custom_call" | custom-call | flops 268435456 | bytes 1179648 | tf_op jit(solution)/shard_map/far/pallas_call | solution.py:275
  25.3 10.2 %all_to_all.5.result_ref = f32[8,2,256]{2,1,0:T(2,128)S(1)} all-to-all(f32[8,2,256]{2,1,0:T(2,128)S(1)} %get-tuple-element.35), channel_id=1, replica_groups=mesh['groups'=2,'shard'=8,'sub'=2] {'shard'}, dimensions={0} | all-to-all | bytes 32768 | tf_op jit(solution)/shard_map/all_to_all | solution.py:287
  35.6 0.7 %pick.1 = (f32[1,128]{1,0:T(1,128)}, f32[1,128]{1,0:T(1,128)}) custom-call(s32[1]{0:T(128)} %bitcast.me_ref, s32[1,128]{1,0:T(1,128)S(1)} %get-tuple-element.21.slot_ref, f32[8,2,256]{2,1,0:T(2,128)S(1)} %all_to_all.5.result_ref), custom_call_target="tpu_custom_call" | custom-call | tf_op jit(solution)/shard_map/pick/pallas_call | solution.py:288
  (8 shorter events, 0.1 us)
Async XLA Ops:
  1.6 1.0 %copy-start = (bf16[128,1024]{1,0:T(8,128)(2,1)S(1)}, bf16[128,1024]{1,0:T(8,128)(2,1)}, u32[]{:S(2)}) copy-start(bf16[128,1024]{1,0:T(8,128)(2,1)} %embed_ref.1) | copy-start | bytes 786436
  3.0 11.0 %collective-permute-start = (bf16[32,1152]{1,0:T(8,128)(2,1)S(1)}, bf16[32,1152]{1,0:T(8,128)(2,1)S(1)}, u32[]{:S(2)}, u32[]{:S(2)}) collective-permute-start(bf16[32,1152]{1,0:T(8,128)(2,1)S(1)} %get-tuple-element.23), channel_id=1, source_target_pairs={{0,8},{2,10},{4,12},{6,14},{8,0},{10,2},{12,4},{14,6},{1,9},{3,11}... | collective-permute-start | bytes 221192 | tf_op jit(solution)/shard_map/ppermute | solution.py:197
  7.1 8.7 %collective-permute-start.1 = (bf16[32,1152]{1,0:T(8,128)(2,1)S(1)}, bf16[32,1152]{1,0:T(8,128)(2,1)S(1)}, u32[]{:S(2)}, u32[]{:S(2)}) collective-permute-start(bf16[32,1152]{1,0:T(8,128)(2,1)S(1)} %get-tuple-element.24), channel_id=1, source_target_pairs={{0,4},{2,6},{4,0},{6,2},{8,12},{10,14},{12,8},{14,10},{1,5},{3,7},... | collective-permute-start | bytes 221192 | tf_op jit(solution)/shard_map/ppermute | solution.py:197
  8.7 7.7 %collective-permute-start.2 = (bf16[32,1152]{1,0:T(8,128)(2,1)S(1)}, bf16[32,1152]{1,0:T(8,128)(2,1)S(1)}, u32[]{:S(2)}, u32[]{:S(2)}) collective-permute-start(bf16[32,1152]{1,0:T(8,128)(2,1)S(1)} %get-tuple-element.25), channel_id=1, source_target_pairs={{0,6},{2,4},{4,2},{6,0},{8,14},{10,12},{12,10},{14,8},{1,7},{3,5},... | collective-permute-start | bytes 221192 | tf_op jit(solution)/shard_map/ppermute | solution.py:197
  10.1 10.2 %collective-permute-start.3 = (bf16[32,1152]{1,0:T(8,128)(2,1)S(1)}, bf16[32,1152]{1,0:T(8,128)(2,1)S(1)}, u32[]{:S(2)}, u32[]{:S(2)}) collective-permute-start(bf16[32,1152]{1,0:T(8,128)(2,1)S(1)} %get-tuple-element.26), channel_id=1, source_target_pairs={{0,10},{2,8},{4,14},{6,12},{8,2},{10,0},{12,6},{14,4},{1,11},{3,9}... | collective-permute-start | bytes 221192 | tf_op jit(solution)/shard_map/ppermute | solution.py:197
  10.1 10.1 %collective-permute-start.4 = (bf16[32,1152]{1,0:T(8,128)(2,1)S(1)}, bf16[32,1152]{1,0:T(8,128)(2,1)S(1)}, u32[]{:S(2)}, u32[]{:S(2)}) collective-permute-start(bf16[32,1152]{1,0:T(8,128)(2,1)S(1)} %get-tuple-element.27), channel_id=1, source_target_pairs={{0,12},{2,14},{4,8},{6,10},{8,4},{10,6},{12,0},{14,2},{1,13},{3,15... | collective-permute-start | bytes 221192 | tf_op jit(solution)/shard_map/ppermute | solution.py:197
  14.0 7.2 %collective-permute-start.5 = (bf16[32,1152]{1,0:T(8,128)(2,1)S(1)}, bf16[32,1152]{1,0:T(8,128)(2,1)S(1)}, u32[]{:S(2)}, u32[]{:S(2)}) collective-permute-start(bf16[32,1152]{1,0:T(8,128)(2,1)S(1)} %get-tuple-element.28), channel_id=1, source_target_pairs={{0,14},{2,12},{4,10},{6,8},{8,6},{10,4},{12,2},{14,0},{1,15},{3,13... | collective-permute-start | bytes 221192 | tf_op jit(solution)/shard_map/ppermute | solution.py:197
  15.8 5.6 %collective-permute-start.6 = (bf16[32,1152]{1,0:T(8,128)(2,1)S(1)}, bf16[32,1152]{1,0:T(8,128)(2,1)S(1)}, u32[]{:S(2)}, u32[]{:S(2)}) collective-permute-start(bf16[32,1152]{1,0:T(8,128)(2,1)S(1)} %get-tuple-element.29), channel_id=1, source_target_pairs={{0,2},{2,0},{4,6},{6,4},{8,10},{10,8},{12,14},{14,12},{1,3},{3,1},... | collective-permute-start | bytes 221192 | tf_op jit(solution)/shard_map/ppermute | solution.py:197
  21.5 2.1 %collective-permute-start.7 = (bf16[256,1152]{1,0:T(8,128)(2,1)S(1)}, bf16[256,1152]{1,0:T(8,128)(2,1)S(1)}, u32[]{:S(2)}, u32[]{:S(2)}) collective-permute-start(bf16[256,1152]{1,0:T(8,128)(2,1)S(1)} %constant_dynamic-update-slice_fusion.query_ref), channel_id=1, source_target_pairs={{0,1},{1,0},{2,3},{3,2},{4,5},{5,4},{6,7},{7,6},{8,9},{9,8},{10,11... | collective-permute-start | bytes 1769480 | tf_op jit(solution)/shard_map/ppermute | solution.py:197

commit v11 on v10

--- a/solution.py
+++ b/solution.py
@@ -149,7 +149,7 @@
 
 
 def far_kernel(
-    rows_all, query_ref, other_ref, lows_ref, key_ref, best_ref, sums_ref, result_ref, cohesion_ref
+    rows_all, query_ref, other_ref, lows_ref, key_ref, best_ref, sums_ref, result_ref, norm_ref
 ):
     queries = query_ref.shape[0]
     width = query_ref.shape[1] - LANES
@@ -174,10 +174,13 @@
     result = jnp.concatenate([best, total[:, :queries]], axis=0)
     for owner in range(result_ref.shape[0]):
         result_ref[owner] = result
-    cohesion_ref[...] = total[:, queries:]
-
-
-def pick_kernel(order, me_ref, slot_ref, result_ref, best_ref, distance_ref):
+    norm_ref[...] = total[:, queries:]
+
+
+def pick_kernel(
+    order, me_ref, slot_ref, result_ref, norm_ref, best_ref, distance_ref, cohesion_ref
+):
+    cohesion_ref[...] = norm_ref[...]
     rows = slot_ref.shape[1]
     owners, lines, slots = result_ref.shape
     place = iota((lines, slots), 1) // (slots // owners)
@@ -244,7 +247,7 @@
         in_specs=[SCALAR, WHOLE],
         out_specs=[WHOLE] * 2,
         compiler_params=params,
-        cost_estimate=pl.CostEstimate(flops=1 << 28, bytes_accessed=1 << 16, transcendentals=0),
+        cost_estimate=pl.CostEstimate(flops=1 << 29, bytes_accessed=1 << 16, transcendentals=0),
         name="slots",
     )(me, ints)
     packed = pl.pallas_call(
@@ -272,7 +275,7 @@
         cost_estimate=compare_cost,
         name="near",
     )(me, ints, query)
-    results, cohesion = pl.pallas_call(
+    results, norms = pl.pallas_call(
         functools.partial(far_kernel, rows_all),
         out_shape=[
             jax.ShapeDtypeStruct((owners, 2, slots), jnp.float32),
@@ -285,14 +288,15 @@
         name="far",
     )(query, other, *near)
     results = lax.all_to_all(results, "shard", 0, 0, tiled=True)
-    best, distance = pl.pallas_call(
+    best, distance, cohesion = pl.pallas_call(
         functools.partial(pick_kernel, order),
-        out_shape=[jax.ShapeDtypeStruct((1, local_rows), jnp.float32)] * 2,
-        in_specs=[SCALAR] + [WHOLE] * 2,
-        out_specs=[WHOLE] * 2,
+        out_shape=[jax.ShapeDtypeStruct((1, local_rows), jnp.float32)] * 2
+        + [jax.ShapeDtypeStruct((1, clus_dev), jnp.float32)],
+        in_specs=[SCALAR] + [WHOLE] * 3,
+        out_specs=[WHOLE] * 3,
         compiler_params=params,
         name="pick",
-    )(me, slot, results)
+    )(me, slot, results, norms)
     return best.reshape(local_rows), distance.reshape(local_rows), cohesion.reshape(clus_dev)
 
 

time: 36.5 us -> 35 us (0.959)
  local copies, waits for them, and re-layouts: 1.05 us -> 0.1 us
  Pallas kernels: 3.88 us -> 3.33 us
    unnamed x9, local copies, waits for them, and re-layouts: 1.04 us -> 0.09 us
    pallas_call x1, Pallas kernels: 1.78 us -> 1.21 us  [local(): pl.pallas_call(functools.partial(far_kernel, rows_all), out_shape=[jax.Sh...]
where the time goes in v11:
time: 35 us; the launch traced here: 34.8 us
  starting transfers between devices  13.4 us (38%)
  blocking collectives  10.3 us (29%)
  waiting for transfers between devices  6.22 us (18%)
  Pallas kernels  3.33 us (10%)
  other arithmetic  0.76 us (2%)
  between operations  0.71 us (2%)
    ppermute x8, starting transfers between devices, from_partner(): lax.ppermute(value, axis, [(i, i ^ k) for i in range(lax.axis_size(axis))])  13.4 us
    all_to_all x1, blocking collectives, local(): results = lax.all_to_all(results, 'shard', 0, 0, tiled=True)  10.3 us
    ppermute x8, waiting for transfers between devices, from_partner(): lax.ppermute(value, axis, [(i, i ^ k) for i in range(lax.axis_size(axis))])  6.22 us
    pallas_call x1, Pallas kernels, local(): pl.pallas_call(functools.partial(far_kernel, rows_all), out_shape=[jax.Sh...  1.21 us
    concatenate x1, other arithmetic, local(): ints = jnp.concatenate([owner_map, cluster_id, item_order]).reshape(1, -1)  0.76 us
    pallas_call x1, Pallas kernels, local(): pl.pallas_call(functools.partial(pick_kernel, order), out_shape=[jax.Shap...  0.71 us
    pallas_call x1, Pallas kernels, local(): pl.pallas_call(functools.partial(near_kernel, rows_all, owner_map.shape[0...  0.71 us
  transfers between devices with their start and end apart: 8, of which 4 were waited for; matrix products, arithmetic and copies ran while one was open for 0% of the time, Pallas kernels for 2%

profile of v11, /device:TPU:0, one launch (start us, length us, event | category | flops | bytes accessed | tf_op | source)
XLA Modules:
  0.0 34.8 jit_solution(2329813259442946060)
XLA Ops:
  0.6 0.0 copy-start
  0.6 0.8 %pad_add_fusion = s32[512]{0:T(512)S(1)} fusion(s32[128]{0:T(128)} %param.6, s32[128]{0:T(128)} %param.5, s32[256]{0:T(256)} %param.7), kind=kLoop, calls=%fused_computation.8 | loop fusion | flops 1024 | bytes 4096 | tf_op jit(solution)/shard_map/concatenate | solution.py:236
  1.4 0.3 slots.1
  1.7 0.0 copy-done
  1.7 0.4 %pack.1 = (bf16[32,1152]{1,0:T(8,128)(2,1)S(1)}, bf16[32,1152]{1,0:T(8,128)(2,1)S(1)}, bf16[32,1152]{1,0:T(8,128)(2,1)S(1)}, bf16[32,1152]{1,0:T(8,128)(2,1)S(1)...) custom-call(s32[1,128]{1,0:T(1,128)S(1)} %get-tuple-element.22.slot_, ...), custom_call_target="tpu_custom_call" | custom-call | tf_op jit(solution)/shard_map/pack/pallas_call | solution.py:253
  2.1 4.1 %collective-permute-start = (bf16[32,1152]{1,0:T(8,128)(2,1)S(1)}, bf16[32,1152]{1,0:T(8,128)(2,1)S(1)}, u32[]{:S(2)}, u32[]{:S(2)}) collective-permute-start(bf16[32,1152]{1,0:T(8,128)(2,1)S(1)} %get-tuple-element.24), channel_id=1, source_target_pairs={{0,8},{2,10},{4,12},{6,14},{8,0},{10,2},{12,4},{14,6},{1,9},{3,11}... | collective-permute-start | bytes 221192 | tf_op jit(solution)/shard_map/ppermute | solution.py:200
  6.2 1.6 %collective-permute-start.1 = (bf16[32,1152]{1,0:T(8,128)(2,1)S(1)}, bf16[32,1152]{1,0:T(8,128)(2,1)S(1)}, u32[]{:S(2)}, u32[]{:S(2)}) collective-permute-start(bf16[32,1152]{1,0:T(8,128)(2,1)S(1)} %get-tuple-element.25), channel_id=1, source_target_pairs={{0,4},{2,6},{4,0},{6,2},{8,12},{10,14},{12,8},{14,10},{1,5},{3,7},... | collective-permute-start | bytes 221192 | tf_op jit(solution)/shard_map/ppermute | solution.py:200
  7.8 1.4 %collective-permute-start.2 = (bf16[32,1152]{1,0:T(8,128)(2,1)S(1)}, bf16[32,1152]{1,0:T(8,128)(2,1)S(1)}, u32[]{:S(2)}, u32[]{:S(2)}) collective-permute-start(bf16[32,1152]{1,0:T(8,128)(2,1)S(1)} %get-tuple-element.26), channel_id=1, source_target_pairs={{0,6},{2,4},{4,2},{6,0},{8,14},{10,12},{12,10},{14,8},{1,7},{3,5},... | collective-permute-start | bytes 221192 | tf_op jit(solution)/shard_map/ppermute | solution.py:200
  9.2 0.1 collective-permute-start.3
  9.2 3.9 %collective-permute-start.4 = (bf16[32,1152]{1,0:T(8,128)(2,1)S(1)}, bf16[32,1152]{1,0:T(8,128)(2,1)S(1)}, u32[]{:S(2)}, u32[]{:S(2)}) collective-permute-start(bf16[32,1152]{1,0:T(8,128)(2,1)S(1)} %get-tuple-element.28), channel_id=1, source_target_pairs={{0,12},{2,14},{4,8},{6,10},{8,4},{10,6},{12,0},{14,2},{1,13},{3,15... | collective-permute-start | bytes 221192 | tf_op jit(solution)/shard_map/ppermute | solution.py:200
  13.1 0.0 collective-permute-done
  13.1 1.9 %collective-permute-start.5 = (bf16[32,1152]{1,0:T(8,128)(2,1)S(1)}, bf16[32,1152]{1,0:T(8,128)(2,1)S(1)}, u32[]{:S(2)}, u32[]{:S(2)}) collective-permute-start(bf16[32,1152]{1,0:T(8,128)(2,1)S(1)} %get-tuple-element.29), channel_id=1, source_target_pairs={{0,14},{2,12},{4,10},{6,8},{8,6},{10,4},{12,2},{14,0},{1,15},{3,13... | collective-permute-start | bytes 221192 | tf_op jit(solution)/shard_map/ppermute | solution.py:200
  14.9 0.0 collective-permute-done.1
  15.0 0.5 %collective-permute-start.6 = (bf16[32,1152]{1,0:T(8,128)(2,1)S(1)}, bf16[32,1152]{1,0:T(8,128)(2,1)S(1)}, u32[]{:S(2)}, u32[]{:S(2)}) collective-permute-start(bf16[32,1152]{1,0:T(8,128)(2,1)S(1)} %get-tuple-element.30), channel_id=1, source_target_pairs={{0,2},{2,0},{4,6},{6,4},{8,10},{10,8},{12,14},{14,12},{1,3},{3,1},... | collective-permute-start | bytes 221192 | tf_op jit(solution)/shard_map/ppermute | solution.py:200
  15.5 0.0 collective-permute-done.2
  15.5 3.8 %collective-permute-done.3 = bf16[32,1152]{1,0:T(8,128)(2,1)S(1)} collective-permute-done((bf16[32,1152]{1,0:T(8,128)(2,1)S(1)}, bf16[32,1152]{1,0:T(8,128)(2,1)S(1)}, u32[]{:S(2)}, u32[]{:S(2)}) %collective-permute-start.3) | collective-permute-done | bytes 73760 | tf_op jit(solution)/shard_map/ppermute | solution.py:200
  19.3 0.0 collective-permute-done.4
  19.4 0.9 %collective-permute-done.5 = bf16[32,1152]{1,0:T(8,128)(2,1)S(1)} collective-permute-done((bf16[32,1152]{1,0:T(8,128)(2,1)S(1)}, bf16[32,1152]{1,0:T(8,128)(2,1)S(1)}, u32[]{:S(2)}, u32[]{:S(2)}) %collective-permute-start.5) | collective-permute-done | bytes 73760 | tf_op jit(solution)/shard_map/ppermute | solution.py:200
  20.3 0.2 collective-permute-done.6
  20.6 0.1 collective-permute-start.7
  20.6 0.7 %near.1 = (s32[288,128]{1,0:T(8,128)S(1)}, s32[2,256]{1,0:T(2,128)S(1)}, f32[1,256]{1,0:T(1,128)S(1)}, f32[288,1152]{1,0:T(8,128)S(1)}) custom-call(s32[1]{0:T(128)} %bitcast.me_ref, s32[1,512]{1,0:T(1,128)S(1)} %bitcast.6, bf16[256,1152]{1,0:T(8,128)(2,1)S(1)} %constant_dynamic-update-slice_fusion.query_ref), custom_call_target="tpu_custom_call" | custom-call | flops 268435456 | bytes 1179648 | tf_op jit(solution)/shard_map/near/pallas_call | solution.py:264
  21.4 1.3 %collective-permute-done.7.other_ref = bf16[256,1152]{1,0:T(8,128)(2,1)S(1)} collective-permute-done((bf16[256,1152]{1,0:T(8,128)(2,1)S(1)}, bf16[256,1152]{1,0:T(8,128)(2,1)S(1)}, u32[]{:S(2)}, u32[]{:S(2)}) %collective-permute-start.7) | collective-permute-done | bytes 589856 | tf_op jit(solution)/shard_map/ppermute | solution.py:200
  22.6 1.2 %far.1 = (f32[8,2,256]{2,1,0:T(2,128)S(1)}, f32[1,32]{1,0:T(1,128)S(1)}) custom-call(bf16[256,1152]{1,0:T(8,128)(2,1)S(1)} %constant_dynamic-update-slice_fusion.query_ref, bf16[256,1152]{1,0:T(8,128)(2,1)S(1)} %collective-permute-done.7.other_ref, s32[288,128]{1,0:T(8,128)S(1)} %get-tuple-element.32.lows_ref, s32[2,256]{1,0:T(2,128)S(1)} %get-tuple-element.33.key_ref, ...), custom_call_target="tpu_custom_call" | custom-call | flops 268435456 | bytes 1179648 | tf_op jit(solution)/shard_map/far/pallas_call | solution.py:278
  23.9 10.3 %all_to_all.5.result_ref = f32[8,2,256]{2,1,0:T(2,128)S(1)} all-to-all(f32[8,2,256]{2,1,0:T(2,128)S(1)} %get-tuple-element.36), channel_id=1, replica_groups=mesh['groups'=2,'shard'=8,'sub'=2] {'shard'}, dimensions={0} | all-to-all | bytes 32768 | tf_op jit(solution)/shard_map/all_to_all | solution.py:290
  34.1 0.7 %pick.1 = (f32[1,128]{1,0:T(1,128)}, f32[1,128]{1,0:T(1,128)}, f32[1,32]{1,0:T(1,128)}) custom-call(s32[1]{0:T(128)} %bitcast.me_ref, s32[1,128]{1,0:T(1,128)S(1)} %get-tuple-element.22.slot_ref, f32[8,2,256]{2,1,0:T(2,128)S(1)} %all_to_all.5.result_ref, f32[1,32]{1,0:T(1,128)S(1)} %get-tuple-element.37.norm_ref), custom_call_target="tpu_custom_call" | custom-call | tf_op jit(solution)/shard_map/pick/pallas_call | solution.py:291
  (8 shorter events, 0.1 us)
Async XLA Ops:
  0.6 1.0 %copy-start = (bf16[128,1024]{1,0:T(8,128)(2,1)S(1)}, bf16[128,1024]{1,0:T(8,128)(2,1)}, u32[]{:S(2)}) copy-start(bf16[128,1024]{1,0:T(8,128)(2,1)} %embed_ref.1) | copy-start | bytes 786436
  2.1 11.0 %collective-permute-start = (bf16[32,1152]{1,0:T(8,128)(2,1)S(1)}, bf16[32,1152]{1,0:T(8,128)(2,1)S(1)}, u32[]{:S(2)}, u32[]{:S(2)}) collective-permute-start(bf16[32,1152]{1,0:T(8,128)(2,1)S(1)} %get-tuple-element.24), channel_id=1, source_target_pairs={{0,8},{2,10},{4,12},{6,14},{8,0},{10,2},{12,4},{14,6},{1,9},{3,11}... | collective-permute-start | bytes 221192 | tf_op jit(solution)/shard_map/ppermute | solution.py:200
  6.2 8.7 %collective-permute-start.1 = (bf16[32,1152]{1,0:T(8,128)(2,1)S(1)}, bf16[32,1152]{1,0:T(8,128)(2,1)S(1)}, u32[]{:S(2)}, u32[]{:S(2)}) collective-permute-start(bf16[32,1152]{1,0:T(8,128)(2,1)S(1)} %get-tuple-element.25), channel_id=1, source_target_pairs={{0,4},{2,6},{4,0},{6,2},{8,12},{10,14},{12,8},{14,10},{1,5},{3,7},... | collective-permute-start | bytes 221192 | tf_op jit(solution)/shard_map/ppermute | solution.py:200
  7.8 7.7 %collective-permute-start.2 = (bf16[32,1152]{1,0:T(8,128)(2,1)S(1)}, bf16[32,1152]{1,0:T(8,128)(2,1)S(1)}, u32[]{:S(2)}, u32[]{:S(2)}) collective-permute-start(bf16[32,1152]{1,0:T(8,128)(2,1)S(1)} %get-tuple-element.26), channel_id=1, source_target_pairs={{0,6},{2,4},{4,2},{6,0},{8,14},{10,12},{12,10},{14,8},{1,7},{3,5},... | collective-permute-start | bytes 221192 | tf_op jit(solution)/shard_map/ppermute | solution.py:200
  9.2 10.2 %collective-permute-start.3 = (bf16[32,1152]{1,0:T(8,128)(2,1)S(1)}, bf16[32,1152]{1,0:T(8,128)(2,1)S(1)}, u32[]{:S(2)}, u32[]{:S(2)}) collective-permute-start(bf16[32,1152]{1,0:T(8,128)(2,1)S(1)} %get-tuple-element.27), channel_id=1, source_target_pairs={{0,10},{2,8},{4,14},{6,12},{8,2},{10,0},{12,6},{14,4},{1,11},{3,9}... | collective-permute-start | bytes 221192 | tf_op jit(solution)/shard_map/ppermute | solution.py:200
  9.2 10.1 %collective-permute-start.4 = (bf16[32,1152]{1,0:T(8,128)(2,1)S(1)}, bf16[32,1152]{1,0:T(8,128)(2,1)S(1)}, u32[]{:S(2)}, u32[]{:S(2)}) collective-permute-start(bf16[32,1152]{1,0:T(8,128)(2,1)S(1)} %get-tuple-element.28), channel_id=1, source_target_pairs={{0,12},{2,14},{4,8},{6,10},{8,4},{10,6},{12,0},{14,2},{1,13},{3,15... | collective-permute-start | bytes 221192 | tf_op jit(solution)/shard_map/ppermute | solution.py:200
  13.1 7.2 %collective-permute-start.5 = (bf16[32,1152]{1,0:T(8,128)(2,1)S(1)}, bf16[32,1152]{1,0:T(8,128)(2,1)S(1)}, u32[]{:S(2)}, u32[]{:S(2)}) collective-permute-start(bf16[32,1152]{1,0:T(8,128)(2,1)S(1)} %get-tuple-element.29), channel_id=1, source_target_pairs={{0,14},{2,12},{4,10},{6,8},{8,6},{10,4},{12,2},{14,0},{1,15},{3,13... | collective-permute-start | bytes 221192 | tf_op jit(solution)/shard_map/ppermute | solution.py:200
  15.0 5.6 %collective-permute-start.6 = (bf16[32,1152]{1,0:T(8,128)(2,1)S(1)}, bf16[32,1152]{1,0:T(8,128)(2,1)S(1)}, u32[]{:S(2)}, u32[]{:S(2)}) collective-permute-start(bf16[32,1152]{1,0:T(8,128)(2,1)S(1)} %get-tuple-element.30), channel_id=1, source_target_pairs={{0,2},{2,0},{4,6},{6,4},{8,10},{10,8},{12,14},{14,12},{1,3},{3,1},... | collective-permute-start | bytes 221192 | tf_op jit(solution)/shard_map/ppermute | solution.py:200
  20.6 2.1 %collective-permute-start.7 = (bf16[256,1152]{1,0:T(8,128)(2,1)S(1)}, bf16[256,1152]{1,0:T(8,128)(2,1)S(1)}, u32[]{:S(2)}, u32[]{:S(2)}) collective-permute-start(bf16[256,1152]{1,0:T(8,128)(2,1)S(1)} %constant_dynamic-update-slice_fusion.query_ref), channel_id=1, source_target_pairs={{0,1},{1,0},{2,3},{3,2},{4,5},{5,4},{6,7},{7,6},{8,9},{9,8},{10,11... | collective-permute-start | bytes 1769480 | tf_op jit(solution)/shard_map/ppermute | solution.py:200

commit v12 on v11

--- a/solution.py
+++ b/solution.py
@@ -44,8 +44,15 @@
     return jnp.concatenate(parts, axis=1)
 
 
+def of_core(me_ref, values):
+    value = values[0]
+    for core, other in enumerate(values[1:], 1):
+        value = jnp.where(me_ref[0] % len(values) == core, other, value)
+    return value
+
+
 def slot_kernel(
-    owners, capacity, order, rows, me_ref, ints_ref, slot_ref, digit_ref
+    owners, capacity, orders, rows, me_ref, ints_ref, slot_ref, digit_ref
 ):
     clusters = ints_ref.shape[1] - 2 * rows
     cluster = ints_ref[:, clusters : clusters + rows]
@@ -55,10 +62,10 @@
     hot = (iota((max(owners, 16), rows), 0) == owner).astype(jnp.float32)
     upto = bf16(iota((rows, rows), 0) <= iota((rows, rows), 1))
     rank = jnp.sum(hot * matmul(bf16(hot), upto), axis=0, keepdims=True) - 1.0
-    partner = owner ^ me_ref[0]
+    partner = owner ^ (me_ref[0] // len(orders))
     place = partner
-    for index, k in enumerate(order):
-        place = jnp.where(partner == k, index, place)
+    for index, ks in enumerate(zip(*orders)):
+        place = jnp.where(partner == of_core(me_ref, ks), index, place)
     slot_ref[...] = place * capacity + rank.astype(jnp.int32)
 
     line = iota((8, rows), 0)
@@ -128,10 +135,10 @@
 
 
 def near_kernel(
-    rows_all, clusters, clus_dev, me_ref, ints_ref, query_ref, lows_ref, key_ref, best_ref, sums_ref
+    rows_all, clusters, clus_dev, cores, me_ref, ints_ref, query_ref, lows_ref, key_ref, best_ref, sums_ref
 ):
     width = query_ref.shape[1] - LANES
-    hot = (ints_ref[:, :clusters] == me_ref[0]).astype(jnp.float32)
+    hot = (ints_ref[:, :clusters] == me_ref[0] // cores).astype(jnp.float32)
     rank = ranked(hot)
     shape = (clus_dev, clusters)
     kth = (rank == iota(shape, 0).astype(jnp.float32) + 1.0) & (hot > 0.0)
@@ -178,15 +185,16 @@
 
 
 def pick_kernel(
-    order, me_ref, slot_ref, result_ref, norm_ref, best_ref, distance_ref, cohesion_ref
+    orders, me_ref, slot_ref, result_ref, norm_ref, best_ref, distance_ref, cohesion_ref
 ):
     cohesion_ref[...] = norm_ref[...]
     rows = slot_ref.shape[1]
     owners, lines, slots = result_ref.shape
     place = iota((lines, slots), 1) // (slots // owners)
     values = jnp.zeros((lines, slots), jnp.float32)
-    for index, k in enumerate(order):
-        values = jnp.where(place == index, result_ref[me_ref[0] ^ k], values)
+    for index, ks in enumerate(zip(*orders)):
+        partner = (me_ref[0] // len(orders)) ^ of_core(me_ref, ks)
+        values = jnp.where(place == index, result_ref[partner], values)
     values = jnp.concatenate([values, jnp.zeros((8 - lines, slots), jnp.float32)], axis=0)
     at = (iota((slots, rows), 0) == slot_ref[...]).astype(jnp.float32)
     picked = jnp.dot(
@@ -196,27 +204,40 @@
     distance_ref[...] = picked[1:2]
 
 
-def from_partner(value, k, axis):
-    return lax.ppermute(value, axis, [(i, i ^ k) for i in range(lax.axis_size(axis))])
-
-
-def partner_order(owners):
+def partner_orders(owners, cores):
     half = owners // 2
     far, near = list(range(half, owners)), list(range(2, half))
-    return far[:1] + near + far[1:] + list(range(1, min(half, 2))) + [0]
-
-
-def exchange(packed, order):
-    return jnp.concatenate(
-        [from_partner(block, k, "shard") if k else block for k, block in zip(order, packed)]
-    )
-
-
-def exchange_all(packed, order, me):
+    orders = []
+    for core in range(cores):
+        order, f, n = [], list(far), list(near)
+        take = [f, n] if core % 2 == 0 else [f, f, n]
+        while f or n:
+            for source in take if f and n else [f or n]:
+                if source:
+                    order.append(source.pop(0))
+            take = [f, n]
+        orders.append(order + list(range(1, min(half, 2))) + [0])
+    return orders
+
+
+def exchange(packed, orders):
+    owners, cores = lax.axis_size("shard"), lax.axis_size("sub")
+    got = []
+    for block, ks in zip(packed, zip(*orders)):
+        pairs = [
+            (i * cores + core, (i ^ k) * cores + core)
+            for i in range(owners)
+            for core, k in enumerate(ks)
+        ]
+        got.append(lax.ppermute(block, ("shard", "sub"), pairs) if any(ks) else block)
+    return jnp.concatenate(got)
+
+
+def exchange_all(packed, me):
     owners = lax.axis_size("shard")
-    partner = me ^ jnp.array(order, jnp.int32)
+    partner = me ^ jnp.arange(owners, dtype=jnp.int32)
     parted = packed.reshape(owners, -1, packed.shape[1])
-    got = lax.all_to_all(parted[jnp.argsort(partner)], "shard", 0, 0, tiled=True)
+    got = lax.all_to_all(parted[partner], "shard", 0, 0, tiled=True)
     return got[partner].reshape(packed.shape)
 
 
@@ -232,14 +253,15 @@
     compare_cost = pl.CostEstimate(
         flops=4 * slots * slots * width, bytes_accessed=4 * slots * wide, transcendentals=0
     )
-    me = lax.axis_index("shard").astype(jnp.int32).reshape(1)
+    me = lax.axis_index(("shard", "sub")).astype(jnp.int32).reshape(1)
     ints = jnp.concatenate([owner_map, cluster_id, item_order]).reshape(1, -1)
 
     direct = owners <= MOST_PERMUTES
-    order = partner_order(owners)
+    cores = lax.axis_size("sub")
+    orders = partner_orders(owners, cores) if direct else [list(range(owners))] * cores
     parts = owners if direct else 1
     slot, digit = pl.pallas_call(
-        functools.partial(slot_kernel, owners, capacity, order, local_rows),
+        functools.partial(slot_kernel, owners, capacity, orders, local_rows),
         out_shape=[
             jax.ShapeDtypeStruct((1, local_rows), jnp.int32),
             jax.ShapeDtypeStruct((LANES, local_rows), jnp.bfloat16),
@@ -258,11 +280,11 @@
         compiler_params=params,
         name="pack",
     )(slot, digit, embeddings)
-    query = exchange(packed, order) if direct else exchange_all(packed[0], order, me)
-    other = from_partner(query, 1, "sub")
+    query = exchange(packed, orders) if direct else exchange_all(packed[0], lax.axis_index("shard"))
+    other = lax.ppermute(query, "sub", [(core, core ^ 1) for core in range(cores)])
     asked = slots + clus_dev
     near = pl.pallas_call(
-        functools.partial(near_kernel, rows_all, owner_map.shape[0], clus_dev),
+        functools.partial(near_kernel, rows_all, owner_map.shape[0], clus_dev, cores),
         out_shape=[
             jax.ShapeDtypeStruct((asked, LANES), jnp.int32),
             jax.ShapeDtypeStruct((2, slots), jnp.int32),
@@ -289,7 +311,7 @@
     )(query, other, *near)
     results = lax.all_to_all(results, "shard", 0, 0, tiled=True)
     best, distance, cohesion = pl.pallas_call(
-        functools.partial(pick_kernel, order),
+        functools.partial(pick_kernel, orders),
         out_shape=[jax.ShapeDtypeStruct((1, local_rows), jnp.float32)] * 2
         + [jax.ShapeDtypeStruct((1, clus_dev), jnp.float32)],
         in_specs=[SCALAR] + [WHOLE] * 3,

time: 35 us -> 36 us (1.029)
  starting transfers between devices: 13.4 us -> 14.2 us
  blocking collectives: 10.3 us -> 10.7 us
    ppermute x8, starting transfers between devices: 13.4 us -> 14.2 us  [the longest x7 14.1 us: exchange(): lax.ppermute(block, ('shard', 'sub'), pairs)]
    all_to_all x1, blocking collectives: 10.3 us -> 10.7 us  [local(): results = lax.all_to_all(results, 'shard', 0, 0, tiled=True)]
  transfers between devices with their start and end apart: 8 -> 8, of which waited for: 4 -> 6; matrix products, arithmetic and copies ran while one was open for 0% -> 0% of each run, Pallas kernels for 2% -> 2%
where the time goes in v12:
time: 36 us; the launch traced here: 35.8 us
  starting transfers between devices  14.2 us (39%)
  blocking collectives  10.7 us (30%)
  waiting for transfers between devices  5.98 us (17%)
  Pallas kernels  3.33 us (9%)
  other arithmetic  0.76 us (2%)
  between operations  0.69 us (2%)
    ppermute x7, starting transfers between devices, exchange(): lax.ppermute(block, ('shard', 'sub'), pairs)  14.1 us
    all_to_all x1, blocking collectives, local(): results = lax.all_to_all(results, 'shard', 0, 0, tiled=True)  10.7 us
    ppermute x7, waiting for transfers between devices, exchange(): lax.ppermute(block, ('shard', 'sub'), pairs)  4.7 us
    ppermute x1, waiting for transfers between devices, local(): lax.ppermute(query, 'sub', [(core, core ^ 1) for core in range(cores)])  1.28 us
    pallas_call x1, Pallas kernels, local(): pl.pallas_call(functools.partial(far_kernel, rows_all), out_shape=[jax.Sh...  1.22 us
    concatenate x1, other arithmetic, local(): ints = jnp.concatenate([owner_map, cluster_id, item_order]).reshape(1, -1)  0.76 us
  transfers between devices with their start and end apart: 8, of which 6 were waited for; matrix products, arithmetic and copies ran while one was open for 0% of the time, Pallas kernels for 2%

profile of v12, /device:TPU:0, one launch (start us, length us, event | category | flops | bytes accessed | tf_op | source)
XLA Modules:
  0.0 35.8 jit_solution(7145875052218933030)
XLA Ops:
  0.6 0.0 copy-start
  0.6 0.8 %pad_add_fusion = s32[512]{0:T(512)S(1)} fusion(s32[128]{0:T(128)} %param.6, s32[128]{0:T(128)} %param.5, s32[256]{0:T(256)} %param.7), kind=kLoop, calls=%fused_computation.8 | loop fusion | flops 1024 | bytes 4096 | tf_op jit(solution)/shard_map/concatenate | solution.py:257
  1.4 0.3 slots.1
  1.7 0.0 copy-done
  1.7 0.4 %pack.1 = (bf16[32,1152]{1,0:T(8,128)(2,1)S(1)}, bf16[32,1152]{1,0:T(8,128)(2,1)S(1)}, bf16[32,1152]{1,0:T(8,128)(2,1)S(1)}, bf16[32,1152]{1,0:T(8,128)(2,1)S(1)...) custom-call(s32[1,128]{1,0:T(1,128)S(1)} %get-tuple-element.22.slot_, ...), custom_call_target="tpu_custom_call" | custom-call | tf_op jit(solution)/shard_map/pack/pallas_call | solution.py:275
  2.1 4.1 %collective-permute-start = (bf16[32,1152]{1,0:T(8,128)(2,1)S(1)}, bf16[32,1152]{1,0:T(8,128)(2,1)S(1)}, u32[]{:S(2)}, u32[]{:S(2)}) collective-permute-start(bf16[32,1152]{1,0:T(8,128)(2,1)S(1)} %get-tuple-element.24), channel_id=1, source_target_pairs={{0,8},{1,9},{2,10},{3,11},{4,12},{5,13},{6,14},{7,15},{8,0},{9,1},... | collective-permute-start | bytes 221192 | tf_op jit(solution)/shard_map/ppermute | solution.py:232
  6.2 1.6 %collective-permute-start.1 = (bf16[32,1152]{1,0:T(8,128)(2,1)S(1)}, bf16[32,1152]{1,0:T(8,128)(2,1)S(1)}, u32[]{:S(2)}, u32[]{:S(2)}) collective-permute-start(bf16[32,1152]{1,0:T(8,128)(2,1)S(1)} %get-tuple-element.25), channel_id=1, source_target_pairs={{0,4},{1,11},{2,6},{3,9},{4,0},{5,15},{6,2},{7,13},{8,12},{9,3},{1... | collective-permute-start | bytes 221192 | tf_op jit(solution)/shard_map/ppermute | solution.py:232
  7.8 1.3 %collective-permute-start.2 = (bf16[32,1152]{1,0:T(8,128)(2,1)S(1)}, bf16[32,1152]{1,0:T(8,128)(2,1)S(1)}, u32[]{:S(2)}, u32[]{:S(2)}) collective-permute-start(bf16[32,1152]{1,0:T(8,128)(2,1)S(1)} %get-tuple-element.26), channel_id=1, source_target_pairs={{0,10},{1,5},{2,8},{3,7},{4,14},{5,1},{6,12},{7,3},{8,2},{9,13},{1... | collective-permute-start | bytes 221192 | tf_op jit(solution)/shard_map/ppermute | solution.py:232
  9.1 0.2 collective-permute-start.3
  9.2 3.9 %collective-permute-start.4 = (bf16[32,1152]{1,0:T(8,128)(2,1)S(1)}, bf16[32,1152]{1,0:T(8,128)(2,1)S(1)}, u32[]{:S(2)}, u32[]{:S(2)}) collective-permute-start(bf16[32,1152]{1,0:T(8,128)(2,1)S(1)} %get-tuple-element.28), channel_id=1, source_target_pairs={{0,12},{1,7},{2,14},{3,5},{4,8},{5,3},{6,10},{7,1},{8,4},{9,15},{1... | collective-permute-start | bytes 221192 | tf_op jit(solution)/shard_map/ppermute | solution.py:232
  13.1 0.0 collective-permute-done
  13.1 2.8 %collective-permute-start.5 = (bf16[32,1152]{1,0:T(8,128)(2,1)S(1)}, bf16[32,1152]{1,0:T(8,128)(2,1)S(1)}, u32[]{:S(2)}, u32[]{:S(2)}) collective-permute-start(bf16[32,1152]{1,0:T(8,128)(2,1)S(1)} %get-tuple-element.29), channel_id=1, source_target_pairs={{0,14},{1,15},{2,12},{3,13},{4,10},{5,11},{6,8},{7,9},{8,6},{9,7},... | collective-permute-start | bytes 221192 | tf_op jit(solution)/shard_map/ppermute | solution.py:232
  15.9 0.0 collective-permute-done.1
  15.9 0.4 %collective-permute-start.6 = (bf16[32,1152]{1,0:T(8,128)(2,1)S(1)}, bf16[32,1152]{1,0:T(8,128)(2,1)S(1)}, u32[]{:S(2)}, u32[]{:S(2)}) collective-permute-start(bf16[32,1152]{1,0:T(8,128)(2,1)S(1)} %get-tuple-element.30), channel_id=1, source_target_pairs={{0,2},{1,3},{2,0},{3,1},{4,6},{5,7},{6,4},{7,5},{8,10},{9,11},{10,... | collective-permute-start | bytes 221192 | tf_op jit(solution)/shard_map/ppermute | solution.py:232
  16.3 0.1 collective-permute-done.2
  16.4 0.1 collective-permute-done.3
  16.5 1.1 %collective-permute-done.4 = bf16[32,1152]{1,0:T(8,128)(2,1)S(1)} collective-permute-done((bf16[32,1152]{1,0:T(8,128)(2,1)S(1)}, bf16[32,1152]{1,0:T(8,128)(2,1)S(1)}, u32[]{:S(2)}, u32[]{:S(2)}) %collective-permute-start.4) | collective-permute-done | bytes 73760 | tf_op jit(solution)/shard_map/ppermute | solution.py:232
  17.6 2.7 %collective-permute-done.5 = bf16[32,1152]{1,0:T(8,128)(2,1)S(1)} collective-permute-done((bf16[32,1152]{1,0:T(8,128)(2,1)S(1)}, bf16[32,1152]{1,0:T(8,128)(2,1)S(1)}, u32[]{:S(2)}, u32[]{:S(2)}) %collective-permute-start.5) | collective-permute-done | bytes 73760 | tf_op jit(solution)/shard_map/ppermute | solution.py:232
  20.3 0.7 %collective-permute-done.6 = bf16[32,1152]{1,0:T(8,128)(2,1)S(1)} collective-permute-done((bf16[32,1152]{1,0:T(8,128)(2,1)S(1)}, bf16[32,1152]{1,0:T(8,128)(2,1)S(1)}, u32[]{:S(2)}, u32[]{:S(2)}) %collective-permute-start.6) | collective-permute-done | bytes 73760 | tf_op jit(solution)/shard_map/ppermute | solution.py:232
  21.1 0.1 collective-permute-start.7
  21.1 0.7 %near.1 = (s32[288,128]{1,0:T(8,128)S(1)}, s32[2,256]{1,0:T(2,128)S(1)}, f32[1,256]{1,0:T(1,128)S(1)}, f32[288,1152]{1,0:T(8,128)S(1)}) custom-call(s32[1]{0:T(128)} %bitcast.me_ref, s32[1,512]{1,0:T(1,128)S(1)} %bitcast.6, bf16[256,1152]{1,0:T(8,128)(2,1)S(1)} %constant_dynamic-update-slice_fusion.query_ref), custom_call_target="tpu_custom_call" | custom-call | flops 268435456 | bytes 1179648 | tf_op jit(solution)/shard_map/near/pallas_call | solution.py:286
  21.8 1.3 %collective-permute-done.7.other_ref = bf16[256,1152]{1,0:T(8,128)(2,1)S(1)} collective-permute-done((bf16[256,1152]{1,0:T(8,128)(2,1)S(1)}, bf16[256,1152]{1,0:T(8,128)(2,1)S(1)}, u32[]{:S(2)}, u32[]{:S(2)}) %collective-permute-start.7) | collective-permute-done | bytes 589856 | tf_op jit(solution)/shard_map/ppermute | solution.py:284
  23.1 1.2 %far.1 = (f32[8,2,256]{2,1,0:T(2,128)S(1)}, f32[1,32]{1,0:T(1,128)S(1)}) custom-call(bf16[256,1152]{1,0:T(8,128)(2,1)S(1)} %constant_dynamic-update-slice_fusion.query_ref, bf16[256,1152]{1,0:T(8,128)(2,1)S(1)} %collective-permute-done.7.other_ref, s32[288,128]{1,0:T(8,128)S(1)} %get-tuple-element.32.lows_ref, s32[2,256]{1,0:T(2,128)S(1)} %get-tuple-element.33.key_ref, ...), custom_call_target="tpu_custom_call" | custom-call | flops 268435456 | bytes 1179648 | tf_op jit(solution)/shard_map/far/pallas_call | solution.py:300
  24.3 10.7 %all_to_all.5.result_ref = f32[8,2,256]{2,1,0:T(2,128)S(1)} all-to-all(f32[8,2,256]{2,1,0:T(2,128)S(1)} %get-tuple-element.36), channel_id=1, replica_groups=mesh['groups'=2,'shard'=8,'sub'=2] {'shard'}, dimensions={0} | all-to-all | bytes 32768 | tf_op jit(solution)/shard_map/all_to_all | solution.py:312
  35.1 0.7 %pick.1 = (f32[1,128]{1,0:T(1,128)}, f32[1,128]{1,0:T(1,128)}, f32[1,32]{1,0:T(1,128)}) custom-call(s32[1]{0:T(128)} %bitcast.me_ref, s32[1,128]{1,0:T(1,128)S(1)} %get-tuple-element.22.slot_ref, f32[8,2,256]{2,1,0:T(2,128)S(1)} %all_to_all.5.result_ref, f32[1,32]{1,0:T(1,128)S(1)} %get-tuple-element.37.norm_ref), custom_call_target="tpu_custom_call" | custom-call | tf_op jit(solution)/shard_map/pick/pallas_call | solution.py:313
  (8 shorter events, 0.1 us)
Async XLA Ops:
  0.6 1.0 %copy-start = (bf16[128,1024]{1,0:T(8,128)(2,1)S(1)}, bf16[128,1024]{1,0:T(8,128)(2,1)}, u32[]{:S(2)}) copy-start(bf16[128,1024]{1,0:T(8,128)(2,1)} %embed_ref.1) | copy-start | bytes 786436
  2.1 11.0 %collective-permute-start = (bf16[32,1152]{1,0:T(8,128)(2,1)S(1)}, bf16[32,1152]{1,0:T(8,128)(2,1)S(1)}, u32[]{:S(2)}, u32[]{:S(2)}) collective-permute-start(bf16[32,1152]{1,0:T(8,128)(2,1)S(1)} %get-tuple-element.24), channel_id=1, source_target_pairs={{0,8},{1,9},{2,10},{3,11},{4,12},{5,13},{6,14},{7,15},{8,0},{9,1},... | collective-permute-start | bytes 221192 | tf_op jit(solution)/shard_map/ppermute | solution.py:232
  6.2 9.6 %collective-permute-start.1 = (bf16[32,1152]{1,0:T(8,128)(2,1)S(1)}, bf16[32,1152]{1,0:T(8,128)(2,1)S(1)}, u32[]{:S(2)}, u32[]{:S(2)}) collective-permute-start(bf16[32,1152]{1,0:T(8,128)(2,1)S(1)} %get-tuple-element.25), channel_id=1, source_target_pairs={{0,4},{1,11},{2,6},{3,9},{4,0},{5,15},{6,2},{7,13},{8,12},{9,3},{1... | collective-permute-start | bytes 221192 | tf_op jit(solution)/shard_map/ppermute | solution.py:232
  7.8 8.6 %collective-permute-start.2 = (bf16[32,1152]{1,0:T(8,128)(2,1)S(1)}, bf16[32,1152]{1,0:T(8,128)(2,1)S(1)}, u32[]{:S(2)}, u32[]{:S(2)}) collective-permute-start(bf16[32,1152]{1,0:T(8,128)(2,1)S(1)} %get-tuple-element.26), channel_id=1, source_target_pairs={{0,10},{1,5},{2,8},{3,7},{4,14},{5,1},{6,12},{7,3},{8,2},{9,13},{1... | collective-permute-start | bytes 221192 | tf_op jit(solution)/shard_map/ppermute | solution.py:232
  9.1 7.4 %collective-permute-start.3 = (bf16[32,1152]{1,0:T(8,128)(2,1)S(1)}, bf16[32,1152]{1,0:T(8,128)(2,1)S(1)}, u32[]{:S(2)}, u32[]{:S(2)}) collective-permute-start(bf16[32,1152]{1,0:T(8,128)(2,1)S(1)} %get-tuple-element.27), channel_id=1, source_target_pairs={{0,6},{1,13},{2,4},{3,15},{4,2},{5,9},{6,0},{7,11},{8,14},{9,5},{1... | collective-permute-start | bytes 221192 | tf_op jit(solution)/shard_map/ppermute | solution.py:232
  9.2 8.3 %collective-permute-start.4 = (bf16[32,1152]{1,0:T(8,128)(2,1)S(1)}, bf16[32,1152]{1,0:T(8,128)(2,1)S(1)}, u32[]{:S(2)}, u32[]{:S(2)}) collective-permute-start(bf16[32,1152]{1,0:T(8,128)(2,1)S(1)} %get-tuple-element.28), channel_id=1, source_target_pairs={{0,12},{1,7},{2,14},{3,5},{4,8},{5,3},{6,10},{7,1},{8,4},{9,15},{1... | collective-permute-start | bytes 221192 | tf_op jit(solution)/shard_map/ppermute | solution.py:232
  13.1 7.2 %collective-permute-start.5 = (bf16[32,1152]{1,0:T(8,128)(2,1)S(1)}, bf16[32,1152]{1,0:T(8,128)(2,1)S(1)}, u32[]{:S(2)}, u32[]{:S(2)}) collective-permute-start(bf16[32,1152]{1,0:T(8,128)(2,1)S(1)} %get-tuple-element.29), channel_id=1, source_target_pairs={{0,14},{1,15},{2,12},{3,13},{4,10},{5,11},{6,8},{7,9},{8,6},{9,7},... | collective-permute-start | bytes 221192 | tf_op jit(solution)/shard_map/ppermute | solution.py:232
  15.9 5.2 %collective-permute-start.6 = (bf16[32,1152]{1,0:T(8,128)(2,1)S(1)}, bf16[32,1152]{1,0:T(8,128)(2,1)S(1)}, u32[]{:S(2)}, u32[]{:S(2)}) collective-permute-start(bf16[32,1152]{1,0:T(8,128)(2,1)S(1)} %get-tuple-element.30), channel_id=1, source_target_pairs={{0,2},{1,3},{2,0},{3,1},{4,6},{5,7},{6,4},{7,5},{8,10},{9,11},{10,... | collective-permute-start | bytes 221192 | tf_op jit(solution)/shard_map/ppermute | solution.py:232
  21.1 2.1 %collective-permute-start.7 = (bf16[256,1152]{1,0:T(8,128)(2,1)S(1)}, bf16[256,1152]{1,0:T(8,128)(2,1)S(1)}, u32[]{:S(2)}, u32[]{:S(2)}) collective-permute-start(bf16[256,1152]{1,0:T(8,128)(2,1)S(1)} %constant_dynamic-update-slice_fusion.query_ref), channel_id=1, source_target_pairs={{0,1},{1,0},{2,3},{3,2},{4,5},{5,4},{6,7},{7,6},{8,9},{9,8},{10,11... | collective-permute-start | bytes 1769480 | tf_op jit(solution)/shard_map/ppermute | solution.py:284

commit v13 on v11

v13 whole, which is shorter than its diff:
```python
import functools

import jax
import jax.numpy as jnp
from jax import lax
from jax.experimental import pallas as pl
from jax.experimental.pallas import tpu as pltpu
from jax.sharding import PartitionSpec as P

LANES = 128
DIGITS = 3
MOST_PERMUTES = 8
WHOLE = pl.BlockSpec(memory_space=pltpu.VMEM)
SCALAR = pl.BlockSpec(memory_space=pltpu.SMEM)


def iota(shape, dim):
    return lax.broadcasted_iota(jnp.int32, shape, dim)


def matmul(a, b):
    return jnp.dot(a, b, preferred_element_type=jnp.float32)


def matmul_t(a, b, precision=None):
    return lax.dot_general(
        a, b, (((1,), (1,)), ((), ())), precision=precision, preferred_element_type=jnp.float32
    )


def bf16(x):
    return x.astype(jnp.float32).astype(jnp.bfloat16)


def ranked(hot):
    upto = (iota((LANES, LANES), 0) <= iota((LANES, LANES), 1)).astype(jnp.bfloat16)
    before, parts = jnp.zeros((1, 1), jnp.float32), []
    for start in range(0, hot.shape[1], LANES):
        piece = hot[:, start : start + LANES]
        spread = jnp.broadcast_to(piece, (16, LANES)).astype(jnp.bfloat16)
        parts.append(matmul(spread, upto)[:1] + before)
        before = before + jnp.sum(piece, axis=1, keepdims=True)
    return jnp.concatenate(parts, axis=1)


def slot_kernel(
    owners, capacity, order, parts, rows, me_ref, ints_ref, slot_ref, digit_ref
):
    clusters = ints_ref.shape[1] - 2 * rows
    cluster = ints_ref[:, clusters : clusters + rows]
    named = bf16(iota((clusters, rows), 0) == cluster)
    owner_map = bf16(jnp.broadcast_to(ints_ref[:, :clusters], (16, clusters)))
    owner = matmul(owner_map, named)[:1].astype(jnp.int32)
    hot = (iota((max(owners, 16), rows), 0) == owner).astype(jnp.float32)
    upto = bf16(iota((rows, rows), 0) <= iota((rows, rows), 1))
    rank = jnp.sum(hot * matmul(bf16(hot), upto), axis=0, keepdims=True) - 1.0
    rank = rank.astype(jnp.int32)
    partner = owner ^ me_ref[0]
    place = partner
    for index, k in enumerate(order):
        place = jnp.where(partner == k, index, place)
    if parts == 1:
        slot_ref[...] = place * capacity + rank
    else:
        half = capacity // 2
        later = (rank >= half).astype(jnp.int32)
        slot_ref[...] = place * half + rank + later * (owners * half - half)

    line = iota((8, rows), 0)
    digit = jnp.zeros((8, rows), jnp.int32)
    for first, number in ((0, cluster + 1), (DIGITS, ints_ref[:, clusters + rows :])):
        for at in range(DIGITS):
            digit = jnp.where(line == first + at, (number >> (8 * at)) & 255, digit)
    empty = jnp.zeros((LANES // 2 - 8, rows), jnp.int32)
    none = jnp.zeros((LANES // 2, rows), jnp.int32)
    early = jnp.concatenate([digit, empty, none], axis=0)
    late = jnp.concatenate([none, digit, empty], axis=0)
    digit_ref[...] = bf16(jnp.concatenate([early, late], axis=1))


def pack_kernel(slot_ref, digit_ref, embed_ref, *out_refs):
    rows, width = embed_ref.shape
    tiles, half, _ = out_refs[0].shape
    values = embed_ref[...].astype(jnp.float32)
    mean_sq = jnp.sum(values * values, axis=1, keepdims=True) * (1.0 / width)
    unit = (values * lax.rsqrt(width * (mean_sq + 1e-06))).astype(jnp.bfloat16)
    late = half * len(out_refs)
    move = bf16(iota((2 * late, rows), 0) == slot_ref[...])
    moved = matmul(move, unit).astype(jnp.bfloat16)
    both = jnp.concatenate([move[:late], move[late:]], axis=1)
    digit = matmul_t(both, digit_ref[...]).astype(jnp.bfloat16)
    each = tiles // 2
    for index, out_ref in enumerate(out_refs):
        start = index * half
        for tile in range(each):
            lanes = slice(tile * LANES, (tile + 1) * LANES)
            out_ref[tile] = moved[start : start + half, lanes]
            out_ref[each + tile] = moved[late + start : late + start + half, lanes]
        out_ref[tiles - 1] = digit[start : start + half]


def unpacked(block_ref, tiles):
    blocks = block_ref.shape[0] // tiles
    each = tiles // 2

    def column(tile):
        return jnp.concatenate([block_ref[i * tiles + tile] for i in range(blocks)], axis=0)

    halves = [
        jnp.concatenate([column(first + tile) for tile in range(each)], axis=1)
        for first in (0, each)
    ]
    return jnp.concatenate(halves, axis=0), column(tiles - 1)


def weights(number, at, half):
    value = jnp.zeros(at.shape, jnp.float32)
    for place in range(DIGITS):
        for which in (0, 1):
            lane = half * (LANES // 2) + which * DIGITS + place
            value = jnp.where((at == lane) & (number == which), 256.0**place, value)
    return value.astype(jnp.bfloat16)


def key_rows(rows_all, digit):
    at = iota((16, LANES), 0), iota((16, LANES), 1)
    numbers = [matmul_t(weights(*at, half), digit) for half in (0, 1)]
    numbers = jnp.concatenate(numbers, axis=1)
    low = (numbers[0:1].astype(jnp.int32) - 1) * rows_all
    return low, low + numbers[1:2].astype(jnp.int32)


def key_columns(rows_all, digit):
    at = iota((LANES, 2 * LANES), 1) // LANES, iota((LANES, 2 * LANES), 0)
    numbers = [matmul(digit, weights(*at, half)) for half in (0, 1)]
    numbers = jnp.concatenate(numbers, axis=0)
    low = (numbers[:, :LANES].astype(jnp.int32) - 1) * rows_all
    return low, low + numbers[:, LANES:].astype(jnp.int32)


def across(column, count):
    return jnp.concatenate([column] * (count // LANES), axis=1)


def compare(rows_all, query, query_low, query_key, lows, rows, digit):
    _, key = key_rows(rows_all, digit)
    bound = across(lows, key.shape[1])
    member = bf16((key >= bound) & (key < bound + rows_all))
    sums = matmul(member, rows)
    counts = matmul(member, jnp.ones((rows.shape[0], LANES), jnp.bfloat16))
    scores = matmul_t(rows, query)
    _, key = key_columns(rows_all, digit)
    key = across(key, query.shape[0])
    earlier = (key >= query_low) & (key < query_key)
    best = jnp.max(jnp.where(earlier, scores, -3.0), axis=0, keepdims=True)
    return best, sums, counts


def near_kernel(
    rows_all, clusters, clus_dev, tiles, me_ref, ints_ref, query_ref,
    lows_ref, key_ref, best_ref, sums_ref, counts_ref,
):
    hot = (ints_ref[:, :clusters] == me_ref[0]).astype(jnp.float32)
    rank = ranked(hot)
    shape = (clus_dev, clusters)
    kth = (rank == iota(shape, 0).astype(jnp.float32) + 1.0) & (hot > 0.0)
    own = jnp.sum(jnp.where(kth, iota(shape, 1).astype(jnp.float32), 0.0), axis=1, keepdims=True)
    own = jnp.broadcast_to(own.astype(jnp.int32) * rows_all, (clus_dev, LANES))
    query, digit = unpacked(query_ref, tiles)
    low, _ = key_columns(rows_all, digit)
    lows = jnp.concatenate([low, own], axis=0)
    query_low, query_key = key_rows(rows_all, digit)
    best, sums, counts = compare(rows_all, query, query_low, query_key, lows, query, digit)
    lows_ref[...] = lows
    key_ref[...] = jnp.concatenate([query_low, query_key], axis=0)
    best_ref[...] = best
    sums_ref[...] = sums
    counts_ref[...] = counts


def far_kernel(
    rows_all, tiles, query_ref, other_ref, lows_ref, key_ref, best_ref, sums_ref, counts_ref,
    result_ref, norm_ref,
):
    query, _ = unpacked(query_ref, tiles)
    queries, width = query.shape
    rows, digit = unpacked(other_ref, tiles)
    best, sums, counts = compare(
        rows_all, query, key_ref[0:1], key_ref[1:2], lows_ref[...], rows, digit
    )
    best = jnp.maximum(best, best_ref[...])
    best = jnp.where(best > -2.0, best, 0.0)
    share = 1.0 / jnp.maximum(counts + counts_ref[...], 1.0)
    squares = jnp.zeros(share.shape, jnp.float32)
    for start in range(0, width, LANES):
        lanes = slice(start, start + LANES)
        centroid = (sums[:, lanes] + sums_ref[:, lanes]) * share
        offset = jnp.concatenate(
            [query[:, lanes].astype(jnp.float32) - centroid[:queries], centroid[queries:]], axis=0
        )
        squares = squares + offset * offset
    ones = jnp.ones((8, LANES), jnp.float32)
    total = matmul_t(ones, squares, lax.Precision.HIGHEST)[:1]
    result = jnp.concatenate([best, total[:, :queries]], axis=0)
    for owner in range(result_ref.shape[0]):
        result_ref[owner] = result
    norm_ref[...] = total[:, queries:]


def pick_kernel(
    order, parts, me_ref, slot_ref, result_ref, norm_ref, best_ref, distance_ref, cohesion_ref
):
    cohesion_ref[...] = norm_ref[...]
    rows = slot_ref.shape[1]
    owners, lines, slots = result_ref.shape
    folds = min(parts, 2)
    place = iota((lines, slots), 1) % (slots // folds) // (slots // owners // folds)
    values = jnp.zeros((lines, slots), jnp.float32)
    for index, k in enumerate(order):
        values = jnp.where(place == index, result_ref[me_ref[0] ^ k], values)
    values = jnp.concatenate([values, jnp.zeros((8 - lines, slots), jnp.float32)], axis=0)
    at = (iota((slots, rows), 0) == slot_ref[...]).astype(jnp.float32)
    picked = jnp.dot(
        values, at, precision=lax.Precision.HIGHEST, preferred_element_type=jnp.float32
    )
    best_ref[...] = picked[0:1]
    distance_ref[...] = picked[1:2]


def from_partner(value, k, axis):
    return lax.ppermute(value, axis, [(i, i ^ k) for i in range(lax.axis_size(axis))])


def partner_order(owners):
    half = owners // 2
    far, near = list(range(half, owners)), list(range(2, half))
    return far[:1] + near + far[1:] + list(range(1, min(half, 2))) + [0]


def exchange(packed, order):
    return jnp.concatenate(
        [from_partner(block, k, "shard") if k else block for k, block in zip(order, packed)]
    )


def exchange_all(packed, me):
    owners = lax.axis_size("shard")
    tiles, half, _ = packed.shape
    each = tiles // 2
    data = packed[:-1].reshape(2, each, half, LANES).transpose(0, 2, 1, 3).reshape(2 * half, -1)
    digit = jnp.concatenate(jnp.split(packed[-1], 2, axis=1))
    parted = jnp.concatenate([data, digit], axis=1).reshape(owners, 2 * half // owners, -1)
    partner = me ^ jnp.arange(owners, dtype=jnp.int32)
    got = lax.all_to_all(parted[partner], "shard", 0, 0, tiled=True)[partner].reshape(2 * half, -1)
    data = got[:, : each * LANES].reshape(2, half, each, LANES).transpose(0, 2, 1, 3)
    digit = jnp.concatenate(jnp.split(got[:, each * LANES :], 2), axis=1)
    return jnp.concatenate([data.reshape(2 * each, half, LANES), digit[None]])


def local(embeddings, cluster_id, item_order, owner_map):
    owners = lax.axis_size("shard")
    local_rows, width = embeddings.shape
    rows_all = local_rows * owners * lax.axis_size("sub")
    clus_dev = owner_map.shape[0] // owners
    capacity = 2 * local_rows // owners
    slots = owners * capacity
    params = pltpu.CompilerParams(vmem_limit_bytes=32 << 20)
    compare_cost = pl.CostEstimate(
        flops=4 * slots * slots * width, bytes_accessed=4 * slots * width, transcendentals=0
    )
    me = lax.axis_index("shard").astype(jnp.int32).reshape(1)
    ints = jnp.concatenate([owner_map, cluster_id, item_order]).reshape(1, -1)

    direct = owners <= MOST_PERMUTES
    order = partner_order(owners) if direct else list(range(owners))
    parts = owners if direct else 1
    tiles = 2 * (width // LANES) + 1
    block = (tiles, slots // parts // 2, LANES)
    slot, digit = pl.pallas_call(
        functools.partial(slot_kernel, owners, capacity, order, parts, local_rows),
        out_shape=[
            jax.ShapeDtypeStruct((1, local_rows), jnp.int32),
            jax.ShapeDtypeStruct((LANES, 2 * local_rows), jnp.bfloat16),
        ],
        in_specs=[SCALAR, WHOLE],
        out_specs=[WHOLE] * 2,
        compiler_params=params,
        cost_estimate=pl.CostEstimate(flops=1 << 29, bytes_accessed=1 << 16, transcendentals=0),
        name="slots",
    )(me, ints)
    packed = pl.pallas_call(
        pack_kernel,
        out_shape=[jax.ShapeDtypeStruct(block, jnp.bfloat16)] * parts,
        in_specs=[WHOLE] * 3,
        out_specs=[WHOLE] * parts,
        compiler_params=params,
        name="pack",
    )(slot, digit, embeddings)
    query = exchange(packed, order) if direct else exchange_all(packed[0], me[0])
    other = from_partner(query, 1, "sub")
    asked = slots + clus_dev
    near = pl.pallas_call(
        functools.partial(near_kernel, rows_all, owner_map.shape[0], clus_dev, tiles),
        out_shape=[
            jax.ShapeDtypeStruct((asked, LANES), jnp.int32),
            jax.ShapeDtypeStruct((2, slots), jnp.int32),
            jax.ShapeDtypeStruct((1, slots), jnp.float32),
            jax.ShapeDtypeStruct((asked, width), jnp.float32),
            jax.ShapeDtypeStruct((asked, LANES), jnp.float32),
        ],
        in_specs=[SCALAR] + [WHOLE] * 2,
        out_specs=[WHOLE] * 5,
        compiler_params=params,
        cost_estimate=compare_cost,
        name="near",
    )(me, ints, query)
    results, norms = pl.pallas_call(
        functools.partial(far_kernel, rows_all, tiles),
        out_shape=[
            jax.ShapeDtypeStruct((owners, 2, slots), jnp.float32),
            jax.ShapeDtypeStruct((1, clus_dev), jnp.float32),
        ],
        in_specs=[WHOLE] * 7,
        out_specs=[WHOLE] * 2,
        compiler_params=params,
        cost_estimate=compare_cost,
        name="far",
    )(query, other, *near)
    results = lax.all_to_all(results, "shard", 0, 0, tiled=True)
    best, distance, cohesion = pl.pallas_call(
        functools.partial(pick_kernel, order, parts),
        out_shape=[jax.ShapeDtypeStruct((1, local_rows), jnp.float32)] * 2
        + [jax.ShapeDtypeStruct((1, clus_dev), jnp.float32)],
        in_specs=[SCALAR] + [WHOLE] * 3,
        out_specs=[WHOLE] * 3,
        compiler_params=params,
        name="pick",
    )(me, slot, results, norms)
    return best.reshape(local_rows), distance.reshape(local_rows), cohesion.reshape(clus_dev)


def solution(mesh):
    in_specs = (
        P(("groups", "shard", "sub"), None),
        P(("groups", "shard", "sub")),
        P(("groups", "shard", "sub")),
        P("groups"),
    )
    out_specs = (
        P(("groups", "shard", "sub")),
        P(("groups", "shard", "sub")),
        P(("groups", "shard")),
    )
    return jax.shard_map(local, mesh=mesh, in_specs=in_specs, out_specs=out_specs, check_vma=False)
```

time: 35 us -> 34.3 us (0.980)
  transfers between devices with their start and end apart: 8 -> 8, of which waited for: 4 -> 3; matrix products, arithmetic and copies ran while one was open for 0% -> 0% of each run, Pallas kernels for 2% -> 2%
where the time goes in v13:
time: 34.3 us; the launch traced here: 34.1 us
  starting transfers between devices  13.3 us (39%)
  blocking collectives  9.99 us (29%)
  waiting for transfers between devices  5.98 us (17%)
  Pallas kernels  3.2 us (9%)
  other arithmetic  0.76 us (2%)
  between operations  0.73 us (2%)
    ppermute x8, starting transfers between devices, from_partner(): lax.ppermute(value, axis, [(i, i ^ k) for i in range(lax.axis_size(axis))])  13.3 us
    all_to_all x1, blocking collectives, local(): results = lax.all_to_all(results, 'shard', 0, 0, tiled=True)  9.99 us
    ppermute x8, waiting for transfers between devices, from_partner(): lax.ppermute(value, axis, [(i, i ^ k) for i in range(lax.axis_size(axis))])  5.98 us
    pallas_call x1, Pallas kernels, local(): pl.pallas_call(functools.partial(far_kernel, rows_all, tiles), out_shape=...  1.1 us
    concatenate x1, other arithmetic, local(): ints = jnp.concatenate([owner_map, cluster_id, item_order]).reshape(1, -1)  0.76 us
    pallas_call x1, Pallas kernels, local(): pl.pallas_call(functools.partial(pick_kernel, order, parts), out_shape=[j...  0.72 us
    pallas_call x1, Pallas kernels, local(): pl.pallas_call(functools.partial(near_kernel, rows_all, owner_map.shape[0...  0.69 us
  transfers between devices with their start and end apart: 8, of which 3 were waited for; matrix products, arithmetic and copies ran while one was open for 0% of the time, Pallas kernels for 2%

profile of v13, /device:TPU:0, one launch (start us, length us, event | category | flops | bytes accessed | tf_op | source)
XLA Modules:
  0.0 34.1 jit_solution(12881475106734584107)
XLA Ops:
  0.6 0.0 copy-start
  0.6 0.8 %pad_add_fusion = s32[512]{0:T(512)S(1)} fusion(s32[128]{0:T(128)} %param.6, s32[128]{0:T(128)} %param.5, s32[256]{0:T(256)} %param.7), kind=kLoop, calls=%fused_computation.8 | loop fusion | flops 1024 | bytes 4096 | tf_op jit(solution)/shard_map/concatenate | solution.py:272
  1.4 0.3 slots.1
  1.7 0.0 copy-done
  1.7 0.4 %pack.1 = (bf16[17,16,128]{2,1,0:T(8,128)(2,1)S(1)}, bf16[17,16,128]{2,1,0:T(8,128)(2,1)S(1)}, bf16[17,16,128]{2,1,0:T(8,128)(2,1)S(1)}, bf16[17,16,128]{2,1,0:T...) custom-call(s32[1,128]{1,0:T(1,128)S(1)} %get-tuple-element.23.slot_, ...), custom_call_target="tpu_custom_call" | custom-call | tf_op jit(solution)/shard_map/pack/pallas_call | solution.py:291
  2.1 4.1 %collective-permute-start = (bf16[17,16,128]{2,1,0:T(8,128)(2,1)S(1)}, bf16[17,16,128]{2,1,0:T(8,128)(2,1)S(1)}, u32[]{:S(2)}, u32[]{:S(2)}) collective-permute-start(bf16[17,16,128]{2,1,0:T(8,128)(2,1)S(1)} %get-tuple-element.25), channel_id=1, source_target_pairs={{0,8},{2,10},{4,12},{6,14},{8,0},{10,2},{12,4},{14,6},{1,9},{3,11}... | collective-permute-start | bytes 208904 | tf_op jit(solution)/shard_map/ppermute | solution.py:231
  6.2 1.6 %collective-permute-start.1 = (bf16[17,16,128]{2,1,0:T(8,128)(2,1)S(1)}, bf16[17,16,128]{2,1,0:T(8,128)(2,1)S(1)}, u32[]{:S(2)}, u32[]{:S(2)}) collective-permute-start(bf16[17,16,128]{2,1,0:T(8,128)(2,1)S(1)} %get-tuple-element.26), channel_id=1, source_target_pairs={{0,4},{2,6},{4,0},{6,2},{8,12},{10,14},{12,8},{14,10},{1,5},{3,7},... | collective-permute-start | bytes 208904 | tf_op jit(solution)/shard_map/ppermute | solution.py:231
  7.8 1.4 %collective-permute-start.2 = (bf16[17,16,128]{2,1,0:T(8,128)(2,1)S(1)}, bf16[17,16,128]{2,1,0:T(8,128)(2,1)S(1)}, u32[]{:S(2)}, u32[]{:S(2)}) collective-permute-start(bf16[17,16,128]{2,1,0:T(8,128)(2,1)S(1)} %get-tuple-element.27), channel_id=1, source_target_pairs={{0,6},{2,4},{4,2},{6,0},{8,14},{10,12},{12,10},{14,8},{1,7},{3,5},... | collective-permute-start | bytes 208904 | tf_op jit(solution)/shard_map/ppermute | solution.py:231
  9.2 0.1 collective-permute-start.3
  9.2 3.9 %collective-permute-start.4 = (bf16[17,16,128]{2,1,0:T(8,128)(2,1)S(1)}, bf16[17,16,128]{2,1,0:T(8,128)(2,1)S(1)}, u32[]{:S(2)}, u32[]{:S(2)}) collective-permute-start(bf16[17,16,128]{2,1,0:T(8,128)(2,1)S(1)} %get-tuple-element.29), channel_id=1, source_target_pairs={{0,12},{2,14},{4,8},{6,10},{8,4},{10,6},{12,0},{14,2},{1,13},{3,15... | collective-permute-start | bytes 208904 | tf_op jit(solution)/shard_map/ppermute | solution.py:231
  13.1 0.0 collective-permute-done
  13.1 1.7 %collective-permute-start.5 = (bf16[17,16,128]{2,1,0:T(8,128)(2,1)S(1)}, bf16[17,16,128]{2,1,0:T(8,128)(2,1)S(1)}, u32[]{:S(2)}, u32[]{:S(2)}) collective-permute-start(bf16[17,16,128]{2,1,0:T(8,128)(2,1)S(1)} %get-tuple-element.30), channel_id=1, source_target_pairs={{0,14},{2,12},{4,10},{6,8},{8,6},{10,4},{12,2},{14,0},{1,15},{3,13... | collective-permute-start | bytes 208904 | tf_op jit(solution)/shard_map/ppermute | solution.py:231
  14.8 0.0 collective-permute-done.1
  14.8 0.6 %collective-permute-start.6 = (bf16[17,16,128]{2,1,0:T(8,128)(2,1)S(1)}, bf16[17,16,128]{2,1,0:T(8,128)(2,1)S(1)}, u32[]{:S(2)}, u32[]{:S(2)}) collective-permute-start(bf16[17,16,128]{2,1,0:T(8,128)(2,1)S(1)} %get-tuple-element.31), channel_id=1, source_target_pairs={{0,2},{2,0},{4,6},{6,4},{8,10},{10,8},{12,14},{14,12},{1,3},{3,1},... | collective-permute-start | bytes 208904 | tf_op jit(solution)/shard_map/ppermute | solution.py:231
  15.4 0.0 collective-permute-done.2
  15.4 3.5 %collective-permute-done.3 = bf16[17,16,128]{2,1,0:T(8,128)(2,1)S(1)} collective-permute-done((bf16[17,16,128]{2,1,0:T(8,128)(2,1)S(1)}, bf16[17,16,128]{2,1,0:T(8,128)(2,1)S(1)}, u32[]{:S(2)}, u32[]{:S(2)}) %collective-permute-start.3) | collective-permute-done | bytes 69664 | tf_op jit(solution)/shard_map/ppermute | solution.py:231
  19.0 0.0 collective-permute-done.4
  19.0 1.2 %collective-permute-done.5 = bf16[17,16,128]{2,1,0:T(8,128)(2,1)S(1)} collective-permute-done((bf16[17,16,128]{2,1,0:T(8,128)(2,1)S(1)}, bf16[17,16,128]{2,1,0:T(8,128)(2,1)S(1)}, u32[]{:S(2)}, u32[]{:S(2)}) %collective-permute-start.5) | collective-permute-done | bytes 69664 | tf_op jit(solution)/shard_map/ppermute | solution.py:231
  20.2 0.0 collective-permute-done.6
  20.3 0.1 collective-permute-start.7
  20.3 0.7 %near.1 = (s32[288,128]{1,0:T(8,128)S(1)}, s32[2,256]{1,0:T(2,128)S(1)}, f32[1,256]{1,0:T(1,128)S(1)}, f32[288,1024]{1,0:T(8,128)S(1)}, f32[288,128]{1,0:T(8,128)S(1)}) custom-call(s32[1]{0:T(128)} %bitcast.me_ref, s32[1,512]{1,0:T(1,128)S(1)} %bitcast.6, bf16[136,16,128]{2,1,0:T(8,128)(2,1)S(1)} %constant_dynamic-update-slice_fusion.query_ref), custom_call_target="tpu_custom_call" | custom-call | flops 268435456 | bytes 1048576 | tf_op jit(solution)/shard_map/near/pallas_call | solution.py:302
  21.0 1.2 %collective-permute-done.7.other_ref = bf16[136,16,128]{2,1,0:T(8,128)(2,1)S(1)} collective-permute-done((bf16[136,16,128]{2,1,0:T(8,128)(2,1)S(1)}, bf16[136,16,128]{2,1,0:T(8,128)(2,1)S(1)}, u32[]{:S(2)}, u32[]{:S(2)}) %collective-permute-start.7) | collective-permute-done | bytes 557088 | tf_op jit(solution)/shard_map/ppermute | solution.py:231
  22.3 1.1 %far.1 = (f32[8,2,256]{2,1,0:T(2,128)S(1)}, f32[1,32]{1,0:T(1,128)S(1)}) custom-call(bf16[136,16,128]{2,1,0:T(8,128)(2,1)S(1)} %constant_dynamic-update-slice_fusion.query_ref, bf16[136,16,128]{2,1,0:T(8,128)(2,1)S(1)} %collective-permute-done.7.other_ref, s32[288,128]{1,0:T(8,128)S(1)} %get-tuple-element.33.lows_ref, ...), custom_call_target="tpu_custom_call" | custom-call | flops 268435456 | bytes 1048576 | tf_op jit(solution)/shard_map/far/pallas_call | solution.py:317
  23.4 10.0 %all_to_all.5.result_ref = f32[8,2,256]{2,1,0:T(2,128)S(1)} all-to-all(f32[8,2,256]{2,1,0:T(2,128)S(1)} %get-tuple-element.38), channel_id=1, replica_groups=mesh['groups'=2,'shard'=8,'sub'=2] {'shard'}, dimensions={0} | all-to-all | bytes 32768 | tf_op jit(solution)/shard_map/all_to_all | solution.py:329
  33.4 0.7 %pick.1 = (f32[1,128]{1,0:T(1,128)}, f32[1,128]{1,0:T(1,128)}, f32[1,32]{1,0:T(1,128)}) custom-call(s32[1]{0:T(128)} %bitcast.me_ref, s32[1,128]{1,0:T(1,128)S(1)} %get-tuple-element.23.slot_ref, f32[8,2,256]{2,1,0:T(2,128)S(1)} %all_to_all.5.result_ref, f32[1,32]{1,0:T(1,128)S(1)} %get-tuple-element.39.norm_ref), custom_call_target="tpu_custom_call" | custom-call | tf_op jit(solution)/shard_map/pick/pallas_call | solution.py:330
  (8 shorter events, 0.1 us)
Async XLA Ops:
  0.6 1.0 %copy-start = (bf16[128,1024]{1,0:T(8,128)(2,1)S(1)}, bf16[128,1024]{1,0:T(8,128)(2,1)}, u32[]{:S(2)}) copy-start(bf16[128,1024]{1,0:T(8,128)(2,1)} %embed_ref.1) | copy-start | bytes 786436
  2.1 11.0 %collective-permute-start = (bf16[17,16,128]{2,1,0:T(8,128)(2,1)S(1)}, bf16[17,16,128]{2,1,0:T(8,128)(2,1)S(1)}, u32[]{:S(2)}, u32[]{:S(2)}) collective-permute-start(bf16[17,16,128]{2,1,0:T(8,128)(2,1)S(1)} %get-tuple-element.25), channel_id=1, source_target_pairs={{0,8},{2,10},{4,12},{6,14},{8,0},{10,2},{12,4},{14,6},{1,9},{3,11}... | collective-permute-start | bytes 208904 | tf_op jit(solution)/shard_map/ppermute | solution.py:231
  6.2 8.6 %collective-permute-start.1 = (bf16[17,16,128]{2,1,0:T(8,128)(2,1)S(1)}, bf16[17,16,128]{2,1,0:T(8,128)(2,1)S(1)}, u32[]{:S(2)}, u32[]{:S(2)}) collective-permute-start(bf16[17,16,128]{2,1,0:T(8,128)(2,1)S(1)} %get-tuple-element.26), channel_id=1, source_target_pairs={{0,4},{2,6},{4,0},{6,2},{8,12},{10,14},{12,8},{14,10},{1,5},{3,7},... | collective-permute-start | bytes 208904 | tf_op jit(solution)/shard_map/ppermute | solution.py:231
  7.8 7.6 %collective-permute-start.2 = (bf16[17,16,128]{2,1,0:T(8,128)(2,1)S(1)}, bf16[17,16,128]{2,1,0:T(8,128)(2,1)S(1)}, u32[]{:S(2)}, u32[]{:S(2)}) collective-permute-start(bf16[17,16,128]{2,1,0:T(8,128)(2,1)S(1)} %get-tuple-element.27), channel_id=1, source_target_pairs={{0,6},{2,4},{4,2},{6,0},{8,14},{10,12},{12,10},{14,8},{1,7},{3,5},... | collective-permute-start | bytes 208904 | tf_op jit(solution)/shard_map/ppermute | solution.py:231
  9.2 9.8 %collective-permute-start.3 = (bf16[17,16,128]{2,1,0:T(8,128)(2,1)S(1)}, bf16[17,16,128]{2,1,0:T(8,128)(2,1)S(1)}, u32[]{:S(2)}, u32[]{:S(2)}) collective-permute-start(bf16[17,16,128]{2,1,0:T(8,128)(2,1)S(1)} %get-tuple-element.28), channel_id=1, source_target_pairs={{0,10},{2,8},{4,14},{6,12},{8,2},{10,0},{12,6},{14,4},{1,11},{3,9}... | collective-permute-start | bytes 208904 | tf_op jit(solution)/shard_map/ppermute | solution.py:231
  9.2 9.7 %collective-permute-start.4 = (bf16[17,16,128]{2,1,0:T(8,128)(2,1)S(1)}, bf16[17,16,128]{2,1,0:T(8,128)(2,1)S(1)}, u32[]{:S(2)}, u32[]{:S(2)}) collective-permute-start(bf16[17,16,128]{2,1,0:T(8,128)(2,1)S(1)} %get-tuple-element.29), channel_id=1, source_target_pairs={{0,12},{2,14},{4,8},{6,10},{8,4},{10,6},{12,0},{14,2},{1,13},{3,15... | collective-permute-start | bytes 208904 | tf_op jit(solution)/shard_map/ppermute | solution.py:231
  13.1 7.1 %collective-permute-start.5 = (bf16[17,16,128]{2,1,0:T(8,128)(2,1)S(1)}, bf16[17,16,128]{2,1,0:T(8,128)(2,1)S(1)}, u32[]{:S(2)}, u32[]{:S(2)}) collective-permute-start(bf16[17,16,128]{2,1,0:T(8,128)(2,1)S(1)} %get-tuple-element.30), channel_id=1, source_target_pairs={{0,14},{2,12},{4,10},{6,8},{8,6},{10,4},{12,2},{14,0},{1,15},{3,13... | collective-permute-start | bytes 208904 | tf_op jit(solution)/shard_map/ppermute | solution.py:231
  14.8 5.4 %collective-permute-start.6 = (bf16[17,16,128]{2,1,0:T(8,128)(2,1)S(1)}, bf16[17,16,128]{2,1,0:T(8,128)(2,1)S(1)}, u32[]{:S(2)}, u32[]{:S(2)}) collective-permute-start(bf16[17,16,128]{2,1,0:T(8,128)(2,1)S(1)} %get-tuple-element.31), channel_id=1, source_target_pairs={{0,2},{2,0},{4,6},{6,4},{8,10},{10,8},{12,14},{14,12},{1,3},{3,1},... | collective-permute-start | bytes 208904 | tf_op jit(solution)/shard_map/ppermute | solution.py:231
  20.3 2.0 %collective-permute-start.7 = (bf16[136,16,128]{2,1,0:T(8,128)(2,1)S(1)}, bf16[136,16,128]{2,1,0:T(8,128)(2,1)S(1)}, u32[]{:S(2)}, u32[]{:S(2)}) collective-permute-start(bf16[136,16,128]{2,1,0:T(8,128)(2,1)S(1)} %constant_dynamic-update-slice_fusion.query_ref), channel_id=1, source_target_pairs={{0,1},{1,0},{2,3},{3,2},{4,5},{5,4},{6,7},{7,6},{8,9},{9,8},{10,11... | collective-permute-start | bytes 1671176 | tf_op jit(solution)/shard_map/ppermute | solution.py:231

commit v14 on v13

--- a/solution.py
+++ b/solution.py
@@ -9,7 +9,7 @@
 
 LANES = 128
 DIGITS = 3
-MOST_PERMUTES = 8
+PARTNERS = (4, 5, 1, 2, 6, 3, 7, 0)
 WHOLE = pl.BlockSpec(memory_space=pltpu.VMEM)
 SCALAR = pl.BlockSpec(memory_space=pltpu.SMEM)
 
@@ -231,12 +231,6 @@
     return lax.ppermute(value, axis, [(i, i ^ k) for i in range(lax.axis_size(axis))])
 
 
-def partner_order(owners):
-    half = owners // 2
-    far, near = list(range(half, owners)), list(range(2, half))
-    return far[:1] + near + far[1:] + list(range(1, min(half, 2))) + [0]
-
-
 def exchange(packed, order):
     return jnp.concatenate(
         [from_partner(block, k, "shard") if k else block for k, block in zip(order, packed)]
@@ -271,8 +265,8 @@
     me = lax.axis_index("shard").astype(jnp.int32).reshape(1)
     ints = jnp.concatenate([owner_map, cluster_id, item_order]).reshape(1, -1)
 
-    direct = owners <= MOST_PERMUTES
-    order = partner_order(owners) if direct else list(range(owners))
+    direct = owners == len(PARTNERS)
+    order = PARTNERS if direct else tuple(range(owners))
     parts = owners if direct else 1
     tiles = 2 * (width // LANES) + 1
     block = (tiles, slots // parts // 2, LANES)

time: 34.3 us -> 37.1 us (1.082)
  starting transfers between devices: 13.3 us -> 14.8 us
  blocking collectives: 9.99 us -> 10.8 us
  waiting for transfers between devices: 5.98 us -> 6.48 us
    ppermute x8, starting transfers between devices: 13.3 us -> 14.8 us  [from_partner(): lax.ppermute(value, axis, [(i, i ^ k) for i in range(lax.axis_size(axis))])]
    all_to_all x1, blocking collectives: 9.99 us -> 10.8 us  [local(): results = lax.all_to_all(results, 'shard', 0, 0, tiled=True)]
    ppermute x8, waiting for transfers between devices: 5.98 us -> 6.48 us  [from_partner(): lax.ppermute(value, axis, [(i, i ^ k) for i in range(lax.axis_size(axis))])]
where the time goes in v14:
time: 37.1 us; the launch traced here: 36.9 us
  starting transfers between devices  14.8 us (40%)
  blocking collectives  10.8 us (29%)
  waiting for transfers between devices  6.48 us (17%)
  Pallas kernels  3.21 us (9%)
  other arithmetic  0.76 us (2%)
  between operations  0.74 us (2%)
    ppermute x8, starting transfers between devices, from_partner(): lax.ppermute(value, axis, [(i, i ^ k) for i in range(lax.axis_size(axis))])  14.8 us
    all_to_all x1, blocking collectives, local(): results = lax.all_to_all(results, 'shard', 0, 0, tiled=True)  10.8 us
    ppermute x8, waiting for transfers between devices, from_partner(): lax.ppermute(value, axis, [(i, i ^ k) for i in range(lax.axis_size(axis))])  6.48 us
    pallas_call x1, Pallas kernels, local(): pl.pallas_call(functools.partial(far_kernel, rows_all, tiles), out_shape=...  1.1 us
    concatenate x1, other arithmetic, local(): ints = jnp.concatenate([owner_map, cluster_id, item_order]).reshape(1, -1)  0.76 us
  transfers between devices with their start and end apart: 8, of which 3 were waited for; matrix products, arithmetic and copies ran while one was open for 0% of the time, Pallas kernels for 2%

profile of v14, /device:TPU:0, one launch (start us, length us, event | category | flops | bytes accessed | tf_op | source)
XLA Modules:
  0.0 36.9 jit_solution(2180485051685962203)
XLA Ops:
  0.6 0.0 copy-start
  0.6 0.8 %pad_add_fusion = s32[512]{0:T(512)S(1)} fusion(s32[128]{0:T(128)} %param.6, s32[128]{0:T(128)} %param.5, s32[256]{0:T(256)} %param.7), kind=kLoop, calls=%fused_computation.8 | loop fusion | flops 1024 | bytes 4096 | tf_op jit(solution)/shard_map/concatenate | solution.py:266
  1.4 0.3 slots.1
  1.7 0.0 copy-done
  1.7 0.4 %pack.1 = (bf16[17,16,128]{2,1,0:T(8,128)(2,1)S(1)}, bf16[17,16,128]{2,1,0:T(8,128)(2,1)S(1)}, bf16[17,16,128]{2,1,0:T(8,128)(2,1)S(1)}, bf16[17,16,128]{2,1,0:T...) custom-call(s32[1,128]{1,0:T(1,128)S(1)} %get-tuple-element.23.slot_, ...), custom_call_target="tpu_custom_call" | custom-call | tf_op jit(solution)/shard_map/pack/pallas_call | solution.py:285
  2.1 4.1 %collective-permute-start = (bf16[17,16,128]{2,1,0:T(8,128)(2,1)S(1)}, bf16[17,16,128]{2,1,0:T(8,128)(2,1)S(1)}, u32[]{:S(2)}, u32[]{:S(2)}) collective-permute-start(bf16[17,16,128]{2,1,0:T(8,128)(2,1)S(1)} %get-tuple-element.25), channel_id=1, source_target_pairs={{0,8},{2,10},{4,12},{6,14},{8,0},{10,2},{12,4},{14,6},{1,9},{3,11}... | collective-permute-start | bytes 208904 | tf_op jit(solution)/shard_map/ppermute | solution.py:231
  6.2 1.3 %collective-permute-start.1 = (bf16[17,16,128]{2,1,0:T(8,128)(2,1)S(1)}, bf16[17,16,128]{2,1,0:T(8,128)(2,1)S(1)}, u32[]{:S(2)}, u32[]{:S(2)}) collective-permute-start(bf16[17,16,128]{2,1,0:T(8,128)(2,1)S(1)} %get-tuple-element.26), channel_id=1, source_target_pairs={{0,10},{2,8},{4,14},{6,12},{8,2},{10,0},{12,6},{14,4},{1,11},{3,9}... | collective-permute-start | bytes 208904 | tf_op jit(solution)/shard_map/ppermute | solution.py:231
  7.5 0.3 collective-permute-start.2
  7.8 1.8 %collective-permute-start.3 = (bf16[17,16,128]{2,1,0:T(8,128)(2,1)S(1)}, bf16[17,16,128]{2,1,0:T(8,128)(2,1)S(1)}, u32[]{:S(2)}, u32[]{:S(2)}) collective-permute-start(bf16[17,16,128]{2,1,0:T(8,128)(2,1)S(1)} %get-tuple-element.28), channel_id=1, source_target_pairs={{0,4},{2,6},{4,0},{6,2},{8,12},{10,14},{12,8},{14,10},{1,5},{3,7},... | collective-permute-start | bytes 208904 | tf_op jit(solution)/shard_map/ppermute | solution.py:231
  9.6 2.5 %collective-permute-start.4 = (bf16[17,16,128]{2,1,0:T(8,128)(2,1)S(1)}, bf16[17,16,128]{2,1,0:T(8,128)(2,1)S(1)}, u32[]{:S(2)}, u32[]{:S(2)}) collective-permute-start(bf16[17,16,128]{2,1,0:T(8,128)(2,1)S(1)} %get-tuple-element.29), channel_id=1, source_target_pairs={{0,12},{2,14},{4,8},{6,10},{8,4},{10,6},{12,0},{14,2},{1,13},{3,15... | collective-permute-start | bytes 208904 | tf_op jit(solution)/shard_map/ppermute | solution.py:231
  12.1 0.0 collective-permute-done
  12.1 1.6 %collective-permute-start.5 = (bf16[17,16,128]{2,1,0:T(8,128)(2,1)S(1)}, bf16[17,16,128]{2,1,0:T(8,128)(2,1)S(1)}, u32[]{:S(2)}, u32[]{:S(2)}) collective-permute-start(bf16[17,16,128]{2,1,0:T(8,128)(2,1)S(1)} %get-tuple-element.30), channel_id=1, source_target_pairs={{0,6},{2,4},{4,2},{6,0},{8,14},{10,12},{12,10},{14,8},{1,7},{3,5},... | collective-permute-start | bytes 208904 | tf_op jit(solution)/shard_map/ppermute | solution.py:231
  13.7 1.5 %collective-permute-done.1 = bf16[17,16,128]{2,1,0:T(8,128)(2,1)S(1)} collective-permute-done((bf16[17,16,128]{2,1,0:T(8,128)(2,1)S(1)}, bf16[17,16,128]{2,1,0:T(8,128)(2,1)S(1)}, u32[]{:S(2)}, u32[]{:S(2)}) %collective-permute-start.1) | collective-permute-done | bytes 69664 | tf_op jit(solution)/shard_map/ppermute | solution.py:231
  15.2 3.2 %collective-permute-start.6 = (bf16[17,16,128]{2,1,0:T(8,128)(2,1)S(1)}, bf16[17,16,128]{2,1,0:T(8,128)(2,1)S(1)}, u32[]{:S(2)}, u32[]{:S(2)}) collective-permute-start(bf16[17,16,128]{2,1,0:T(8,128)(2,1)S(1)} %get-tuple-element.31), channel_id=1, source_target_pairs={{0,14},{2,12},{4,10},{6,8},{8,6},{10,4},{12,2},{14,0},{1,15},{3,13... | collective-permute-start | bytes 208904 | tf_op jit(solution)/shard_map/ppermute | solution.py:231
  18.4 0.0 collective-permute-done.2
  18.4 0.0 collective-permute-done.3
  18.5 0.0 collective-permute-done.4
  18.5 0.0 collective-permute-done.5
  18.5 3.7 %collective-permute-done.6 = bf16[17,16,128]{2,1,0:T(8,128)(2,1)S(1)} collective-permute-done((bf16[17,16,128]{2,1,0:T(8,128)(2,1)S(1)}, bf16[17,16,128]{2,1,0:T(8,128)(2,1)S(1)}, u32[]{:S(2)}, u32[]{:S(2)}) %collective-permute-start.6) | collective-permute-done | bytes 69664 | tf_op jit(solution)/shard_map/ppermute | solution.py:231
  22.3 0.1 collective-permute-start.7
  22.3 0.7 %near.1 = (s32[288,128]{1,0:T(8,128)S(1)}, s32[2,256]{1,0:T(2,128)S(1)}, f32[1,256]{1,0:T(1,128)S(1)}, f32[288,1024]{1,0:T(8,128)S(1)}, f32[288,128]{1,0:T(8,128)S(1)}) custom-call(s32[1]{0:T(128)} %bitcast.me_ref, s32[1,512]{1,0:T(1,128)S(1)} %bitcast.6, bf16[136,16,128]{2,1,0:T(8,128)(2,1)S(1)} %constant_dynamic-update-slice_fusion.query_ref), custom_call_target="tpu_custom_call" | custom-call | flops 268435456 | bytes 1048576 | tf_op jit(solution)/shard_map/near/pallas_call | solution.py:296
  23.0 1.2 %collective-permute-done.7.other_ref = bf16[136,16,128]{2,1,0:T(8,128)(2,1)S(1)} collective-permute-done((bf16[136,16,128]{2,1,0:T(8,128)(2,1)S(1)}, bf16[136,16,128]{2,1,0:T(8,128)(2,1)S(1)}, u32[]{:S(2)}, u32[]{:S(2)}) %collective-permute-start.7) | collective-permute-done | bytes 557088 | tf_op jit(solution)/shard_map/ppermute | solution.py:231
  24.3 1.1 %far.1 = (f32[8,2,256]{2,1,0:T(2,128)S(1)}, f32[1,32]{1,0:T(1,128)S(1)}) custom-call(bf16[136,16,128]{2,1,0:T(8,128)(2,1)S(1)} %constant_dynamic-update-slice_fusion.query_ref, bf16[136,16,128]{2,1,0:T(8,128)(2,1)S(1)} %collective-permute-done.7.other_ref, s32[288,128]{1,0:T(8,128)S(1)} %get-tuple-element.33.lows_ref, ...), custom_call_target="tpu_custom_call" | custom-call | flops 268435456 | bytes 1048576 | tf_op jit(solution)/shard_map/far/pallas_call | solution.py:311
  25.4 10.8 %all_to_all.5.result_ref = f32[8,2,256]{2,1,0:T(2,128)S(1)} all-to-all(f32[8,2,256]{2,1,0:T(2,128)S(1)} %get-tuple-element.38), channel_id=1, replica_groups=mesh['groups'=2,'shard'=8,'sub'=2] {'shard'}, dimensions={0} | all-to-all | bytes 32768 | tf_op jit(solution)/shard_map/all_to_all | solution.py:323
  36.2 0.7 %pick.1 = (f32[1,128]{1,0:T(1,128)}, f32[1,128]{1,0:T(1,128)}, f32[1,32]{1,0:T(1,128)}) custom-call(s32[1]{0:T(128)} %bitcast.me_ref, s32[1,128]{1,0:T(1,128)S(1)} %get-tuple-element.23.slot_ref, f32[8,2,256]{2,1,0:T(2,128)S(1)} %all_to_all.5.result_ref, f32[1,32]{1,0:T(1,128)S(1)} %get-tuple-element.39.norm_ref), custom_call_target="tpu_custom_call" | custom-call | tf_op jit(solution)/shard_map/pick/pallas_call | solution.py:324
  (8 shorter events, 0.1 us)
Async XLA Ops:
  0.6 1.0 %copy-start = (bf16[128,1024]{1,0:T(8,128)(2,1)S(1)}, bf16[128,1024]{1,0:T(8,128)(2,1)}, u32[]{:S(2)}) copy-start(bf16[128,1024]{1,0:T(8,128)(2,1)} %embed_ref.1) | copy-start | bytes 786436
  2.1 10.0 %collective-permute-start = (bf16[17,16,128]{2,1,0:T(8,128)(2,1)S(1)}, bf16[17,16,128]{2,1,0:T(8,128)(2,1)S(1)}, u32[]{:S(2)}, u32[]{:S(2)}) collective-permute-start(bf16[17,16,128]{2,1,0:T(8,128)(2,1)S(1)} %get-tuple-element.25), channel_id=1, source_target_pairs={{0,8},{2,10},{4,12},{6,14},{8,0},{10,2},{12,4},{14,6},{1,9},{3,11}... | collective-permute-start | bytes 208904 | tf_op jit(solution)/shard_map/ppermute | solution.py:231
  6.2 9.0 %collective-permute-start.1 = (bf16[17,16,128]{2,1,0:T(8,128)(2,1)S(1)}, bf16[17,16,128]{2,1,0:T(8,128)(2,1)S(1)}, u32[]{:S(2)}, u32[]{:S(2)}) collective-permute-start(bf16[17,16,128]{2,1,0:T(8,128)(2,1)S(1)} %get-tuple-element.26), channel_id=1, source_target_pairs={{0,10},{2,8},{4,14},{6,12},{8,2},{10,0},{12,6},{14,4},{1,11},{3,9}... | collective-permute-start | bytes 208904 | tf_op jit(solution)/shard_map/ppermute | solution.py:231
  7.5 10.9 %collective-permute-start.2 = (bf16[17,16,128]{2,1,0:T(8,128)(2,1)S(1)}, bf16[17,16,128]{2,1,0:T(8,128)(2,1)S(1)}, u32[]{:S(2)}, u32[]{:S(2)}) collective-permute-start(bf16[17,16,128]{2,1,0:T(8,128)(2,1)S(1)} %get-tuple-element.27), channel_id=1, source_target_pairs={{0,2},{2,0},{4,6},{6,4},{8,10},{10,8},{12,14},{14,12},{1,3},{3,1},... | collective-permute-start | bytes 208904 | tf_op jit(solution)/shard_map/ppermute | solution.py:231
  7.8 10.7 %collective-permute-start.3 = (bf16[17,16,128]{2,1,0:T(8,128)(2,1)S(1)}, bf16[17,16,128]{2,1,0:T(8,128)(2,1)S(1)}, u32[]{:S(2)}, u32[]{:S(2)}) collective-permute-start(bf16[17,16,128]{2,1,0:T(8,128)(2,1)S(1)} %get-tuple-element.28), channel_id=1, source_target_pairs={{0,4},{2,6},{4,0},{6,2},{8,12},{10,14},{12,8},{14,10},{1,5},{3,7},... | collective-permute-start | bytes 208904 | tf_op jit(solution)/shard_map/ppermute | solution.py:231
  9.6 8.8 %collective-permute-start.4 = (bf16[17,16,128]{2,1,0:T(8,128)(2,1)S(1)}, bf16[17,16,128]{2,1,0:T(8,128)(2,1)S(1)}, u32[]{:S(2)}, u32[]{:S(2)}) collective-permute-start(bf16[17,16,128]{2,1,0:T(8,128)(2,1)S(1)} %get-tuple-element.29), channel_id=1, source_target_pairs={{0,12},{2,14},{4,8},{6,10},{8,4},{10,6},{12,0},{14,2},{1,13},{3,15... | collective-permute-start | bytes 208904 | tf_op jit(solution)/shard_map/ppermute | solution.py:231
  12.1 6.4 %collective-permute-start.5 = (bf16[17,16,128]{2,1,0:T(8,128)(2,1)S(1)}, bf16[17,16,128]{2,1,0:T(8,128)(2,1)S(1)}, u32[]{:S(2)}, u32[]{:S(2)}) collective-permute-start(bf16[17,16,128]{2,1,0:T(8,128)(2,1)S(1)} %get-tuple-element.30), channel_id=1, source_target_pairs={{0,6},{2,4},{4,2},{6,0},{8,14},{10,12},{12,10},{14,8},{1,7},{3,5},... | collective-permute-start | bytes 208904 | tf_op jit(solution)/shard_map/ppermute | solution.py:231
  15.2 7.0 %collective-permute-start.6 = (bf16[17,16,128]{2,1,0:T(8,128)(2,1)S(1)}, bf16[17,16,128]{2,1,0:T(8,128)(2,1)S(1)}, u32[]{:S(2)}, u32[]{:S(2)}) collective-permute-start(bf16[17,16,128]{2,1,0:T(8,128)(2,1)S(1)} %get-tuple-element.31), channel_id=1, source_target_pairs={{0,14},{2,12},{4,10},{6,8},{8,6},{10,4},{12,2},{14,0},{1,15},{3,13... | collective-permute-start | bytes 208904 | tf_op jit(solution)/shard_map/ppermute | solution.py:231
  22.3 2.0 %collective-permute-start.7 = (bf16[136,16,128]{2,1,0:T(8,128)(2,1)S(1)}, bf16[136,16,128]{2,1,0:T(8,128)(2,1)S(1)}, u32[]{:S(2)}, u32[]{:S(2)}) collective-permute-start(bf16[136,16,128]{2,1,0:T(8,128)(2,1)S(1)} %constant_dynamic-update-slice_fusion.query_ref), channel_id=1, source_target_pairs={{0,1},{1,0},{2,3},{3,2},{4,5},{5,4},{6,7},{7,6},{8,9},{9,8},{10,11... | collective-permute-start | bytes 1671176 | tf_op jit(solution)/shard_map/ppermute | solution.py:231

commit v15 on v14

--- a/solution.py
+++ b/solution.py
@@ -9,7 +9,7 @@
 
 LANES = 128
 DIGITS = 3
-PARTNERS = (4, 5, 1, 2, 6, 3, 7, 0)
+PARTNERS = (4, 2, 3, 5, 6, 7, 1, 0)
 WHOLE = pl.BlockSpec(memory_space=pltpu.VMEM)
 SCALAR = pl.BlockSpec(memory_space=pltpu.SMEM)
 
@@ -237,6 +237,15 @@
     )
 
 
+def gather_pairs(value):
+    owners, step = lax.axis_size("shard"), 1
+    while step < owners:
+        pairs = [[i, i + step] for i in range(owners) if not i & step]
+        value = lax.all_gather(value, "shard", axis_index_groups=pairs, axis=0, tiled=True)
+        step *= 2
+    return value
+
+
 def exchange_all(packed, me):
     owners = lax.axis_size("shard")
     tiles, half, _ = packed.shape
@@ -311,7 +320,7 @@
     results, norms = pl.pallas_call(
         functools.partial(far_kernel, rows_all, tiles),
         out_shape=[
-            jax.ShapeDtypeStruct((owners, 2, slots), jnp.float32),
+            jax.ShapeDtypeStruct((1 if direct else owners, 2, slots), jnp.float32),
             jax.ShapeDtypeStruct((1, clus_dev), jnp.float32),
         ],
         in_specs=[WHOLE] * 7,
@@ -320,7 +329,10 @@
         cost_estimate=compare_cost,
         name="far",
     )(query, other, *near)
-    results = lax.all_to_all(results, "shard", 0, 0, tiled=True)
+    if direct:
+        results = gather_pairs(results)
+    else:
+        results = lax.all_to_all(results, "shard", 0, 0, tiled=True)
     best, distance, cohesion = pl.pallas_call(
         functools.partial(pick_kernel, order, parts),
         out_shape=[jax.ShapeDtypeStruct((1, local_rows), jnp.float32)] * 2

time: 37.1 us -> 38.2 us (1.030)
  blocking collectives: 10.8 us -> 13.9 us
  starting transfers between devices: 14.8 us -> 13.3 us
  waiting for transfers between devices: 6.48 us -> 5.98 us
    all_gather x0 -> x3, blocking collectives: none -> 13.9 us  [gather_pairs(): lax.all_gather(value, 'shard', axis_index_groups=pairs, axis=0, tiled=True)]
    all_to_all x1 -> x0, blocking collectives: 10.8 us -> none  [local(): results = lax.all_to_all(results, 'shard', 0, 0, tiled=True)]
    ppermute x8, starting transfers between devices: 14.8 us -> 13.3 us  [from_partner(): lax.ppermute(value, axis, [(i, i ^ k) for i in range(lax.axis_size(axis))])]
    ppermute x8, waiting for transfers between devices: 6.48 us -> 5.98 us  [from_partner(): lax.ppermute(value, axis, [(i, i ^ k) for i in range(lax.axis_size(axis))])]
where the time goes in v15:
time: 38.2 us; the launch traced here: 38 us
  blocking collectives  13.9 us (36%)
  starting transfers between devices  13.3 us (35%)
  waiting for transfers between devices  5.98 us (16%)
  Pallas kernels  3.17 us (8%)
  other arithmetic  0.76 us (2%)
  between operations  0.73 us (2%)
    all_gather x3, blocking collectives, gather_pairs(): lax.all_gather(value, 'shard', axis_index_groups=pairs, axis=0, tiled=True)  13.9 us
    ppermute x8, starting transfers between devices, from_partner(): lax.ppermute(value, axis, [(i, i ^ k) for i in range(lax.axis_size(axis))])  13.3 us
    ppermute x8, waiting for transfers between devices, from_partner(): lax.ppermute(value, axis, [(i, i ^ k) for i in range(lax.axis_size(axis))])  5.98 us
    pallas_call x1, Pallas kernels, local(): pl.pallas_call(functools.partial(far_kernel, rows_all, tiles), out_shape=...  1.06 us
  transfers between devices with their start and end apart: 8, of which 3 were waited for; matrix products, arithmetic and copies ran while one was open for 0% of the time, Pallas kernels for 2%

profile of v15, /device:TPU:0, one launch (start us, length us, event | category | flops | bytes accessed | tf_op | source)
XLA Modules:
  0.0 38.0 jit_solution(15717385093651121974)
XLA Ops:
  0.6 0.0 copy-start
  0.6 0.8 %pad_add_fusion = s32[512]{0:T(512)S(1)} fusion(s32[128]{0:T(128)} %param.6, s32[128]{0:T(128)} %param.5, s32[256]{0:T(256)} %param.7), kind=kLoop, calls=%fused_computation.8 | loop fusion | flops 1024 | bytes 4096 | tf_op jit(solution)/shard_map/concatenate | solution.py:275
  1.4 0.3 slots.1
  1.7 0.0 copy-done
  1.7 0.4 %pack.1 = (bf16[17,16,128]{2,1,0:T(8,128)(2,1)S(1)}, bf16[17,16,128]{2,1,0:T(8,128)(2,1)S(1)}, bf16[17,16,128]{2,1,0:T(8,128)(2,1)S(1)}, bf16[17,16,128]{2,1,0:T...) custom-call(s32[1,128]{1,0:T(1,128)S(1)} %get-tuple-element.23.slot_, ...), custom_call_target="tpu_custom_call" | custom-call | tf_op jit(solution)/shard_map/pack/pallas_call | solution.py:294
  2.1 4.1 %collective-permute-start = (bf16[17,16,128]{2,1,0:T(8,128)(2,1)S(1)}, bf16[17,16,128]{2,1,0:T(8,128)(2,1)S(1)}, u32[]{:S(2)}, u32[]{:S(2)}) collective-permute-start(bf16[17,16,128]{2,1,0:T(8,128)(2,1)S(1)} %get-tuple-element.25), channel_id=1, source_target_pairs={{0,8},{2,10},{4,12},{6,14},{8,0},{10,2},{12,4},{14,6},{1,9},{3,11}... | collective-permute-start | bytes 208904 | tf_op jit(solution)/shard_map/ppermute | solution.py:231
  6.2 1.6 %collective-permute-start.1 = (bf16[17,16,128]{2,1,0:T(8,128)(2,1)S(1)}, bf16[17,16,128]{2,1,0:T(8,128)(2,1)S(1)}, u32[]{:S(2)}, u32[]{:S(2)}) collective-permute-start(bf16[17,16,128]{2,1,0:T(8,128)(2,1)S(1)} %get-tuple-element.26), channel_id=1, source_target_pairs={{0,4},{2,6},{4,0},{6,2},{8,12},{10,14},{12,8},{14,10},{1,5},{3,7},... | collective-permute-start | bytes 208904 | tf_op jit(solution)/shard_map/ppermute | solution.py:231
  7.8 1.4 %collective-permute-start.2 = (bf16[17,16,128]{2,1,0:T(8,128)(2,1)S(1)}, bf16[17,16,128]{2,1,0:T(8,128)(2,1)S(1)}, u32[]{:S(2)}, u32[]{:S(2)}) collective-permute-start(bf16[17,16,128]{2,1,0:T(8,128)(2,1)S(1)} %get-tuple-element.27), channel_id=1, source_target_pairs={{0,6},{2,4},{4,2},{6,0},{8,14},{10,12},{12,10},{14,8},{1,7},{3,5},... | collective-permute-start | bytes 208904 | tf_op jit(solution)/shard_map/ppermute | solution.py:231
  9.2 0.1 collective-permute-start.3
  9.2 3.9 %collective-permute-start.4 = (bf16[17,16,128]{2,1,0:T(8,128)(2,1)S(1)}, bf16[17,16,128]{2,1,0:T(8,128)(2,1)S(1)}, u32[]{:S(2)}, u32[]{:S(2)}) collective-permute-start(bf16[17,16,128]{2,1,0:T(8,128)(2,1)S(1)} %get-tuple-element.29), channel_id=1, source_target_pairs={{0,12},{2,14},{4,8},{6,10},{8,4},{10,6},{12,0},{14,2},{1,13},{3,15... | collective-permute-start | bytes 208904 | tf_op jit(solution)/shard_map/ppermute | solution.py:231
  13.1 0.0 collective-permute-done
  13.1 1.7 %collective-permute-start.5 = (bf16[17,16,128]{2,1,0:T(8,128)(2,1)S(1)}, bf16[17,16,128]{2,1,0:T(8,128)(2,1)S(1)}, u32[]{:S(2)}, u32[]{:S(2)}) collective-permute-start(bf16[17,16,128]{2,1,0:T(8,128)(2,1)S(1)} %get-tuple-element.30), channel_id=1, source_target_pairs={{0,14},{2,12},{4,10},{6,8},{8,6},{10,4},{12,2},{14,0},{1,15},{3,13... | collective-permute-start | bytes 208904 | tf_op jit(solution)/shard_map/ppermute | solution.py:231
  14.8 0.0 collective-permute-done.1
  14.8 0.6 %collective-permute-start.6 = (bf16[17,16,128]{2,1,0:T(8,128)(2,1)S(1)}, bf16[17,16,128]{2,1,0:T(8,128)(2,1)S(1)}, u32[]{:S(2)}, u32[]{:S(2)}) collective-permute-start(bf16[17,16,128]{2,1,0:T(8,128)(2,1)S(1)} %get-tuple-element.31), channel_id=1, source_target_pairs={{0,2},{2,0},{4,6},{6,4},{8,10},{10,8},{12,14},{14,12},{1,3},{3,1},... | collective-permute-start | bytes 208904 | tf_op jit(solution)/shard_map/ppermute | solution.py:231
  15.4 0.0 collective-permute-done.2
  15.4 3.5 %collective-permute-done.3 = bf16[17,16,128]{2,1,0:T(8,128)(2,1)S(1)} collective-permute-done((bf16[17,16,128]{2,1,0:T(8,128)(2,1)S(1)}, bf16[17,16,128]{2,1,0:T(8,128)(2,1)S(1)}, u32[]{:S(2)}, u32[]{:S(2)}) %collective-permute-start.3) | collective-permute-done | bytes 69664 | tf_op jit(solution)/shard_map/ppermute | solution.py:231
  19.0 0.0 collective-permute-done.4
  19.0 1.2 %collective-permute-done.5 = bf16[17,16,128]{2,1,0:T(8,128)(2,1)S(1)} collective-permute-done((bf16[17,16,128]{2,1,0:T(8,128)(2,1)S(1)}, bf16[17,16,128]{2,1,0:T(8,128)(2,1)S(1)}, u32[]{:S(2)}, u32[]{:S(2)}) %collective-permute-start.5) | collective-permute-done | bytes 69664 | tf_op jit(solution)/shard_map/ppermute | solution.py:231
  20.2 0.0 collective-permute-done.6
  20.3 0.1 collective-permute-start.7
  20.3 0.7 %near.1 = (s32[288,128]{1,0:T(8,128)S(1)}, s32[2,256]{1,0:T(2,128)S(1)}, f32[1,256]{1,0:T(1,128)S(1)}, f32[288,1024]{1,0:T(8,128)S(1)}, f32[288,128]{1,0:T(8,128)S(1)}) custom-call(s32[1]{0:T(128)} %bitcast.me_ref, s32[1,512]{1,0:T(1,128)S(1)} %bitcast.6, bf16[136,16,128]{2,1,0:T(8,128)(2,1)S(1)} %constant_dynamic-update-slice_fusion.query_ref), custom_call_target="tpu_custom_call" | custom-call | flops 268435456 | bytes 1048576 | tf_op jit(solution)/shard_map/near/pallas_call | solution.py:305
  21.0 1.2 %collective-permute-done.7.other_ref = bf16[136,16,128]{2,1,0:T(8,128)(2,1)S(1)} collective-permute-done((bf16[136,16,128]{2,1,0:T(8,128)(2,1)S(1)}, bf16[136,16,128]{2,1,0:T(8,128)(2,1)S(1)}, u32[]{:S(2)}, u32[]{:S(2)}) %collective-permute-start.7) | collective-permute-done | bytes 557088 | tf_op jit(solution)/shard_map/ppermute | solution.py:231
  22.3 1.1 %far.1 = (f32[1,2,256]{2,1,0:T(2,128)S(1)}, f32[1,32]{1,0:T(1,128)S(1)}) custom-call(bf16[136,16,128]{2,1,0:T(8,128)(2,1)S(1)} %constant_dynamic-update-slice_fusion.query_ref, bf16[136,16,128]{2,1,0:T(8,128)(2,1)S(1)} %collective-permute-done.7.other_ref, s32[288,128]{1,0:T(8,128)S(1)} %get-tuple-element.33.lows_ref, ...), custom_call_target="tpu_custom_call" | custom-call | flops 268435456 | bytes 1048576 | tf_op jit(solution)/shard_map/far/pallas_call | solution.py:320
  23.3 4.3 %all_gather.9 = f32[2,2,256]{2,1,0:T(2,128)S(1)} all-gather(f32[1,2,256]{2,1,0:T(2,128)S(1)} %get-tuple-element.38), channel_id=1, replica_groups={{0,2},{4,6},{8,10},{12,14},{1,3},{5,7},{9,11},{13,15},{16,18},{20,22},{..., dimensions={0}, use_global_device_ids=true | all-gather | bytes 6144 | tf_op jit(solution)/shard_map/all_gather | solution.py:244
  27.7 4.3 %all_gather.10 = f32[4,2,256]{2,1,0:T(2,128)S(1)} all-gather(f32[2,2,256]{2,1,0:T(2,128)S(1)} %all_gather.9), channel_id=1, replica_groups={{0,4},{2,6},{8,12},{10,14},{1,5},{3,7},{9,13},{11,15},{16,20},{18,22},{..., dimensions={0}, use_global_device_ids=true | all-gather | bytes 12288 | tf_op jit(solution)/shard_map/all_gather | solution.py:244
  32.0 5.3 %all_gather.11.result_ref = f32[8,2,256]{2,1,0:T(2,128)S(1)} all-gather(f32[4,2,256]{2,1,0:T(2,128)S(1)} %all_gather.10), channel_id=1, replica_groups={{0,8},{2,10},{4,12},{6,14},{1,9},{3,11},{5,13},{7,15},{16,24},{18,26},{..., dimensions={0}, use_global_device_ids=true | all-gather | bytes 24576 | tf_op jit(solution)/shard_map/all_gather | solution.py:244
  37.3 0.7 %pick.1 = (f32[1,128]{1,0:T(1,128)}, f32[1,128]{1,0:T(1,128)}, f32[1,32]{1,0:T(1,128)}) custom-call(s32[1]{0:T(128)} %bitcast.me_ref, s32[1,128]{1,0:T(1,128)S(1)} %get-tuple-element.23.slot_ref, f32[8,2,256]{2,1,0:T(2,128)S(1)} %all_gather.11.result_ref, f32[1,32]{1,0:T(1,128)S(1)} %get-tuple-element.39.norm_ref), custom_call_target="tpu_custom_call" | custom-call | tf_op jit(solution)/shard_map/pick/pallas_call | solution.py:336
  (8 shorter events, 0.1 us)
Async XLA Ops:
  0.6 1.0 %copy-start = (bf16[128,1024]{1,0:T(8,128)(2,1)S(1)}, bf16[128,1024]{1,0:T(8,128)(2,1)}, u32[]{:S(2)}) copy-start(bf16[128,1024]{1,0:T(8,128)(2,1)} %embed_ref.1) | copy-start | bytes 786436
  2.1 11.0 %collective-permute-start = (bf16[17,16,128]{2,1,0:T(8,128)(2,1)S(1)}, bf16[17,16,128]{2,1,0:T(8,128)(2,1)S(1)}, u32[]{:S(2)}, u32[]{:S(2)}) collective-permute-start(bf16[17,16,128]{2,1,0:T(8,128)(2,1)S(1)} %get-tuple-element.25), channel_id=1, source_target_pairs={{0,8},{2,10},{4,12},{6,14},{8,0},{10,2},{12,4},{14,6},{1,9},{3,11}... | collective-permute-start | bytes 208904 | tf_op jit(solution)/shard_map/ppermute | solution.py:231
  6.2 8.6 %collective-permute-start.1 = (bf16[17,16,128]{2,1,0:T(8,128)(2,1)S(1)}, bf16[17,16,128]{2,1,0:T(8,128)(2,1)S(1)}, u32[]{:S(2)}, u32[]{:S(2)}) collective-permute-start(bf16[17,16,128]{2,1,0:T(8,128)(2,1)S(1)} %get-tuple-element.26), channel_id=1, source_target_pairs={{0,4},{2,6},{4,0},{6,2},{8,12},{10,14},{12,8},{14,10},{1,5},{3,7},... | collective-permute-start | bytes 208904 | tf_op jit(solution)/shard_map/ppermute | solution.py:231
  7.8 7.6 %collective-permute-start.2 = (bf16[17,16,128]{2,1,0:T(8,128)(2,1)S(1)}, bf16[17,16,128]{2,1,0:T(8,128)(2,1)S(1)}, u32[]{:S(2)}, u32[]{:S(2)}) collective-permute-start(bf16[17,16,128]{2,1,0:T(8,128)(2,1)S(1)} %get-tuple-element.27), channel_id=1, source_target_pairs={{0,6},{2,4},{4,2},{6,0},{8,14},{10,12},{12,10},{14,8},{1,7},{3,5},... | collective-permute-start | bytes 208904 | tf_op jit(solution)/shard_map/ppermute | solution.py:231
  9.2 9.8 %collective-permute-start.3 = (bf16[17,16,128]{2,1,0:T(8,128)(2,1)S(1)}, bf16[17,16,128]{2,1,0:T(8,128)(2,1)S(1)}, u32[]{:S(2)}, u32[]{:S(2)}) collective-permute-start(bf16[17,16,128]{2,1,0:T(8,128)(2,1)S(1)} %get-tuple-element.28), channel_id=1, source_target_pairs={{0,10},{2,8},{4,14},{6,12},{8,2},{10,0},{12,6},{14,4},{1,11},{3,9}... | collective-permute-start | bytes 208904 | tf_op jit(solution)/shard_map/ppermute | solution.py:231
  9.2 9.7 %collective-permute-start.4 = (bf16[17,16,128]{2,1,0:T(8,128)(2,1)S(1)}, bf16[17,16,128]{2,1,0:T(8,128)(2,1)S(1)}, u32[]{:S(2)}, u32[]{:S(2)}) collective-permute-start(bf16[17,16,128]{2,1,0:T(8,128)(2,1)S(1)} %get-tuple-element.29), channel_id=1, source_target_pairs={{0,12},{2,14},{4,8},{6,10},{8,4},{10,6},{12,0},{14,2},{1,13},{3,15... | collective-permute-start | bytes 208904 | tf_op jit(solution)/shard_map/ppermute | solution.py:231
  13.1 7.1 %collective-permute-start.5 = (bf16[17,16,128]{2,1,0:T(8,128)(2,1)S(1)}, bf16[17,16,128]{2,1,0:T(8,128)(2,1)S(1)}, u32[]{:S(2)}, u32[]{:S(2)}) collective-permute-start(bf16[17,16,128]{2,1,0:T(8,128)(2,1)S(1)} %get-tuple-element.30), channel_id=1, source_target_pairs={{0,14},{2,12},{4,10},{6,8},{8,6},{10,4},{12,2},{14,0},{1,15},{3,13... | collective-permute-start | bytes 208904 | tf_op jit(solution)/shard_map/ppermute | solution.py:231
  14.8 5.4 %collective-permute-start.6 = (bf16[17,16,128]{2,1,0:T(8,128)(2,1)S(1)}, bf16[17,16,128]{2,1,0:T(8,128)(2,1)S(1)}, u32[]{:S(2)}, u32[]{:S(2)}) collective-permute-start(bf16[17,16,128]{2,1,0:T(8,128)(2,1)S(1)} %get-tuple-element.31), channel_id=1, source_target_pairs={{0,2},{2,0},{4,6},{6,4},{8,10},{10,8},{12,14},{14,12},{1,3},{3,1},... | collective-permute-start | bytes 208904 | tf_op jit(solution)/shard_map/ppermute | solution.py:231
  20.3 2.0 %collective-permute-start.7 = (bf16[136,16,128]{2,1,0:T(8,128)(2,1)S(1)}, bf16[136,16,128]{2,1,0:T(8,128)(2,1)S(1)}, u32[]{:S(2)}, u32[]{:S(2)}) collective-permute-start(bf16[136,16,128]{2,1,0:T(8,128)(2,1)S(1)} %constant_dynamic-update-slice_fusion.query_ref), channel_id=1, source_target_pairs={{0,1},{1,0},{2,3},{3,2},{4,5},{5,4},{6,7},{7,6},{8,9},{9,8},{10,11... | collective-permute-start | bytes 1671176 | tf_op jit(solution)/shard_map/ppermute | solution.py:231

commit v16 on v14

--- a/solution.py
+++ b/solution.py
@@ -9,7 +9,7 @@
 
 LANES = 128
 DIGITS = 3
-PARTNERS = (4, 5, 1, 2, 6, 3, 7, 0)
+PARTNERS = (4, 2, 3, 7, 6, 5, 1, 0)
 WHOLE = pl.BlockSpec(memory_space=pltpu.VMEM)
 SCALAR = pl.BlockSpec(memory_space=pltpu.SMEM)
 
@@ -22,10 +22,8 @@
     return jnp.dot(a, b, preferred_element_type=jnp.float32)
 
 
-def matmul_t(a, b, precision=None):
-    return lax.dot_general(
-        a, b, (((1,), (1,)), ((), ())), precision=precision, preferred_element_type=jnp.float32
-    )
+def matmul_t(a, b):
+    return lax.dot_general(a, b, (((1,), (1,)), ((), ())), preferred_element_type=jnp.float32)
 
 
 def bf16(x):
@@ -142,15 +140,15 @@
     return jnp.concatenate([column] * (count // LANES), axis=1)
 
 
-def compare(rows_all, query, query_low, query_key, lows, rows, digit):
+def compare(rows_all, query_t, query_low, query_key, lows, rows, digit):
     _, key = key_rows(rows_all, digit)
     bound = across(lows, key.shape[1])
     member = bf16((key >= bound) & (key < bound + rows_all))
     sums = matmul(member, rows)
     counts = matmul(member, jnp.ones((rows.shape[0], LANES), jnp.bfloat16))
-    scores = matmul_t(rows, query)
+    scores = matmul(rows, query_t)
     _, key = key_columns(rows_all, digit)
-    key = across(key, query.shape[0])
+    key = across(key, query_t.shape[1])
     earlier = (key >= query_low) & (key < query_key)
     best = jnp.max(jnp.where(earlier, scores, -3.0), axis=0, keepdims=True)
     return best, sums, counts
@@ -158,7 +156,7 @@
 
 def near_kernel(
     rows_all, clusters, clus_dev, tiles, me_ref, ints_ref, query_ref,
-    lows_ref, key_ref, best_ref, sums_ref, counts_ref,
+    query_t_ref, lows_ref, key_ref, best_ref, sums_ref, counts_ref,
 ):
     hot = (ints_ref[:, :clusters] == me_ref[0]).astype(jnp.float32)
     rank = ranked(hot)
@@ -170,7 +168,9 @@
     low, _ = key_columns(rows_all, digit)
     lows = jnp.concatenate([low, own], axis=0)
     query_low, query_key = key_rows(rows_all, digit)
-    best, sums, counts = compare(rows_all, query, query_low, query_key, lows, query, digit)
+    query_t = jnp.transpose(query)
+    query_t_ref[...] = query_t
+    best, sums, counts = compare(rows_all, query_t, query_low, query_key, lows, query, digit)
     lows_ref[...] = lows
     key_ref[...] = jnp.concatenate([query_low, query_key], axis=0)
     best_ref[...] = best
@@ -179,14 +179,14 @@
 
 
 def far_kernel(
-    rows_all, tiles, query_ref, other_ref, lows_ref, key_ref, best_ref, sums_ref, counts_ref,
+    rows_all, tiles, query_ref, other_ref, query_t_ref, lows_ref, key_ref, best_ref, sums_ref, counts_ref,
     result_ref, norm_ref,
 ):
     query, _ = unpacked(query_ref, tiles)
     queries, width = query.shape
     rows, digit = unpacked(other_ref, tiles)
     best, sums, counts = compare(
-        rows_all, query, key_ref[0:1], key_ref[1:2], lows_ref[...], rows, digit
+        rows_all, query_t_ref[...], key_ref[0:1], key_ref[1:2], lows_ref[...], rows, digit
     )
     best = jnp.maximum(best, best_ref[...])
     best = jnp.where(best > -2.0, best, 0.0)
@@ -199,8 +199,7 @@
             [query[:, lanes].astype(jnp.float32) - centroid[:queries], centroid[queries:]], axis=0
         )
         squares = squares + offset * offset
-    ones = jnp.ones((8, LANES), jnp.float32)
-    total = matmul_t(ones, squares, lax.Precision.HIGHEST)[:1]
+    total = jnp.sum(jnp.transpose(squares), axis=0, keepdims=True)
     result = jnp.concatenate([best, total[:, :queries]], axis=0)
     for owner in range(result_ref.shape[0]):
         result_ref[owner] = result
@@ -296,6 +295,7 @@
     near = pl.pallas_call(
         functools.partial(near_kernel, rows_all, owner_map.shape[0], clus_dev, tiles),
         out_shape=[
+            jax.ShapeDtypeStruct((width, slots), jnp.bfloat16),
             jax.ShapeDtypeStruct((asked, LANES), jnp.int32),
             jax.ShapeDtypeStruct((2, slots), jnp.int32),
             jax.ShapeDtypeStruct((1, slots), jnp.float32),
@@ -303,7 +303,7 @@
             jax.ShapeDtypeStruct((asked, LANES), jnp.float32),
         ],
         in_specs=[SCALAR] + [WHOLE] * 2,
-        out_specs=[WHOLE] * 5,
+        out_specs=[WHOLE] * 6,
         compiler_params=params,
         cost_estimate=compare_cost,
         name="near",
@@ -314,7 +314,7 @@
             jax.ShapeDtypeStruct((owners, 2, slots), jnp.float32),
             jax.ShapeDtypeStruct((1, clus_dev), jnp.float32),
         ],
-        in_specs=[WHOLE] * 7,
+        in_specs=[WHOLE] * 8,
         out_specs=[WHOLE] * 2,
         compiler_params=params,
         cost_estimate=compare_cost,

time: 37.1 us -> 35.2 us (0.949)
  starting transfers between devices: 14.8 us -> 12.5 us
  waiting for transfers between devices: 6.48 us -> 8.24 us
  blocking collectives: 10.8 us -> 9.52 us
    ppermute x8, starting transfers between devices: 14.8 us -> 12.5 us  [from_partner(): lax.ppermute(value, axis, [(i, i ^ k) for i in range(lax.axis_size(axis))])]
    ppermute x8, waiting for transfers between devices: 6.48 us -> 8.24 us  [from_partner(): lax.ppermute(value, axis, [(i, i ^ k) for i in range(lax.axis_size(axis))])]
    all_to_all x1, blocking collectives: 10.8 us -> 9.52 us  [local(): results = lax.all_to_all(results, 'shard', 0, 0, tiled=True)]
where the time goes in v16:
time: 35.2 us; the launch traced here: 35 us
  starting transfers between devices  12.5 us (36%)
  blocking collectives  9.52 us (27%)
  waiting for transfers between devices  8.24 us (23%)
  Pallas kernels  3.12 us (9%)
  other arithmetic  0.76 us (2%)
  between operations  0.73 us (2%)
    ppermute x8, starting transfers between devices, from_partner(): lax.ppermute(value, axis, [(i, i ^ k) for i in range(lax.axis_size(axis))])  12.5 us
    all_to_all x1, blocking collectives, local(): results = lax.all_to_all(results, 'shard', 0, 0, tiled=True)  9.52 us
    ppermute x8, waiting for transfers between devices, from_partner(): lax.ppermute(value, axis, [(i, i ^ k) for i in range(lax.axis_size(axis))])  8.24 us
    pallas_call x1, Pallas kernels, local(): pl.pallas_call(functools.partial(far_kernel, rows_all, tiles), out_shape=...  1.01 us
    concatenate x1, other arithmetic, local(): ints = jnp.concatenate([owner_map, cluster_id, item_order]).reshape(1, -1)  0.76 us
    pallas_call x1, Pallas kernels, local(): pl.pallas_call(functools.partial(pick_kernel, order, parts), out_shape=[j...  0.72 us
  transfers between devices with their start and end apart: 8, of which 3 were waited for; matrix products, arithmetic and copies ran while one was open for 0% of the time, Pallas kernels for 2%

profile of v16, /device:TPU:0, one launch (start us, length us, event | category | flops | bytes accessed | tf_op | source)
XLA Modules:
  0.0 35.0 jit_solution(8247015546696547591)
XLA Ops:
  0.6 0.0 copy-start
  0.6 0.8 %pad_add_fusion = s32[512]{0:T(512)S(1)} fusion(s32[128]{0:T(128)} %param.6, s32[128]{0:T(128)} %param.5, s32[256]{0:T(256)} %param.7), kind=kLoop, calls=%fused_computation.8 | loop fusion | flops 1024 | bytes 4096 | tf_op jit(solution)/shard_map/concatenate | solution.py:265
  1.4 0.3 slots.1
  1.7 0.0 copy-done
  1.7 0.4 %pack.1 = (bf16[17,16,128]{2,1,0:T(8,128)(2,1)S(1)}, bf16[17,16,128]{2,1,0:T(8,128)(2,1)S(1)}, bf16[17,16,128]{2,1,0:T(8,128)(2,1)S(1)}, bf16[17,16,128]{2,1,0:T...) custom-call(s32[1,128]{1,0:T(1,128)S(1)} %get-tuple-element.24.slot_, ...), custom_call_target="tpu_custom_call" | custom-call | tf_op jit(solution)/shard_map/pack/pallas_call | solution.py:284
  2.1 4.1 %collective-permute-start = (bf16[17,16,128]{2,1,0:T(8,128)(2,1)S(1)}, bf16[17,16,128]{2,1,0:T(8,128)(2,1)S(1)}, u32[]{:S(2)}, u32[]{:S(2)}) collective-permute-start(bf16[17,16,128]{2,1,0:T(8,128)(2,1)S(1)} %get-tuple-element.26), channel_id=1, source_target_pairs={{0,8},{2,10},{4,12},{6,14},{8,0},{10,2},{12,4},{14,6},{1,9},{3,11}... | collective-permute-start | bytes 208904 | tf_op jit(solution)/shard_map/ppermute | solution.py:230
  6.2 1.6 %collective-permute-start.1 = (bf16[17,16,128]{2,1,0:T(8,128)(2,1)S(1)}, bf16[17,16,128]{2,1,0:T(8,128)(2,1)S(1)}, u32[]{:S(2)}, u32[]{:S(2)}) collective-permute-start(bf16[17,16,128]{2,1,0:T(8,128)(2,1)S(1)} %get-tuple-element.27), channel_id=1, source_target_pairs={{0,4},{2,6},{4,0},{6,2},{8,12},{10,14},{12,8},{14,10},{1,5},{3,7},... | collective-permute-start | bytes 208904 | tf_op jit(solution)/shard_map/ppermute | solution.py:230
  7.8 1.4 %collective-permute-start.2 = (bf16[17,16,128]{2,1,0:T(8,128)(2,1)S(1)}, bf16[17,16,128]{2,1,0:T(8,128)(2,1)S(1)}, u32[]{:S(2)}, u32[]{:S(2)}) collective-permute-start(bf16[17,16,128]{2,1,0:T(8,128)(2,1)S(1)} %get-tuple-element.28), channel_id=1, source_target_pairs={{0,6},{2,4},{4,2},{6,0},{8,14},{10,12},{12,10},{14,8},{1,7},{3,5},... | collective-permute-start | bytes 208904 | tf_op jit(solution)/shard_map/ppermute | solution.py:230
  9.2 1.3 %collective-permute-start.3 = (bf16[17,16,128]{2,1,0:T(8,128)(2,1)S(1)}, bf16[17,16,128]{2,1,0:T(8,128)(2,1)S(1)}, u32[]{:S(2)}, u32[]{:S(2)}) collective-permute-start(bf16[17,16,128]{2,1,0:T(8,128)(2,1)S(1)} %get-tuple-element.29), channel_id=1, source_target_pairs={{0,14},{2,12},{4,10},{6,8},{8,6},{10,4},{12,2},{14,0},{1,15},{3,13... | collective-permute-start | bytes 208904 | tf_op jit(solution)/shard_map/ppermute | solution.py:230
  10.5 2.5 %collective-permute-start.4 = (bf16[17,16,128]{2,1,0:T(8,128)(2,1)S(1)}, bf16[17,16,128]{2,1,0:T(8,128)(2,1)S(1)}, u32[]{:S(2)}, u32[]{:S(2)}) collective-permute-start(bf16[17,16,128]{2,1,0:T(8,128)(2,1)S(1)} %get-tuple-element.30), channel_id=1, source_target_pairs={{0,12},{2,14},{4,8},{6,10},{8,4},{10,6},{12,0},{14,2},{1,13},{3,15... | collective-permute-start | bytes 208904 | tf_op jit(solution)/shard_map/ppermute | solution.py:230
  13.0 0.0 collective-permute-done
  13.0 0.2 collective-permute-start.5
  13.1 0.0 collective-permute-done.1
  13.2 1.4 %collective-permute-start.6 = (bf16[17,16,128]{2,1,0:T(8,128)(2,1)S(1)}, bf16[17,16,128]{2,1,0:T(8,128)(2,1)S(1)}, u32[]{:S(2)}, u32[]{:S(2)}) collective-permute-start(bf16[17,16,128]{2,1,0:T(8,128)(2,1)S(1)} %get-tuple-element.32), channel_id=1, source_target_pairs={{0,2},{2,0},{4,6},{6,4},{8,10},{10,8},{12,14},{14,12},{1,3},{3,1},... | collective-permute-start | bytes 208904 | tf_op jit(solution)/shard_map/ppermute | solution.py:230
  14.6 0.0 collective-permute-done.2
  14.6 2.2 %collective-permute-done.3 = bf16[17,16,128]{2,1,0:T(8,128)(2,1)S(1)} collective-permute-done((bf16[17,16,128]{2,1,0:T(8,128)(2,1)S(1)}, bf16[17,16,128]{2,1,0:T(8,128)(2,1)S(1)}, u32[]{:S(2)}, u32[]{:S(2)}) %collective-permute-start.3) | collective-permute-done | bytes 69664 | tf_op jit(solution)/shard_map/ppermute | solution.py:230
  16.8 0.0 collective-permute-done.4
  16.9 4.8 %collective-permute-done.5 = bf16[17,16,128]{2,1,0:T(8,128)(2,1)S(1)} collective-permute-done((bf16[17,16,128]{2,1,0:T(8,128)(2,1)S(1)}, bf16[17,16,128]{2,1,0:T(8,128)(2,1)S(1)}, u32[]{:S(2)}, u32[]{:S(2)}) %collective-permute-start.5) | collective-permute-done | bytes 69664 | tf_op jit(solution)/shard_map/ppermute | solution.py:230
  21.6 0.0 collective-permute-done.6
  21.7 0.1 collective-permute-start.7
  21.8 0.7 %near.1 = (bf16[1024,256]{1,0:T(8,128)(2,1)S(1)}, s32[288,128]{1,0:T(8,128)S(1)}, s32[2,256]{1,0:T(2,128)S(1)}, f32[1,256]{1,0:T(1,128)S(1)}, f32[288,1024]{1,0:T(8,128)S(1)}, /*index=5*/f32[288,128]{1,0:T(8,128)S(1)}) custom-call(s32[1]{0:T(128)} %bitcast.me_ref, s32[1,512]{1,0:T(1,128)S(1)} %bitcast.6, ...), custom_call_target="tpu_custom_call" | custom-call | flops 268435456 | bytes 1048576 | tf_op jit(solution)/shard_map/near/pallas_call | solution.py:295
  22.5 1.2 %collective-permute-done.7.other_ref = bf16[136,16,128]{2,1,0:T(8,128)(2,1)S(1)} collective-permute-done((bf16[136,16,128]{2,1,0:T(8,128)(2,1)S(1)}, bf16[136,16,128]{2,1,0:T(8,128)(2,1)S(1)}, u32[]{:S(2)}, u32[]{:S(2)}) %collective-permute-start.7) | collective-permute-done | bytes 557088 | tf_op jit(solution)/shard_map/ppermute | solution.py:230
  23.7 1.0 %far.1 = (f32[8,2,256]{2,1,0:T(2,128)S(1)}, f32[1,32]{1,0:T(1,128)S(1)}) custom-call(bf16[136,16,128]{2,1,0:T(8,128)(2,1)S(1)} %constant_dynamic-update-slice_fusion.query_ref, bf16[136,16,128]{2,1,0:T(8,128)(2,1)S(1)} %collective-permute-done.7.other_ref, bf16[1024,256]{1,0:T(8,128)(2,1)S(1)} %get-tuple-element.34.query_t_ref, ...), custom_call_target="tpu_custom_call" | custom-call | flops 268435456 | bytes 1048576 | tf_op jit(solution)/shard_map/far/pallas_call | solution.py:311
  24.7 9.5 %all_to_all.5.result_ref = f32[8,2,256]{2,1,0:T(2,128)S(1)} all-to-all(f32[8,2,256]{2,1,0:T(2,128)S(1)} %get-tuple-element.40), channel_id=1, replica_groups=mesh['groups'=2,'shard'=8,'sub'=2] {'shard'}, dimensions={0} | all-to-all | bytes 32768 | tf_op jit(solution)/shard_map/all_to_all | solution.py:323
  34.2 0.7 %pick.1 = (f32[1,128]{1,0:T(1,128)}, f32[1,128]{1,0:T(1,128)}, f32[1,32]{1,0:T(1,128)}) custom-call(s32[1]{0:T(128)} %bitcast.me_ref, s32[1,128]{1,0:T(1,128)S(1)} %get-tuple-element.24.slot_ref, f32[8,2,256]{2,1,0:T(2,128)S(1)} %all_to_all.5.result_ref, f32[1,32]{1,0:T(1,128)S(1)} %get-tuple-element.41.norm_ref), custom_call_target="tpu_custom_call" | custom-call | tf_op jit(solution)/shard_map/pick/pallas_call | solution.py:324
  (8 shorter events, 0.1 us)
Async XLA Ops:
  0.6 1.0 %copy-start = (bf16[128,1024]{1,0:T(8,128)(2,1)S(1)}, bf16[128,1024]{1,0:T(8,128)(2,1)}, u32[]{:S(2)}) copy-start(bf16[128,1024]{1,0:T(8,128)(2,1)} %embed_ref.1) | copy-start | bytes 786436
  2.1 10.9 %collective-permute-start = (bf16[17,16,128]{2,1,0:T(8,128)(2,1)S(1)}, bf16[17,16,128]{2,1,0:T(8,128)(2,1)S(1)}, u32[]{:S(2)}, u32[]{:S(2)}) collective-permute-start(bf16[17,16,128]{2,1,0:T(8,128)(2,1)S(1)} %get-tuple-element.26), channel_id=1, source_target_pairs={{0,8},{2,10},{4,12},{6,14},{8,0},{10,2},{12,4},{14,6},{1,9},{3,11}... | collective-permute-start | bytes 208904 | tf_op jit(solution)/shard_map/ppermute | solution.py:230
  6.2 6.9 %collective-permute-start.1 = (bf16[17,16,128]{2,1,0:T(8,128)(2,1)S(1)}, bf16[17,16,128]{2,1,0:T(8,128)(2,1)S(1)}, u32[]{:S(2)}, u32[]{:S(2)}) collective-permute-start(bf16[17,16,128]{2,1,0:T(8,128)(2,1)S(1)} %get-tuple-element.27), channel_id=1, source_target_pairs={{0,4},{2,6},{4,0},{6,2},{8,12},{10,14},{12,8},{14,10},{1,5},{3,7},... | collective-permute-start | bytes 208904 | tf_op jit(solution)/shard_map/ppermute | solution.py:230
  7.8 6.8 %collective-permute-start.2 = (bf16[17,16,128]{2,1,0:T(8,128)(2,1)S(1)}, bf16[17,16,128]{2,1,0:T(8,128)(2,1)S(1)}, u32[]{:S(2)}, u32[]{:S(2)}) collective-permute-start(bf16[17,16,128]{2,1,0:T(8,128)(2,1)S(1)} %get-tuple-element.28), channel_id=1, source_target_pairs={{0,6},{2,4},{4,2},{6,0},{8,14},{10,12},{12,10},{14,8},{1,7},{3,5},... | collective-permute-start | bytes 208904 | tf_op jit(solution)/shard_map/ppermute | solution.py:230
  9.2 7.6 %collective-permute-start.3 = (bf16[17,16,128]{2,1,0:T(8,128)(2,1)S(1)}, bf16[17,16,128]{2,1,0:T(8,128)(2,1)S(1)}, u32[]{:S(2)}, u32[]{:S(2)}) collective-permute-start(bf16[17,16,128]{2,1,0:T(8,128)(2,1)S(1)} %get-tuple-element.29), channel_id=1, source_target_pairs={{0,14},{2,12},{4,10},{6,8},{8,6},{10,4},{12,2},{14,0},{1,15},{3,13... | collective-permute-start | bytes 208904 | tf_op jit(solution)/shard_map/ppermute | solution.py:230
  10.5 6.3 %collective-permute-start.4 = (bf16[17,16,128]{2,1,0:T(8,128)(2,1)S(1)}, bf16[17,16,128]{2,1,0:T(8,128)(2,1)S(1)}, u32[]{:S(2)}, u32[]{:S(2)}) collective-permute-start(bf16[17,16,128]{2,1,0:T(8,128)(2,1)S(1)} %get-tuple-element.30), channel_id=1, source_target_pairs={{0,12},{2,14},{4,8},{6,10},{8,4},{10,6},{12,0},{14,2},{1,13},{3,15... | collective-permute-start | bytes 208904 | tf_op jit(solution)/shard_map/ppermute | solution.py:230
  13.0 8.7 %collective-permute-start.5 = (bf16[17,16,128]{2,1,0:T(8,128)(2,1)S(1)}, bf16[17,16,128]{2,1,0:T(8,128)(2,1)S(1)}, u32[]{:S(2)}, u32[]{:S(2)}) collective-permute-start(bf16[17,16,128]{2,1,0:T(8,128)(2,1)S(1)} %get-tuple-element.31), channel_id=1, source_target_pairs={{0,10},{2,8},{4,14},{6,12},{8,2},{10,0},{12,6},{14,4},{1,11},{3,9}... | collective-permute-start | bytes 208904 | tf_op jit(solution)/shard_map/ppermute | solution.py:230
  13.2 8.5 %collective-permute-start.6 = (bf16[17,16,128]{2,1,0:T(8,128)(2,1)S(1)}, bf16[17,16,128]{2,1,0:T(8,128)(2,1)S(1)}, u32[]{:S(2)}, u32[]{:S(2)}) collective-permute-start(bf16[17,16,128]{2,1,0:T(8,128)(2,1)S(1)} %get-tuple-element.32), channel_id=1, source_target_pairs={{0,2},{2,0},{4,6},{6,4},{8,10},{10,8},{12,14},{14,12},{1,3},{3,1},... | collective-permute-start | bytes 208904 | tf_op jit(solution)/shard_map/ppermute | solution.py:230
  21.7 2.0 %collective-permute-start.7 = (bf16[136,16,128]{2,1,0:T(8,128)(2,1)S(1)}, bf16[136,16,128]{2,1,0:T(8,128)(2,1)S(1)}, u32[]{:S(2)}, u32[]{:S(2)}) collective-permute-start(bf16[136,16,128]{2,1,0:T(8,128)(2,1)S(1)} %constant_dynamic-update-slice_fusion.query_ref), channel_id=1, source_target_pairs={{0,1},{1,0},{2,3},{3,2},{4,5},{5,4},{6,7},{7,6},{8,9},{9,8},{10,11... | collective-permute-start | bytes 1671176 | tf_op jit(solution)/shard_map/ppermute | solution.py:230

commit v17 on v16

--- a/solution.py
+++ b/solution.py
@@ -9,7 +9,7 @@
 
 LANES = 128
 DIGITS = 3
-PARTNERS = (4, 2, 3, 7, 6, 5, 1, 0)
+PARTNERS = (4, 2, 3, 5, 7, 6, 1, 0)
 WHOLE = pl.BlockSpec(memory_space=pltpu.VMEM)
 SCALAR = pl.BlockSpec(memory_space=pltpu.SMEM)
 

time: 35.2 us -> 34.1 us (0.969)
  waiting for transfers between devices: 8.24 us -> 5.97 us
  starting transfers between devices: 12.5 us -> 13.4 us
  blocking collectives: 9.52 us -> 9.89 us
    ppermute x8, waiting for transfers between devices: 8.24 us -> 5.97 us  [from_partner(): lax.ppermute(value, axis, [(i, i ^ k) for i in range(lax.axis_size(axis))])]
    ppermute x8, starting transfers between devices: 12.5 us -> 13.4 us  [from_partner(): lax.ppermute(value, axis, [(i, i ^ k) for i in range(lax.axis_size(axis))])]
    all_to_all x1, blocking collectives: 9.52 us -> 9.89 us  [local(): results = lax.all_to_all(results, 'shard', 0, 0, tiled=True)]
where the time goes in v17:
time: 34.1 us; the launch traced here: 34 us
  starting transfers between devices  13.4 us (39%)
  blocking collectives  9.89 us (29%)
  waiting for transfers between devices  5.97 us (18%)
  Pallas kernels  3.12 us (9%)
  other arithmetic  0.76 us (2%)
  between operations  0.73 us (2%)
    ppermute x8, starting transfers between devices, from_partner(): lax.ppermute(value, axis, [(i, i ^ k) for i in range(lax.axis_size(axis))])  13.4 us
    all_to_all x1, blocking collectives, local(): results = lax.all_to_all(results, 'shard', 0, 0, tiled=True)  9.89 us
    ppermute x8, waiting for transfers between devices, from_partner(): lax.ppermute(value, axis, [(i, i ^ k) for i in range(lax.axis_size(axis))])  5.97 us
    pallas_call x1, Pallas kernels, local(): pl.pallas_call(functools.partial(far_kernel, rows_all, tiles), out_shape=...  1.01 us
    concatenate x1, other arithmetic, local(): ints = jnp.concatenate([owner_map, cluster_id, item_order]).reshape(1, -1)  0.76 us
    pallas_call x1, Pallas kernels, local(): pl.pallas_call(functools.partial(pick_kernel, order, parts), out_shape=[j...  0.72 us
    pallas_call x1, Pallas kernels, local(): pl.pallas_call(functools.partial(near_kernel, rows_all, owner_map.shape[0...  0.69 us
  transfers between devices with their start and end apart: 8, of which 3 were waited for; matrix products, arithmetic and copies ran while one was open for 0% of the time, Pallas kernels for 2%

profile of v17, /device:TPU:0, one launch (start us, length us, event | category | flops | bytes accessed | tf_op | source)
XLA Modules:
  0.0 34.0 jit_solution(5880146595127820120)
XLA Ops:
  0.6 0.0 copy-start
  0.6 0.8 %pad_add_fusion = s32[512]{0:T(512)S(1)} fusion(s32[128]{0:T(128)} %param.6, s32[128]{0:T(128)} %param.5, s32[256]{0:T(256)} %param.7), kind=kLoop, calls=%fused_computation.8 | loop fusion | flops 1024 | bytes 4096 | tf_op jit(solution)/shard_map/concatenate | solution.py:265
  1.4 0.3 slots.1
  1.7 0.0 copy-done
  1.7 0.4 %pack.1 = (bf16[17,16,128]{2,1,0:T(8,128)(2,1)S(1)}, bf16[17,16,128]{2,1,0:T(8,128)(2,1)S(1)}, bf16[17,16,128]{2,1,0:T(8,128)(2,1)S(1)}, bf16[17,16,128]{2,1,0:T...) custom-call(s32[1,128]{1,0:T(1,128)S(1)} %get-tuple-element.24.slot_, ...), custom_call_target="tpu_custom_call" | custom-call | tf_op jit(solution)/shard_map/pack/pallas_call | solution.py:284
  2.1 4.1 %collective-permute-start = (bf16[17,16,128]{2,1,0:T(8,128)(2,1)S(1)}, bf16[17,16,128]{2,1,0:T(8,128)(2,1)S(1)}, u32[]{:S(2)}, u32[]{:S(2)}) collective-permute-start(bf16[17,16,128]{2,1,0:T(8,128)(2,1)S(1)} %get-tuple-element.26), channel_id=1, source_target_pairs={{0,8},{2,10},{4,12},{6,14},{8,0},{10,2},{12,4},{14,6},{1,9},{3,11}... | collective-permute-start | bytes 208904 | tf_op jit(solution)/shard_map/ppermute | solution.py:230
  6.2 1.6 %collective-permute-start.1 = (bf16[17,16,128]{2,1,0:T(8,128)(2,1)S(1)}, bf16[17,16,128]{2,1,0:T(8,128)(2,1)S(1)}, u32[]{:S(2)}, u32[]{:S(2)}) collective-permute-start(bf16[17,16,128]{2,1,0:T(8,128)(2,1)S(1)} %get-tuple-element.27), channel_id=1, source_target_pairs={{0,4},{2,6},{4,0},{6,2},{8,12},{10,14},{12,8},{14,10},{1,5},{3,7},... | collective-permute-start | bytes 208904 | tf_op jit(solution)/shard_map/ppermute | solution.py:230
  7.8 1.4 %collective-permute-start.2 = (bf16[17,16,128]{2,1,0:T(8,128)(2,1)S(1)}, bf16[17,16,128]{2,1,0:T(8,128)(2,1)S(1)}, u32[]{:S(2)}, u32[]{:S(2)}) collective-permute-start(bf16[17,16,128]{2,1,0:T(8,128)(2,1)S(1)} %get-tuple-element.28), channel_id=1, source_target_pairs={{0,6},{2,4},{4,2},{6,0},{8,14},{10,12},{12,10},{14,8},{1,7},{3,5},... | collective-permute-start | bytes 208904 | tf_op jit(solution)/shard_map/ppermute | solution.py:230
  9.2 0.1 collective-permute-start.3
  9.2 4.8 %collective-permute-start.4 = (bf16[17,16,128]{2,1,0:T(8,128)(2,1)S(1)}, bf16[17,16,128]{2,1,0:T(8,128)(2,1)S(1)}, u32[]{:S(2)}, u32[]{:S(2)}) collective-permute-start(bf16[17,16,128]{2,1,0:T(8,128)(2,1)S(1)} %get-tuple-element.30), channel_id=1, source_target_pairs={{0,14},{2,12},{4,10},{6,8},{8,6},{10,4},{12,2},{14,0},{1,15},{3,13... | collective-permute-start | bytes 208904 | tf_op jit(solution)/shard_map/ppermute | solution.py:230
  14.0 0.0 collective-permute-done
  14.0 0.2 collective-permute-start.5
  14.2 0.0 collective-permute-done.1
  14.3 1.2 %collective-permute-start.6 = (bf16[17,16,128]{2,1,0:T(8,128)(2,1)S(1)}, bf16[17,16,128]{2,1,0:T(8,128)(2,1)S(1)}, u32[]{:S(2)}, u32[]{:S(2)}) collective-permute-start(bf16[17,16,128]{2,1,0:T(8,128)(2,1)S(1)} %get-tuple-element.32), channel_id=1, source_target_pairs={{0,2},{2,0},{4,6},{6,4},{8,10},{10,8},{12,14},{14,12},{1,3},{3,1},... | collective-permute-start | bytes 208904 | tf_op jit(solution)/shard_map/ppermute | solution.py:230
  15.5 0.0 collective-permute-done.2
  15.5 3.5 %collective-permute-done.3 = bf16[17,16,128]{2,1,0:T(8,128)(2,1)S(1)} collective-permute-done((bf16[17,16,128]{2,1,0:T(8,128)(2,1)S(1)}, bf16[17,16,128]{2,1,0:T(8,128)(2,1)S(1)}, u32[]{:S(2)}, u32[]{:S(2)}) %collective-permute-start.3) | collective-permute-done | bytes 69664 | tf_op jit(solution)/shard_map/ppermute | solution.py:230
  19.0 0.0 collective-permute-done.4
  19.0 1.2 %collective-permute-done.5 = bf16[17,16,128]{2,1,0:T(8,128)(2,1)S(1)} collective-permute-done((bf16[17,16,128]{2,1,0:T(8,128)(2,1)S(1)}, bf16[17,16,128]{2,1,0:T(8,128)(2,1)S(1)}, u32[]{:S(2)}, u32[]{:S(2)}) %collective-permute-start.5) | collective-permute-done | bytes 69664 | tf_op jit(solution)/shard_map/ppermute | solution.py:230
  20.3 0.0 collective-permute-done.6
  20.3 0.1 collective-permute-start.7
  20.4 0.7 %near.1 = (bf16[1024,256]{1,0:T(8,128)(2,1)S(1)}, s32[288,128]{1,0:T(8,128)S(1)}, s32[2,256]{1,0:T(2,128)S(1)}, f32[1,256]{1,0:T(1,128)S(1)}, f32[288,1024]{1,0:T(8,128)S(1)}, /*index=5*/f32[288,128]{1,0:T(8,128)S(1)}) custom-call(s32[1]{0:T(128)} %bitcast.me_ref, s32[1,512]{1,0:T(1,128)S(1)} %bitcast.6, ...), custom_call_target="tpu_custom_call" | custom-call | flops 268435456 | bytes 1048576 | tf_op jit(solution)/shard_map/near/pallas_call | solution.py:295
  21.1 1.2 %collective-permute-done.7.other_ref = bf16[136,16,128]{2,1,0:T(8,128)(2,1)S(1)} collective-permute-done((bf16[136,16,128]{2,1,0:T(8,128)(2,1)S(1)}, bf16[136,16,128]{2,1,0:T(8,128)(2,1)S(1)}, u32[]{:S(2)}, u32[]{:S(2)}) %collective-permute-start.7) | collective-permute-done | bytes 557088 | tf_op jit(solution)/shard_map/ppermute | solution.py:230
  22.3 1.0 %far.1 = (f32[8,2,256]{2,1,0:T(2,128)S(1)}, f32[1,32]{1,0:T(1,128)S(1)}) custom-call(bf16[136,16,128]{2,1,0:T(8,128)(2,1)S(1)} %constant_dynamic-update-slice_fusion.query_ref, bf16[136,16,128]{2,1,0:T(8,128)(2,1)S(1)} %collective-permute-done.7.other_ref, bf16[1024,256]{1,0:T(8,128)(2,1)S(1)} %get-tuple-element.34.query_t_ref, ...), custom_call_target="tpu_custom_call" | custom-call | flops 268435456 | bytes 1048576 | tf_op jit(solution)/shard_map/far/pallas_call | solution.py:311
  23.3 9.9 %all_to_all.5.result_ref = f32[8,2,256]{2,1,0:T(2,128)S(1)} all-to-all(f32[8,2,256]{2,1,0:T(2,128)S(1)} %get-tuple-element.40), channel_id=1, replica_groups=mesh['groups'=2,'shard'=8,'sub'=2] {'shard'}, dimensions={0} | all-to-all | bytes 32768 | tf_op jit(solution)/shard_map/all_to_all | solution.py:323
  33.2 0.7 %pick.1 = (f32[1,128]{1,0:T(1,128)}, f32[1,128]{1,0:T(1,128)}, f32[1,32]{1,0:T(1,128)}) custom-call(s32[1]{0:T(128)} %bitcast.me_ref, s32[1,128]{1,0:T(1,128)S(1)} %get-tuple-element.24.slot_ref, f32[8,2,256]{2,1,0:T(2,128)S(1)} %all_to_all.5.result_ref, f32[1,32]{1,0:T(1,128)S(1)} %get-tuple-element.41.norm_ref), custom_call_target="tpu_custom_call" | custom-call | tf_op jit(solution)/shard_map/pick/pallas_call | solution.py:324
  (8 shorter events, 0.1 us)
Async XLA Ops:
  0.6 1.0 %copy-start = (bf16[128,1024]{1,0:T(8,128)(2,1)S(1)}, bf16[128,1024]{1,0:T(8,128)(2,1)}, u32[]{:S(2)}) copy-start(bf16[128,1024]{1,0:T(8,128)(2,1)} %embed_ref.1) | copy-start | bytes 786436
  2.1 11.9 %collective-permute-start = (bf16[17,16,128]{2,1,0:T(8,128)(2,1)S(1)}, bf16[17,16,128]{2,1,0:T(8,128)(2,1)S(1)}, u32[]{:S(2)}, u32[]{:S(2)}) collective-permute-start(bf16[17,16,128]{2,1,0:T(8,128)(2,1)S(1)} %get-tuple-element.26), channel_id=1, source_target_pairs={{0,8},{2,10},{4,12},{6,14},{8,0},{10,2},{12,4},{14,6},{1,9},{3,11}... | collective-permute-start | bytes 208904 | tf_op jit(solution)/shard_map/ppermute | solution.py:230
  6.2 8.0 %collective-permute-start.1 = (bf16[17,16,128]{2,1,0:T(8,128)(2,1)S(1)}, bf16[17,16,128]{2,1,0:T(8,128)(2,1)S(1)}, u32[]{:S(2)}, u32[]{:S(2)}) collective-permute-start(bf16[17,16,128]{2,1,0:T(8,128)(2,1)S(1)} %get-tuple-element.27), channel_id=1, source_target_pairs={{0,4},{2,6},{4,0},{6,2},{8,12},{10,14},{12,8},{14,10},{1,5},{3,7},... | collective-permute-start | bytes 208904 | tf_op jit(solution)/shard_map/ppermute | solution.py:230
  7.8 7.7 %collective-permute-start.2 = (bf16[17,16,128]{2,1,0:T(8,128)(2,1)S(1)}, bf16[17,16,128]{2,1,0:T(8,128)(2,1)S(1)}, u32[]{:S(2)}, u32[]{:S(2)}) collective-permute-start(bf16[17,16,128]{2,1,0:T(8,128)(2,1)S(1)} %get-tuple-element.28), channel_id=1, source_target_pairs={{0,6},{2,4},{4,2},{6,0},{8,14},{10,12},{12,10},{14,8},{1,7},{3,5},... | collective-permute-start | bytes 208904 | tf_op jit(solution)/shard_map/ppermute | solution.py:230
  9.2 9.8 %collective-permute-start.3 = (bf16[17,16,128]{2,1,0:T(8,128)(2,1)S(1)}, bf16[17,16,128]{2,1,0:T(8,128)(2,1)S(1)}, u32[]{:S(2)}, u32[]{:S(2)}) collective-permute-start(bf16[17,16,128]{2,1,0:T(8,128)(2,1)S(1)} %get-tuple-element.29), channel_id=1, source_target_pairs={{0,10},{2,8},{4,14},{6,12},{8,2},{10,0},{12,6},{14,4},{1,11},{3,9}... | collective-permute-start | bytes 208904 | tf_op jit(solution)/shard_map/ppermute | solution.py:230
  9.2 9.8 %collective-permute-start.4 = (bf16[17,16,128]{2,1,0:T(8,128)(2,1)S(1)}, bf16[17,16,128]{2,1,0:T(8,128)(2,1)S(1)}, u32[]{:S(2)}, u32[]{:S(2)}) collective-permute-start(bf16[17,16,128]{2,1,0:T(8,128)(2,1)S(1)} %get-tuple-element.30), channel_id=1, source_target_pairs={{0,14},{2,12},{4,10},{6,8},{8,6},{10,4},{12,2},{14,0},{1,15},{3,13... | collective-permute-start | bytes 208904 | tf_op jit(solution)/shard_map/ppermute | solution.py:230
  14.0 6.2 %collective-permute-start.5 = (bf16[17,16,128]{2,1,0:T(8,128)(2,1)S(1)}, bf16[17,16,128]{2,1,0:T(8,128)(2,1)S(1)}, u32[]{:S(2)}, u32[]{:S(2)}) collective-permute-start(bf16[17,16,128]{2,1,0:T(8,128)(2,1)S(1)} %get-tuple-element.31), channel_id=1, source_target_pairs={{0,12},{2,14},{4,8},{6,10},{8,4},{10,6},{12,0},{14,2},{1,13},{3,15... | collective-permute-start | bytes 208904 | tf_op jit(solution)/shard_map/ppermute | solution.py:230
  14.3 6.0 %collective-permute-start.6 = (bf16[17,16,128]{2,1,0:T(8,128)(2,1)S(1)}, bf16[17,16,128]{2,1,0:T(8,128)(2,1)S(1)}, u32[]{:S(2)}, u32[]{:S(2)}) collective-permute-start(bf16[17,16,128]{2,1,0:T(8,128)(2,1)S(1)} %get-tuple-element.32), channel_id=1, source_target_pairs={{0,2},{2,0},{4,6},{6,4},{8,10},{10,8},{12,14},{14,12},{1,3},{3,1},... | collective-permute-start | bytes 208904 | tf_op jit(solution)/shard_map/ppermute | solution.py:230
  20.3 2.0 %collective-permute-start.7 = (bf16[136,16,128]{2,1,0:T(8,128)(2,1)S(1)}, bf16[136,16,128]{2,1,0:T(8,128)(2,1)S(1)}, u32[]{:S(2)}, u32[]{:S(2)}) collective-permute-start(bf16[136,16,128]{2,1,0:T(8,128)(2,1)S(1)} %constant_dynamic-update-slice_fusion.query_ref), channel_id=1, source_target_pairs={{0,1},{1,0},{2,3},{3,2},{4,5},{5,4},{6,7},{7,6},{8,9},{9,8},{10,11... | collective-permute-start | bytes 1671176 | tf_op jit(solution)/shard_map/ppermute | solution.py:230

commit v18 on v17

--- a/solution.py
+++ b/solution.py
@@ -9,7 +9,7 @@
 
 LANES = 128
 DIGITS = 3
-PARTNERS = (4, 2, 3, 5, 7, 6, 1, 0)
+PARTNERS = (4, 3, 2, 5, 6, 7, 1, 0)
 WHOLE = pl.BlockSpec(memory_space=pltpu.VMEM)
 SCALAR = pl.BlockSpec(memory_space=pltpu.SMEM)
 

time: 34.1 us -> 34.2 us (level)
  no operation moved by 1% of the time
where the time goes in v18:
time: 34.2 us; the launch traced here: 34 us
  starting transfers between devices  13.4 us (39%)
  blocking collectives  9.99 us (29%)
  waiting for transfers between devices  5.89 us (17%)
  Pallas kernels  3.13 us (9%)
  other arithmetic  0.76 us (2%)
  between operations  0.73 us (2%)
    ppermute x8, starting transfers between devices, from_partner(): lax.ppermute(value, axis, [(i, i ^ k) for i in range(lax.axis_size(axis))])  13.4 us
    all_to_all x1, blocking collectives, local(): results = lax.all_to_all(results, 'shard', 0, 0, tiled=True)  9.99 us
    ppermute x8, waiting for transfers between devices, from_partner(): lax.ppermute(value, axis, [(i, i ^ k) for i in range(lax.axis_size(axis))])  5.89 us
    pallas_call x1, Pallas kernels, local(): pl.pallas_call(functools.partial(far_kernel, rows_all, tiles), out_shape=...  1.01 us
    concatenate x1, other arithmetic, local(): ints = jnp.concatenate([owner_map, cluster_id, item_order]).reshape(1, -1)  0.76 us
    pallas_call x1, Pallas kernels, local(): pl.pallas_call(functools.partial(pick_kernel, order, parts), out_shape=[j...  0.72 us
    pallas_call x1, Pallas kernels, local(): pl.pallas_call(functools.partial(near_kernel, rows_all, owner_map.shape[0...  0.7 us
  transfers between devices with their start and end apart: 8, of which 3 were waited for; matrix products, arithmetic and copies ran while one was open for 0% of the time, Pallas kernels for 2%

profile of v18, /device:TPU:0, one launch (start us, length us, event | category | flops | bytes accessed | tf_op | source)
XLA Modules:
  0.0 34.0 jit_solution(8190503907106455353)
XLA Ops:
  0.6 0.0 copy-start
  0.6 0.8 %pad_add_fusion = s32[512]{0:T(512)S(1)} fusion(s32[128]{0:T(128)} %param.6, s32[128]{0:T(128)} %param.5, s32[256]{0:T(256)} %param.7), kind=kLoop, calls=%fused_computation.8 | loop fusion | flops 1024 | bytes 4096 | tf_op jit(solution)/shard_map/concatenate | solution.py:265
  1.4 0.3 slots.1
  1.7 0.0 copy-done
  1.7 0.4 %pack.1 = (bf16[17,16,128]{2,1,0:T(8,128)(2,1)S(1)}, bf16[17,16,128]{2,1,0:T(8,128)(2,1)S(1)}, bf16[17,16,128]{2,1,0:T(8,128)(2,1)S(1)}, bf16[17,16,128]{2,1,0:T...) custom-call(s32[1,128]{1,0:T(1,128)S(1)} %get-tuple-element.24.slot_, ...), custom_call_target="tpu_custom_call" | custom-call | tf_op jit(solution)/shard_map/pack/pallas_call | solution.py:284
  2.1 4.1 %collective-permute-start = (bf16[17,16,128]{2,1,0:T(8,128)(2,1)S(1)}, bf16[17,16,128]{2,1,0:T(8,128)(2,1)S(1)}, u32[]{:S(2)}, u32[]{:S(2)}) collective-permute-start(bf16[17,16,128]{2,1,0:T(8,128)(2,1)S(1)} %get-tuple-element.26), channel_id=1, source_target_pairs={{0,8},{2,10},{4,12},{6,14},{8,0},{10,2},{12,4},{14,6},{1,9},{3,11}... | collective-permute-start | bytes 208904 | tf_op jit(solution)/shard_map/ppermute | solution.py:230
  6.2 2.5 %collective-permute-start.1 = (bf16[17,16,128]{2,1,0:T(8,128)(2,1)S(1)}, bf16[17,16,128]{2,1,0:T(8,128)(2,1)S(1)}, u32[]{:S(2)}, u32[]{:S(2)}) collective-permute-start(bf16[17,16,128]{2,1,0:T(8,128)(2,1)S(1)} %get-tuple-element.27), channel_id=1, source_target_pairs={{0,6},{2,4},{4,2},{6,0},{8,14},{10,12},{12,10},{14,8},{1,7},{3,5},... | collective-permute-start | bytes 208904 | tf_op jit(solution)/shard_map/ppermute | solution.py:230
  8.7 0.4 %collective-permute-start.2 = (bf16[17,16,128]{2,1,0:T(8,128)(2,1)S(1)}, bf16[17,16,128]{2,1,0:T(8,128)(2,1)S(1)}, u32[]{:S(2)}, u32[]{:S(2)}) collective-permute-start(bf16[17,16,128]{2,1,0:T(8,128)(2,1)S(1)} %get-tuple-element.28), channel_id=1, source_target_pairs={{0,4},{2,6},{4,0},{6,2},{8,12},{10,14},{12,8},{14,10},{1,5},{3,7},... | collective-permute-start | bytes 208904 | tf_op jit(solution)/shard_map/ppermute | solution.py:230
  9.2 0.1 collective-permute-start.3
  9.2 3.9 %collective-permute-start.4 = (bf16[17,16,128]{2,1,0:T(8,128)(2,1)S(1)}, bf16[17,16,128]{2,1,0:T(8,128)(2,1)S(1)}, u32[]{:S(2)}, u32[]{:S(2)}) collective-permute-start(bf16[17,16,128]{2,1,0:T(8,128)(2,1)S(1)} %get-tuple-element.30), channel_id=1, source_target_pairs={{0,12},{2,14},{4,8},{6,10},{8,4},{10,6},{12,0},{14,2},{1,13},{3,15... | collective-permute-start | bytes 208904 | tf_op jit(solution)/shard_map/ppermute | solution.py:230
  13.1 0.0 collective-permute-done
  13.1 1.7 %collective-permute-start.5 = (bf16[17,16,128]{2,1,0:T(8,128)(2,1)S(1)}, bf16[17,16,128]{2,1,0:T(8,128)(2,1)S(1)}, u32[]{:S(2)}, u32[]{:S(2)}) collective-permute-start(bf16[17,16,128]{2,1,0:T(8,128)(2,1)S(1)} %get-tuple-element.31), channel_id=1, source_target_pairs={{0,14},{2,12},{4,10},{6,8},{8,6},{10,4},{12,2},{14,0},{1,15},{3,13... | collective-permute-start | bytes 208904 | tf_op jit(solution)/shard_map/ppermute | solution.py:230
  14.8 0.0 collective-permute-done.1
  14.8 0.6 %collective-permute-start.6 = (bf16[17,16,128]{2,1,0:T(8,128)(2,1)S(1)}, bf16[17,16,128]{2,1,0:T(8,128)(2,1)S(1)}, u32[]{:S(2)}, u32[]{:S(2)}) collective-permute-start(bf16[17,16,128]{2,1,0:T(8,128)(2,1)S(1)} %get-tuple-element.32), channel_id=1, source_target_pairs={{0,2},{2,0},{4,6},{6,4},{8,10},{10,8},{12,14},{14,12},{1,3},{3,1},... | collective-permute-start | bytes 208904 | tf_op jit(solution)/shard_map/ppermute | solution.py:230
  15.5 0.0 collective-permute-done.2
  15.5 3.4 %collective-permute-done.3 = bf16[17,16,128]{2,1,0:T(8,128)(2,1)S(1)} collective-permute-done((bf16[17,16,128]{2,1,0:T(8,128)(2,1)S(1)}, bf16[17,16,128]{2,1,0:T(8,128)(2,1)S(1)}, u32[]{:S(2)}, u32[]{:S(2)}) %collective-permute-start.3) | collective-permute-done | bytes 69664 | tf_op jit(solution)/shard_map/ppermute | solution.py:230
  19.0 0.0 collective-permute-done.4
  19.0 1.2 %collective-permute-done.5 = bf16[17,16,128]{2,1,0:T(8,128)(2,1)S(1)} collective-permute-done((bf16[17,16,128]{2,1,0:T(8,128)(2,1)S(1)}, bf16[17,16,128]{2,1,0:T(8,128)(2,1)S(1)}, u32[]{:S(2)}, u32[]{:S(2)}) %collective-permute-start.5) | collective-permute-done | bytes 69664 | tf_op jit(solution)/shard_map/ppermute | solution.py:230
  20.2 0.0 collective-permute-done.6
  20.3 0.1 collective-permute-start.7
  20.4 0.7 %near.1 = (bf16[1024,256]{1,0:T(8,128)(2,1)S(1)}, s32[288,128]{1,0:T(8,128)S(1)}, s32[2,256]{1,0:T(2,128)S(1)}, f32[1,256]{1,0:T(1,128)S(1)}, f32[288,1024]{1,0:T(8,128)S(1)}, /*index=5*/f32[288,128]{1,0:T(8,128)S(1)}) custom-call(s32[1]{0:T(128)} %bitcast.me_ref, s32[1,512]{1,0:T(1,128)S(1)} %bitcast.6, ...), custom_call_target="tpu_custom_call" | custom-call | flops 268435456 | bytes 1048576 | tf_op jit(solution)/shard_map/near/pallas_call | solution.py:295
  21.1 1.2 %collective-permute-done.7.other_ref = bf16[136,16,128]{2,1,0:T(8,128)(2,1)S(1)} collective-permute-done((bf16[136,16,128]{2,1,0:T(8,128)(2,1)S(1)}, bf16[136,16,128]{2,1,0:T(8,128)(2,1)S(1)}, u32[]{:S(2)}, u32[]{:S(2)}) %collective-permute-start.7) | collective-permute-done | bytes 557088 | tf_op jit(solution)/shard_map/ppermute | solution.py:230
  22.3 1.0 %far.1 = (f32[8,2,256]{2,1,0:T(2,128)S(1)}, f32[1,32]{1,0:T(1,128)S(1)}) custom-call(bf16[136,16,128]{2,1,0:T(8,128)(2,1)S(1)} %constant_dynamic-update-slice_fusion.query_ref, bf16[136,16,128]{2,1,0:T(8,128)(2,1)S(1)} %collective-permute-done.7.other_ref, bf16[1024,256]{1,0:T(8,128)(2,1)S(1)} %get-tuple-element.34.query_t_ref, ...), custom_call_target="tpu_custom_call" | custom-call | flops 268435456 | bytes 1048576 | tf_op jit(solution)/shard_map/far/pallas_call | solution.py:311
  23.3 10.0 %all_to_all.5.result_ref = f32[8,2,256]{2,1,0:T(2,128)S(1)} all-to-all(f32[8,2,256]{2,1,0:T(2,128)S(1)} %get-tuple-element.40), channel_id=1, replica_groups=mesh['groups'=2,'shard'=8,'sub'=2] {'shard'}, dimensions={0} | all-to-all | bytes 32768 | tf_op jit(solution)/shard_map/all_to_all | solution.py:323
  33.3 0.7 %pick.1 = (f32[1,128]{1,0:T(1,128)}, f32[1,128]{1,0:T(1,128)}, f32[1,32]{1,0:T(1,128)}) custom-call(s32[1]{0:T(128)} %bitcast.me_ref, s32[1,128]{1,0:T(1,128)S(1)} %get-tuple-element.24.slot_ref, f32[8,2,256]{2,1,0:T(2,128)S(1)} %all_to_all.5.result_ref, f32[1,32]{1,0:T(1,128)S(1)} %get-tuple-element.41.norm_ref), custom_call_target="tpu_custom_call" | custom-call | tf_op jit(solution)/shard_map/pick/pallas_call | solution.py:324
  (8 shorter events, 0.1 us)
Async XLA Ops:
  0.6 1.0 %copy-start = (bf16[128,1024]{1,0:T(8,128)(2,1)S(1)}, bf16[128,1024]{1,0:T(8,128)(2,1)}, u32[]{:S(2)}) copy-start(bf16[128,1024]{1,0:T(8,128)(2,1)} %embed_ref.1) | copy-start | bytes 786436
  2.1 11.0 %collective-permute-start = (bf16[17,16,128]{2,1,0:T(8,128)(2,1)S(1)}, bf16[17,16,128]{2,1,0:T(8,128)(2,1)S(1)}, u32[]{:S(2)}, u32[]{:S(2)}) collective-permute-start(bf16[17,16,128]{2,1,0:T(8,128)(2,1)S(1)} %get-tuple-element.26), channel_id=1, source_target_pairs={{0,8},{2,10},{4,12},{6,14},{8,0},{10,2},{12,4},{14,6},{1,9},{3,11}... | collective-permute-start | bytes 208904 | tf_op jit(solution)/shard_map/ppermute | solution.py:230
  6.2 8.6 %collective-permute-start.1 = (bf16[17,16,128]{2,1,0:T(8,128)(2,1)S(1)}, bf16[17,16,128]{2,1,0:T(8,128)(2,1)S(1)}, u32[]{:S(2)}, u32[]{:S(2)}) collective-permute-start(bf16[17,16,128]{2,1,0:T(8,128)(2,1)S(1)} %get-tuple-element.27), channel_id=1, source_target_pairs={{0,6},{2,4},{4,2},{6,0},{8,14},{10,12},{12,10},{14,8},{1,7},{3,5},... | collective-permute-start | bytes 208904 | tf_op jit(solution)/shard_map/ppermute | solution.py:230
  8.7 6.8 %collective-permute-start.2 = (bf16[17,16,128]{2,1,0:T(8,128)(2,1)S(1)}, bf16[17,16,128]{2,1,0:T(8,128)(2,1)S(1)}, u32[]{:S(2)}, u32[]{:S(2)}) collective-permute-start(bf16[17,16,128]{2,1,0:T(8,128)(2,1)S(1)} %get-tuple-element.28), channel_id=1, source_target_pairs={{0,4},{2,6},{4,0},{6,2},{8,12},{10,14},{12,8},{14,10},{1,5},{3,7},... | collective-permute-start | bytes 208904 | tf_op jit(solution)/shard_map/ppermute | solution.py:230
  9.2 9.8 %collective-permute-start.3 = (bf16[17,16,128]{2,1,0:T(8,128)(2,1)S(1)}, bf16[17,16,128]{2,1,0:T(8,128)(2,1)S(1)}, u32[]{:S(2)}, u32[]{:S(2)}) collective-permute-start(bf16[17,16,128]{2,1,0:T(8,128)(2,1)S(1)} %get-tuple-element.29), channel_id=1, source_target_pairs={{0,10},{2,8},{4,14},{6,12},{8,2},{10,0},{12,6},{14,4},{1,11},{3,9}... | collective-permute-start | bytes 208904 | tf_op jit(solution)/shard_map/ppermute | solution.py:230
  9.2 9.7 %collective-permute-start.4 = (bf16[17,16,128]{2,1,0:T(8,128)(2,1)S(1)}, bf16[17,16,128]{2,1,0:T(8,128)(2,1)S(1)}, u32[]{:S(2)}, u32[]{:S(2)}) collective-permute-start(bf16[17,16,128]{2,1,0:T(8,128)(2,1)S(1)} %get-tuple-element.30), channel_id=1, source_target_pairs={{0,12},{2,14},{4,8},{6,10},{8,4},{10,6},{12,0},{14,2},{1,13},{3,15... | collective-permute-start | bytes 208904 | tf_op jit(solution)/shard_map/ppermute | solution.py:230
  13.1 7.1 %collective-permute-start.5 = (bf16[17,16,128]{2,1,0:T(8,128)(2,1)S(1)}, bf16[17,16,128]{2,1,0:T(8,128)(2,1)S(1)}, u32[]{:S(2)}, u32[]{:S(2)}) collective-permute-start(bf16[17,16,128]{2,1,0:T(8,128)(2,1)S(1)} %get-tuple-element.31), channel_id=1, source_target_pairs={{0,14},{2,12},{4,10},{6,8},{8,6},{10,4},{12,2},{14,0},{1,15},{3,13... | collective-permute-start | bytes 208904 | tf_op jit(solution)/shard_map/ppermute | solution.py:230
  14.8 5.4 %collective-permute-start.6 = (bf16[17,16,128]{2,1,0:T(8,128)(2,1)S(1)}, bf16[17,16,128]{2,1,0:T(8,128)(2,1)S(1)}, u32[]{:S(2)}, u32[]{:S(2)}) collective-permute-start(bf16[17,16,128]{2,1,0:T(8,128)(2,1)S(1)} %get-tuple-element.32), channel_id=1, source_target_pairs={{0,2},{2,0},{4,6},{6,4},{8,10},{10,8},{12,14},{14,12},{1,3},{3,1},... | collective-permute-start | bytes 208904 | tf_op jit(solution)/shard_map/ppermute | solution.py:230
  20.3 2.0 %collective-permute-start.7 = (bf16[136,16,128]{2,1,0:T(8,128)(2,1)S(1)}, bf16[136,16,128]{2,1,0:T(8,128)(2,1)S(1)}, u32[]{:S(2)}, u32[]{:S(2)}) collective-permute-start(bf16[136,16,128]{2,1,0:T(8,128)(2,1)S(1)} %constant_dynamic-update-slice_fusion.query_ref), channel_id=1, source_target_pairs={{0,1},{1,0},{2,3},{3,2},{4,5},{5,4},{6,7},{7,6},{8,9},{9,8},{10,11... | collective-permute-start | bytes 1671176 | tf_op jit(solution)/shard_map/ppermute | solution.py:230

commit v19 on v18

--- a/solution.py
+++ b/solution.py
@@ -9,7 +9,7 @@
 
 LANES = 128
 DIGITS = 3
-PARTNERS = (4, 3, 2, 5, 6, 7, 1, 0)
+PARTNERS = (4, 3, 2, 0, 5, 6, 7, 1)
 WHOLE = pl.BlockSpec(memory_space=pltpu.VMEM)
 SCALAR = pl.BlockSpec(memory_space=pltpu.SMEM)
 
@@ -140,14 +140,15 @@
     return jnp.concatenate([column] * (count // LANES), axis=1)
 
 
-def compare(rows_all, query_t, query_low, query_key, lows, rows, digit):
-    _, key = key_rows(rows_all, digit)
+def compare(rows_all, query_t, query_low, query_key, lows, parts):
+    rows = jnp.concatenate([rows for rows, _ in parts], axis=0)
+    key = jnp.concatenate([key_rows(rows_all, digit)[1] for _, digit in parts], axis=1)
     bound = across(lows, key.shape[1])
     member = bf16((key >= bound) & (key < bound + rows_all))
     sums = matmul(member, rows)
     counts = matmul(member, jnp.ones((rows.shape[0], LANES), jnp.bfloat16))
     scores = matmul(rows, query_t)
-    _, key = key_columns(rows_all, digit)
+    key = jnp.concatenate([key_columns(rows_all, digit)[1] for _, digit in parts], axis=0)
     key = across(key, query_t.shape[1])
     earlier = (key >= query_low) & (key < query_key)
     best = jnp.max(jnp.where(earlier, scores, -3.0), axis=0, keepdims=True)
@@ -155,7 +156,7 @@
 
 
 def near_kernel(
-    rows_all, clusters, clus_dev, tiles, me_ref, ints_ref, query_ref,
+    rows_all, clusters, clus_dev, tiles, me_ref, ints_ref, query_ref, other_ref,
     query_t_ref, lows_ref, key_ref, best_ref, sums_ref, counts_ref,
 ):
     hot = (ints_ref[:, :clusters] == me_ref[0]).astype(jnp.float32)
@@ -170,7 +171,8 @@
     query_low, query_key = key_rows(rows_all, digit)
     query_t = jnp.transpose(query)
     query_t_ref[...] = query_t
-    best, sums, counts = compare(rows_all, query_t, query_low, query_key, lows, query, digit)
+    parts = [(query, digit), unpacked(other_ref, tiles)]
+    best, sums, counts = compare(rows_all, query_t, query_low, query_key, lows, parts)
     lows_ref[...] = lows
     key_ref[...] = jnp.concatenate([query_low, query_key], axis=0)
     best_ref[...] = best
@@ -184,9 +186,8 @@
 ):
     query, _ = unpacked(query_ref, tiles)
     queries, width = query.shape
-    rows, digit = unpacked(other_ref, tiles)
     best, sums, counts = compare(
-        rows_all, query_t_ref[...], key_ref[0:1], key_ref[1:2], lows_ref[...], rows, digit
+        rows_all, query_t_ref[...], key_ref[0:1], key_ref[1:2], lows_ref[...], [unpacked(other_ref, tiles)]
     )
     best = jnp.maximum(best, best_ref[...])
     best = jnp.where(best > -2.0, best, 0.0)
@@ -231,9 +232,9 @@
 
 
 def exchange(packed, order):
-    return jnp.concatenate(
-        [from_partner(block, k, "shard") if k else block for k, block in zip(order, packed)]
-    )
+    got = [from_partner(block, k, "shard") if k else block for k, block in zip(order, packed)]
+    half = len(got) // 2
+    return jnp.concatenate(got[:half]), jnp.concatenate(got[half:])
 
 
 def exchange_all(packed, me):
@@ -247,7 +248,8 @@
     got = lax.all_to_all(parted[partner], "shard", 0, 0, tiled=True)[partner].reshape(2 * half, -1)
     data = got[:, : each * LANES].reshape(2, half, each, LANES).transpose(0, 2, 1, 3)
     digit = jnp.concatenate(jnp.split(got[:, each * LANES :], 2), axis=1)
-    return jnp.concatenate([data.reshape(2 * each, half, LANES), digit[None]])
+    got = jnp.concatenate([data.reshape(2 * each, half, LANES), digit[None]])
+    return jnp.split(got, 2, axis=1)
 
 
 def local(embeddings, cluster_id, item_order, owner_map):
@@ -289,8 +291,9 @@
         compiler_params=params,
         name="pack",
     )(slot, digit, embeddings)
-    query = exchange(packed, order) if direct else exchange_all(packed[0], me[0])
-    other = from_partner(query, 1, "sub")
+    first, second = exchange(packed, order) if direct else exchange_all(packed[0], me[0])
+    other_first, other_second = (from_partner(rows, 1, "sub") for rows in (first, second))
+    query = jnp.concatenate([first, second])
     asked = slots + clus_dev
     near = pl.pallas_call(
         functools.partial(near_kernel, rows_all, owner_map.shape[0], clus_dev, tiles),
@@ -302,12 +305,12 @@
             jax.ShapeDtypeStruct((asked, width), jnp.float32),
             jax.ShapeDtypeStruct((asked, LANES), jnp.float32),
         ],
-        in_specs=[SCALAR] + [WHOLE] * 2,
+        in_specs=[SCALAR] + [WHOLE] * 3,
         out_specs=[WHOLE] * 6,
         compiler_params=params,
         cost_estimate=compare_cost,
         name="near",
-    )(me, ints, query)
+    )(me, ints, query, other_first)
     results, norms = pl.pallas_call(
         functools.partial(far_kernel, rows_all, tiles),
         out_shape=[
@@ -319,7 +322,7 @@
         compiler_params=params,
         cost_estimate=compare_cost,
         name="far",
-    )(query, other, *near)
+    )(query, other_second, *near)
     results = lax.all_to_all(results, "shard", 0, 0, tiled=True)
     best, distance, cohesion = pl.pallas_call(
         functools.partial(pick_kernel, order, parts),

time: 34.2 us -> 33.8 us (0.988)
  waiting for transfers between devices: 5.89 us -> 5.07 us
    ppermute x8 -> x9, waiting for transfers between devices: 5.89 us -> 5.07 us  [from_partner(): lax.ppermute(value, axis, [(i, i ^ k) for i in range(lax.axis_size(axis))])]
    ppermute x8 -> x9, starting transfers between devices: 13.4 us -> 13.4 us  [from_partner(): lax.ppermute(value, axis, [(i, i ^ k) for i in range(lax.axis_size(axis))])]
  transfers between devices with their start and end apart: 8 -> 9, of which waited for: 3 -> 3; matrix products, arithmetic and copies ran while one was open for 0% -> 1% of each run, Pallas kernels for 2% -> 3%
where the time goes in v19:
time: 33.8 us; the launch traced here: 33.6 us
  starting transfers between devices  13.4 us (40%)
  blocking collectives  10 us (30%)
  waiting for transfers between devices  5.07 us (15%)
  Pallas kernels  3.37 us (10%)
  other arithmetic  0.84 us (2%)
  between operations  0.75 us (2%)
    ppermute x9, starting transfers between devices, from_partner(): lax.ppermute(value, axis, [(i, i ^ k) for i in range(lax.axis_size(axis))])  13.4 us
    all_to_all x1, blocking collectives, local(): results = lax.all_to_all(results, 'shard', 0, 0, tiled=True)  10 us
    ppermute x9, waiting for transfers between devices, from_partner(): lax.ppermute(value, axis, [(i, i ^ k) for i in range(lax.axis_size(axis))])  5.07 us
    pallas_call x1, Pallas kernels, local(): pl.pallas_call(functools.partial(near_kernel, rows_all, owner_map.shape[0...  0.98 us
    pallas_call x1, Pallas kernels, local(): pl.pallas_call(functools.partial(far_kernel, rows_all, tiles), out_shape=...  0.97 us
    concatenate x1, other arithmetic, local(): ints = jnp.concatenate([owner_map, cluster_id, item_order]).reshape(1, -1)  0.76 us
    pallas_call x1, Pallas kernels, local(): pl.pallas_call(functools.partial(pick_kernel, order, parts), out_shape=[j...  0.72 us
  transfers between devices with their start and end apart: 9, of which 3 were waited for; matrix products, arithmetic and copies ran while one was open for 1% of the time, Pallas kernels for 3%

profile of v19, /device:TPU:0, one launch (start us, length us, event | category | flops | bytes accessed | tf_op | source)
XLA Modules:
  0.0 33.6 jit_solution(12915452373327699644)
XLA Ops:
  0.6 0.0 copy-start
  0.6 0.8 %pad_add_fusion = s32[512]{0:T(512)S(1)} fusion(s32[128]{0:T(128)} %param.6, s32[128]{0:T(128)} %param.5, s32[256]{0:T(256)} %param.7), kind=kLoop, calls=%fused_computation.10 | loop fusion | flops 1024 | bytes 4096 | tf_op jit(solution)/shard_map/concatenate | solution.py:267
  1.4 0.3 slots.1
  1.7 0.0 copy-done
  1.7 0.4 %pack.1 = (bf16[17,16,128]{2,1,0:T(8,128)(2,1)S(1)}, bf16[17,16,128]{2,1,0:T(8,128)(2,1)S(1)}, bf16[17,16,128]{2,1,0:T(8,128)(2,1)S(1)}, bf16[17,16,128]{2,1,0:T...) custom-call(s32[1,128]{1,0:T(1,128)S(1)} %get-tuple-element.24.slot_, ...), custom_call_target="tpu_custom_call" | custom-call | tf_op jit(solution)/shard_map/pack/pallas_call | solution.py:286
  2.1 4.1 %collective-permute-start = (bf16[17,16,128]{2,1,0:T(8,128)(2,1)S(1)}, bf16[17,16,128]{2,1,0:T(8,128)(2,1)S(1)}, u32[]{:S(2)}, u32[]{:S(2)}) collective-permute-start(bf16[17,16,128]{2,1,0:T(8,128)(2,1)S(1)} %get-tuple-element.26), channel_id=1, source_target_pairs={{0,8},{2,10},{4,12},{6,14},{8,0},{10,2},{12,4},{14,6},{1,9},{3,11}... | collective-permute-start | bytes 208904 | tf_op jit(solution)/shard_map/ppermute | solution.py:231
  6.2 2.5 %collective-permute-start.1 = (bf16[17,16,128]{2,1,0:T(8,128)(2,1)S(1)}, bf16[17,16,128]{2,1,0:T(8,128)(2,1)S(1)}, u32[]{:S(2)}, u32[]{:S(2)}) collective-permute-start(bf16[17,16,128]{2,1,0:T(8,128)(2,1)S(1)} %get-tuple-element.27), channel_id=1, source_target_pairs={{0,6},{2,4},{4,2},{6,0},{8,14},{10,12},{12,10},{14,8},{1,7},{3,5},... | collective-permute-start | bytes 208904 | tf_op jit(solution)/shard_map/ppermute | solution.py:231
  8.7 0.4 %collective-permute-start.2 = (bf16[17,16,128]{2,1,0:T(8,128)(2,1)S(1)}, bf16[17,16,128]{2,1,0:T(8,128)(2,1)S(1)}, u32[]{:S(2)}, u32[]{:S(2)}) collective-permute-start(bf16[17,16,128]{2,1,0:T(8,128)(2,1)S(1)} %get-tuple-element.28), channel_id=1, source_target_pairs={{0,4},{2,6},{4,0},{6,2},{8,12},{10,14},{12,8},{14,10},{1,5},{3,7},... | collective-permute-start | bytes 208904 | tf_op jit(solution)/shard_map/ppermute | solution.py:231
  9.2 0.1 collective-permute-start.3
  9.2 3.9 %collective-permute-start.4 = (bf16[17,16,128]{2,1,0:T(8,128)(2,1)S(1)}, bf16[17,16,128]{2,1,0:T(8,128)(2,1)S(1)}, u32[]{:S(2)}, u32[]{:S(2)}) collective-permute-start(bf16[17,16,128]{2,1,0:T(8,128)(2,1)S(1)} %get-tuple-element.31), channel_id=1, source_target_pairs={{0,12},{2,14},{4,8},{6,10},{8,4},{10,6},{12,0},{14,2},{1,13},{3,15... | collective-permute-start | bytes 208904 | tf_op jit(solution)/shard_map/ppermute | solution.py:231
  13.1 0.0 collective-permute-done
  13.1 1.7 %collective-permute-start.5 = (bf16[17,16,128]{2,1,0:T(8,128)(2,1)S(1)}, bf16[17,16,128]{2,1,0:T(8,128)(2,1)S(1)}, u32[]{:S(2)}, u32[]{:S(2)}) collective-permute-start(bf16[17,16,128]{2,1,0:T(8,128)(2,1)S(1)} %get-tuple-element.32), channel_id=1, source_target_pairs={{0,14},{2,12},{4,10},{6,8},{8,6},{10,4},{12,2},{14,0},{1,15},{3,13... | collective-permute-start | bytes 208904 | tf_op jit(solution)/shard_map/ppermute | solution.py:231
  14.8 0.0 collective-permute-done.1
  14.8 0.6 %collective-permute-start.6 = (bf16[17,16,128]{2,1,0:T(8,128)(2,1)S(1)}, bf16[17,16,128]{2,1,0:T(8,128)(2,1)S(1)}, u32[]{:S(2)}, u32[]{:S(2)}) collective-permute-start(bf16[17,16,128]{2,1,0:T(8,128)(2,1)S(1)} %get-tuple-element.33), channel_id=1, source_target_pairs={{0,2},{2,0},{4,6},{6,4},{8,10},{10,8},{12,14},{14,12},{1,3},{3,1},... | collective-permute-start | bytes 208904 | tf_op jit(solution)/shard_map/ppermute | solution.py:231
  15.4 0.0 collective-permute-done.2
  15.5 0.1 collective-permute-start.8
  15.5 3.4 %collective-permute-done.3 = bf16[17,16,128]{2,1,0:T(8,128)(2,1)S(1)} collective-permute-done((bf16[17,16,128]{2,1,0:T(8,128)(2,1)S(1)}, bf16[17,16,128]{2,1,0:T(8,128)(2,1)S(1)}, u32[]{:S(2)}, u32[]{:S(2)}) %collective-permute-start.3) | collective-permute-done | bytes 69664 | tf_op jit(solution)/shard_map/ppermute | solution.py:231
  19.0 0.0 collective-permute-done.4
  19.0 1.2 %collective-permute-done.5 = bf16[17,16,128]{2,1,0:T(8,128)(2,1)S(1)} collective-permute-done((bf16[17,16,128]{2,1,0:T(8,128)(2,1)S(1)}, bf16[17,16,128]{2,1,0:T(8,128)(2,1)S(1)}, u32[]{:S(2)}, u32[]{:S(2)}) %collective-permute-start.5) | collective-permute-done | bytes 69664 | tf_op jit(solution)/shard_map/ppermute | solution.py:231
  20.2 0.0 collective-permute-done.6
  20.2 0.1 collective-permute-start.7
  20.5 0.0 collective-permute-done.8.other_ref
  20.5 1.0 %near.1 = (bf16[1024,256]{1,0:T(8,128)(2,1)S(1)}, s32[288,128]{1,0:T(8,128)S(1)}, s32[2,256]{1,0:T(2,128)S(1)}, f32[1,256]{1,0:T(1,128)S(1)}, f32[288,1024]{1,0:T(8,128)S(1)}, /*index=5*/f32[288,128]{1,0:T(8,128)S(1)}) custom-call(s32[1]{0:T(128)} %bitcast.me_ref, s32[1,512]{1,0:T(1,128)S(1)} %bitcast.6, ...), custom_call_target="tpu_custom_call" | custom-call | flops 268435456 | bytes 1048576 | tf_op jit(solution)/shard_map/near/pallas_call | solution.py:298
  21.5 0.4 %collective-permute-done.7.other_ref = bf16[68,16,128]{2,1,0:T(8,128)(2,1)S(1)} collective-permute-done((bf16[68,16,128]{2,1,0:T(8,128)(2,1)S(1)}, bf16[68,16,128]{2,1,0:T(8,128)(2,1)S(1)}, u32[]{:S(2)}, u32[]{:S(2)}) %collective-permute-start.7) | collective-permute-done | bytes 278560 | tf_op jit(solution)/shard_map/ppermute | solution.py:231
  21.9 1.0 %far.1 = (f32[8,2,256]{2,1,0:T(2,128)S(1)}, f32[1,32]{1,0:T(1,128)S(1)}) custom-call(bf16[136,16,128]{2,1,0:T(8,128)(2,1)S(1)} %constant_dynamic-update-slice_fusion.query_ref, bf16[68,16,128]{2,1,0:T(8,128)(2,1)S(1)} %collective-permute-done.7.other_ref, bf16[1024,256]{1,0:T(8,128)(2,1)S(1)} %get-tuple-element.34.query_t_ref, ...), custom_call_target="tpu_custom_call" | custom-call | flops 268435456 | bytes 1048576 | tf_op jit(solution)/shard_map/far/pallas_call | solution.py:314
  22.8 10.0 %all_to_all.5.result_ref = f32[8,2,256]{2,1,0:T(2,128)S(1)} all-to-all(f32[8,2,256]{2,1,0:T(2,128)S(1)} %get-tuple-element.40), channel_id=1, replica_groups=mesh['groups'=2,'shard'=8,'sub'=2] {'shard'}, dimensions={0} | all-to-all | bytes 32768 | tf_op jit(solution)/shard_map/all_to_all | solution.py:326
  32.9 0.7 %pick.1 = (f32[1,128]{1,0:T(1,128)}, f32[1,128]{1,0:T(1,128)}, f32[1,32]{1,0:T(1,128)}) custom-call(s32[1]{0:T(128)} %bitcast.me_ref, s32[1,128]{1,0:T(1,128)S(1)} %get-tuple-element.24.slot_ref, f32[8,2,256]{2,1,0:T(2,128)S(1)} %all_to_all.5.result_ref, f32[1,32]{1,0:T(1,128)S(1)} %get-tuple-element.41.norm_ref), custom_call_target="tpu_custom_call" | custom-call | tf_op jit(solution)/shard_map/pick/pallas_call | solution.py:327
  (10 shorter events, 0.2 us)
Async XLA Ops:
  0.6 1.0 %copy-start = (bf16[128,1024]{1,0:T(8,128)(2,1)S(1)}, bf16[128,1024]{1,0:T(8,128)(2,1)}, u32[]{:S(2)}) copy-start(bf16[128,1024]{1,0:T(8,128)(2,1)} %embed_ref.1) | copy-start | bytes 786436
  2.1 11.0 %collective-permute-start = (bf16[17,16,128]{2,1,0:T(8,128)(2,1)S(1)}, bf16[17,16,128]{2,1,0:T(8,128)(2,1)S(1)}, u32[]{:S(2)}, u32[]{:S(2)}) collective-permute-start(bf16[17,16,128]{2,1,0:T(8,128)(2,1)S(1)} %get-tuple-element.26), channel_id=1, source_target_pairs={{0,8},{2,10},{4,12},{6,14},{8,0},{10,2},{12,4},{14,6},{1,9},{3,11}... | collective-permute-start | bytes 208904 | tf_op jit(solution)/shard_map/ppermute | solution.py:231
  6.2 8.6 %collective-permute-start.1 = (bf16[17,16,128]{2,1,0:T(8,128)(2,1)S(1)}, bf16[17,16,128]{2,1,0:T(8,128)(2,1)S(1)}, u32[]{:S(2)}, u32[]{:S(2)}) collective-permute-start(bf16[17,16,128]{2,1,0:T(8,128)(2,1)S(1)} %get-tuple-element.27), channel_id=1, source_target_pairs={{0,6},{2,4},{4,2},{6,0},{8,14},{10,12},{12,10},{14,8},{1,7},{3,5},... | collective-permute-start | bytes 208904 | tf_op jit(solution)/shard_map/ppermute | solution.py:231
  8.7 6.7 %collective-permute-start.2 = (bf16[17,16,128]{2,1,0:T(8,128)(2,1)S(1)}, bf16[17,16,128]{2,1,0:T(8,128)(2,1)S(1)}, u32[]{:S(2)}, u32[]{:S(2)}) collective-permute-start(bf16[17,16,128]{2,1,0:T(8,128)(2,1)S(1)} %get-tuple-element.28), channel_id=1, source_target_pairs={{0,4},{2,6},{4,0},{6,2},{8,12},{10,14},{12,8},{14,10},{1,5},{3,7},... | collective-permute-start | bytes 208904 | tf_op jit(solution)/shard_map/ppermute | solution.py:231
  9.2 9.8 %collective-permute-start.3 = (bf16[17,16,128]{2,1,0:T(8,128)(2,1)S(1)}, bf16[17,16,128]{2,1,0:T(8,128)(2,1)S(1)}, u32[]{:S(2)}, u32[]{:S(2)}) collective-permute-start(bf16[17,16,128]{2,1,0:T(8,128)(2,1)S(1)} %get-tuple-element.30), channel_id=1, source_target_pairs={{0,10},{2,8},{4,14},{6,12},{8,2},{10,0},{12,6},{14,4},{1,11},{3,9}... | collective-permute-start | bytes 208904 | tf_op jit(solution)/shard_map/ppermute | solution.py:231
  9.2 9.7 %collective-permute-start.4 = (bf16[17,16,128]{2,1,0:T(8,128)(2,1)S(1)}, bf16[17,16,128]{2,1,0:T(8,128)(2,1)S(1)}, u32[]{:S(2)}, u32[]{:S(2)}) collective-permute-start(bf16[17,16,128]{2,1,0:T(8,128)(2,1)S(1)} %get-tuple-element.31), channel_id=1, source_target_pairs={{0,12},{2,14},{4,8},{6,10},{8,4},{10,6},{12,0},{14,2},{1,13},{3,15... | collective-permute-start | bytes 208904 | tf_op jit(solution)/shard_map/ppermute | solution.py:231
  13.1 7.1 %collective-permute-start.5 = (bf16[17,16,128]{2,1,0:T(8,128)(2,1)S(1)}, bf16[17,16,128]{2,1,0:T(8,128)(2,1)S(1)}, u32[]{:S(2)}, u32[]{:S(2)}) collective-permute-start(bf16[17,16,128]{2,1,0:T(8,128)(2,1)S(1)} %get-tuple-element.32), channel_id=1, source_target_pairs={{0,14},{2,12},{4,10},{6,8},{8,6},{10,4},{12,2},{14,0},{1,15},{3,13... | collective-permute-start | bytes 208904 | tf_op jit(solution)/shard_map/ppermute | solution.py:231
  14.8 5.4 %collective-permute-start.6 = (bf16[17,16,128]{2,1,0:T(8,128)(2,1)S(1)}, bf16[17,16,128]{2,1,0:T(8,128)(2,1)S(1)}, u32[]{:S(2)}, u32[]{:S(2)}) collective-permute-start(bf16[17,16,128]{2,1,0:T(8,128)(2,1)S(1)} %get-tuple-element.33), channel_id=1, source_target_pairs={{0,2},{2,0},{4,6},{6,4},{8,10},{10,8},{12,14},{14,12},{1,3},{3,1},... | collective-permute-start | bytes 208904 | tf_op jit(solution)/shard_map/ppermute | solution.py:231
  15.5 5.0 %collective-permute-start.8 = (bf16[68,16,128]{2,1,0:T(8,128)(2,1)S(1)}, bf16[68,16,128]{2,1,0:T(8,128)(2,1)S(1)}, u32[]{:S(2)}, u32[]{:S(2)}) collective-permute-start(bf16[68,16,128]{2,1,0:T(8,128)(2,1)S(1)} %pad_maximum_fusion.1), channel_id=1, source_target_pairs={{0,1},{1,0},{2,3},{3,2},{4,5},{5,4},{6,7},{7,6},{8,9},{9,8},{10,11... | collective-permute-start | bytes 835592 | tf_op jit(solution)/shard_map/ppermute | solution.py:231
  20.2 1.6 %collective-permute-start.7 = (bf16[68,16,128]{2,1,0:T(8,128)(2,1)S(1)}, bf16[68,16,128]{2,1,0:T(8,128)(2,1)S(1)}, u32[]{:S(2)}, u32[]{:S(2)}) collective-permute-start(bf16[68,16,128]{2,1,0:T(8,128)(2,1)S(1)} %pad_maximum_fusion), channel_id=1, source_target_pairs={{0,1},{1,0},{2,3},{3,2},{4,5},{5,4},{6,7},{7,6},{8,9},{9,8},{10,11... | collective-permute-start | bytes 835592 | tf_op jit(solution)/shard_map/ppermute | solution.py:231

commit v20 on v19

--- a/solution.py
+++ b/solution.py
@@ -9,7 +9,7 @@
 
 LANES = 128
 DIGITS = 3
-PARTNERS = (4, 3, 2, 0, 5, 6, 7, 1)
+PARTNERS = (4, 3, 5, 0, 2, 6, 7, 1)
 WHOLE = pl.BlockSpec(memory_space=pltpu.VMEM)
 SCALAR = pl.BlockSpec(memory_space=pltpu.SMEM)
 

time: 33.8 us -> 34.1 us (level)
  starting transfers between devices: 13.4 us -> 14.2 us
  waiting for transfers between devices: 5.07 us -> 4.67 us
    ppermute x9, starting transfers between devices: 13.4 us -> 14.2 us  [from_partner(): lax.ppermute(value, axis, [(i, i ^ k) for i in range(lax.axis_size(axis))])]
    ppermute x9, waiting for transfers between devices: 5.07 us -> 4.67 us  [from_partner(): lax.ppermute(value, axis, [(i, i ^ k) for i in range(lax.axis_size(axis))])]
  transfers between devices with their start and end apart: 9 -> 9, of which waited for: 3 -> 4; matrix products, arithmetic and copies ran while one was open for 1% -> 1% of each run, Pallas kernels for 3% -> 3%
where the time goes in v20:
time: 34.1 us; the launch traced here: 33.9 us
  starting transfers between devices  14.2 us (42%)
  blocking collectives  9.93 us (29%)
  waiting for transfers between devices  4.67 us (14%)
  Pallas kernels  3.35 us (10%)
  other arithmetic  0.84 us (2%)
  between operations  0.76 us (2%)
    ppermute x9, starting transfers between devices, from_partner(): lax.ppermute(value, axis, [(i, i ^ k) for i in range(lax.axis_size(axis))])  14.2 us
    all_to_all x1, blocking collectives, local(): results = lax.all_to_all(results, 'shard', 0, 0, tiled=True)  9.93 us
    ppermute x9, waiting for transfers between devices, from_partner(): lax.ppermute(value, axis, [(i, i ^ k) for i in range(lax.axis_size(axis))])  4.67 us
    pallas_call x1, Pallas kernels, local(): pl.pallas_call(functools.partial(near_kernel, rows_all, owner_map.shape[0...  0.97 us
    pallas_call x1, Pallas kernels, local(): pl.pallas_call(functools.partial(far_kernel, rows_all, tiles), out_shape=...  0.96 us
    concatenate x1, other arithmetic, local(): ints = jnp.concatenate([owner_map, cluster_id, item_order]).reshape(1, -1)  0.76 us
    pallas_call x1, Pallas kernels, local(): pl.pallas_call(functools.partial(pick_kernel, order, parts), out_shape=[j...  0.72 us
  transfers between devices with their start and end apart: 9, of which 4 were waited for; matrix products, arithmetic and copies ran while one was open for 1% of the time, Pallas kernels for 3%

profile of v20, /device:TPU:0, one launch (start us, length us, event | category | flops | bytes accessed | tf_op | source)
XLA Modules:
  0.0 33.9 jit_solution(762174729214773701)
XLA Ops:
  0.6 0.0 copy-start
  0.6 0.8 %pad_add_fusion = s32[512]{0:T(512)S(1)} fusion(s32[128]{0:T(128)} %param.6, s32[128]{0:T(128)} %param.5, s32[256]{0:T(256)} %param.7), kind=kLoop, calls=%fused_computation.10 | loop fusion | flops 1024 | bytes 4096 | tf_op jit(solution)/shard_map/concatenate | solution.py:267
  1.4 0.3 slots.1
  1.7 0.0 copy-done
  1.7 0.4 %pack.1 = (bf16[17,16,128]{2,1,0:T(8,128)(2,1)S(1)}, bf16[17,16,128]{2,1,0:T(8,128)(2,1)S(1)}, bf16[17,16,128]{2,1,0:T(8,128)(2,1)S(1)}, bf16[17,16,128]{2,1,0:T...) custom-call(s32[1,128]{1,0:T(1,128)S(1)} %get-tuple-element.24.slot_, ...), custom_call_target="tpu_custom_call" | custom-call | tf_op jit(solution)/shard_map/pack/pallas_call | solution.py:286
  2.1 4.1 %collective-permute-start = (bf16[17,16,128]{2,1,0:T(8,128)(2,1)S(1)}, bf16[17,16,128]{2,1,0:T(8,128)(2,1)S(1)}, u32[]{:S(2)}, u32[]{:S(2)}) collective-permute-start(bf16[17,16,128]{2,1,0:T(8,128)(2,1)S(1)} %get-tuple-element.26), channel_id=1, source_target_pairs={{0,8},{2,10},{4,12},{6,14},{8,0},{10,2},{12,4},{14,6},{1,9},{3,11}... | collective-permute-start | bytes 208904 | tf_op jit(solution)/shard_map/ppermute | solution.py:231
  6.2 2.5 %collective-permute-start.1 = (bf16[17,16,128]{2,1,0:T(8,128)(2,1)S(1)}, bf16[17,16,128]{2,1,0:T(8,128)(2,1)S(1)}, u32[]{:S(2)}, u32[]{:S(2)}) collective-permute-start(bf16[17,16,128]{2,1,0:T(8,128)(2,1)S(1)} %get-tuple-element.27), channel_id=1, source_target_pairs={{0,6},{2,4},{4,2},{6,0},{8,14},{10,12},{12,10},{14,8},{1,7},{3,5},... | collective-permute-start | bytes 208904 | tf_op jit(solution)/shard_map/ppermute | solution.py:231
  8.7 0.3 collective-permute-start.2
  9.1 0.2 collective-permute-start.3
  9.2 3.9 %collective-permute-start.4 = (bf16[17,16,128]{2,1,0:T(8,128)(2,1)S(1)}, bf16[17,16,128]{2,1,0:T(8,128)(2,1)S(1)}, u32[]{:S(2)}, u32[]{:S(2)}) collective-permute-start(bf16[17,16,128]{2,1,0:T(8,128)(2,1)S(1)} %get-tuple-element.31), channel_id=1, source_target_pairs={{0,12},{2,14},{4,8},{6,10},{8,4},{10,6},{12,0},{14,2},{1,13},{3,15... | collective-permute-start | bytes 208904 | tf_op jit(solution)/shard_map/ppermute | solution.py:231
  13.1 0.0 collective-permute-done
  13.1 2.4 %collective-permute-start.5 = (bf16[17,16,128]{2,1,0:T(8,128)(2,1)S(1)}, bf16[17,16,128]{2,1,0:T(8,128)(2,1)S(1)}, u32[]{:S(2)}, u32[]{:S(2)}) collective-permute-start(bf16[17,16,128]{2,1,0:T(8,128)(2,1)S(1)} %get-tuple-element.32), channel_id=1, source_target_pairs={{0,14},{2,12},{4,10},{6,8},{8,6},{10,4},{12,2},{14,0},{1,15},{3,13... | collective-permute-start | bytes 208904 | tf_op jit(solution)/shard_map/ppermute | solution.py:231
  15.5 0.0 collective-permute-done.1
  15.5 0.7 %collective-permute-start.6 = (bf16[17,16,128]{2,1,0:T(8,128)(2,1)S(1)}, bf16[17,16,128]{2,1,0:T(8,128)(2,1)S(1)}, u32[]{:S(2)}, u32[]{:S(2)}) collective-permute-start(bf16[17,16,128]{2,1,0:T(8,128)(2,1)S(1)} %get-tuple-element.33), channel_id=1, source_target_pairs={{0,2},{2,0},{4,6},{6,4},{8,10},{10,8},{12,14},{14,12},{1,3},{3,1},... | collective-permute-start | bytes 208904 | tf_op jit(solution)/shard_map/ppermute | solution.py:231
  16.2 2.4 %collective-permute-done.2 = bf16[17,16,128]{2,1,0:T(8,128)(2,1)S(1)} collective-permute-done((bf16[17,16,128]{2,1,0:T(8,128)(2,1)S(1)}, bf16[17,16,128]{2,1,0:T(8,128)(2,1)S(1)}, u32[]{:S(2)}, u32[]{:S(2)}) %collective-permute-start.2) | collective-permute-done | bytes 69664 | tf_op jit(solution)/shard_map/ppermute | solution.py:231
  18.7 0.1 collective-permute-start.8
  18.7 0.0 collective-permute-done.3
  18.8 0.0 collective-permute-done.4
  18.8 1.5 %collective-permute-done.5 = bf16[17,16,128]{2,1,0:T(8,128)(2,1)S(1)} collective-permute-done((bf16[17,16,128]{2,1,0:T(8,128)(2,1)S(1)}, bf16[17,16,128]{2,1,0:T(8,128)(2,1)S(1)}, u32[]{:S(2)}, u32[]{:S(2)}) %collective-permute-start.5) | collective-permute-done | bytes 69664 | tf_op jit(solution)/shard_map/ppermute | solution.py:231
  20.3 0.3 collective-permute-done.6
  20.6 0.1 collective-permute-start.7
  20.9 0.0 collective-permute-done.8.other_ref
  20.9 1.0 %near.1 = (bf16[1024,256]{1,0:T(8,128)(2,1)S(1)}, s32[288,128]{1,0:T(8,128)S(1)}, s32[2,256]{1,0:T(2,128)S(1)}, f32[1,256]{1,0:T(1,128)S(1)}, f32[288,1024]{1,0:T(8,128)S(1)}, /*index=5*/f32[288,128]{1,0:T(8,128)S(1)}) custom-call(s32[1]{0:T(128)} %bitcast.me_ref, s32[1,512]{1,0:T(1,128)S(1)} %bitcast.6, ...), custom_call_target="tpu_custom_call" | custom-call | flops 268435456 | bytes 1048576 | tf_op jit(solution)/shard_map/near/pallas_call | solution.py:298
  21.8 0.4 %collective-permute-done.7.other_ref = bf16[68,16,128]{2,1,0:T(8,128)(2,1)S(1)} collective-permute-done((bf16[68,16,128]{2,1,0:T(8,128)(2,1)S(1)}, bf16[68,16,128]{2,1,0:T(8,128)(2,1)S(1)}, u32[]{:S(2)}, u32[]{:S(2)}) %collective-permute-start.7) | collective-permute-done | bytes 278560 | tf_op jit(solution)/shard_map/ppermute | solution.py:231
  22.3 1.0 %far.1 = (f32[8,2,256]{2,1,0:T(2,128)S(1)}, f32[1,32]{1,0:T(1,128)S(1)}) custom-call(bf16[136,16,128]{2,1,0:T(8,128)(2,1)S(1)} %constant_dynamic-update-slice_fusion.query_ref, bf16[68,16,128]{2,1,0:T(8,128)(2,1)S(1)} %collective-permute-done.7.other_ref, bf16[1024,256]{1,0:T(8,128)(2,1)S(1)} %get-tuple-element.34.query_t_ref, ...), custom_call_target="tpu_custom_call" | custom-call | flops 268435456 | bytes 1048576 | tf_op jit(solution)/shard_map/far/pallas_call | solution.py:314
  23.2 9.9 %all_to_all.5.result_ref = f32[8,2,256]{2,1,0:T(2,128)S(1)} all-to-all(f32[8,2,256]{2,1,0:T(2,128)S(1)} %get-tuple-element.40), channel_id=1, replica_groups=mesh['groups'=2,'shard'=8,'sub'=2] {'shard'}, dimensions={0} | all-to-all | bytes 32768 | tf_op jit(solution)/shard_map/all_to_all | solution.py:326
  33.2 0.7 %pick.1 = (f32[1,128]{1,0:T(1,128)}, f32[1,128]{1,0:T(1,128)}, f32[1,32]{1,0:T(1,128)}) custom-call(s32[1]{0:T(128)} %bitcast.me_ref, s32[1,128]{1,0:T(1,128)S(1)} %get-tuple-element.24.slot_ref, f32[8,2,256]{2,1,0:T(2,128)S(1)} %all_to_all.5.result_ref, f32[1,32]{1,0:T(1,128)S(1)} %get-tuple-element.41.norm_ref), custom_call_target="tpu_custom_call" | custom-call | tf_op jit(solution)/shard_map/pick/pallas_call | solution.py:327
  (10 shorter events, 0.2 us)
Async XLA Ops:
  0.6 1.0 %copy-start = (bf16[128,1024]{1,0:T(8,128)(2,1)S(1)}, bf16[128,1024]{1,0:T(8,128)(2,1)}, u32[]{:S(2)}) copy-start(bf16[128,1024]{1,0:T(8,128)(2,1)} %embed_ref.1) | copy-start | bytes 786436
  2.1 11.0 %collective-permute-start = (bf16[17,16,128]{2,1,0:T(8,128)(2,1)S(1)}, bf16[17,16,128]{2,1,0:T(8,128)(2,1)S(1)}, u32[]{:S(2)}, u32[]{:S(2)}) collective-permute-start(bf16[17,16,128]{2,1,0:T(8,128)(2,1)S(1)} %get-tuple-element.26), channel_id=1, source_target_pairs={{0,8},{2,10},{4,12},{6,14},{8,0},{10,2},{12,4},{14,6},{1,9},{3,11}... | collective-permute-start | bytes 208904 | tf_op jit(solution)/shard_map/ppermute | solution.py:231
  6.2 9.3 %collective-permute-start.1 = (bf16[17,16,128]{2,1,0:T(8,128)(2,1)S(1)}, bf16[17,16,128]{2,1,0:T(8,128)(2,1)S(1)}, u32[]{:S(2)}, u32[]{:S(2)}) collective-permute-start(bf16[17,16,128]{2,1,0:T(8,128)(2,1)S(1)} %get-tuple-element.27), channel_id=1, source_target_pairs={{0,6},{2,4},{4,2},{6,0},{8,14},{10,12},{12,10},{14,8},{1,7},{3,5},... | collective-permute-start | bytes 208904 | tf_op jit(solution)/shard_map/ppermute | solution.py:231
  8.7 9.9 %collective-permute-start.2 = (bf16[17,16,128]{2,1,0:T(8,128)(2,1)S(1)}, bf16[17,16,128]{2,1,0:T(8,128)(2,1)S(1)}, u32[]{:S(2)}, u32[]{:S(2)}) collective-permute-start(bf16[17,16,128]{2,1,0:T(8,128)(2,1)S(1)} %get-tuple-element.28), channel_id=1, source_target_pairs={{0,10},{2,8},{4,14},{6,12},{8,2},{10,0},{12,6},{14,4},{1,11},{3,9}... | collective-permute-start | bytes 208904 | tf_op jit(solution)/shard_map/ppermute | solution.py:231
  9.1 9.7 %collective-permute-start.3 = (bf16[17,16,128]{2,1,0:T(8,128)(2,1)S(1)}, bf16[17,16,128]{2,1,0:T(8,128)(2,1)S(1)}, u32[]{:S(2)}, u32[]{:S(2)}) collective-permute-start(bf16[17,16,128]{2,1,0:T(8,128)(2,1)S(1)} %get-tuple-element.30), channel_id=1, source_target_pairs={{0,4},{2,6},{4,0},{6,2},{8,12},{10,14},{12,8},{14,10},{1,5},{3,7},... | collective-permute-start | bytes 208904 | tf_op jit(solution)/shard_map/ppermute | solution.py:231
  9.2 9.5 %collective-permute-start.4 = (bf16[17,16,128]{2,1,0:T(8,128)(2,1)S(1)}, bf16[17,16,128]{2,1,0:T(8,128)(2,1)S(1)}, u32[]{:S(2)}, u32[]{:S(2)}) collective-permute-start(bf16[17,16,128]{2,1,0:T(8,128)(2,1)S(1)} %get-tuple-element.31), channel_id=1, source_target_pairs={{0,12},{2,14},{4,8},{6,10},{8,4},{10,6},{12,0},{14,2},{1,13},{3,15... | collective-permute-start | bytes 208904 | tf_op jit(solution)/shard_map/ppermute | solution.py:231
  13.1 7.2 %collective-permute-start.5 = (bf16[17,16,128]{2,1,0:T(8,128)(2,1)S(1)}, bf16[17,16,128]{2,1,0:T(8,128)(2,1)S(1)}, u32[]{:S(2)}, u32[]{:S(2)}) collective-permute-start(bf16[17,16,128]{2,1,0:T(8,128)(2,1)S(1)} %get-tuple-element.32), channel_id=1, source_target_pairs={{0,14},{2,12},{4,10},{6,8},{8,6},{10,4},{12,2},{14,0},{1,15},{3,13... | collective-permute-start | bytes 208904 | tf_op jit(solution)/shard_map/ppermute | solution.py:231
  15.5 5.1 %collective-permute-start.6 = (bf16[17,16,128]{2,1,0:T(8,128)(2,1)S(1)}, bf16[17,16,128]{2,1,0:T(8,128)(2,1)S(1)}, u32[]{:S(2)}, u32[]{:S(2)}) collective-permute-start(bf16[17,16,128]{2,1,0:T(8,128)(2,1)S(1)} %get-tuple-element.33), channel_id=1, source_target_pairs={{0,2},{2,0},{4,6},{6,4},{8,10},{10,8},{12,14},{14,12},{1,3},{3,1},... | collective-permute-start | bytes 208904 | tf_op jit(solution)/shard_map/ppermute | solution.py:231
  18.7 2.2 %collective-permute-start.8 = (bf16[68,16,128]{2,1,0:T(8,128)(2,1)S(1)}, bf16[68,16,128]{2,1,0:T(8,128)(2,1)S(1)}, u32[]{:S(2)}, u32[]{:S(2)}) collective-permute-start(bf16[68,16,128]{2,1,0:T(8,128)(2,1)S(1)} %pad_maximum_fusion.1), channel_id=1, source_target_pairs={{0,1},{1,0},{2,3},{3,2},{4,5},{5,4},{6,7},{7,6},{8,9},{9,8},{10,11... | collective-permute-start | bytes 835592 | tf_op jit(solution)/shard_map/ppermute | solution.py:231
  20.6 1.6 %collective-permute-start.7 = (bf16[68,16,128]{2,1,0:T(8,128)(2,1)S(1)}, bf16[68,16,128]{2,1,0:T(8,128)(2,1)S(1)}, u32[]{:S(2)}, u32[]{:S(2)}) collective-permute-start(bf16[68,16,128]{2,1,0:T(8,128)(2,1)S(1)} %pad_maximum_fusion), channel_id=1, source_target_pairs={{0,1},{1,0},{2,3},{3,2},{4,5},{5,4},{6,7},{7,6},{8,9},{9,8},{10,11... | collective-permute-start | bytes 835592 | tf_op jit(solution)/shard_map/ppermute | solution.py:231

commit v21 on v20

--- a/solution.py
+++ b/solution.py
@@ -9,7 +9,7 @@
 
 LANES = 128
 DIGITS = 3
-PARTNERS = (4, 3, 5, 0, 2, 6, 7, 1)
+PARTNERS = (3, 4, 2, 0, 5, 6, 7, 1)
 WHOLE = pl.BlockSpec(memory_space=pltpu.VMEM)
 SCALAR = pl.BlockSpec(memory_space=pltpu.SMEM)
 

time: 34.1 us -> 35.1 us (1.029)
  blocking collectives: 9.93 us -> 11.1 us
    all_to_all x1, blocking collectives: 9.93 us -> 11.1 us  [local(): results = lax.all_to_all(results, 'shard', 0, 0, tiled=True)]
where the time goes in v21:
time: 35.1 us; the launch traced here: 34.9 us
  starting transfers between devices  13.9 us (40%)
  blocking collectives  11.1 us (32%)
  waiting for transfers between devices  4.86 us (14%)
  Pallas kernels  3.35 us (10%)
  other arithmetic  0.84 us (2%)
  between operations  0.75 us (2%)
    ppermute x9, starting transfers between devices, from_partner(): lax.ppermute(value, axis, [(i, i ^ k) for i in range(lax.axis_size(axis))])  13.9 us
    all_to_all x1, blocking collectives, local(): results = lax.all_to_all(results, 'shard', 0, 0, tiled=True)  11.1 us
    ppermute x9, waiting for transfers between devices, from_partner(): lax.ppermute(value, axis, [(i, i ^ k) for i in range(lax.axis_size(axis))])  4.86 us
    pallas_call x1, Pallas kernels, local(): pl.pallas_call(functools.partial(near_kernel, rows_all, owner_map.shape[0...  0.97 us
    pallas_call x1, Pallas kernels, local(): pl.pallas_call(functools.partial(far_kernel, rows_all, tiles), out_shape=...  0.97 us
    concatenate x1, other arithmetic, local(): ints = jnp.concatenate([owner_map, cluster_id, item_order]).reshape(1, -1)  0.76 us
    pallas_call x1, Pallas kernels, local(): pl.pallas_call(functools.partial(pick_kernel, order, parts), out_shape=[j...  0.72 us
  transfers between devices with their start and end apart: 9, of which 4 were waited for; matrix products, arithmetic and copies ran while one was open for 1% of the time, Pallas kernels for 3%

profile of v21, /device:TPU:0, one launch (start us, length us, event | category | flops | bytes accessed | tf_op | source)
XLA Modules:
  0.0 34.9 jit_solution(800839828254975255)
XLA Ops:
  0.6 0.0 copy-start
  0.6 0.8 %pad_add_fusion = s32[512]{0:T(512)S(1)} fusion(s32[128]{0:T(128)} %param.6, s32[128]{0:T(128)} %param.5, s32[256]{0:T(256)} %param.7), kind=kLoop, calls=%fused_computation.10 | loop fusion | flops 1024 | bytes 4096 | tf_op jit(solution)/shard_map/concatenate | solution.py:267
  1.4 0.3 slots.1
  1.7 0.0 copy-done
  1.7 0.4 %pack.1 = (bf16[17,16,128]{2,1,0:T(8,128)(2,1)S(1)}, bf16[17,16,128]{2,1,0:T(8,128)(2,1)S(1)}, bf16[17,16,128]{2,1,0:T(8,128)(2,1)S(1)}, bf16[17,16,128]{2,1,0:T...) custom-call(s32[1,128]{1,0:T(1,128)S(1)} %get-tuple-element.24.slot_, ...), custom_call_target="tpu_custom_call" | custom-call | tf_op jit(solution)/shard_map/pack/pallas_call | solution.py:286
  2.1 4.0 %collective-permute-start = (bf16[17,16,128]{2,1,0:T(8,128)(2,1)S(1)}, bf16[17,16,128]{2,1,0:T(8,128)(2,1)S(1)}, u32[]{:S(2)}, u32[]{:S(2)}) collective-permute-start(bf16[17,16,128]{2,1,0:T(8,128)(2,1)S(1)} %get-tuple-element.26), channel_id=1, source_target_pairs={{0,6},{2,4},{4,2},{6,0},{8,14},{10,12},{12,10},{14,8},{1,7},{3,5},... | collective-permute-start | bytes 208904 | tf_op jit(solution)/shard_map/ppermute | solution.py:231
  6.1 2.6 %collective-permute-start.1 = (bf16[17,16,128]{2,1,0:T(8,128)(2,1)S(1)}, bf16[17,16,128]{2,1,0:T(8,128)(2,1)S(1)}, u32[]{:S(2)}, u32[]{:S(2)}) collective-permute-start(bf16[17,16,128]{2,1,0:T(8,128)(2,1)S(1)} %get-tuple-element.27), channel_id=1, source_target_pairs={{0,8},{2,10},{4,12},{6,14},{8,0},{10,2},{12,4},{14,6},{1,9},{3,11}... | collective-permute-start | bytes 208904 | tf_op jit(solution)/shard_map/ppermute | solution.py:231
  8.7 0.4 %collective-permute-start.2 = (bf16[17,16,128]{2,1,0:T(8,128)(2,1)S(1)}, bf16[17,16,128]{2,1,0:T(8,128)(2,1)S(1)}, u32[]{:S(2)}, u32[]{:S(2)}) collective-permute-start(bf16[17,16,128]{2,1,0:T(8,128)(2,1)S(1)} %get-tuple-element.28), channel_id=1, source_target_pairs={{0,4},{2,6},{4,0},{6,2},{8,12},{10,14},{12,8},{14,10},{1,5},{3,7},... | collective-permute-start | bytes 208904 | tf_op jit(solution)/shard_map/ppermute | solution.py:231
  9.2 0.0 collective-permute-start.3
  9.2 3.9 %collective-permute-start.4 = (bf16[17,16,128]{2,1,0:T(8,128)(2,1)S(1)}, bf16[17,16,128]{2,1,0:T(8,128)(2,1)S(1)}, u32[]{:S(2)}, u32[]{:S(2)}) collective-permute-start(bf16[17,16,128]{2,1,0:T(8,128)(2,1)S(1)} %get-tuple-element.31), channel_id=1, source_target_pairs={{0,12},{2,14},{4,8},{6,10},{8,4},{10,6},{12,0},{14,2},{1,13},{3,15... | collective-permute-start | bytes 208904 | tf_op jit(solution)/shard_map/ppermute | solution.py:231
  13.1 0.0 collective-permute-done
  13.1 2.2 %collective-permute-start.5 = (bf16[17,16,128]{2,1,0:T(8,128)(2,1)S(1)}, bf16[17,16,128]{2,1,0:T(8,128)(2,1)S(1)}, u32[]{:S(2)}, u32[]{:S(2)}) collective-permute-start(bf16[17,16,128]{2,1,0:T(8,128)(2,1)S(1)} %get-tuple-element.32), channel_id=1, source_target_pairs={{0,14},{2,12},{4,10},{6,8},{8,6},{10,4},{12,2},{14,0},{1,15},{3,13... | collective-permute-start | bytes 208904 | tf_op jit(solution)/shard_map/ppermute | solution.py:231
  15.3 0.0 collective-permute-done.1
  15.3 0.5 %collective-permute-start.6 = (bf16[17,16,128]{2,1,0:T(8,128)(2,1)S(1)}, bf16[17,16,128]{2,1,0:T(8,128)(2,1)S(1)}, u32[]{:S(2)}, u32[]{:S(2)}) collective-permute-start(bf16[17,16,128]{2,1,0:T(8,128)(2,1)S(1)} %get-tuple-element.33), channel_id=1, source_target_pairs={{0,2},{2,0},{4,6},{6,4},{8,10},{10,8},{12,14},{14,12},{1,3},{3,1},... | collective-permute-start | bytes 208904 | tf_op jit(solution)/shard_map/ppermute | solution.py:231
  15.9 0.0 collective-permute-done.2
  15.9 0.1 collective-permute-start.8
  16.0 3.0 %collective-permute-done.3 = bf16[17,16,128]{2,1,0:T(8,128)(2,1)S(1)} collective-permute-done((bf16[17,16,128]{2,1,0:T(8,128)(2,1)S(1)}, bf16[17,16,128]{2,1,0:T(8,128)(2,1)S(1)}, u32[]{:S(2)}, u32[]{:S(2)}) %collective-permute-start.3) | collective-permute-done | bytes 69664 | tf_op jit(solution)/shard_map/ppermute | solution.py:231
  19.0 0.0 collective-permute-done.4
  19.0 1.3 %collective-permute-done.5 = bf16[17,16,128]{2,1,0:T(8,128)(2,1)S(1)} collective-permute-done((bf16[17,16,128]{2,1,0:T(8,128)(2,1)S(1)}, bf16[17,16,128]{2,1,0:T(8,128)(2,1)S(1)}, u32[]{:S(2)}, u32[]{:S(2)}) %collective-permute-start.5) | collective-permute-done | bytes 69664 | tf_op jit(solution)/shard_map/ppermute | solution.py:231
  20.3 0.2 collective-permute-done.6
  20.5 0.1 collective-permute-start.7
  20.7 0.0 collective-permute-done.8.other_ref
  20.7 1.0 %near.1 = (bf16[1024,256]{1,0:T(8,128)(2,1)S(1)}, s32[288,128]{1,0:T(8,128)S(1)}, s32[2,256]{1,0:T(2,128)S(1)}, f32[1,256]{1,0:T(1,128)S(1)}, f32[288,1024]{1,0:T(8,128)S(1)}, /*index=5*/f32[288,128]{1,0:T(8,128)S(1)}) custom-call(s32[1]{0:T(128)} %bitcast.me_ref, s32[1,512]{1,0:T(1,128)S(1)} %bitcast.6, ...), custom_call_target="tpu_custom_call" | custom-call | flops 268435456 | bytes 1048576 | tf_op jit(solution)/shard_map/near/pallas_call | solution.py:298
  21.7 0.4 %collective-permute-done.7.other_ref = bf16[68,16,128]{2,1,0:T(8,128)(2,1)S(1)} collective-permute-done((bf16[68,16,128]{2,1,0:T(8,128)(2,1)S(1)}, bf16[68,16,128]{2,1,0:T(8,128)(2,1)S(1)}, u32[]{:S(2)}, u32[]{:S(2)}) %collective-permute-start.7) | collective-permute-done | bytes 278560 | tf_op jit(solution)/shard_map/ppermute | solution.py:231
  22.1 1.0 %far.1 = (f32[8,2,256]{2,1,0:T(2,128)S(1)}, f32[1,32]{1,0:T(1,128)S(1)}) custom-call(bf16[136,16,128]{2,1,0:T(8,128)(2,1)S(1)} %constant_dynamic-update-slice_fusion.query_ref, bf16[68,16,128]{2,1,0:T(8,128)(2,1)S(1)} %collective-permute-done.7.other_ref, bf16[1024,256]{1,0:T(8,128)(2,1)S(1)} %get-tuple-element.34.query_t_ref, ...), custom_call_target="tpu_custom_call" | custom-call | flops 268435456 | bytes 1048576 | tf_op jit(solution)/shard_map/far/pallas_call | solution.py:314
  23.1 11.1 %all_to_all.5.result_ref = f32[8,2,256]{2,1,0:T(2,128)S(1)} all-to-all(f32[8,2,256]{2,1,0:T(2,128)S(1)} %get-tuple-element.40), channel_id=1, replica_groups=mesh['groups'=2,'shard'=8,'sub'=2] {'shard'}, dimensions={0} | all-to-all | bytes 32768 | tf_op jit(solution)/shard_map/all_to_all | solution.py:326
  34.2 0.7 %pick.1 = (f32[1,128]{1,0:T(1,128)}, f32[1,128]{1,0:T(1,128)}, f32[1,32]{1,0:T(1,128)}) custom-call(s32[1]{0:T(128)} %bitcast.me_ref, s32[1,128]{1,0:T(1,128)S(1)} %get-tuple-element.24.slot_ref, f32[8,2,256]{2,1,0:T(2,128)S(1)} %all_to_all.5.result_ref, f32[1,32]{1,0:T(1,128)S(1)} %get-tuple-element.41.norm_ref), custom_call_target="tpu_custom_call" | custom-call | tf_op jit(solution)/shard_map/pick/pallas_call | solution.py:327
  (10 shorter events, 0.2 us)
Async XLA Ops:
  0.6 1.0 %copy-start = (bf16[128,1024]{1,0:T(8,128)(2,1)S(1)}, bf16[128,1024]{1,0:T(8,128)(2,1)}, u32[]{:S(2)}) copy-start(bf16[128,1024]{1,0:T(8,128)(2,1)} %embed_ref.1) | copy-start | bytes 786436
  2.1 11.0 %collective-permute-start = (bf16[17,16,128]{2,1,0:T(8,128)(2,1)S(1)}, bf16[17,16,128]{2,1,0:T(8,128)(2,1)S(1)}, u32[]{:S(2)}, u32[]{:S(2)}) collective-permute-start(bf16[17,16,128]{2,1,0:T(8,128)(2,1)S(1)} %get-tuple-element.26), channel_id=1, source_target_pairs={{0,6},{2,4},{4,2},{6,0},{8,14},{10,12},{12,10},{14,8},{1,7},{3,5},... | collective-permute-start | bytes 208904 | tf_op jit(solution)/shard_map/ppermute | solution.py:231
  6.1 9.2 %collective-permute-start.1 = (bf16[17,16,128]{2,1,0:T(8,128)(2,1)S(1)}, bf16[17,16,128]{2,1,0:T(8,128)(2,1)S(1)}, u32[]{:S(2)}, u32[]{:S(2)}) collective-permute-start(bf16[17,16,128]{2,1,0:T(8,128)(2,1)S(1)} %get-tuple-element.27), channel_id=1, source_target_pairs={{0,8},{2,10},{4,12},{6,14},{8,0},{10,2},{12,4},{14,6},{1,9},{3,11}... | collective-permute-start | bytes 208904 | tf_op jit(solution)/shard_map/ppermute | solution.py:231
  8.7 7.1 %collective-permute-start.2 = (bf16[17,16,128]{2,1,0:T(8,128)(2,1)S(1)}, bf16[17,16,128]{2,1,0:T(8,128)(2,1)S(1)}, u32[]{:S(2)}, u32[]{:S(2)}) collective-permute-start(bf16[17,16,128]{2,1,0:T(8,128)(2,1)S(1)} %get-tuple-element.28), channel_id=1, source_target_pairs={{0,4},{2,6},{4,0},{6,2},{8,12},{10,14},{12,8},{14,10},{1,5},{3,7},... | collective-permute-start | bytes 208904 | tf_op jit(solution)/shard_map/ppermute | solution.py:231
  9.2 9.8 %collective-permute-start.3 = (bf16[17,16,128]{2,1,0:T(8,128)(2,1)S(1)}, bf16[17,16,128]{2,1,0:T(8,128)(2,1)S(1)}, u32[]{:S(2)}, u32[]{:S(2)}) collective-permute-start(bf16[17,16,128]{2,1,0:T(8,128)(2,1)S(1)} %get-tuple-element.30), channel_id=1, source_target_pairs={{0,10},{2,8},{4,14},{6,12},{8,2},{10,0},{12,6},{14,4},{1,11},{3,9}... | collective-permute-start | bytes 208904 | tf_op jit(solution)/shard_map/ppermute | solution.py:231
  9.2 9.8 %collective-permute-start.4 = (bf16[17,16,128]{2,1,0:T(8,128)(2,1)S(1)}, bf16[17,16,128]{2,1,0:T(8,128)(2,1)S(1)}, u32[]{:S(2)}, u32[]{:S(2)}) collective-permute-start(bf16[17,16,128]{2,1,0:T(8,128)(2,1)S(1)} %get-tuple-element.31), channel_id=1, source_target_pairs={{0,12},{2,14},{4,8},{6,10},{8,4},{10,6},{12,0},{14,2},{1,13},{3,15... | collective-permute-start | bytes 208904 | tf_op jit(solution)/shard_map/ppermute | solution.py:231
  13.1 7.2 %collective-permute-start.5 = (bf16[17,16,128]{2,1,0:T(8,128)(2,1)S(1)}, bf16[17,16,128]{2,1,0:T(8,128)(2,1)S(1)}, u32[]{:S(2)}, u32[]{:S(2)}) collective-permute-start(bf16[17,16,128]{2,1,0:T(8,128)(2,1)S(1)} %get-tuple-element.32), channel_id=1, source_target_pairs={{0,14},{2,12},{4,10},{6,8},{8,6},{10,4},{12,2},{14,0},{1,15},{3,13... | collective-permute-start | bytes 208904 | tf_op jit(solution)/shard_map/ppermute | solution.py:231
  15.3 5.1 %collective-permute-start.6 = (bf16[17,16,128]{2,1,0:T(8,128)(2,1)S(1)}, bf16[17,16,128]{2,1,0:T(8,128)(2,1)S(1)}, u32[]{:S(2)}, u32[]{:S(2)}) collective-permute-start(bf16[17,16,128]{2,1,0:T(8,128)(2,1)S(1)} %get-tuple-element.33), channel_id=1, source_target_pairs={{0,2},{2,0},{4,6},{6,4},{8,10},{10,8},{12,14},{14,12},{1,3},{3,1},... | collective-permute-start | bytes 208904 | tf_op jit(solution)/shard_map/ppermute | solution.py:231
  15.9 4.8 %collective-permute-start.8 = (bf16[68,16,128]{2,1,0:T(8,128)(2,1)S(1)}, bf16[68,16,128]{2,1,0:T(8,128)(2,1)S(1)}, u32[]{:S(2)}, u32[]{:S(2)}) collective-permute-start(bf16[68,16,128]{2,1,0:T(8,128)(2,1)S(1)} %pad_maximum_fusion.1), channel_id=1, source_target_pairs={{0,1},{1,0},{2,3},{3,2},{4,5},{5,4},{6,7},{7,6},{8,9},{9,8},{10,11... | collective-permute-start | bytes 835592 | tf_op jit(solution)/shard_map/ppermute | solution.py:231
  20.5 1.6 %collective-permute-start.7 = (bf16[68,16,128]{2,1,0:T(8,128)(2,1)S(1)}, bf16[68,16,128]{2,1,0:T(8,128)(2,1)S(1)}, u32[]{:S(2)}, u32[]{:S(2)}) collective-permute-start(bf16[68,16,128]{2,1,0:T(8,128)(2,1)S(1)} %pad_maximum_fusion), channel_id=1, source_target_pairs={{0,1},{1,0},{2,3},{3,2},{4,5},{5,4},{6,7},{7,6},{8,9},{9,8},{10,11... | collective-permute-start | bytes 835592 | tf_op jit(solution)/shard_map/ppermute | solution.py:231

commit v22 on v21

--- a/solution.py
+++ b/solution.py
@@ -9,7 +9,7 @@
 
 LANES = 128
 DIGITS = 3
-PARTNERS = (3, 4, 2, 0, 5, 6, 7, 1)
+PARTNERS = (4, 3, 2, 0, 5, 7, 6, 1)
 WHOLE = pl.BlockSpec(memory_space=pltpu.VMEM)
 SCALAR = pl.BlockSpec(memory_space=pltpu.SMEM)
 
@@ -192,19 +192,20 @@
     best = jnp.maximum(best, best_ref[...])
     best = jnp.where(best > -2.0, best, 0.0)
     share = 1.0 / jnp.maximum(counts + counts_ref[...], 1.0)
-    squares = jnp.zeros(share.shape, jnp.float32)
+    squares = jnp.zeros((queries, LANES), jnp.float32)
+    norms = jnp.zeros((share.shape[0] - queries, LANES), jnp.float32)
     for start in range(0, width, LANES):
         lanes = slice(start, start + LANES)
         centroid = (sums[:, lanes] + sums_ref[:, lanes]) * share
-        offset = jnp.concatenate(
-            [query[:, lanes].astype(jnp.float32) - centroid[:queries], centroid[queries:]], axis=0
-        )
+        offset = query[:, lanes].astype(jnp.float32) - centroid[:queries]
         squares = squares + offset * offset
-    total = jnp.sum(jnp.transpose(squares), axis=0, keepdims=True)
-    result = jnp.concatenate([best, total[:, :queries]], axis=0)
+        norms = norms + centroid[queries:] * centroid[queries:]
+    distance = jnp.sum(jnp.transpose(squares), axis=0, keepdims=True)
+    result = jnp.concatenate([best, distance], axis=0)
     for owner in range(result_ref.shape[0]):
         result_ref[owner] = result
-    norm_ref[...] = total[:, queries:]
+    norms = jnp.concatenate([norms] * (LANES // norms.shape[0]), axis=0)
+    norm_ref[...] = jnp.sum(jnp.transpose(norms), axis=0, keepdims=True)[:, : norm_ref.shape[1]]
 
 
 def pick_kernel(

time: 35.1 us -> 33.7 us (0.960)
  blocking collectives: 11.1 us -> 9.89 us
  starting transfers between devices: 13.9 us -> 13.4 us
    all_to_all x1, blocking collectives: 11.1 us -> 9.89 us  [local(): results = lax.all_to_all(results, 'shard', 0, 0, tiled=True)]
    ppermute x9, starting transfers between devices: 13.9 us -> 13.4 us  [from_partner(): lax.ppermute(value, axis, [(i, i ^ k) for i in range(lax.axis_size(axis))])]
  transfers between devices with their start and end apart: 9 -> 9, of which waited for: 4 -> 3; matrix products, arithmetic and copies ran while one was open for 1% -> 1% of each run, Pallas kernels for 3% -> 3%
where the time goes in v22:
time: 33.7 us; the launch traced here: 33.5 us
  starting transfers between devices  13.4 us (40%)
  blocking collectives  9.89 us (29%)
  waiting for transfers between devices  5.16 us (15%)
  Pallas kernels  3.35 us (10%)
  other arithmetic  0.84 us (2%)
  between operations  0.75 us (2%)
    ppermute x9, starting transfers between devices, from_partner(): lax.ppermute(value, axis, [(i, i ^ k) for i in range(lax.axis_size(axis))])  13.4 us
    all_to_all x1, blocking collectives, local(): results = lax.all_to_all(results, 'shard', 0, 0, tiled=True)  9.89 us
    ppermute x9, waiting for transfers between devices, from_partner(): lax.ppermute(value, axis, [(i, i ^ k) for i in range(lax.axis_size(axis))])  5.16 us
    pallas_call x1, Pallas kernels, local(): pl.pallas_call(functools.partial(near_kernel, rows_all, owner_map.shape[0...  0.97 us
    pallas_call x1, Pallas kernels, local(): pl.pallas_call(functools.partial(far_kernel, rows_all, tiles), out_shape=...  0.96 us
    concatenate x1, other arithmetic, local(): ints = jnp.concatenate([owner_map, cluster_id, item_order]).reshape(1, -1)  0.76 us
    pallas_call x1, Pallas kernels, local(): pl.pallas_call(functools.partial(pick_kernel, order, parts), out_shape=[j...  0.72 us
  transfers between devices with their start and end apart: 9, of which 3 were waited for; matrix products, arithmetic and copies ran while one was open for 1% of the time, Pallas kernels for 3%

profile of v22, /device:TPU:0, one launch (start us, length us, event | category | flops | bytes accessed | tf_op | source)
XLA Modules:
  0.0 33.5 jit_solution(10908590790770147476)
XLA Ops:
  0.6 0.0 copy-start
  0.6 0.8 %pad_add_fusion = s32[512]{0:T(512)S(1)} fusion(s32[128]{0:T(128)} %param.6, s32[128]{0:T(128)} %param.5, s32[256]{0:T(256)} %param.7), kind=kLoop, calls=%fused_computation.10 | loop fusion | flops 1024 | bytes 4096 | tf_op jit(solution)/shard_map/concatenate | solution.py:268
  1.4 0.3 slots.1
  1.7 0.0 copy-done
  1.7 0.4 %pack.1 = (bf16[17,16,128]{2,1,0:T(8,128)(2,1)S(1)}, bf16[17,16,128]{2,1,0:T(8,128)(2,1)S(1)}, bf16[17,16,128]{2,1,0:T(8,128)(2,1)S(1)}, bf16[17,16,128]{2,1,0:T...) custom-call(s32[1,128]{1,0:T(1,128)S(1)} %get-tuple-element.24.slot_, ...), custom_call_target="tpu_custom_call" | custom-call | tf_op jit(solution)/shard_map/pack/pallas_call | solution.py:287
  2.1 4.1 %collective-permute-start = (bf16[17,16,128]{2,1,0:T(8,128)(2,1)S(1)}, bf16[17,16,128]{2,1,0:T(8,128)(2,1)S(1)}, u32[]{:S(2)}, u32[]{:S(2)}) collective-permute-start(bf16[17,16,128]{2,1,0:T(8,128)(2,1)S(1)} %get-tuple-element.26), channel_id=1, source_target_pairs={{0,8},{2,10},{4,12},{6,14},{8,0},{10,2},{12,4},{14,6},{1,9},{3,11}... | collective-permute-start | bytes 208904 | tf_op jit(solution)/shard_map/ppermute | solution.py:232
  6.2 2.5 %collective-permute-start.1 = (bf16[17,16,128]{2,1,0:T(8,128)(2,1)S(1)}, bf16[17,16,128]{2,1,0:T(8,128)(2,1)S(1)}, u32[]{:S(2)}, u32[]{:S(2)}) collective-permute-start(bf16[17,16,128]{2,1,0:T(8,128)(2,1)S(1)} %get-tuple-element.27), channel_id=1, source_target_pairs={{0,6},{2,4},{4,2},{6,0},{8,14},{10,12},{12,10},{14,8},{1,7},{3,5},... | collective-permute-start | bytes 208904 | tf_op jit(solution)/shard_map/ppermute | solution.py:232
  8.7 0.4 %collective-permute-start.2 = (bf16[17,16,128]{2,1,0:T(8,128)(2,1)S(1)}, bf16[17,16,128]{2,1,0:T(8,128)(2,1)S(1)}, u32[]{:S(2)}, u32[]{:S(2)}) collective-permute-start(bf16[17,16,128]{2,1,0:T(8,128)(2,1)S(1)} %get-tuple-element.28), channel_id=1, source_target_pairs={{0,4},{2,6},{4,0},{6,2},{8,12},{10,14},{12,8},{14,10},{1,5},{3,7},... | collective-permute-start | bytes 208904 | tf_op jit(solution)/shard_map/ppermute | solution.py:232
  9.2 0.1 collective-permute-start.3
  9.2 4.8 %collective-permute-start.4 = (bf16[17,16,128]{2,1,0:T(8,128)(2,1)S(1)}, bf16[17,16,128]{2,1,0:T(8,128)(2,1)S(1)}, u32[]{:S(2)}, u32[]{:S(2)}) collective-permute-start(bf16[17,16,128]{2,1,0:T(8,128)(2,1)S(1)} %get-tuple-element.31), channel_id=1, source_target_pairs={{0,14},{2,12},{4,10},{6,8},{8,6},{10,4},{12,2},{14,0},{1,15},{3,13... | collective-permute-start | bytes 208904 | tf_op jit(solution)/shard_map/ppermute | solution.py:232
  14.0 0.0 collective-permute-done
  14.0 0.2 collective-permute-start.5
  14.2 0.0 collective-permute-done.1
  14.2 1.1 %collective-permute-start.6 = (bf16[17,16,128]{2,1,0:T(8,128)(2,1)S(1)}, bf16[17,16,128]{2,1,0:T(8,128)(2,1)S(1)}, u32[]{:S(2)}, u32[]{:S(2)}) collective-permute-start(bf16[17,16,128]{2,1,0:T(8,128)(2,1)S(1)} %get-tuple-element.33), channel_id=1, source_target_pairs={{0,2},{2,0},{4,6},{6,4},{8,10},{10,8},{12,14},{14,12},{1,3},{3,1},... | collective-permute-start | bytes 208904 | tf_op jit(solution)/shard_map/ppermute | solution.py:232
  15.4 0.0 collective-permute-done.2
  15.4 0.1 collective-permute-start.8
  15.5 3.4 %collective-permute-done.3 = bf16[17,16,128]{2,1,0:T(8,128)(2,1)S(1)} collective-permute-done((bf16[17,16,128]{2,1,0:T(8,128)(2,1)S(1)}, bf16[17,16,128]{2,1,0:T(8,128)(2,1)S(1)}, u32[]{:S(2)}, u32[]{:S(2)}) %collective-permute-start.3) | collective-permute-done | bytes 69664 | tf_op jit(solution)/shard_map/ppermute | solution.py:232
  19.0 0.0 collective-permute-done.4
  19.0 1.3 %collective-permute-done.5 = bf16[17,16,128]{2,1,0:T(8,128)(2,1)S(1)} collective-permute-done((bf16[17,16,128]{2,1,0:T(8,128)(2,1)S(1)}, bf16[17,16,128]{2,1,0:T(8,128)(2,1)S(1)}, u32[]{:S(2)}, u32[]{:S(2)}) %collective-permute-start.5) | collective-permute-done | bytes 69664 | tf_op jit(solution)/shard_map/ppermute | solution.py:232
  20.2 0.0 collective-permute-done.6
  20.3 0.1 collective-permute-start.7
  20.5 0.0 collective-permute-done.8.other_ref
  20.5 1.0 %near.1 = (bf16[1024,256]{1,0:T(8,128)(2,1)S(1)}, s32[288,128]{1,0:T(8,128)S(1)}, s32[2,256]{1,0:T(2,128)S(1)}, f32[1,256]{1,0:T(1,128)S(1)}, f32[288,1024]{1,0:T(8,128)S(1)}, /*index=5*/f32[288,128]{1,0:T(8,128)S(1)}) custom-call(s32[1]{0:T(128)} %bitcast.me_ref, s32[1,512]{1,0:T(1,128)S(1)} %bitcast.6, ...), custom_call_target="tpu_custom_call" | custom-call | flops 268435456 | bytes 1048576 | tf_op jit(solution)/shard_map/near/pallas_call | solution.py:299
  21.5 0.4 %collective-permute-done.7.other_ref = bf16[68,16,128]{2,1,0:T(8,128)(2,1)S(1)} collective-permute-done((bf16[68,16,128]{2,1,0:T(8,128)(2,1)S(1)}, bf16[68,16,128]{2,1,0:T(8,128)(2,1)S(1)}, u32[]{:S(2)}, u32[]{:S(2)}) %collective-permute-start.7) | collective-permute-done | bytes 278560 | tf_op jit(solution)/shard_map/ppermute | solution.py:232
  21.9 1.0 %far.1 = (f32[8,2,256]{2,1,0:T(2,128)S(1)}, f32[1,32]{1,0:T(1,128)S(1)}) custom-call(bf16[136,16,128]{2,1,0:T(8,128)(2,1)S(1)} %constant_dynamic-update-slice_fusion.query_ref, bf16[68,16,128]{2,1,0:T(8,128)(2,1)S(1)} %collective-permute-done.7.other_ref, bf16[1024,256]{1,0:T(8,128)(2,1)S(1)} %get-tuple-element.34.query_t_ref, ...), custom_call_target="tpu_custom_call" | custom-call | flops 268435456 | bytes 1048576 | tf_op jit(solution)/shard_map/far/pallas_call | solution.py:315
  22.9 9.9 %all_to_all.5.result_ref = f32[8,2,256]{2,1,0:T(2,128)S(1)} all-to-all(f32[8,2,256]{2,1,0:T(2,128)S(1)} %get-tuple-element.40), channel_id=1, replica_groups=mesh['groups'=2,'shard'=8,'sub'=2] {'shard'}, dimensions={0} | all-to-all | bytes 32768 | tf_op jit(solution)/shard_map/all_to_all | solution.py:327
  32.8 0.7 %pick.1 = (f32[1,128]{1,0:T(1,128)}, f32[1,128]{1,0:T(1,128)}, f32[1,32]{1,0:T(1,128)}) custom-call(s32[1]{0:T(128)} %bitcast.me_ref, s32[1,128]{1,0:T(1,128)S(1)} %get-tuple-element.24.slot_ref, f32[8,2,256]{2,1,0:T(2,128)S(1)} %all_to_all.5.result_ref, f32[1,32]{1,0:T(1,128)S(1)} %get-tuple-element.41.norm_ref), custom_call_target="tpu_custom_call" | custom-call | tf_op jit(solution)/shard_map/pick/pallas_call | solution.py:328
  (10 shorter events, 0.2 us)
Async XLA Ops:
  0.6 1.0 %copy-start = (bf16[128,1024]{1,0:T(8,128)(2,1)S(1)}, bf16[128,1024]{1,0:T(8,128)(2,1)}, u32[]{:S(2)}) copy-start(bf16[128,1024]{1,0:T(8,128)(2,1)} %embed_ref.1) | copy-start | bytes 786436
  2.1 11.9 %collective-permute-start = (bf16[17,16,128]{2,1,0:T(8,128)(2,1)S(1)}, bf16[17,16,128]{2,1,0:T(8,128)(2,1)S(1)}, u32[]{:S(2)}, u32[]{:S(2)}) collective-permute-start(bf16[17,16,128]{2,1,0:T(8,128)(2,1)S(1)} %get-tuple-element.26), channel_id=1, source_target_pairs={{0,8},{2,10},{4,12},{6,14},{8,0},{10,2},{12,4},{14,6},{1,9},{3,11}... | collective-permute-start | bytes 208904 | tf_op jit(solution)/shard_map/ppermute | solution.py:232
  6.2 8.0 %collective-permute-start.1 = (bf16[17,16,128]{2,1,0:T(8,128)(2,1)S(1)}, bf16[17,16,128]{2,1,0:T(8,128)(2,1)S(1)}, u32[]{:S(2)}, u32[]{:S(2)}) collective-permute-start(bf16[17,16,128]{2,1,0:T(8,128)(2,1)S(1)} %get-tuple-element.27), channel_id=1, source_target_pairs={{0,6},{2,4},{4,2},{6,0},{8,14},{10,12},{12,10},{14,8},{1,7},{3,5},... | collective-permute-start | bytes 208904 | tf_op jit(solution)/shard_map/ppermute | solution.py:232
  8.7 6.7 %collective-permute-start.2 = (bf16[17,16,128]{2,1,0:T(8,128)(2,1)S(1)}, bf16[17,16,128]{2,1,0:T(8,128)(2,1)S(1)}, u32[]{:S(2)}, u32[]{:S(2)}) collective-permute-start(bf16[17,16,128]{2,1,0:T(8,128)(2,1)S(1)} %get-tuple-element.28), channel_id=1, source_target_pairs={{0,4},{2,6},{4,0},{6,2},{8,12},{10,14},{12,8},{14,10},{1,5},{3,7},... | collective-permute-start | bytes 208904 | tf_op jit(solution)/shard_map/ppermute | solution.py:232
  9.2 9.8 %collective-permute-start.3 = (bf16[17,16,128]{2,1,0:T(8,128)(2,1)S(1)}, bf16[17,16,128]{2,1,0:T(8,128)(2,1)S(1)}, u32[]{:S(2)}, u32[]{:S(2)}) collective-permute-start(bf16[17,16,128]{2,1,0:T(8,128)(2,1)S(1)} %get-tuple-element.30), channel_id=1, source_target_pairs={{0,10},{2,8},{4,14},{6,12},{8,2},{10,0},{12,6},{14,4},{1,11},{3,9}... | collective-permute-start | bytes 208904 | tf_op jit(solution)/shard_map/ppermute | solution.py:232
  9.2 9.7 %collective-permute-start.4 = (bf16[17,16,128]{2,1,0:T(8,128)(2,1)S(1)}, bf16[17,16,128]{2,1,0:T(8,128)(2,1)S(1)}, u32[]{:S(2)}, u32[]{:S(2)}) collective-permute-start(bf16[17,16,128]{2,1,0:T(8,128)(2,1)S(1)} %get-tuple-element.31), channel_id=1, source_target_pairs={{0,14},{2,12},{4,10},{6,8},{8,6},{10,4},{12,2},{14,0},{1,15},{3,13... | collective-permute-start | bytes 208904 | tf_op jit(solution)/shard_map/ppermute | solution.py:232
  14.0 6.2 %collective-permute-start.5 = (bf16[17,16,128]{2,1,0:T(8,128)(2,1)S(1)}, bf16[17,16,128]{2,1,0:T(8,128)(2,1)S(1)}, u32[]{:S(2)}, u32[]{:S(2)}) collective-permute-start(bf16[17,16,128]{2,1,0:T(8,128)(2,1)S(1)} %get-tuple-element.32), channel_id=1, source_target_pairs={{0,12},{2,14},{4,8},{6,10},{8,4},{10,6},{12,0},{14,2},{1,13},{3,15... | collective-permute-start | bytes 208904 | tf_op jit(solution)/shard_map/ppermute | solution.py:232
  14.2 6.0 %collective-permute-start.6 = (bf16[17,16,128]{2,1,0:T(8,128)(2,1)S(1)}, bf16[17,16,128]{2,1,0:T(8,128)(2,1)S(1)}, u32[]{:S(2)}, u32[]{:S(2)}) collective-permute-start(bf16[17,16,128]{2,1,0:T(8,128)(2,1)S(1)} %get-tuple-element.33), channel_id=1, source_target_pairs={{0,2},{2,0},{4,6},{6,4},{8,10},{10,8},{12,14},{14,12},{1,3},{3,1},... | collective-permute-start | bytes 208904 | tf_op jit(solution)/shard_map/ppermute | solution.py:232
  15.4 5.1 %collective-permute-start.8 = (bf16[68,16,128]{2,1,0:T(8,128)(2,1)S(1)}, bf16[68,16,128]{2,1,0:T(8,128)(2,1)S(1)}, u32[]{:S(2)}, u32[]{:S(2)}) collective-permute-start(bf16[68,16,128]{2,1,0:T(8,128)(2,1)S(1)} %pad_maximum_fusion.1), channel_id=1, source_target_pairs={{0,1},{1,0},{2,3},{3,2},{4,5},{5,4},{6,7},{7,6},{8,9},{9,8},{10,11... | collective-permute-start | bytes 835592 | tf_op jit(solution)/shard_map/ppermute | solution.py:232
  20.3 1.6 %collective-permute-start.7 = (bf16[68,16,128]{2,1,0:T(8,128)(2,1)S(1)}, bf16[68,16,128]{2,1,0:T(8,128)(2,1)S(1)}, u32[]{:S(2)}, u32[]{:S(2)}) collective-permute-start(bf16[68,16,128]{2,1,0:T(8,128)(2,1)S(1)} %pad_maximum_fusion), channel_id=1, source_target_pairs={{0,1},{1,0},{2,3},{3,2},{4,5},{5,4},{6,7},{7,6},{8,9},{9,8},{10,11... | collective-permute-start | bytes 835592 | tf_op jit(solution)/shard_map/ppermute | solution.py:232

commit v23 on v22

--- a/solution.py
+++ b/solution.py
@@ -9,7 +9,8 @@
 
 LANES = 128
 DIGITS = 3
-PARTNERS = (4, 3, 2, 0, 5, 7, 6, 1)
+SENDS = ((4,), (2, 3), (5,), (7,), (6,), (1,), (0,))
+PARTNERS = (4, 2, 0, 5, 7, 6, 1, 3)
 WHOLE = pl.BlockSpec(memory_space=pltpu.VMEM)
 SCALAR = pl.BlockSpec(memory_space=pltpu.SMEM)
 
@@ -76,25 +77,27 @@
     digit_ref[...] = bf16(jnp.concatenate([early, late], axis=1))
 
 
-def pack_kernel(slot_ref, digit_ref, embed_ref, *out_refs):
+def pack_kernel(sends, slot_ref, digit_ref, embed_ref, *out_refs):
     rows, width = embed_ref.shape
-    tiles, half, _ = out_refs[0].shape
+    half = out_refs[0].shape[1]
+    tiles = 2 * (width // LANES) + 1
     values = embed_ref[...].astype(jnp.float32)
     mean_sq = jnp.sum(values * values, axis=1, keepdims=True) * (1.0 / width)
     unit = (values * lax.rsqrt(width * (mean_sq + 1e-06))).astype(jnp.bfloat16)
-    late = half * len(out_refs)
+    late = half * sum(len(places) for places in sends)
     move = bf16(iota((2 * late, rows), 0) == slot_ref[...])
     moved = matmul(move, unit).astype(jnp.bfloat16)
     both = jnp.concatenate([move[:late], move[late:]], axis=1)
     digit = matmul_t(both, digit_ref[...]).astype(jnp.bfloat16)
     each = tiles // 2
-    for index, out_ref in enumerate(out_refs):
-        start = index * half
-        for tile in range(each):
-            lanes = slice(tile * LANES, (tile + 1) * LANES)
-            out_ref[tile] = moved[start : start + half, lanes]
-            out_ref[each + tile] = moved[late + start : late + start + half, lanes]
-        out_ref[tiles - 1] = digit[start : start + half]
+    for places, out_ref in zip(sends, out_refs):
+        for index, place in enumerate(places):
+            base, start = index * tiles, place * half
+            for tile in range(each):
+                lanes = slice(tile * LANES, (tile + 1) * LANES)
+                out_ref[base + tile] = moved[start : start + half, lanes]
+                out_ref[base + each + tile] = moved[late + start : late + start + half, lanes]
+            out_ref[base + tiles - 1] = digit[start : start + half]
 
 
 def unpacked(block_ref, tiles):
@@ -232,8 +235,16 @@
     return lax.ppermute(value, axis, [(i, i ^ k) for i in range(lax.axis_size(axis))])
 
 
-def exchange(packed, order):
-    got = [from_partner(block, k, "shard") if k else block for k, block in zip(order, packed)]
+def exchange(packed, tiles):
+    sent = dict(zip(SENDS, packed))
+    got = {0: sent[0,]}
+    for k in (4, 5, 7, 6):
+        got[k] = from_partner(sent[k,], k, "shard")
+    pair = from_partner(sent[2, 3], 2, "shard")
+    got[2] = pair[:tiles]
+    pair = from_partner(jnp.concatenate([sent[1,], pair[tiles:]]), 1, "shard")
+    got[1], got[3] = pair[:tiles], pair[tiles:]
+    got = [got[k] for k in PARTNERS]
     half = len(got) // 2
     return jnp.concatenate(got[:half]), jnp.concatenate(got[half:])
 
@@ -271,7 +282,8 @@
     order = PARTNERS if direct else tuple(range(owners))
     parts = owners if direct else 1
     tiles = 2 * (width // LANES) + 1
-    block = (tiles, slots // parts // 2, LANES)
+    sends = [[PARTNERS.index(k) for k in ks] for ks in SENDS] if direct else [[0]]
+    half = slots // parts // 2
     slot, digit = pl.pallas_call(
         functools.partial(slot_kernel, owners, capacity, order, parts, local_rows),
         out_shape=[
@@ -285,14 +297,16 @@
         name="slots",
     )(me, ints)
     packed = pl.pallas_call(
-        pack_kernel,
-        out_shape=[jax.ShapeDtypeStruct(block, jnp.bfloat16)] * parts,
+        functools.partial(pack_kernel, sends),
+        out_shape=[
+            jax.ShapeDtypeStruct((len(places) * tiles, half, LANES), jnp.bfloat16) for places in sends
+        ],
         in_specs=[WHOLE] * 3,
-        out_specs=[WHOLE] * parts,
+        out_specs=[WHOLE] * len(sends),
         compiler_params=params,
         name="pack",
     )(slot, digit, embeddings)
-    first, second = exchange(packed, order) if direct else exchange_all(packed[0], me[0])
+    first, second = exchange(packed, tiles) if direct else exchange_all(packed[0], me[0])
     other_first, other_second = (from_partner(rows, 1, "sub") for rows in (first, second))
     query = jnp.concatenate([first, second])
     asked = slots + clus_dev

time: 33.7 us -> 33.6 us (level)
  blocking collectives: 9.89 us -> 10.3 us
    all_to_all x1, blocking collectives: 9.89 us -> 10.3 us  [local(): results = lax.all_to_all(results, 'shard', 0, 0, tiled=True)]
    ppermute x9 -> x8, starting transfers between devices: 13.4 us -> 13.1 us  [from_partner(): lax.ppermute(value, axis, [(i, i ^ k) for i in range(lax.axis_size(axis))])]
    ppermute x9 -> x8, waiting for transfers between devices: 5.16 us -> 4.91 us  [from_partner(): lax.ppermute(value, axis, [(i, i ^ k) for i in range(lax.axis_size(axis))])]
  transfers between devices with their start and end apart: 9 -> 8, of which waited for: 3 -> 3; matrix products, arithmetic and copies ran while one was open for 1% -> 1% of each run, Pallas kernels for 3% -> 3%
where the time goes in v23:
time: 33.6 us; the launch traced here: 33.4 us
  starting transfers between devices  13.1 us (39%)
  blocking collectives  10.3 us (31%)
  waiting for transfers between devices  4.91 us (15%)
  Pallas kernels  3.35 us (10%)
  other arithmetic  0.84 us (2%)
  between operations  0.76 us (2%)
    ppermute x8, starting transfers between devices, from_partner(): lax.ppermute(value, axis, [(i, i ^ k) for i in range(lax.axis_size(axis))])  13.1 us
    all_to_all x1, blocking collectives, local(): results = lax.all_to_all(results, 'shard', 0, 0, tiled=True)  10.3 us
    ppermute x8, waiting for transfers between devices, from_partner(): lax.ppermute(value, axis, [(i, i ^ k) for i in range(lax.axis_size(axis))])  4.91 us
    pallas_call x1, Pallas kernels, local(): pl.pallas_call(functools.partial(near_kernel, rows_all, owner_map.shape[0...  0.97 us
    pallas_call x1, Pallas kernels, local(): pl.pallas_call(functools.partial(far_kernel, rows_all, tiles), out_shape=...  0.97 us
    concatenate x1, other arithmetic, local(): ints = jnp.concatenate([owner_map, cluster_id, item_order]).reshape(1, -1)  0.76 us
    pallas_call x1, Pallas kernels, local(): pl.pallas_call(functools.partial(pick_kernel, order, parts), out_shape=[j...  0.72 us
  transfers between devices with their start and end apart: 8, of which 3 were waited for; matrix products, arithmetic and copies ran while one was open for 1% of the time, Pallas kernels for 3%

profile of v23, /device:TPU:0, one launch (start us, length us, event | category | flops | bytes accessed | tf_op | source)
XLA Modules:
  0.0 33.4 jit_solution(13412433273163101554)
XLA Ops:
  0.6 0.0 copy-start
  0.6 0.8 %pad_add_fusion = s32[512]{0:T(512)S(1)} fusion(s32[128]{0:T(128)} %param.6, s32[128]{0:T(128)} %param.5, s32[256]{0:T(256)} %param.7), kind=kLoop, calls=%fused_computation.10 | loop fusion | flops 1024 | bytes 4096 | tf_op jit(solution)/shard_map/concatenate | solution.py:279
  1.4 0.3 slots.1
  1.7 0.0 copy-done
  1.7 0.4 %pack.1 = (bf16[17,16,128]{2,1,0:T(8,128)(2,1)S(1)}, bf16[34,16,128]{2,1,0:T(8,128)(2,1)S(1)}, bf16[17,16,128]{2,1,0:T(8,128)(2,1)S(1)}, bf16[17,16,128]{2,1,0:T...) custom-call(s32[1,128]{1,0:T(1,128)S(1)} %get-tuple-element.23.slot_, ...), custom_call_target="tpu_custom_call" | custom-call | tf_op jit(solution)/shard_map/pack/pallas_call | solution.py:299
  2.1 4.1 %collective-permute-start = (bf16[17,16,128]{2,1,0:T(8,128)(2,1)S(1)}, bf16[17,16,128]{2,1,0:T(8,128)(2,1)S(1)}, u32[]{:S(2)}, u32[]{:S(2)}) collective-permute-start(bf16[17,16,128]{2,1,0:T(8,128)(2,1)S(1)} %get-tuple-element.25), channel_id=1, source_target_pairs={{0,8},{2,10},{4,12},{6,14},{8,0},{10,2},{12,4},{14,6},{1,9},{3,11}... | collective-permute-start | bytes 208904 | tf_op jit(solution)/shard_map/ppermute | solution.py:235
  6.2 1.6 %collective-permute-start.1 = (bf16[34,16,128]{2,1,0:T(8,128)(2,1)S(1)}, bf16[34,16,128]{2,1,0:T(8,128)(2,1)S(1)}, u32[]{:S(2)}, u32[]{:S(2)}) collective-permute-start(bf16[34,16,128]{2,1,0:T(8,128)(2,1)S(1)} %get-tuple-element.26), channel_id=1, source_target_pairs={{0,4},{2,6},{4,0},{6,2},{8,12},{10,14},{12,8},{14,10},{1,5},{3,7},... | collective-permute-start | bytes 417800 | tf_op jit(solution)/shard_map/ppermute | solution.py:235
  7.8 1.3 %collective-permute-start.2 = (bf16[17,16,128]{2,1,0:T(8,128)(2,1)S(1)}, bf16[17,16,128]{2,1,0:T(8,128)(2,1)S(1)}, u32[]{:S(2)}, u32[]{:S(2)}) collective-permute-start(bf16[17,16,128]{2,1,0:T(8,128)(2,1)S(1)} %get-tuple-element.28), channel_id=1, source_target_pairs={{0,10},{2,8},{4,14},{6,12},{8,2},{10,0},{12,6},{14,4},{1,11},{3,9}... | collective-permute-start | bytes 208904 | tf_op jit(solution)/shard_map/ppermute | solution.py:235
  9.1 2.4 %collective-permute-start.3 = (bf16[17,16,128]{2,1,0:T(8,128)(2,1)S(1)}, bf16[17,16,128]{2,1,0:T(8,128)(2,1)S(1)}, u32[]{:S(2)}, u32[]{:S(2)}) collective-permute-start(bf16[17,16,128]{2,1,0:T(8,128)(2,1)S(1)} %get-tuple-element.29), channel_id=1, source_target_pairs={{0,14},{2,12},{4,10},{6,8},{8,6},{10,4},{12,2},{14,0},{1,15},{3,13... | collective-permute-start | bytes 208904 | tf_op jit(solution)/shard_map/ppermute | solution.py:235
  11.5 1.4 %collective-permute-start.4 = (bf16[17,16,128]{2,1,0:T(8,128)(2,1)S(1)}, bf16[17,16,128]{2,1,0:T(8,128)(2,1)S(1)}, u32[]{:S(2)}, u32[]{:S(2)}) collective-permute-start(bf16[17,16,128]{2,1,0:T(8,128)(2,1)S(1)} %get-tuple-element.30), channel_id=1, source_target_pairs={{0,12},{2,14},{4,8},{6,10},{8,4},{10,6},{12,0},{14,2},{1,13},{3,15... | collective-permute-start | bytes 208904 | tf_op jit(solution)/shard_map/ppermute | solution.py:235
  12.9 0.0 collective-permute-done
  12.9 0.0 collective-permute-done.1
  13.0 1.9 %collective-permute-start.5 = (bf16[34,16,128]{2,1,0:T(8,128)(2,1)S(1)}, bf16[34,16,128]{2,1,0:T(8,128)(2,1)S(1)}, u32[]{:S(2)}, u32[]{:S(2)}) collective-permute-start(bf16[34,16,128]{2,1,0:T(8,128)(2,1)S(1)} %pad_maximum_fusion.2), channel_id=1, source_target_pairs={{0,2},{2,0},{4,6},{6,4},{8,10},{10,8},{12,14},{14,12},{1,3},{3,1},... | collective-permute-start | bytes 417800 | tf_op jit(solution)/shard_map/ppermute | solution.py:235
  14.9 3.9 %collective-permute-done.2 = bf16[17,16,128]{2,1,0:T(8,128)(2,1)S(1)} collective-permute-done((bf16[17,16,128]{2,1,0:T(8,128)(2,1)S(1)}, bf16[17,16,128]{2,1,0:T(8,128)(2,1)S(1)}, u32[]{:S(2)}, u32[]{:S(2)}) %collective-permute-start.2) | collective-permute-done | bytes 69664 | tf_op jit(solution)/shard_map/ppermute | solution.py:235
  18.8 0.1 collective-permute-start.7
  18.9 0.0 collective-permute-done.3
  18.9 0.0 collective-permute-done.4
  18.9 0.2 collective-permute-done.5
  19.1 0.4 %collective-permute-start.6 = (bf16[68,16,128]{2,1,0:T(8,128)(2,1)S(1)}, bf16[68,16,128]{2,1,0:T(8,128)(2,1)S(1)}, u32[]{:S(2)}, u32[]{:S(2)}) collective-permute-start(bf16[68,16,128]{2,1,0:T(8,128)(2,1)S(1)} %pad_maximum_fusion), channel_id=1, source_target_pairs={{0,1},{1,0},{2,3},{3,2},{4,5},{5,4},{6,7},{7,6},{8,9},{9,8},{10,11... | collective-permute-start | bytes 835592 | tf_op jit(solution)/shard_map/ppermute | solution.py:235
  19.6 0.8 %collective-permute-done.7.other_ref = bf16[68,16,128]{2,1,0:T(8,128)(2,1)S(1)} collective-permute-done((bf16[68,16,128]{2,1,0:T(8,128)(2,1)S(1)}, bf16[68,16,128]{2,1,0:T(8,128)(2,1)S(1)}, u32[]{:S(2)}, u32[]{:S(2)}) %collective-permute-start.7) | collective-permute-done | bytes 278560 | tf_op jit(solution)/shard_map/ppermute | solution.py:235
  20.4 1.0 %near.1 = (bf16[1024,256]{1,0:T(8,128)(2,1)S(1)}, s32[288,128]{1,0:T(8,128)S(1)}, s32[2,256]{1,0:T(2,128)S(1)}, f32[1,256]{1,0:T(1,128)S(1)}, f32[288,1024]{1,0:T(8,128)S(1)}, /*index=5*/f32[288,128]{1,0:T(8,128)S(1)}) custom-call(s32[1]{0:T(128)} %bitcast.me_ref, s32[1,512]{1,0:T(1,128)S(1)} %bitcast.6, ...), custom_call_target="tpu_custom_call" | custom-call | flops 268435456 | bytes 1048576 | tf_op jit(solution)/shard_map/near/pallas_call | solution.py:313
  21.4 0.0 collective-permute-done.6.other_ref
  21.4 1.0 %far.1 = (f32[8,2,256]{2,1,0:T(2,128)S(1)}, f32[1,32]{1,0:T(1,128)S(1)}) custom-call(bf16[136,16,128]{2,1,0:T(8,128)(2,1)S(1)} %constant_dynamic-update-slice_fusion.query_ref, bf16[68,16,128]{2,1,0:T(8,128)(2,1)S(1)} %collective-permute-done.6.other_ref, bf16[1024,256]{1,0:T(8,128)(2,1)S(1)} %get-tuple-element.32.query_t_ref, ...), custom_call_target="tpu_custom_call" | custom-call | flops 268435456 | bytes 1048576 | tf_op jit(solution)/shard_map/far/pallas_call | solution.py:329
  22.4 10.3 %all_to_all.5.result_ref = f32[8,2,256]{2,1,0:T(2,128)S(1)} all-to-all(f32[8,2,256]{2,1,0:T(2,128)S(1)} %get-tuple-element.38), channel_id=1, replica_groups=mesh['groups'=2,'shard'=8,'sub'=2] {'shard'}, dimensions={0} | all-to-all | bytes 32768 | tf_op jit(solution)/shard_map/all_to_all | solution.py:341
  32.7 0.7 %pick.1 = (f32[1,128]{1,0:T(1,128)}, f32[1,128]{1,0:T(1,128)}, f32[1,32]{1,0:T(1,128)}) custom-call(s32[1]{0:T(128)} %bitcast.me_ref, s32[1,128]{1,0:T(1,128)S(1)} %get-tuple-element.23.slot_ref, f32[8,2,256]{2,1,0:T(2,128)S(1)} %all_to_all.5.result_ref, f32[1,32]{1,0:T(1,128)S(1)} %get-tuple-element.39.norm_ref), custom_call_target="tpu_custom_call" | custom-call | tf_op jit(solution)/shard_map/pick/pallas_call | solution.py:342
  (10 shorter events, 0.2 us)
Async XLA Ops:
  0.6 1.0 %copy-start = (bf16[128,1024]{1,0:T(8,128)(2,1)S(1)}, bf16[128,1024]{1,0:T(8,128)(2,1)}, u32[]{:S(2)}) copy-start(bf16[128,1024]{1,0:T(8,128)(2,1)} %embed_ref.1) | copy-start | bytes 786436
  2.1 10.7 %collective-permute-start = (bf16[17,16,128]{2,1,0:T(8,128)(2,1)S(1)}, bf16[17,16,128]{2,1,0:T(8,128)(2,1)S(1)}, u32[]{:S(2)}, u32[]{:S(2)}) collective-permute-start(bf16[17,16,128]{2,1,0:T(8,128)(2,1)S(1)} %get-tuple-element.25), channel_id=1, source_target_pairs={{0,8},{2,10},{4,12},{6,14},{8,0},{10,2},{12,4},{14,6},{1,9},{3,11}... | collective-permute-start | bytes 208904 | tf_op jit(solution)/shard_map/ppermute | solution.py:235
  6.2 6.7 %collective-permute-start.1 = (bf16[34,16,128]{2,1,0:T(8,128)(2,1)S(1)}, bf16[34,16,128]{2,1,0:T(8,128)(2,1)S(1)}, u32[]{:S(2)}, u32[]{:S(2)}) collective-permute-start(bf16[34,16,128]{2,1,0:T(8,128)(2,1)S(1)} %get-tuple-element.26), channel_id=1, source_target_pairs={{0,4},{2,6},{4,0},{6,2},{8,12},{10,14},{12,8},{14,10},{1,5},{3,7},... | collective-permute-start | bytes 417800 | tf_op jit(solution)/shard_map/ppermute | solution.py:235
  7.8 10.9 %collective-permute-start.2 = (bf16[17,16,128]{2,1,0:T(8,128)(2,1)S(1)}, bf16[17,16,128]{2,1,0:T(8,128)(2,1)S(1)}, u32[]{:S(2)}, u32[]{:S(2)}) collective-permute-start(bf16[17,16,128]{2,1,0:T(8,128)(2,1)S(1)} %get-tuple-element.28), channel_id=1, source_target_pairs={{0,10},{2,8},{4,14},{6,12},{8,2},{10,0},{12,6},{14,4},{1,11},{3,9}... | collective-permute-start | bytes 208904 | tf_op jit(solution)/shard_map/ppermute | solution.py:235
  9.1 9.8 %collective-permute-start.3 = (bf16[17,16,128]{2,1,0:T(8,128)(2,1)S(1)}, bf16[17,16,128]{2,1,0:T(8,128)(2,1)S(1)}, u32[]{:S(2)}, u32[]{:S(2)}) collective-permute-start(bf16[17,16,128]{2,1,0:T(8,128)(2,1)S(1)} %get-tuple-element.29), channel_id=1, source_target_pairs={{0,14},{2,12},{4,10},{6,8},{8,6},{10,4},{12,2},{14,0},{1,15},{3,13... | collective-permute-start | bytes 208904 | tf_op jit(solution)/shard_map/ppermute | solution.py:235
  11.5 7.4 %collective-permute-start.4 = (bf16[17,16,128]{2,1,0:T(8,128)(2,1)S(1)}, bf16[17,16,128]{2,1,0:T(8,128)(2,1)S(1)}, u32[]{:S(2)}, u32[]{:S(2)}) collective-permute-start(bf16[17,16,128]{2,1,0:T(8,128)(2,1)S(1)} %get-tuple-element.30), channel_id=1, source_target_pairs={{0,12},{2,14},{4,8},{6,10},{8,4},{10,6},{12,0},{14,2},{1,13},{3,15... | collective-permute-start | bytes 208904 | tf_op jit(solution)/shard_map/ppermute | solution.py:235
  13.0 6.2 %collective-permute-start.5 = (bf16[34,16,128]{2,1,0:T(8,128)(2,1)S(1)}, bf16[34,16,128]{2,1,0:T(8,128)(2,1)S(1)}, u32[]{:S(2)}, u32[]{:S(2)}) collective-permute-start(bf16[34,16,128]{2,1,0:T(8,128)(2,1)S(1)} %pad_maximum_fusion.2), channel_id=1, source_target_pairs={{0,2},{2,0},{4,6},{6,4},{8,10},{10,8},{12,14},{14,12},{1,3},{3,1},... | collective-permute-start | bytes 417800 | tf_op jit(solution)/shard_map/ppermute | solution.py:235
  18.8 1.6 %collective-permute-start.7 = (bf16[68,16,128]{2,1,0:T(8,128)(2,1)S(1)}, bf16[68,16,128]{2,1,0:T(8,128)(2,1)S(1)}, u32[]{:S(2)}, u32[]{:S(2)}) collective-permute-start(bf16[68,16,128]{2,1,0:T(8,128)(2,1)S(1)} %pad_maximum_fusion.1), channel_id=1, source_target_pairs={{0,1},{1,0},{2,3},{3,2},{4,5},{5,4},{6,7},{7,6},{8,9},{9,8},{10,11... | collective-permute-start | bytes 835592 | tf_op jit(solution)/shard_map/ppermute | solution.py:235
  19.1 2.3 %collective-permute-start.6 = (bf16[68,16,128]{2,1,0:T(8,128)(2,1)S(1)}, bf16[68,16,128]{2,1,0:T(8,128)(2,1)S(1)}, u32[]{:S(2)}, u32[]{:S(2)}) collective-permute-start(bf16[68,16,128]{2,1,0:T(8,128)(2,1)S(1)} %pad_maximum_fusion), channel_id=1, source_target_pairs={{0,1},{1,0},{2,3},{3,2},{4,5},{5,4},{6,7},{7,6},{8,9},{9,8},{10,11... | collective-permute-start | bytes 835592 | tf_op jit(solution)/shard_map/ppermute | solution.py:235

commit v24 on v23

--- a/solution.py
+++ b/solution.py
@@ -10,7 +10,7 @@
 LANES = 128
 DIGITS = 3
 SENDS = ((4,), (2, 3), (5,), (7,), (6,), (1,), (0,))
-PARTNERS = (4, 2, 0, 5, 7, 6, 1, 3)
+PARTNERS = (4, 2, 0, 6, 5, 7, 1, 3)
 WHOLE = pl.BlockSpec(memory_space=pltpu.VMEM)
 SCALAR = pl.BlockSpec(memory_space=pltpu.SMEM)
 

time: 33.6 us -> 33.9 us (level)
  transfers between devices with their start and end apart: 8 -> 8, of which waited for: 3 -> 4; matrix products, arithmetic and copies ran while one was open for 1% -> 1% of each run, Pallas kernels for 3% -> 3%
where the time goes in v24:
time: 33.9 us; the launch traced here: 33.7 us
  starting transfers between devices  13.3 us (39%)
  blocking collectives  10.3 us (30%)
  waiting for transfers between devices  5 us (15%)
  Pallas kernels  3.35 us (10%)
  other arithmetic  0.84 us (2%)
  between operations  0.74 us (2%)
    ppermute x8, starting transfers between devices, from_partner(): lax.ppermute(value, axis, [(i, i ^ k) for i in range(lax.axis_size(axis))])  13.3 us
    all_to_all x1, blocking collectives, local(): results = lax.all_to_all(results, 'shard', 0, 0, tiled=True)  10.3 us
    ppermute x8, waiting for transfers between devices, from_partner(): lax.ppermute(value, axis, [(i, i ^ k) for i in range(lax.axis_size(axis))])  5 us
    pallas_call x1, Pallas kernels, local(): pl.pallas_call(functools.partial(near_kernel, rows_all, owner_map.shape[0...  0.97 us
    pallas_call x1, Pallas kernels, local(): pl.pallas_call(functools.partial(far_kernel, rows_all, tiles), out_shape=...  0.96 us
    concatenate x1, other arithmetic, local(): ints = jnp.concatenate([owner_map, cluster_id, item_order]).reshape(1, -1)  0.76 us
    pallas_call x1, Pallas kernels, local(): pl.pallas_call(functools.partial(pick_kernel, order, parts), out_shape=[j...  0.72 us
  transfers between devices with their start and end apart: 8, of which 4 were waited for; matrix products, arithmetic and copies ran while one was open for 1% of the time, Pallas kernels for 3%

profile of v24, /device:TPU:0, one launch (start us, length us, event | category | flops | bytes accessed | tf_op | source)
XLA Modules:
  0.0 33.7 jit_solution(380831393717616238)
XLA Ops:
  0.6 0.0 copy-start
  0.6 0.8 %pad_add_fusion = s32[512]{0:T(512)S(1)} fusion(s32[128]{0:T(128)} %param.6, s32[128]{0:T(128)} %param.5, s32[256]{0:T(256)} %param.7), kind=kLoop, calls=%fused_computation.10 | loop fusion | flops 1024 | bytes 4096 | tf_op jit(solution)/shard_map/concatenate | solution.py:279
  1.4 0.3 slots.1
  1.7 0.0 copy-done
  1.7 0.4 %pack.1 = (bf16[17,16,128]{2,1,0:T(8,128)(2,1)S(1)}, bf16[34,16,128]{2,1,0:T(8,128)(2,1)S(1)}, bf16[17,16,128]{2,1,0:T(8,128)(2,1)S(1)}, bf16[17,16,128]{2,1,0:T...) custom-call(s32[1,128]{1,0:T(1,128)S(1)} %get-tuple-element.23.slot_, ...), custom_call_target="tpu_custom_call" | custom-call | tf_op jit(solution)/shard_map/pack/pallas_call | solution.py:299
  2.1 4.1 %collective-permute-start = (bf16[17,16,128]{2,1,0:T(8,128)(2,1)S(1)}, bf16[17,16,128]{2,1,0:T(8,128)(2,1)S(1)}, u32[]{:S(2)}, u32[]{:S(2)}) collective-permute-start(bf16[17,16,128]{2,1,0:T(8,128)(2,1)S(1)} %get-tuple-element.25), channel_id=1, source_target_pairs={{0,8},{2,10},{4,12},{6,14},{8,0},{10,2},{12,4},{14,6},{1,9},{3,11}... | collective-permute-start | bytes 208904 | tf_op jit(solution)/shard_map/ppermute | solution.py:235
  6.2 1.6 %collective-permute-start.1 = (bf16[34,16,128]{2,1,0:T(8,128)(2,1)S(1)}, bf16[34,16,128]{2,1,0:T(8,128)(2,1)S(1)}, u32[]{:S(2)}, u32[]{:S(2)}) collective-permute-start(bf16[34,16,128]{2,1,0:T(8,128)(2,1)S(1)} %get-tuple-element.26), channel_id=1, source_target_pairs={{0,4},{2,6},{4,0},{6,2},{8,12},{10,14},{12,8},{14,10},{1,5},{3,7},... | collective-permute-start | bytes 417800 | tf_op jit(solution)/shard_map/ppermute | solution.py:235
  7.8 0.0 collective-permute-start.2
  7.8 2.8 %collective-permute-start.3 = (bf16[17,16,128]{2,1,0:T(8,128)(2,1)S(1)}, bf16[17,16,128]{2,1,0:T(8,128)(2,1)S(1)}, u32[]{:S(2)}, u32[]{:S(2)}) collective-permute-start(bf16[17,16,128]{2,1,0:T(8,128)(2,1)S(1)} %get-tuple-element.29), channel_id=1, source_target_pairs={{0,10},{2,8},{4,14},{6,12},{8,2},{10,0},{12,6},{14,4},{1,11},{3,9}... | collective-permute-start | bytes 208904 | tf_op jit(solution)/shard_map/ppermute | solution.py:235
  10.6 1.9 %collective-permute-start.4 = (bf16[17,16,128]{2,1,0:T(8,128)(2,1)S(1)}, bf16[17,16,128]{2,1,0:T(8,128)(2,1)S(1)}, u32[]{:S(2)}, u32[]{:S(2)}) collective-permute-start(bf16[17,16,128]{2,1,0:T(8,128)(2,1)S(1)} %get-tuple-element.30), channel_id=1, source_target_pairs={{0,14},{2,12},{4,10},{6,8},{8,6},{10,4},{12,2},{14,0},{1,15},{3,13... | collective-permute-start | bytes 208904 | tf_op jit(solution)/shard_map/ppermute | solution.py:235
  12.6 0.0 collective-permute-done
  12.6 0.1 collective-permute-done.1
  12.7 2.8 %collective-permute-start.5 = (bf16[34,16,128]{2,1,0:T(8,128)(2,1)S(1)}, bf16[34,16,128]{2,1,0:T(8,128)(2,1)S(1)}, u32[]{:S(2)}, u32[]{:S(2)}) collective-permute-start(bf16[34,16,128]{2,1,0:T(8,128)(2,1)S(1)} %pad_maximum_fusion.2), channel_id=1, source_target_pairs={{0,2},{2,0},{4,6},{6,4},{8,10},{10,8},{12,14},{14,12},{1,3},{3,1},... | collective-permute-start | bytes 417800 | tf_op jit(solution)/shard_map/ppermute | solution.py:235
  15.5 0.0 collective-permute-done.2
  15.5 0.1 collective-permute-start.7
  15.6 3.6 %collective-permute-done.3 = bf16[17,16,128]{2,1,0:T(8,128)(2,1)S(1)} collective-permute-done((bf16[17,16,128]{2,1,0:T(8,128)(2,1)S(1)}, bf16[17,16,128]{2,1,0:T(8,128)(2,1)S(1)}, u32[]{:S(2)}, u32[]{:S(2)}) %collective-permute-start.3) | collective-permute-done | bytes 69664 | tf_op jit(solution)/shard_map/ppermute | solution.py:235
  19.2 0.0 collective-permute-done.4
  19.2 0.9 %collective-permute-done.5 = bf16[34,16,128]{2,1,0:T(8,128)(2,1)S(1)} collective-permute-done((bf16[34,16,128]{2,1,0:T(8,128)(2,1)S(1)}, bf16[34,16,128]{2,1,0:T(8,128)(2,1)S(1)}, u32[]{:S(2)}, u32[]{:S(2)}) %collective-permute-start.5) | collective-permute-done | bytes 139296 | tf_op jit(solution)/shard_map/ppermute | solution.py:235
  20.1 0.1 collective-permute-start.6
  20.2 0.0 collective-permute-done.7.other_ref
  20.3 1.0 %near.1 = (bf16[1024,256]{1,0:T(8,128)(2,1)S(1)}, s32[288,128]{1,0:T(8,128)S(1)}, s32[2,256]{1,0:T(2,128)S(1)}, f32[1,256]{1,0:T(1,128)S(1)}, f32[288,1024]{1,0:T(8,128)S(1)}, /*index=5*/f32[288,128]{1,0:T(8,128)S(1)}) custom-call(s32[1]{0:T(128)} %bitcast.me_ref, s32[1,512]{1,0:T(1,128)S(1)} %bitcast.6, ...), custom_call_target="tpu_custom_call" | custom-call | flops 268435456 | bytes 1048576 | tf_op jit(solution)/shard_map/near/pallas_call | solution.py:313
  21.2 0.5 %collective-permute-done.6.other_ref = bf16[68,16,128]{2,1,0:T(8,128)(2,1)S(1)} collective-permute-done((bf16[68,16,128]{2,1,0:T(8,128)(2,1)S(1)}, bf16[68,16,128]{2,1,0:T(8,128)(2,1)S(1)}, u32[]{:S(2)}, u32[]{:S(2)}) %collective-permute-start.6) | collective-permute-done | bytes 278560 | tf_op jit(solution)/shard_map/ppermute | solution.py:235
  21.7 1.0 %far.1 = (f32[8,2,256]{2,1,0:T(2,128)S(1)}, f32[1,32]{1,0:T(1,128)S(1)}) custom-call(bf16[136,16,128]{2,1,0:T(8,128)(2,1)S(1)} %constant_dynamic-update-slice_fusion.query_ref, bf16[68,16,128]{2,1,0:T(8,128)(2,1)S(1)} %collective-permute-done.6.other_ref, bf16[1024,256]{1,0:T(8,128)(2,1)S(1)} %get-tuple-element.32.query_t_ref, ...), custom_call_target="tpu_custom_call" | custom-call | flops 268435456 | bytes 1048576 | tf_op jit(solution)/shard_map/far/pallas_call | solution.py:329
  22.7 10.3 %all_to_all.5.result_ref = f32[8,2,256]{2,1,0:T(2,128)S(1)} all-to-all(f32[8,2,256]{2,1,0:T(2,128)S(1)} %get-tuple-element.38), channel_id=1, replica_groups=mesh['groups'=2,'shard'=8,'sub'=2] {'shard'}, dimensions={0} | all-to-all | bytes 32768 | tf_op jit(solution)/shard_map/all_to_all | solution.py:341
  33.0 0.7 %pick.1 = (f32[1,128]{1,0:T(1,128)}, f32[1,128]{1,0:T(1,128)}, f32[1,32]{1,0:T(1,128)}) custom-call(s32[1]{0:T(128)} %bitcast.me_ref, s32[1,128]{1,0:T(1,128)S(1)} %get-tuple-element.23.slot_ref, f32[8,2,256]{2,1,0:T(2,128)S(1)} %all_to_all.5.result_ref, f32[1,32]{1,0:T(1,128)S(1)} %get-tuple-element.39.norm_ref), custom_call_target="tpu_custom_call" | custom-call | tf_op jit(solution)/shard_map/pick/pallas_call | solution.py:342
  (10 shorter events, 0.2 us)
Async XLA Ops:
  0.6 1.0 %copy-start = (bf16[128,1024]{1,0:T(8,128)(2,1)S(1)}, bf16[128,1024]{1,0:T(8,128)(2,1)}, u32[]{:S(2)}) copy-start(bf16[128,1024]{1,0:T(8,128)(2,1)} %embed_ref.1) | copy-start | bytes 786436
  2.1 10.4 %collective-permute-start = (bf16[17,16,128]{2,1,0:T(8,128)(2,1)S(1)}, bf16[17,16,128]{2,1,0:T(8,128)(2,1)S(1)}, u32[]{:S(2)}, u32[]{:S(2)}) collective-permute-start(bf16[17,16,128]{2,1,0:T(8,128)(2,1)S(1)} %get-tuple-element.25), channel_id=1, source_target_pairs={{0,8},{2,10},{4,12},{6,14},{8,0},{10,2},{12,4},{14,6},{1,9},{3,11}... | collective-permute-start | bytes 208904 | tf_op jit(solution)/shard_map/ppermute | solution.py:235
  6.2 6.4 %collective-permute-start.1 = (bf16[34,16,128]{2,1,0:T(8,128)(2,1)S(1)}, bf16[34,16,128]{2,1,0:T(8,128)(2,1)S(1)}, u32[]{:S(2)}, u32[]{:S(2)}) collective-permute-start(bf16[34,16,128]{2,1,0:T(8,128)(2,1)S(1)} %get-tuple-element.26), channel_id=1, source_target_pairs={{0,4},{2,6},{4,0},{6,2},{8,12},{10,14},{12,8},{14,10},{1,5},{3,7},... | collective-permute-start | bytes 417800 | tf_op jit(solution)/shard_map/ppermute | solution.py:235
  7.8 7.7 %collective-permute-start.2 = (bf16[17,16,128]{2,1,0:T(8,128)(2,1)S(1)}, bf16[17,16,128]{2,1,0:T(8,128)(2,1)S(1)}, u32[]{:S(2)}, u32[]{:S(2)}) collective-permute-start(bf16[17,16,128]{2,1,0:T(8,128)(2,1)S(1)} %get-tuple-element.28), channel_id=1, source_target_pairs={{0,12},{2,14},{4,8},{6,10},{8,4},{10,6},{12,0},{14,2},{1,13},{3,15... | collective-permute-start | bytes 208904 | tf_op jit(solution)/shard_map/ppermute | solution.py:235
  7.8 11.4 %collective-permute-start.3 = (bf16[17,16,128]{2,1,0:T(8,128)(2,1)S(1)}, bf16[17,16,128]{2,1,0:T(8,128)(2,1)S(1)}, u32[]{:S(2)}, u32[]{:S(2)}) collective-permute-start(bf16[17,16,128]{2,1,0:T(8,128)(2,1)S(1)} %get-tuple-element.29), channel_id=1, source_target_pairs={{0,10},{2,8},{4,14},{6,12},{8,2},{10,0},{12,6},{14,4},{1,11},{3,9}... | collective-permute-start | bytes 208904 | tf_op jit(solution)/shard_map/ppermute | solution.py:235
  10.6 8.6 %collective-permute-start.4 = (bf16[17,16,128]{2,1,0:T(8,128)(2,1)S(1)}, bf16[17,16,128]{2,1,0:T(8,128)(2,1)S(1)}, u32[]{:S(2)}, u32[]{:S(2)}) collective-permute-start(bf16[17,16,128]{2,1,0:T(8,128)(2,1)S(1)} %get-tuple-element.30), channel_id=1, source_target_pairs={{0,14},{2,12},{4,10},{6,8},{8,6},{10,4},{12,2},{14,0},{1,15},{3,13... | collective-permute-start | bytes 208904 | tf_op jit(solution)/shard_map/ppermute | solution.py:235
  12.7 7.4 %collective-permute-start.5 = (bf16[34,16,128]{2,1,0:T(8,128)(2,1)S(1)}, bf16[34,16,128]{2,1,0:T(8,128)(2,1)S(1)}, u32[]{:S(2)}, u32[]{:S(2)}) collective-permute-start(bf16[34,16,128]{2,1,0:T(8,128)(2,1)S(1)} %pad_maximum_fusion.2), channel_id=1, source_target_pairs={{0,2},{2,0},{4,6},{6,4},{8,10},{10,8},{12,14},{14,12},{1,3},{3,1},... | collective-permute-start | bytes 417800 | tf_op jit(solution)/shard_map/ppermute | solution.py:235
  15.5 4.7 %collective-permute-start.7 = (bf16[68,16,128]{2,1,0:T(8,128)(2,1)S(1)}, bf16[68,16,128]{2,1,0:T(8,128)(2,1)S(1)}, u32[]{:S(2)}, u32[]{:S(2)}) collective-permute-start(bf16[68,16,128]{2,1,0:T(8,128)(2,1)S(1)} %pad_maximum_fusion.1), channel_id=1, source_target_pairs={{0,1},{1,0},{2,3},{3,2},{4,5},{5,4},{6,7},{7,6},{8,9},{9,8},{10,11... | collective-permute-start | bytes 835592 | tf_op jit(solution)/shard_map/ppermute | solution.py:235
  20.1 1.6 %collective-permute-start.6 = (bf16[68,16,128]{2,1,0:T(8,128)(2,1)S(1)}, bf16[68,16,128]{2,1,0:T(8,128)(2,1)S(1)}, u32[]{:S(2)}, u32[]{:S(2)}) collective-permute-start(bf16[68,16,128]{2,1,0:T(8,128)(2,1)S(1)} %pad_maximum_fusion), channel_id=1, source_target_pairs={{0,1},{1,0},{2,3},{3,2},{4,5},{5,4},{6,7},{7,6},{8,9},{9,8},{10,11... | collective-permute-start | bytes 835592 | tf_op jit(solution)/shard_map/ppermute | solution.py:235

commit v25 on v24

--- a/solution.py
+++ b/solution.py
@@ -10,7 +10,7 @@
 LANES = 128
 DIGITS = 3
 SENDS = ((4,), (2, 3), (5,), (7,), (6,), (1,), (0,))
-PARTNERS = (4, 2, 0, 6, 5, 7, 1, 3)
+PARTNERS = (2, 4, 5, 0, 7, 6, 1, 3)
 WHOLE = pl.BlockSpec(memory_space=pltpu.VMEM)
 SCALAR = pl.BlockSpec(memory_space=pltpu.SMEM)
 

time: 33.9 us -> 34.1 us (level)
  waiting for transfers between devices: 5 us -> 5.86 us
  starting transfers between devices: 13.3 us -> 12.9 us
    ppermute x8, waiting for transfers between devices: 5 us -> 5.86 us  [from_partner(): lax.ppermute(value, axis, [(i, i ^ k) for i in range(lax.axis_size(axis))])]
    ppermute x8, starting transfers between devices: 13.3 us -> 12.9 us  [from_partner(): lax.ppermute(value, axis, [(i, i ^ k) for i in range(lax.axis_size(axis))])]
  transfers between devices with their start and end apart: 8 -> 8, of which waited for: 4 -> 2; matrix products, arithmetic and copies ran while one was open for 1% -> 1% of each run, Pallas kernels for 3% -> 3%
where the time goes in v25:
time: 34.1 us; the launch traced here: 33.9 us
  starting transfers between devices  12.9 us (38%)
  blocking collectives  10 us (29%)
  waiting for transfers between devices  5.86 us (17%)
  Pallas kernels  3.35 us (10%)
  other arithmetic  0.85 us (2%)
  between operations  0.76 us (2%)
    ppermute x8, starting transfers between devices, from_partner(): lax.ppermute(value, axis, [(i, i ^ k) for i in range(lax.axis_size(axis))])  12.9 us
    all_to_all x1, blocking collectives, local(): results = lax.all_to_all(results, 'shard', 0, 0, tiled=True)  10 us
    ppermute x8, waiting for transfers between devices, from_partner(): lax.ppermute(value, axis, [(i, i ^ k) for i in range(lax.axis_size(axis))])  5.86 us
    pallas_call x1, Pallas kernels, local(): pl.pallas_call(functools.partial(near_kernel, rows_all, owner_map.shape[0...  0.97 us
    pallas_call x1, Pallas kernels, local(): pl.pallas_call(functools.partial(far_kernel, rows_all, tiles), out_shape=...  0.97 us
    concatenate x1, other arithmetic, local(): ints = jnp.concatenate([owner_map, cluster_id, item_order]).reshape(1, -1)  0.76 us
    pallas_call x1, Pallas kernels, local(): pl.pallas_call(functools.partial(pick_kernel, order, parts), out_shape=[j...  0.72 us
  transfers between devices with their start and end apart: 8, of which 2 were waited for; matrix products, arithmetic and copies ran while one was open for 1% of the time, Pallas kernels for 3%

profile of v25, /device:TPU:0, one launch (start us, length us, event | category | flops | bytes accessed | tf_op | source)
XLA Modules:
  0.0 33.9 jit_solution(16559698199236930895)
XLA Ops:
  0.6 0.0 copy-start
  0.6 0.8 %pad_add_fusion = s32[512]{0:T(512)S(1)} fusion(s32[128]{0:T(128)} %param.6, s32[128]{0:T(128)} %param.5, s32[256]{0:T(256)} %param.7), kind=kLoop, calls=%fused_computation.10 | loop fusion | flops 1024 | bytes 4096 | tf_op jit(solution)/shard_map/concatenate | solution.py:279
  1.4 0.3 slots.1
  1.7 0.0 copy-done
  1.7 0.4 %pack.1 = (bf16[17,16,128]{2,1,0:T(8,128)(2,1)S(1)}, bf16[34,16,128]{2,1,0:T(8,128)(2,1)S(1)}, bf16[17,16,128]{2,1,0:T(8,128)(2,1)S(1)}, bf16[17,16,128]{2,1,0:T...) custom-call(s32[1,128]{1,0:T(1,128)S(1)} %get-tuple-element.23.slot_, ...), custom_call_target="tpu_custom_call" | custom-call | tf_op jit(solution)/shard_map/pack/pallas_call | solution.py:299
  2.1 3.1 %collective-permute-start = (bf16[34,16,128]{2,1,0:T(8,128)(2,1)S(1)}, bf16[34,16,128]{2,1,0:T(8,128)(2,1)S(1)}, u32[]{:S(2)}, u32[]{:S(2)}) collective-permute-start(bf16[34,16,128]{2,1,0:T(8,128)(2,1)S(1)} %get-tuple-element.25), channel_id=1, source_target_pairs={{0,4},{2,6},{4,0},{6,2},{8,12},{10,14},{12,8},{14,10},{1,5},{3,7},... | collective-permute-start | bytes 417800 | tf_op jit(solution)/shard_map/ppermute | solution.py:235
  5.2 2.6 %collective-permute-start.1 = (bf16[17,16,128]{2,1,0:T(8,128)(2,1)S(1)}, bf16[17,16,128]{2,1,0:T(8,128)(2,1)S(1)}, u32[]{:S(2)}, u32[]{:S(2)}) collective-permute-start(bf16[17,16,128]{2,1,0:T(8,128)(2,1)S(1)} %get-tuple-element.26), channel_id=1, source_target_pairs={{0,8},{2,10},{4,12},{6,14},{8,0},{10,2},{12,4},{14,6},{1,9},{3,11}... | collective-permute-start | bytes 208904 | tf_op jit(solution)/shard_map/ppermute | solution.py:235
  7.8 1.3 %collective-permute-start.2 = (bf16[17,16,128]{2,1,0:T(8,128)(2,1)S(1)}, bf16[17,16,128]{2,1,0:T(8,128)(2,1)S(1)}, u32[]{:S(2)}, u32[]{:S(2)}) collective-permute-start(bf16[17,16,128]{2,1,0:T(8,128)(2,1)S(1)} %get-tuple-element.27), channel_id=1, source_target_pairs={{0,10},{2,8},{4,14},{6,12},{8,2},{10,0},{12,6},{14,4},{1,11},{3,9}... | collective-permute-start | bytes 208904 | tf_op jit(solution)/shard_map/ppermute | solution.py:235
  9.1 2.4 %collective-permute-start.3 = (bf16[17,16,128]{2,1,0:T(8,128)(2,1)S(1)}, bf16[17,16,128]{2,1,0:T(8,128)(2,1)S(1)}, u32[]{:S(2)}, u32[]{:S(2)}) collective-permute-start(bf16[17,16,128]{2,1,0:T(8,128)(2,1)S(1)} %get-tuple-element.29), channel_id=1, source_target_pairs={{0,14},{2,12},{4,10},{6,8},{8,6},{10,4},{12,2},{14,0},{1,15},{3,13... | collective-permute-start | bytes 208904 | tf_op jit(solution)/shard_map/ppermute | solution.py:235
  11.5 1.4 %collective-permute-start.4 = (bf16[17,16,128]{2,1,0:T(8,128)(2,1)S(1)}, bf16[17,16,128]{2,1,0:T(8,128)(2,1)S(1)}, u32[]{:S(2)}, u32[]{:S(2)}) collective-permute-start(bf16[17,16,128]{2,1,0:T(8,128)(2,1)S(1)} %get-tuple-element.30), channel_id=1, source_target_pairs={{0,12},{2,14},{4,8},{6,10},{8,4},{10,6},{12,0},{14,2},{1,13},{3,15... | collective-permute-start | bytes 208904 | tf_op jit(solution)/shard_map/ppermute | solution.py:235
  12.9 0.0 collective-permute-done
  12.9 1.6 %collective-permute-start.5 = (bf16[34,16,128]{2,1,0:T(8,128)(2,1)S(1)}, bf16[34,16,128]{2,1,0:T(8,128)(2,1)S(1)}, u32[]{:S(2)}, u32[]{:S(2)}) collective-permute-start(bf16[34,16,128]{2,1,0:T(8,128)(2,1)S(1)} %pad_maximum_fusion.2), channel_id=1, source_target_pairs={{0,2},{2,0},{4,6},{6,4},{8,10},{10,8},{12,14},{14,12},{1,3},{3,1},... | collective-permute-start | bytes 417800 | tf_op jit(solution)/shard_map/ppermute | solution.py:235
  14.5 0.0 collective-permute-done.1
  14.5 5.0 %collective-permute-done.2 = bf16[17,16,128]{2,1,0:T(8,128)(2,1)S(1)} collective-permute-done((bf16[17,16,128]{2,1,0:T(8,128)(2,1)S(1)}, bf16[17,16,128]{2,1,0:T(8,128)(2,1)S(1)}, u32[]{:S(2)}, u32[]{:S(2)}) %collective-permute-start.2) | collective-permute-done | bytes 69664 | tf_op jit(solution)/shard_map/ppermute | solution.py:235
  19.6 0.1 collective-permute-start.7
  19.7 0.0 collective-permute-done.3
  19.7 0.0 collective-permute-done.4
  19.7 0.0 collective-permute-done.5
  19.8 0.6 %collective-permute-start.6 = (bf16[68,16,128]{2,1,0:T(8,128)(2,1)S(1)}, bf16[68,16,128]{2,1,0:T(8,128)(2,1)S(1)}, u32[]{:S(2)}, u32[]{:S(2)}) collective-permute-start(bf16[68,16,128]{2,1,0:T(8,128)(2,1)S(1)} %pad_maximum_fusion), channel_id=1, source_target_pairs={{0,1},{1,0},{2,3},{3,2},{4,5},{5,4},{6,7},{7,6},{8,9},{9,8},{10,11... | collective-permute-start | bytes 835592 | tf_op jit(solution)/shard_map/ppermute | solution.py:235
  20.4 0.8 %collective-permute-done.7.other_ref = bf16[68,16,128]{2,1,0:T(8,128)(2,1)S(1)} collective-permute-done((bf16[68,16,128]{2,1,0:T(8,128)(2,1)S(1)}, bf16[68,16,128]{2,1,0:T(8,128)(2,1)S(1)}, u32[]{:S(2)}, u32[]{:S(2)}) %collective-permute-start.7) | collective-permute-done | bytes 278560 | tf_op jit(solution)/shard_map/ppermute | solution.py:235
  21.2 1.0 %near.1 = (bf16[1024,256]{1,0:T(8,128)(2,1)S(1)}, s32[288,128]{1,0:T(8,128)S(1)}, s32[2,256]{1,0:T(2,128)S(1)}, f32[1,256]{1,0:T(1,128)S(1)}, f32[288,1024]{1,0:T(8,128)S(1)}, /*index=5*/f32[288,128]{1,0:T(8,128)S(1)}) custom-call(s32[1]{0:T(128)} %bitcast.me_ref, s32[1,512]{1,0:T(1,128)S(1)} %bitcast.6, ...), custom_call_target="tpu_custom_call" | custom-call | flops 268435456 | bytes 1048576 | tf_op jit(solution)/shard_map/near/pallas_call | solution.py:313
  22.2 0.0 collective-permute-done.6.other_ref
  22.2 1.0 %far.1 = (f32[8,2,256]{2,1,0:T(2,128)S(1)}, f32[1,32]{1,0:T(1,128)S(1)}) custom-call(bf16[136,16,128]{2,1,0:T(8,128)(2,1)S(1)} %constant_dynamic-update-slice_fusion.query_ref, bf16[68,16,128]{2,1,0:T(8,128)(2,1)S(1)} %collective-permute-done.6.other_ref, bf16[1024,256]{1,0:T(8,128)(2,1)S(1)} %get-tuple-element.32.query_t_ref, ...), custom_call_target="tpu_custom_call" | custom-call | flops 268435456 | bytes 1048576 | tf_op jit(solution)/shard_map/far/pallas_call | solution.py:329
  23.1 10.0 %all_to_all.5.result_ref = f32[8,2,256]{2,1,0:T(2,128)S(1)} all-to-all(f32[8,2,256]{2,1,0:T(2,128)S(1)} %get-tuple-element.38), channel_id=1, replica_groups=mesh['groups'=2,'shard'=8,'sub'=2] {'shard'}, dimensions={0} | all-to-all | bytes 32768 | tf_op jit(solution)/shard_map/all_to_all | solution.py:341
  33.2 0.7 %pick.1 = (f32[1,128]{1,0:T(1,128)}, f32[1,128]{1,0:T(1,128)}, f32[1,32]{1,0:T(1,128)}) custom-call(s32[1]{0:T(128)} %bitcast.me_ref, s32[1,128]{1,0:T(1,128)S(1)} %get-tuple-element.23.slot_ref, f32[8,2,256]{2,1,0:T(2,128)S(1)} %all_to_all.5.result_ref, f32[1,32]{1,0:T(1,128)S(1)} %get-tuple-element.39.norm_ref), custom_call_target="tpu_custom_call" | custom-call | tf_op jit(solution)/shard_map/pick/pallas_call | solution.py:342
  (10 shorter events, 0.2 us)
Async XLA Ops:
  0.6 1.0 %copy-start = (bf16[128,1024]{1,0:T(8,128)(2,1)S(1)}, bf16[128,1024]{1,0:T(8,128)(2,1)}, u32[]{:S(2)}) copy-start(bf16[128,1024]{1,0:T(8,128)(2,1)} %embed_ref.1) | copy-start | bytes 786436
  2.1 10.7 %collective-permute-start = (bf16[34,16,128]{2,1,0:T(8,128)(2,1)S(1)}, bf16[34,16,128]{2,1,0:T(8,128)(2,1)S(1)}, u32[]{:S(2)}, u32[]{:S(2)}) collective-permute-start(bf16[34,16,128]{2,1,0:T(8,128)(2,1)S(1)} %get-tuple-element.25), channel_id=1, source_target_pairs={{0,4},{2,6},{4,0},{6,2},{8,12},{10,14},{12,8},{14,10},{1,5},{3,7},... | collective-permute-start | bytes 417800 | tf_op jit(solution)/shard_map/ppermute | solution.py:235
  5.2 9.3 %collective-permute-start.1 = (bf16[17,16,128]{2,1,0:T(8,128)(2,1)S(1)}, bf16[17,16,128]{2,1,0:T(8,128)(2,1)S(1)}, u32[]{:S(2)}, u32[]{:S(2)}) collective-permute-start(bf16[17,16,128]{2,1,0:T(8,128)(2,1)S(1)} %get-tuple-element.26), channel_id=1, source_target_pairs={{0,8},{2,10},{4,12},{6,14},{8,0},{10,2},{12,4},{14,6},{1,9},{3,11}... | collective-permute-start | bytes 208904 | tf_op jit(solution)/shard_map/ppermute | solution.py:235
  7.8 11.7 %collective-permute-start.2 = (bf16[17,16,128]{2,1,0:T(8,128)(2,1)S(1)}, bf16[17,16,128]{2,1,0:T(8,128)(2,1)S(1)}, u32[]{:S(2)}, u32[]{:S(2)}) collective-permute-start(bf16[17,16,128]{2,1,0:T(8,128)(2,1)S(1)} %get-tuple-element.27), channel_id=1, source_target_pairs={{0,10},{2,8},{4,14},{6,12},{8,2},{10,0},{12,6},{14,4},{1,11},{3,9}... | collective-permute-start | bytes 208904 | tf_op jit(solution)/shard_map/ppermute | solution.py:235
  9.1 10.6 %collective-permute-start.3 = (bf16[17,16,128]{2,1,0:T(8,128)(2,1)S(1)}, bf16[17,16,128]{2,1,0:T(8,128)(2,1)S(1)}, u32[]{:S(2)}, u32[]{:S(2)}) collective-permute-start(bf16[17,16,128]{2,1,0:T(8,128)(2,1)S(1)} %get-tuple-element.29), channel_id=1, source_target_pairs={{0,14},{2,12},{4,10},{6,8},{8,6},{10,4},{12,2},{14,0},{1,15},{3,13... | collective-permute-start | bytes 208904 | tf_op jit(solution)/shard_map/ppermute | solution.py:235
  11.5 8.2 %collective-permute-start.4 = (bf16[17,16,128]{2,1,0:T(8,128)(2,1)S(1)}, bf16[17,16,128]{2,1,0:T(8,128)(2,1)S(1)}, u32[]{:S(2)}, u32[]{:S(2)}) collective-permute-start(bf16[17,16,128]{2,1,0:T(8,128)(2,1)S(1)} %get-tuple-element.30), channel_id=1, source_target_pairs={{0,12},{2,14},{4,8},{6,10},{8,4},{10,6},{12,0},{14,2},{1,13},{3,15... | collective-permute-start | bytes 208904 | tf_op jit(solution)/shard_map/ppermute | solution.py:235
  12.9 6.8 %collective-permute-start.5 = (bf16[34,16,128]{2,1,0:T(8,128)(2,1)S(1)}, bf16[34,16,128]{2,1,0:T(8,128)(2,1)S(1)}, u32[]{:S(2)}, u32[]{:S(2)}) collective-permute-start(bf16[34,16,128]{2,1,0:T(8,128)(2,1)S(1)} %pad_maximum_fusion.2), channel_id=1, source_target_pairs={{0,2},{2,0},{4,6},{6,4},{8,10},{10,8},{12,14},{14,12},{1,3},{3,1},... | collective-permute-start | bytes 417800 | tf_op jit(solution)/shard_map/ppermute | solution.py:235
  19.6 1.6 %collective-permute-start.7 = (bf16[68,16,128]{2,1,0:T(8,128)(2,1)S(1)}, bf16[68,16,128]{2,1,0:T(8,128)(2,1)S(1)}, u32[]{:S(2)}, u32[]{:S(2)}) collective-permute-start(bf16[68,16,128]{2,1,0:T(8,128)(2,1)S(1)} %pad_maximum_fusion.1), channel_id=1, source_target_pairs={{0,1},{1,0},{2,3},{3,2},{4,5},{5,4},{6,7},{7,6},{8,9},{9,8},{10,11... | collective-permute-start | bytes 835592 | tf_op jit(solution)/shard_map/ppermute | solution.py:235
  19.8 2.4 %collective-permute-start.6 = (bf16[68,16,128]{2,1,0:T(8,128)(2,1)S(1)}, bf16[68,16,128]{2,1,0:T(8,128)(2,1)S(1)}, u32[]{:S(2)}, u32[]{:S(2)}) collective-permute-start(bf16[68,16,128]{2,1,0:T(8,128)(2,1)S(1)} %pad_maximum_fusion), channel_id=1, source_target_pairs={{0,1},{1,0},{2,3},{3,2},{4,5},{5,4},{6,7},{7,6},{8,9},{9,8},{10,11... | collective-permute-start | bytes 835592 | tf_op jit(solution)/shard_map/ppermute | solution.py:235

commit v26 on v23

--- a/solution.py
+++ b/solution.py
@@ -184,7 +184,7 @@
 
 
 def far_kernel(
-    rows_all, tiles, query_ref, other_ref, query_t_ref, lows_ref, key_ref, best_ref, sums_ref, counts_ref,
+    rows_all, tiles, summed, me_ref, query_ref, other_ref, query_t_ref, lows_ref, key_ref, best_ref, sums_ref, counts_ref,
     result_ref, norm_ref,
 ):
     query, _ = unpacked(query_ref, tiles)
@@ -206,7 +206,8 @@
     distance = jnp.sum(jnp.transpose(squares), axis=0, keepdims=True)
     result = jnp.concatenate([best, distance], axis=0)
     for owner in range(result_ref.shape[0]):
-        result_ref[owner] = result
+        mine = jnp.where(owner == me_ref[0], 1.0, 0.0) if summed else 1.0
+        result_ref[owner] = result * mine
     norms = jnp.concatenate([norms] * (LANES // norms.shape[0]), axis=0)
     norm_ref[...] = jnp.sum(jnp.transpose(norms), axis=0, keepdims=True)[:, : norm_ref.shape[1]]
 
@@ -327,18 +328,21 @@
         name="near",
     )(me, ints, query, other_first)
     results, norms = pl.pallas_call(
-        functools.partial(far_kernel, rows_all, tiles),
+        functools.partial(far_kernel, rows_all, tiles, direct),
         out_shape=[
             jax.ShapeDtypeStruct((owners, 2, slots), jnp.float32),
             jax.ShapeDtypeStruct((1, clus_dev), jnp.float32),
         ],
-        in_specs=[WHOLE] * 8,
+        in_specs=[SCALAR] + [WHOLE] * 8,
         out_specs=[WHOLE] * 2,
         compiler_params=params,
         cost_estimate=compare_cost,
         name="far",
-    )(query, other_second, *near)
-    results = lax.all_to_all(results, "shard", 0, 0, tiled=True)
+    )(me, query, other_second, *near)
+    if direct:
+        results = lax.psum(results, "shard")
+    else:
+        results = lax.all_to_all(results, "shard", 0, 0, tiled=True)
     best, distance, cohesion = pl.pallas_call(
         functools.partial(pick_kernel, order, parts),
         out_shape=[jax.ShapeDtypeStruct((1, local_rows), jnp.float32)] * 2

time: 33.6 us -> 58 us (1.73)
  blocking collectives: 10.3 us -> 34.8 us
    psum x0 -> x1, blocking collectives: none -> 34.8 us  [local(): results = lax.psum(results, 'shard')]
    all_to_all x1 -> x0, blocking collectives: 10.3 us -> none  [local(): results = lax.all_to_all(results, 'shard', 0, 0, tiled=True)]
  transfers between devices with their start and end apart: 8 -> 8, of which waited for: 3 -> 3; matrix products, arithmetic and copies ran while one was open for 1% -> 0% of each run, Pallas kernels for 3% -> 2%
where the time goes in v26:
time: 58 us; the launch traced here: 57.8 us
  blocking collectives  34.8 us (60%)
  starting transfers between devices  13.1 us (23%)
  waiting for transfers between devices  4.91 us (8%)
  Pallas kernels  3.32 us (6%)
  other arithmetic  0.84 us (1%)
  between operations  0.75 us (1%)
    psum x1, blocking collectives, local(): results = lax.psum(results, 'shard')  34.8 us
    ppermute x8, starting transfers between devices, from_partner(): lax.ppermute(value, axis, [(i, i ^ k) for i in range(lax.axis_size(axis))])  13.1 us
    ppermute x8, waiting for transfers between devices, from_partner(): lax.ppermute(value, axis, [(i, i ^ k) for i in range(lax.axis_size(axis))])  4.91 us
  transfers between devices with their start and end apart: 8, of which 3 were waited for; matrix products, arithmetic and copies ran while one was open for 0% of the time, Pallas kernels for 2%

profile of v26, /device:TPU:0, one launch (start us, length us, event | category | flops | bytes accessed | tf_op | source)
XLA Modules:
  0.0 57.8 jit_solution(7850117002892172241)
XLA Ops:
  0.6 0.0 copy-start
  0.6 0.8 %pad_add_fusion = s32[512]{0:T(512)S(1)} fusion(s32[128]{0:T(128)} %param.6, s32[128]{0:T(128)} %param.5, s32[256]{0:T(256)} %param.7), kind=kLoop, calls=%fused_computation.10 | loop fusion | flops 1024 | bytes 4096 | tf_op jit(solution)/shard_map/concatenate | solution.py:280
  1.4 0.3 slots.1
  1.7 0.0 copy-done
  1.7 0.4 pack.1
  2.1 4.1 %collective-permute-start = (bf16[17,16,128]{2,1,0:T(8,128)(2,1)S(1)}, bf16[17,16,128]{2,1,0:T(8,128)(2,1)S(1)}, u32[]{:S(2)}, u32[]{:S(2)}) collective-permute-start(bf16[17,16,128]{2,1,0:T(8,128)(2,1)S(1)} %get-tuple-element.25), channel_id=1, source_target_pairs={{0,8},{2,10},{4,12},{6,14},{8,0},{10,2},{12,4},{14,6},{1,9},{3,11}... | collective-permute-start | bytes 208904 | tf_op jit(solution)/shard_map/ppermute | solution.py:236
  6.2 1.6 %collective-permute-start.1 = (bf16[34,16,128]{2,1,0:T(8,128)(2,1)S(1)}, bf16[34,16,128]{2,1,0:T(8,128)(2,1)S(1)}, u32[]{:S(2)}, u32[]{:S(2)}) collective-permute-start(bf16[34,16,128]{2,1,0:T(8,128)(2,1)S(1)} %get-tuple-element.26), channel_id=1, source_target_pairs={{0,4},{2,6},{4,0},{6,2},{8,12},{10,14},{12,8},{14,10},{1,5},{3,7},... | collective-permute-start | bytes 417800 | tf_op jit(solution)/shard_map/ppermute | solution.py:236
  7.8 1.3 %collective-permute-start.2 = (bf16[17,16,128]{2,1,0:T(8,128)(2,1)S(1)}, bf16[17,16,128]{2,1,0:T(8,128)(2,1)S(1)}, u32[]{:S(2)}, u32[]{:S(2)}) collective-permute-start(bf16[17,16,128]{2,1,0:T(8,128)(2,1)S(1)} %get-tuple-element.28), channel_id=1, source_target_pairs={{0,10},{2,8},{4,14},{6,12},{8,2},{10,0},{12,6},{14,4},{1,11},{3,9}... | collective-permute-start | bytes 208904 | tf_op jit(solution)/shard_map/ppermute | solution.py:236
  9.1 2.4 %collective-permute-start.3 = (bf16[17,16,128]{2,1,0:T(8,128)(2,1)S(1)}, bf16[17,16,128]{2,1,0:T(8,128)(2,1)S(1)}, u32[]{:S(2)}, u32[]{:S(2)}) collective-permute-start(bf16[17,16,128]{2,1,0:T(8,128)(2,1)S(1)} %get-tuple-element.29), channel_id=1, source_target_pairs={{0,14},{2,12},{4,10},{6,8},{8,6},{10,4},{12,2},{14,0},{1,15},{3,13... | collective-permute-start | bytes 208904 | tf_op jit(solution)/shard_map/ppermute | solution.py:236
  11.5 1.4 %collective-permute-start.4 = (bf16[17,16,128]{2,1,0:T(8,128)(2,1)S(1)}, bf16[17,16,128]{2,1,0:T(8,128)(2,1)S(1)}, u32[]{:S(2)}, u32[]{:S(2)}) collective-permute-start(bf16[17,16,128]{2,1,0:T(8,128)(2,1)S(1)} %get-tuple-element.30), channel_id=1, source_target_pairs={{0,12},{2,14},{4,8},{6,10},{8,4},{10,6},{12,0},{14,2},{1,13},{3,15... | collective-permute-start | bytes 208904 | tf_op jit(solution)/shard_map/ppermute | solution.py:236
  12.9 0.0 collective-permute-done
  12.9 0.0 collective-permute-done.1
  13.0 1.9 %collective-permute-start.5 = (bf16[34,16,128]{2,1,0:T(8,128)(2,1)S(1)}, bf16[34,16,128]{2,1,0:T(8,128)(2,1)S(1)}, u32[]{:S(2)}, u32[]{:S(2)}) collective-permute-start(bf16[34,16,128]{2,1,0:T(8,128)(2,1)S(1)} %pad_maximum_fusion.2), channel_id=1, source_target_pairs={{0,2},{2,0},{4,6},{6,4},{8,10},{10,8},{12,14},{14,12},{1,3},{3,1},... | collective-permute-start | bytes 417800 | tf_op jit(solution)/shard_map/ppermute | solution.py:236
  14.9 3.9 %collective-permute-done.2 = bf16[17,16,128]{2,1,0:T(8,128)(2,1)S(1)} collective-permute-done((bf16[17,16,128]{2,1,0:T(8,128)(2,1)S(1)}, bf16[17,16,128]{2,1,0:T(8,128)(2,1)S(1)}, u32[]{:S(2)}, u32[]{:S(2)}) %collective-permute-start.2) | collective-permute-done | bytes 69664 | tf_op jit(solution)/shard_map/ppermute | solution.py:236
  18.8 0.1 collective-permute-start.7
  18.9 0.0 collective-permute-done.3
  18.9 0.0 collective-permute-done.4
  18.9 0.2 collective-permute-done.5
  19.1 0.4 collective-permute-start.6
  19.6 0.8 %collective-permute-done.7.other_ref = bf16[68,16,128]{2,1,0:T(8,128)(2,1)S(1)} collective-permute-done((bf16[68,16,128]{2,1,0:T(8,128)(2,1)S(1)}, bf16[68,16,128]{2,1,0:T(8,128)(2,1)S(1)}, u32[]{:S(2)}, u32[]{:S(2)}) %collective-permute-start.7) | collective-permute-done | bytes 278560 | tf_op jit(solution)/shard_map/ppermute | solution.py:236
  20.4 1.0 %near.1 = (bf16[1024,256]{1,0:T(8,128)(2,1)S(1)}, s32[288,128]{1,0:T(8,128)S(1)}, s32[2,256]{1,0:T(2,128)S(1)}, f32[1,256]{1,0:T(1,128)S(1)}, f32[288,1024]{1,0:T(8,128)S(1)}, /*index=5*/f32[288,128]{1,0:T(8,128)S(1)}) custom-call(s32[1]{0:T(128)} %bitcast.me_ref, s32[1,512]{1,0:T(1,128)S(1)} %bitcast.6, ...), custom_call_target="tpu_custom_call" | custom-call | flops 268435456 | bytes 1048576 | tf_op jit(solution)/shard_map/near/pallas_call | solution.py:314
  21.4 0.0 collective-permute-done.6.other_ref
  21.4 0.9 %far.1 = (f32[8,2,256]{2,1,0:T(2,128)S(1)}, f32[1,32]{1,0:T(1,128)S(1)}) custom-call(s32[1]{0:T(128)} %bitcast.me_ref, bf16[136,16,128]{2,1,0:T(8,128)(2,1)S(1)} %constant_dynamic-update-slice_fusion.query_ref, bf16[68,16,128]{2,1,0:T(8,128)(2,1)S(1)} %collective-permute-done.6.other_ref, bf16[1024,256]{1,0:T(8,128)(2,1)S(1)} %get-tuple-element.32.query_t_ref, ...), custom_call_target="tpu_custom_call" | custom-call | flops 268435456 | bytes 1048576 | tf_op jit(solution)/shard_map/far/pallas_call | solution.py:330
  22.3 34.8 %psum.7.result_ref = f32[8,2,256]{2,1,0:T(2,128)S(1)} all-reduce(f32[8,2,256]{2,1,0:T(2,128)S(1)} %get-tuple-element.38), channel_id=1, replica_groups=mesh['groups'=2,'shard'=8,'sub'=2] {'shard'}, use_global_device_ids=true, to_apply=%region_0.0 | all-reduce | flops 4096 | bytes 32768 | tf_op jit(solution)/shard_map/psum | solution.py:343
  57.1 0.7 %pick.1 = (f32[1,128]{1,0:T(1,128)}, f32[1,128]{1,0:T(1,128)}, f32[1,32]{1,0:T(1,128)}) custom-call(s32[1]{0:T(128)} %bitcast.me_ref, s32[1,128]{1,0:T(1,128)S(1)} %get-tuple-element.23.slot_ref, f32[8,2,256]{2,1,0:T(2,128)S(1)} %psum.7.result_ref, f32[1,32]{1,0:T(1,128)S(1)} %get-tuple-element.39.norm_ref), custom_call_target="tpu_custom_call" | custom-call | tf_op jit(solution)/shard_map/pick/pallas_call | solution.py:346
  (10 shorter events, 0.2 us)
Async XLA Ops:
  0.6 1.0 %copy-start = (bf16[128,1024]{1,0:T(8,128)(2,1)S(1)}, bf16[128,1024]{1,0:T(8,128)(2,1)}, u32[]{:S(2)}) copy-start(bf16[128,1024]{1,0:T(8,128)(2,1)} %embed_ref.1) | copy-start | bytes 786436
  2.1 10.7 %collective-permute-start = (bf16[17,16,128]{2,1,0:T(8,128)(2,1)S(1)}, bf16[17,16,128]{2,1,0:T(8,128)(2,1)S(1)}, u32[]{:S(2)}, u32[]{:S(2)}) collective-permute-start(bf16[17,16,128]{2,1,0:T(8,128)(2,1)S(1)} %get-tuple-element.25), channel_id=1, source_target_pairs={{0,8},{2,10},{4,12},{6,14},{8,0},{10,2},{12,4},{14,6},{1,9},{3,11}... | collective-permute-start | bytes 208904 | tf_op jit(solution)/shard_map/ppermute | solution.py:236
  6.2 6.7 %collective-permute-start.1 = (bf16[34,16,128]{2,1,0:T(8,128)(2,1)S(1)}, bf16[34,16,128]{2,1,0:T(8,128)(2,1)S(1)}, u32[]{:S(2)}, u32[]{:S(2)}) collective-permute-start(bf16[34,16,128]{2,1,0:T(8,128)(2,1)S(1)} %get-tuple-element.26), channel_id=1, source_target_pairs={{0,4},{2,6},{4,0},{6,2},{8,12},{10,14},{12,8},{14,10},{1,5},{3,7},... | collective-permute-start | bytes 417800 | tf_op jit(solution)/shard_map/ppermute | solution.py:236
  7.8 10.9 %collective-permute-start.2 = (bf16[17,16,128]{2,1,0:T(8,128)(2,1)S(1)}, bf16[17,16,128]{2,1,0:T(8,128)(2,1)S(1)}, u32[]{:S(2)}, u32[]{:S(2)}) collective-permute-start(bf16[17,16,128]{2,1,0:T(8,128)(2,1)S(1)} %get-tuple-element.28), channel_id=1, source_target_pairs={{0,10},{2,8},{4,14},{6,12},{8,2},{10,0},{12,6},{14,4},{1,11},{3,9}... | collective-permute-start | bytes 208904 | tf_op jit(solution)/shard_map/ppermute | solution.py:236
  9.1 9.8 %collective-permute-start.3 = (bf16[17,16,128]{2,1,0:T(8,128)(2,1)S(1)}, bf16[17,16,128]{2,1,0:T(8,128)(2,1)S(1)}, u32[]{:S(2)}, u32[]{:S(2)}) collective-permute-start(bf16[17,16,128]{2,1,0:T(8,128)(2,1)S(1)} %get-tuple-element.29), channel_id=1, source_target_pairs={{0,14},{2,12},{4,10},{6,8},{8,6},{10,4},{12,2},{14,0},{1,15},{3,13... | collective-permute-start | bytes 208904 | tf_op jit(solution)/shard_map/ppermute | solution.py:236
  11.5 7.4 %collective-permute-start.4 = (bf16[17,16,128]{2,1,0:T(8,128)(2,1)S(1)}, bf16[17,16,128]{2,1,0:T(8,128)(2,1)S(1)}, u32[]{:S(2)}, u32[]{:S(2)}) collective-permute-start(bf16[17,16,128]{2,1,0:T(8,128)(2,1)S(1)} %get-tuple-element.30), channel_id=1, source_target_pairs={{0,12},{2,14},{4,8},{6,10},{8,4},{10,6},{12,0},{14,2},{1,13},{3,15... | collective-permute-start | bytes 208904 | tf_op jit(solution)/shard_map/ppermute | solution.py:236
  13.0 6.2 %collective-permute-start.5 = (bf16[34,16,128]{2,1,0:T(8,128)(2,1)S(1)}, bf16[34,16,128]{2,1,0:T(8,128)(2,1)S(1)}, u32[]{:S(2)}, u32[]{:S(2)}) collective-permute-start(bf16[34,16,128]{2,1,0:T(8,128)(2,1)S(1)} %pad_maximum_fusion.2), channel_id=1, source_target_pairs={{0,2},{2,0},{4,6},{6,4},{8,10},{10,8},{12,14},{14,12},{1,3},{3,1},... | collective-permute-start | bytes 417800 | tf_op jit(solution)/shard_map/ppermute | solution.py:236
  18.8 1.6 %collective-permute-start.7 = (bf16[68,16,128]{2,1,0:T(8,128)(2,1)S(1)}, bf16[68,16,128]{2,1,0:T(8,128)(2,1)S(1)}, u32[]{:S(2)}, u32[]{:S(2)}) collective-permute-start(bf16[68,16,128]{2,1,0:T(8,128)(2,1)S(1)} %pad_maximum_fusion.1), channel_id=1, source_target_pairs={{0,1},{1,0},{2,3},{3,2},{4,5},{5,4},{6,7},{7,6},{8,9},{9,8},{10,11... | collective-permute-start | bytes 835592 | tf_op jit(solution)/shard_map/ppermute | solution.py:236
  19.1 2.2 %collective-permute-start.6 = (bf16[68,16,128]{2,1,0:T(8,128)(2,1)S(1)}, bf16[68,16,128]{2,1,0:T(8,128)(2,1)S(1)}, u32[]{:S(2)}, u32[]{:S(2)}) collective-permute-start(bf16[68,16,128]{2,1,0:T(8,128)(2,1)S(1)} %pad_maximum_fusion), channel_id=1, source_target_pairs={{0,1},{1,0},{2,3},{3,2},{4,5},{5,4},{6,7},{7,6},{8,9},{9,8},{10,11... | collective-permute-start | bytes 835592 | tf_op jit(solution)/shard_map/ppermute | solution.py:236

commit v27 on v23

--- a/solution.py
+++ b/solution.py
@@ -212,16 +212,18 @@
 
 
 def pick_kernel(
-    order, parts, me_ref, slot_ref, result_ref, norm_ref, best_ref, distance_ref, cohesion_ref
+    order, parts, me_ref, slot_ref, norm_ref, *refs
 ):
+    *result_refs, best_ref, distance_ref, cohesion_ref = refs
     cohesion_ref[...] = norm_ref[...]
     rows = slot_ref.shape[1]
-    owners, lines, slots = result_ref.shape
+    _, lines, slots = result_refs[0].shape
+    owners, sides = len(order), len(result_refs)
     folds = min(parts, 2)
     place = iota((lines, slots), 1) % (slots // folds) // (slots // owners // folds)
     values = jnp.zeros((lines, slots), jnp.float32)
     for index, k in enumerate(order):
-        values = jnp.where(place == index, result_ref[me_ref[0] ^ k], values)
+        values = jnp.where(place == index, result_refs[k % sides][(me_ref[0] ^ k) // sides], values)
     values = jnp.concatenate([values, jnp.zeros((8 - lines, slots), jnp.float32)], axis=0)
     at = (iota((slots, rows), 0) == slot_ref[...]).astype(jnp.float32)
     picked = jnp.dot(
@@ -329,7 +331,7 @@
     results, norms = pl.pallas_call(
         functools.partial(far_kernel, rows_all, tiles),
         out_shape=[
-            jax.ShapeDtypeStruct((owners, 2, slots), jnp.float32),
+            jax.ShapeDtypeStruct((owners // 2 if direct else owners, 2, slots), jnp.float32),
             jax.ShapeDtypeStruct((1, clus_dev), jnp.float32),
         ],
         in_specs=[WHOLE] * 8,
@@ -338,16 +340,21 @@
         cost_estimate=compare_cost,
         name="far",
     )(query, other_second, *near)
-    results = lax.all_to_all(results, "shard", 0, 0, tiled=True)
+    if direct:
+        lines = [list(range(side, owners, 2)) for side in (0, 1)]
+        results = lax.all_to_all(results, "shard", 0, 0, axis_index_groups=lines, tiled=True)
+        results = [results, from_partner(results, 1, "shard")]
+    else:
+        results = [lax.all_to_all(results, "shard", 0, 0, tiled=True)]
     best, distance, cohesion = pl.pallas_call(
         functools.partial(pick_kernel, order, parts),
         out_shape=[jax.ShapeDtypeStruct((1, local_rows), jnp.float32)] * 2
         + [jax.ShapeDtypeStruct((1, clus_dev), jnp.float32)],
-        in_specs=[SCALAR] + [WHOLE] * 3,
+        in_specs=[SCALAR] + [WHOLE] * (2 + len(results)),
         out_specs=[WHOLE] * 3,
         compiler_params=params,
         name="pick",
-    )(me, slot, results, norms)
+    )(me, slot, norms, *results)
     return best.reshape(local_rows), distance.reshape(local_rows), cohesion.reshape(clus_dev)
 
 

time: 33.6 us -> 35.3 us (1.051)
  waiting for transfers between devices: 4.91 us -> 7.06 us
  blocking collectives: 10.3 us -> 8.41 us
  starting transfers between devices: 13.1 us -> 14.6 us
    ppermute x8 -> x9, waiting for transfers between devices: 4.91 us -> 7.06 us  [from_partner(): lax.ppermute(value, axis, [(i, i ^ k) for i in range(lax.axis_size(axis))])]
    all_to_all x1, blocking collectives: 10.3 us -> 8.41 us  [local(): lax.all_to_all(results, 'shard', 0, 0, axis_index_groups=lines, tiled=True)]
    ppermute x8 -> x9, starting transfers between devices: 13.1 us -> 14.6 us  [from_partner(): lax.ppermute(value, axis, [(i, i ^ k) for i in range(lax.axis_size(axis))])]
  transfers between devices with their start and end apart: 8 -> 9, of which waited for: 3 -> 4; matrix products, arithmetic and copies ran while one was open for 1% -> 1% of each run, Pallas kernels for 3% -> 3%
where the time goes in v27:
time: 35.3 us; the launch traced here: 35.2 us
  starting transfers between devices  14.6 us (41%)
  blocking collectives  8.41 us (24%)
  waiting for transfers between devices  7.06 us (20%)
  Pallas kernels  3.37 us (10%)
  other arithmetic  0.84 us (2%)
  between operations  0.76 us (2%)
    ppermute x9, starting transfers between devices, from_partner(): lax.ppermute(value, axis, [(i, i ^ k) for i in range(lax.axis_size(axis))])  14.6 us
    all_to_all x1, blocking collectives, local(): lax.all_to_all(results, 'shard', 0, 0, axis_index_groups=lines, tiled=True)  8.41 us
    ppermute x9, waiting for transfers between devices, from_partner(): lax.ppermute(value, axis, [(i, i ^ k) for i in range(lax.axis_size(axis))])  7.06 us
    pallas_call x1, Pallas kernels, local(): pl.pallas_call(functools.partial(far_kernel, rows_all, tiles), out_shape=...  0.97 us
    pallas_call x1, Pallas kernels, local(): pl.pallas_call(functools.partial(near_kernel, rows_all, owner_map.shape[0...  0.97 us
    concatenate x1, other arithmetic, local(): ints = jnp.concatenate([owner_map, cluster_id, item_order]).reshape(1, -1)  0.76 us
    pallas_call x1, Pallas kernels, local(): pl.pallas_call(functools.partial(pick_kernel, order, parts), out_shape=[j...  0.73 us
  transfers between devices with their start and end apart: 9, of which 4 were waited for; matrix products, arithmetic and copies ran while one was open for 1% of the time, Pallas kernels for 3%

profile of v27, /device:TPU:0, one launch (start us, length us, event | category | flops | bytes accessed | tf_op | source)
XLA Modules:
  0.0 35.2 jit_solution(13697993644760045917)
XLA Ops:
  0.6 0.0 copy-start
  0.6 0.8 %pad_add_fusion = s32[512]{0:T(512)S(1)} fusion(s32[128]{0:T(128)} %param.6, s32[128]{0:T(128)} %param.5, s32[256]{0:T(256)} %param.7), kind=kLoop, calls=%fused_computation.10 | loop fusion | flops 1024 | bytes 4096 | tf_op jit(solution)/shard_map/concatenate | solution.py:281
  1.4 0.3 slots.1
  1.7 0.0 copy-done
  1.7 0.4 %pack.1 = (bf16[17,16,128]{2,1,0:T(8,128)(2,1)S(1)}, bf16[34,16,128]{2,1,0:T(8,128)(2,1)S(1)}, bf16[17,16,128]{2,1,0:T(8,128)(2,1)S(1)}, bf16[17,16,128]{2,1,0:T...) custom-call(s32[1,128]{1,0:T(1,128)S(1)} %get-tuple-element.23.slot_, ...), custom_call_target="tpu_custom_call" | custom-call | tf_op jit(solution)/shard_map/pack/pallas_call | solution.py:301
  2.1 4.1 %collective-permute-start = (bf16[17,16,128]{2,1,0:T(8,128)(2,1)S(1)}, bf16[17,16,128]{2,1,0:T(8,128)(2,1)S(1)}, u32[]{:S(2)}, u32[]{:S(2)}) collective-permute-start(bf16[17,16,128]{2,1,0:T(8,128)(2,1)S(1)} %get-tuple-element.25), channel_id=1, source_target_pairs={{0,8},{2,10},{4,12},{6,14},{8,0},{10,2},{12,4},{14,6},{1,9},{3,11}... | collective-permute-start | bytes 208904 | tf_op jit(solution)/shard_map/ppermute | solution.py:237
  6.2 1.6 %collective-permute-start.1 = (bf16[34,16,128]{2,1,0:T(8,128)(2,1)S(1)}, bf16[34,16,128]{2,1,0:T(8,128)(2,1)S(1)}, u32[]{:S(2)}, u32[]{:S(2)}) collective-permute-start(bf16[34,16,128]{2,1,0:T(8,128)(2,1)S(1)} %get-tuple-element.26), channel_id=1, source_target_pairs={{0,4},{2,6},{4,0},{6,2},{8,12},{10,14},{12,8},{14,10},{1,5},{3,7},... | collective-permute-start | bytes 417800 | tf_op jit(solution)/shard_map/ppermute | solution.py:237
  7.8 1.3 %collective-permute-start.2 = (bf16[17,16,128]{2,1,0:T(8,128)(2,1)S(1)}, bf16[17,16,128]{2,1,0:T(8,128)(2,1)S(1)}, u32[]{:S(2)}, u32[]{:S(2)}) collective-permute-start(bf16[17,16,128]{2,1,0:T(8,128)(2,1)S(1)} %get-tuple-element.28), channel_id=1, source_target_pairs={{0,10},{2,8},{4,14},{6,12},{8,2},{10,0},{12,6},{14,4},{1,11},{3,9}... | collective-permute-start | bytes 208904 | tf_op jit(solution)/shard_map/ppermute | solution.py:237
  9.1 2.4 %collective-permute-start.3 = (bf16[17,16,128]{2,1,0:T(8,128)(2,1)S(1)}, bf16[17,16,128]{2,1,0:T(8,128)(2,1)S(1)}, u32[]{:S(2)}, u32[]{:S(2)}) collective-permute-start(bf16[17,16,128]{2,1,0:T(8,128)(2,1)S(1)} %get-tuple-element.29), channel_id=1, source_target_pairs={{0,14},{2,12},{4,10},{6,8},{8,6},{10,4},{12,2},{14,0},{1,15},{3,13... | collective-permute-start | bytes 208904 | tf_op jit(solution)/shard_map/ppermute | solution.py:237
  11.5 1.4 %collective-permute-start.4 = (bf16[17,16,128]{2,1,0:T(8,128)(2,1)S(1)}, bf16[17,16,128]{2,1,0:T(8,128)(2,1)S(1)}, u32[]{:S(2)}, u32[]{:S(2)}) collective-permute-start(bf16[17,16,128]{2,1,0:T(8,128)(2,1)S(1)} %get-tuple-element.30), channel_id=1, source_target_pairs={{0,12},{2,14},{4,8},{6,10},{8,4},{10,6},{12,0},{14,2},{1,13},{3,15... | collective-permute-start | bytes 208904 | tf_op jit(solution)/shard_map/ppermute | solution.py:237
  12.9 0.0 collective-permute-done
  12.9 0.0 collective-permute-done.1
  13.0 1.9 %collective-permute-start.5 = (bf16[34,16,128]{2,1,0:T(8,128)(2,1)S(1)}, bf16[34,16,128]{2,1,0:T(8,128)(2,1)S(1)}, u32[]{:S(2)}, u32[]{:S(2)}) collective-permute-start(bf16[34,16,128]{2,1,0:T(8,128)(2,1)S(1)} %pad_maximum_fusion.2), channel_id=1, source_target_pairs={{0,2},{2,0},{4,6},{6,4},{8,10},{10,8},{12,14},{14,12},{1,3},{3,1},... | collective-permute-start | bytes 417800 | tf_op jit(solution)/shard_map/ppermute | solution.py:237
  14.9 3.9 %collective-permute-done.2 = bf16[17,16,128]{2,1,0:T(8,128)(2,1)S(1)} collective-permute-done((bf16[17,16,128]{2,1,0:T(8,128)(2,1)S(1)}, bf16[17,16,128]{2,1,0:T(8,128)(2,1)S(1)}, u32[]{:S(2)}, u32[]{:S(2)}) %collective-permute-start.2) | collective-permute-done | bytes 69664 | tf_op jit(solution)/shard_map/ppermute | solution.py:237
  18.8 0.1 collective-permute-start.7
  18.9 0.0 collective-permute-done.3
  18.9 0.0 collective-permute-done.4
  18.9 0.2 collective-permute-done.5
  19.1 0.4 %collective-permute-start.6 = (bf16[68,16,128]{2,1,0:T(8,128)(2,1)S(1)}, bf16[68,16,128]{2,1,0:T(8,128)(2,1)S(1)}, u32[]{:S(2)}, u32[]{:S(2)}) collective-permute-start(bf16[68,16,128]{2,1,0:T(8,128)(2,1)S(1)} %pad_maximum_fusion), channel_id=1, source_target_pairs={{0,1},{1,0},{2,3},{3,2},{4,5},{5,4},{6,7},{7,6},{8,9},{9,8},{10,11... | collective-permute-start | bytes 835592 | tf_op jit(solution)/shard_map/ppermute | solution.py:237
  19.6 0.8 %collective-permute-done.7.other_ref = bf16[68,16,128]{2,1,0:T(8,128)(2,1)S(1)} collective-permute-done((bf16[68,16,128]{2,1,0:T(8,128)(2,1)S(1)}, bf16[68,16,128]{2,1,0:T(8,128)(2,1)S(1)}, u32[]{:S(2)}, u32[]{:S(2)}) %collective-permute-start.7) | collective-permute-done | bytes 278560 | tf_op jit(solution)/shard_map/ppermute | solution.py:237
  20.4 1.0 %near.1 = (bf16[1024,256]{1,0:T(8,128)(2,1)S(1)}, s32[288,128]{1,0:T(8,128)S(1)}, s32[2,256]{1,0:T(2,128)S(1)}, f32[1,256]{1,0:T(1,128)S(1)}, f32[288,1024]{1,0:T(8,128)S(1)}, /*index=5*/f32[288,128]{1,0:T(8,128)S(1)}) custom-call(s32[1]{0:T(128)} %bitcast.me_ref, s32[1,512]{1,0:T(1,128)S(1)} %bitcast.6, ...), custom_call_target="tpu_custom_call" | custom-call | flops 268435456 | bytes 1048576 | tf_op jit(solution)/shard_map/near/pallas_call | solution.py:315
  21.4 0.0 collective-permute-done.6.other_ref
  21.4 1.0 %far.1 = (f32[4,2,256]{2,1,0:T(2,128)S(1)}, f32[1,32]{1,0:T(1,128)S(1)}) custom-call(bf16[136,16,128]{2,1,0:T(8,128)(2,1)S(1)} %constant_dynamic-update-slice_fusion.query_ref, bf16[68,16,128]{2,1,0:T(8,128)(2,1)S(1)} %collective-permute-done.6.other_ref, bf16[1024,256]{1,0:T(8,128)(2,1)S(1)} %get-tuple-element.32.query_t_ref, ...), custom_call_target="tpu_custom_call" | custom-call | flops 268435456 | bytes 1048576 | tf_op jit(solution)/shard_map/far/pallas_call | solution.py:331
  22.4 8.4 %all_to_all.5.refs_0_ = f32[4,2,256]{2,1,0:T(2,128)S(1)} all-to-all(f32[4,2,256]{2,1,0:T(2,128)S(1)} %get-tuple-element.39), channel_id=1, replica_groups={{0,4,8,12},{2,6,10,14},{1,5,9,13},{3,7,11,15},{16,20,24,28},{18,22,26,3..., dimensions={0} | all-to-all | bytes 16384 | tf_op jit(solution)/shard_map/all_to_all | solution.py:345
  30.8 1.5 %collective-permute-start.8 = (f32[4,2,256]{2,1,0:T(2,128)S(1)}, f32[4,2,256]{2,1,0:T(2,128)S(1)}, u32[]{:S(2)}, u32[]{:S(2)}) collective-permute-start(f32[4,2,256]{2,1,0:T(2,128)S(1)} %all_to_all.5.refs_0_), channel_id=1, source_target_pairs={{0,2},{2,0},{4,6},{6,4},{8,10},{10,8},{12,14},{14,12},{1,3},{3,1},... | collective-permute-start | bytes 24584 | tf_op jit(solution)/shard_map/ppermute | solution.py:237
  32.3 2.2 %collective-permute-done.8.refs_1_ = f32[4,2,256]{2,1,0:T(2,128)S(1)} collective-permute-done((f32[4,2,256]{2,1,0:T(2,128)S(1)}, f32[4,2,256]{2,1,0:T(2,128)S(1)}, u32[]{:S(2)}, u32[]{:S(2)}) %collective-permute-start.8) | collective-permute-done | bytes 8224 | tf_op jit(solution)/shard_map/ppermute | solution.py:237
  34.4 0.7 %pick.1 = (f32[1,128]{1,0:T(1,128)}, f32[1,128]{1,0:T(1,128)}, f32[1,32]{1,0:T(1,128)}) custom-call(s32[1]{0:T(128)} %bitcast.me_ref, s32[1,128]{1,0:T(1,128)S(1)} %get-tuple-element.23.slot_ref, f32[1,32]{1,0:T(1,128)S(1)} %get-tuple-element.38.norm_ref, f32[4,2,256]{2,1,0:T(2,128)S(1)} %all_to_all.5.refs_0_, f32[4,2,256]{2,1,0:T(2,128)S(1)} %collective-permute-done.8.refs_1_), custom_call_target="tpu_custom_call" | custom-call | tf_op jit(solution)/shard_map/pick/pallas_call | solution.py:349
  (10 shorter events, 0.2 us)
Async XLA Ops:
  0.6 1.0 %copy-start = (bf16[128,1024]{1,0:T(8,128)(2,1)S(1)}, bf16[128,1024]{1,0:T(8,128)(2,1)}, u32[]{:S(2)}) copy-start(bf16[128,1024]{1,0:T(8,128)(2,1)} %embed_ref.1) | copy-start | bytes 786436
  2.1 10.7 %collective-permute-start = (bf16[17,16,128]{2,1,0:T(8,128)(2,1)S(1)}, bf16[17,16,128]{2,1,0:T(8,128)(2,1)S(1)}, u32[]{:S(2)}, u32[]{:S(2)}) collective-permute-start(bf16[17,16,128]{2,1,0:T(8,128)(2,1)S(1)} %get-tuple-element.25), channel_id=1, source_target_pairs={{0,8},{2,10},{4,12},{6,14},{8,0},{10,2},{12,4},{14,6},{1,9},{3,11}... | collective-permute-start | bytes 208904 | tf_op jit(solution)/shard_map/ppermute | solution.py:237
  6.2 6.7 %collective-permute-start.1 = (bf16[34,16,128]{2,1,0:T(8,128)(2,1)S(1)}, bf16[34,16,128]{2,1,0:T(8,128)(2,1)S(1)}, u32[]{:S(2)}, u32[]{:S(2)}) collective-permute-start(bf16[34,16,128]{2,1,0:T(8,128)(2,1)S(1)} %get-tuple-element.26), channel_id=1, source_target_pairs={{0,4},{2,6},{4,0},{6,2},{8,12},{10,14},{12,8},{14,10},{1,5},{3,7},... | collective-permute-start | bytes 417800 | tf_op jit(solution)/shard_map/ppermute | solution.py:237
  7.8 10.9 %collective-permute-start.2 = (bf16[17,16,128]{2,1,0:T(8,128)(2,1)S(1)}, bf16[17,16,128]{2,1,0:T(8,128)(2,1)S(1)}, u32[]{:S(2)}, u32[]{:S(2)}) collective-permute-start(bf16[17,16,128]{2,1,0:T(8,128)(2,1)S(1)} %get-tuple-element.28), channel_id=1, source_target_pairs={{0,10},{2,8},{4,14},{6,12},{8,2},{10,0},{12,6},{14,4},{1,11},{3,9}... | collective-permute-start | bytes 208904 | tf_op jit(solution)/shard_map/ppermute | solution.py:237
  9.1 9.8 %collective-permute-start.3 = (bf16[17,16,128]{2,1,0:T(8,128)(2,1)S(1)}, bf16[17,16,128]{2,1,0:T(8,128)(2,1)S(1)}, u32[]{:S(2)}, u32[]{:S(2)}) collective-permute-start(bf16[17,16,128]{2,1,0:T(8,128)(2,1)S(1)} %get-tuple-element.29), channel_id=1, source_target_pairs={{0,14},{2,12},{4,10},{6,8},{8,6},{10,4},{12,2},{14,0},{1,15},{3,13... | collective-permute-start | bytes 208904 | tf_op jit(solution)/shard_map/ppermute | solution.py:237
  11.5 7.4 %collective-permute-start.4 = (bf16[17,16,128]{2,1,0:T(8,128)(2,1)S(1)}, bf16[17,16,128]{2,1,0:T(8,128)(2,1)S(1)}, u32[]{:S(2)}, u32[]{:S(2)}) collective-permute-start(bf16[17,16,128]{2,1,0:T(8,128)(2,1)S(1)} %get-tuple-element.30), channel_id=1, source_target_pairs={{0,12},{2,14},{4,8},{6,10},{8,4},{10,6},{12,0},{14,2},{1,13},{3,15... | collective-permute-start | bytes 208904 | tf_op jit(solution)/shard_map/ppermute | solution.py:237
  13.0 6.2 %collective-permute-start.5 = (bf16[34,16,128]{2,1,0:T(8,128)(2,1)S(1)}, bf16[34,16,128]{2,1,0:T(8,128)(2,1)S(1)}, u32[]{:S(2)}, u32[]{:S(2)}) collective-permute-start(bf16[34,16,128]{2,1,0:T(8,128)(2,1)S(1)} %pad_maximum_fusion.2), channel_id=1, source_target_pairs={{0,2},{2,0},{4,6},{6,4},{8,10},{10,8},{12,14},{14,12},{1,3},{3,1},... | collective-permute-start | bytes 417800 | tf_op jit(solution)/shard_map/ppermute | solution.py:237
  18.8 1.6 %collective-permute-start.7 = (bf16[68,16,128]{2,1,0:T(8,128)(2,1)S(1)}, bf16[68,16,128]{2,1,0:T(8,128)(2,1)S(1)}, u32[]{:S(2)}, u32[]{:S(2)}) collective-permute-start(bf16[68,16,128]{2,1,0:T(8,128)(2,1)S(1)} %pad_maximum_fusion.1), channel_id=1, source_target_pairs={{0,1},{1,0},{2,3},{3,2},{4,5},{5,4},{6,7},{7,6},{8,9},{9,8},{10,11... | collective-permute-start | bytes 835592 | tf_op jit(solution)/shard_map/ppermute | solution.py:237
  19.1 2.3 %collective-permute-start.6 = (bf16[68,16,128]{2,1,0:T(8,128)(2,1)S(1)}, bf16[68,16,128]{2,1,0:T(8,128)(2,1)S(1)}, u32[]{:S(2)}, u32[]{:S(2)}) collective-permute-start(bf16[68,16,128]{2,1,0:T(8,128)(2,1)S(1)} %pad_maximum_fusion), channel_id=1, source_target_pairs={{0,1},{1,0},{2,3},{3,2},{4,5},{5,4},{6,7},{7,6},{8,9},{9,8},{10,11... | collective-permute-start | bytes 835592 | tf_op jit(solution)/shard_map/ppermute | solution.py:237
  30.8 3.7 %collective-permute-start.8 = (f32[4,2,256]{2,1,0:T(2,128)S(1)}, f32[4,2,256]{2,1,0:T(2,128)S(1)}, u32[]{:S(2)}, u32[]{:S(2)}) collective-permute-start(f32[4,2,256]{2,1,0:T(2,128)S(1)} %all_to_all.5.refs_0_), channel_id=1, source_target_pairs={{0,2},{2,0},{4,6},{6,4},{8,10},{10,8},{12,14},{14,12},{1,3},{3,1},... | collective-permute-start | bytes 24584 | tf_op jit(solution)/shard_map/ppermute | solution.py:237

commit v28 on v23

--- a/solution.py
+++ b/solution.py
@@ -11,6 +11,7 @@
 DIGITS = 3
 SENDS = ((4,), (2, 3), (5,), (7,), (6,), (1,), (0,))
 PARTNERS = (4, 2, 0, 5, 7, 6, 1, 3)
+EARLY = 3
 WHOLE = pl.BlockSpec(memory_space=pltpu.VMEM)
 SCALAR = pl.BlockSpec(memory_space=pltpu.SMEM)
 
@@ -101,11 +102,12 @@
 
 
 def unpacked(block_ref, tiles):
-    blocks = block_ref.shape[0] // tiles
+    blocks, half = block_ref.shape[0] // tiles, block_ref.shape[1]
     each = tiles // 2
+    empty = [jnp.zeros((half, LANES), block_ref.dtype)] * (-blocks % max(LANES // (2 * half), 1))
 
     def column(tile):
-        return jnp.concatenate([block_ref[i * tiles + tile] for i in range(blocks)], axis=0)
+        return jnp.concatenate([block_ref[i * tiles + tile] for i in range(blocks)] + empty, axis=0)
 
     halves = [
         jnp.concatenate([column(first + tile) for tile in range(each)], axis=1)
@@ -245,8 +247,7 @@
     pair = from_partner(jnp.concatenate([sent[1,], pair[tiles:]]), 1, "shard")
     got[1], got[3] = pair[:tiles], pair[tiles:]
     got = [got[k] for k in PARTNERS]
-    half = len(got) // 2
-    return jnp.concatenate(got[:half]), jnp.concatenate(got[half:])
+    return jnp.concatenate(got[:EARLY]), jnp.concatenate(got[EARLY:])
 
 
 def exchange_all(packed, me):

time: 33.6 us -> 33.8 us (level)
  blocking collectives: 10.3 us -> 11 us
    all_to_all x1, blocking collectives: 10.3 us -> 11 us  [local(): results = lax.all_to_all(results, 'shard', 0, 0, tiled=True)]
where the time goes in v28:
time: 33.8 us; the launch traced here: 33.6 us
  starting transfers between devices  12.8 us (38%)
  blocking collectives  11 us (33%)
  waiting for transfers between devices  4.68 us (14%)
  Pallas kernels  3.39 us (10%)
  other arithmetic  0.84 us (2%)
  between operations  0.76 us (2%)
    ppermute x8, starting transfers between devices, from_partner(): lax.ppermute(value, axis, [(i, i ^ k) for i in range(lax.axis_size(axis))])  12.8 us
    all_to_all x1, blocking collectives, local(): results = lax.all_to_all(results, 'shard', 0, 0, tiled=True)  11 us
    ppermute x8, waiting for transfers between devices, from_partner(): lax.ppermute(value, axis, [(i, i ^ k) for i in range(lax.axis_size(axis))])  4.68 us
    pallas_call x1, Pallas kernels, local(): pl.pallas_call(functools.partial(far_kernel, rows_all, tiles), out_shape=...  1 us
    pallas_call x1, Pallas kernels, local(): pl.pallas_call(functools.partial(near_kernel, rows_all, owner_map.shape[0...  0.97 us
    concatenate x1, other arithmetic, local(): ints = jnp.concatenate([owner_map, cluster_id, item_order]).reshape(1, -1)  0.76 us
    pallas_call x1, Pallas kernels, local(): pl.pallas_call(functools.partial(pick_kernel, order, parts), out_shape=[j...  0.72 us
  transfers between devices with their start and end apart: 8, of which 3 were waited for; matrix products, arithmetic and copies ran while one was open for 1% of the time, Pallas kernels for 3%

profile of v28, /device:TPU:0, one launch (start us, length us, event | category | flops | bytes accessed | tf_op | source)
XLA Modules:
  0.0 33.6 jit_solution(1893718059740278151)
XLA Ops:
  0.6 0.0 copy-start
  0.6 0.8 %pad_add_fusion = s32[512]{0:T(512)S(1)} fusion(s32[128]{0:T(128)} %param.6, s32[128]{0:T(128)} %param.5, s32[256]{0:T(256)} %param.7), kind=kLoop, calls=%fused_computation.10 | loop fusion | flops 1024 | bytes 4096 | tf_op jit(solution)/shard_map/concatenate | solution.py:280
  1.4 0.3 slots.1
  1.7 0.0 copy-done
  1.7 0.4 %pack.1 = (bf16[17,16,128]{2,1,0:T(8,128)(2,1)S(1)}, bf16[34,16,128]{2,1,0:T(8,128)(2,1)S(1)}, bf16[17,16,128]{2,1,0:T(8,128)(2,1)S(1)}, bf16[17,16,128]{2,1,0:T...) custom-call(s32[1,128]{1,0:T(1,128)S(1)} %get-tuple-element.23.slot_, ...), custom_call_target="tpu_custom_call" | custom-call | tf_op jit(solution)/shard_map/pack/pallas_call | solution.py:300
  2.1 4.1 %collective-permute-start = (bf16[17,16,128]{2,1,0:T(8,128)(2,1)S(1)}, bf16[17,16,128]{2,1,0:T(8,128)(2,1)S(1)}, u32[]{:S(2)}, u32[]{:S(2)}) collective-permute-start(bf16[17,16,128]{2,1,0:T(8,128)(2,1)S(1)} %get-tuple-element.25), channel_id=1, source_target_pairs={{0,8},{2,10},{4,12},{6,14},{8,0},{10,2},{12,4},{14,6},{1,9},{3,11}... | collective-permute-start | bytes 208904 | tf_op jit(solution)/shard_map/ppermute | solution.py:237
  6.2 1.6 %collective-permute-start.1 = (bf16[34,16,128]{2,1,0:T(8,128)(2,1)S(1)}, bf16[34,16,128]{2,1,0:T(8,128)(2,1)S(1)}, u32[]{:S(2)}, u32[]{:S(2)}) collective-permute-start(bf16[34,16,128]{2,1,0:T(8,128)(2,1)S(1)} %get-tuple-element.26), channel_id=1, source_target_pairs={{0,4},{2,6},{4,0},{6,2},{8,12},{10,14},{12,8},{14,10},{1,5},{3,7},... | collective-permute-start | bytes 417800 | tf_op jit(solution)/shard_map/ppermute | solution.py:237
  7.8 1.3 %collective-permute-start.2 = (bf16[17,16,128]{2,1,0:T(8,128)(2,1)S(1)}, bf16[17,16,128]{2,1,0:T(8,128)(2,1)S(1)}, u32[]{:S(2)}, u32[]{:S(2)}) collective-permute-start(bf16[17,16,128]{2,1,0:T(8,128)(2,1)S(1)} %get-tuple-element.28), channel_id=1, source_target_pairs={{0,10},{2,8},{4,14},{6,12},{8,2},{10,0},{12,6},{14,4},{1,11},{3,9}... | collective-permute-start | bytes 208904 | tf_op jit(solution)/shard_map/ppermute | solution.py:237
  9.1 2.4 %collective-permute-start.3 = (bf16[17,16,128]{2,1,0:T(8,128)(2,1)S(1)}, bf16[17,16,128]{2,1,0:T(8,128)(2,1)S(1)}, u32[]{:S(2)}, u32[]{:S(2)}) collective-permute-start(bf16[17,16,128]{2,1,0:T(8,128)(2,1)S(1)} %get-tuple-element.29), channel_id=1, source_target_pairs={{0,14},{2,12},{4,10},{6,8},{8,6},{10,4},{12,2},{14,0},{1,15},{3,13... | collective-permute-start | bytes 208904 | tf_op jit(solution)/shard_map/ppermute | solution.py:237
  11.5 1.4 %collective-permute-start.4 = (bf16[17,16,128]{2,1,0:T(8,128)(2,1)S(1)}, bf16[17,16,128]{2,1,0:T(8,128)(2,1)S(1)}, u32[]{:S(2)}, u32[]{:S(2)}) collective-permute-start(bf16[17,16,128]{2,1,0:T(8,128)(2,1)S(1)} %get-tuple-element.30), channel_id=1, source_target_pairs={{0,12},{2,14},{4,8},{6,10},{8,4},{10,6},{12,0},{14,2},{1,13},{3,15... | collective-permute-start | bytes 208904 | tf_op jit(solution)/shard_map/ppermute | solution.py:237
  12.9 0.0 collective-permute-done
  12.9 0.0 collective-permute-done.1
  13.0 1.9 %collective-permute-start.5 = (bf16[34,16,128]{2,1,0:T(8,128)(2,1)S(1)}, bf16[34,16,128]{2,1,0:T(8,128)(2,1)S(1)}, u32[]{:S(2)}, u32[]{:S(2)}) collective-permute-start(bf16[34,16,128]{2,1,0:T(8,128)(2,1)S(1)} %pad_maximum_fusion.2), channel_id=1, source_target_pairs={{0,2},{2,0},{4,6},{6,4},{8,10},{10,8},{12,14},{14,12},{1,3},{3,1},... | collective-permute-start | bytes 417800 | tf_op jit(solution)/shard_map/ppermute | solution.py:237
  14.9 0.1 collective-permute-start.7
  15.0 3.7 %collective-permute-done.2 = bf16[17,16,128]{2,1,0:T(8,128)(2,1)S(1)} collective-permute-done((bf16[17,16,128]{2,1,0:T(8,128)(2,1)S(1)}, bf16[17,16,128]{2,1,0:T(8,128)(2,1)S(1)}, u32[]{:S(2)}, u32[]{:S(2)}) %collective-permute-start.2) | collective-permute-done | bytes 69664 | tf_op jit(solution)/shard_map/ppermute | solution.py:237
  18.7 0.0 collective-permute-done.3
  18.8 0.0 collective-permute-done.4
  18.8 0.3 collective-permute-done.5
  19.1 0.1 collective-permute-start.6
  19.3 0.0 collective-permute-done.7.other_ref
  19.3 1.0 %near.1 = (bf16[1024,256]{1,0:T(8,128)(2,1)S(1)}, s32[288,128]{1,0:T(8,128)S(1)}, s32[2,256]{1,0:T(2,128)S(1)}, f32[1,256]{1,0:T(1,128)S(1)}, f32[288,1024]{1,0:T(8,128)S(1)}, /*index=5*/f32[288,128]{1,0:T(8,128)S(1)}) custom-call(s32[1]{0:T(128)} %bitcast.me_ref, s32[1,512]{1,0:T(1,128)S(1)} %bitcast.6, ...), custom_call_target="tpu_custom_call" | custom-call | flops 268435456 | bytes 1048576 | tf_op jit(solution)/shard_map/near/pallas_call | solution.py:314
  20.3 0.6 %collective-permute-done.6.other_ref = bf16[85,16,128]{2,1,0:T(8,128)(2,1)S(1)} collective-permute-done((bf16[85,16,128]{2,1,0:T(8,128)(2,1)S(1)}, bf16[85,16,128]{2,1,0:T(8,128)(2,1)S(1)}, u32[]{:S(2)}, u32[]{:S(2)}) %collective-permute-start.6) | collective-permute-done | bytes 348192 | tf_op jit(solution)/shard_map/ppermute | solution.py:237
  20.9 1.0 %far.1 = (f32[8,2,256]{2,1,0:T(2,128)S(1)}, f32[1,32]{1,0:T(1,128)S(1)}) custom-call(bf16[136,16,128]{2,1,0:T(8,128)(2,1)S(1)} %constant_dynamic-update-slice_fusion.query_ref, bf16[85,16,128]{2,1,0:T(8,128)(2,1)S(1)} %collective-permute-done.6.other_ref, bf16[1024,256]{1,0:T(8,128)(2,1)S(1)} %get-tuple-element.32.query_t_ref, ...), custom_call_target="tpu_custom_call" | custom-call | flops 268435456 | bytes 1048576 | tf_op jit(solution)/shard_map/far/pallas_call | solution.py:330
  21.9 11.0 %all_to_all.5.result_ref = f32[8,2,256]{2,1,0:T(2,128)S(1)} all-to-all(f32[8,2,256]{2,1,0:T(2,128)S(1)} %get-tuple-element.38), channel_id=1, replica_groups=mesh['groups'=2,'shard'=8,'sub'=2] {'shard'}, dimensions={0} | all-to-all | bytes 32768 | tf_op jit(solution)/shard_map/all_to_all | solution.py:342
  32.9 0.7 %pick.1 = (f32[1,128]{1,0:T(1,128)}, f32[1,128]{1,0:T(1,128)}, f32[1,32]{1,0:T(1,128)}) custom-call(s32[1]{0:T(128)} %bitcast.me_ref, s32[1,128]{1,0:T(1,128)S(1)} %get-tuple-element.23.slot_ref, f32[8,2,256]{2,1,0:T(2,128)S(1)} %all_to_all.5.result_ref, f32[1,32]{1,0:T(1,128)S(1)} %get-tuple-element.39.norm_ref), custom_call_target="tpu_custom_call" | custom-call | tf_op jit(solution)/shard_map/pick/pallas_call | solution.py:343
  (10 shorter events, 0.2 us)
Async XLA Ops:
  0.6 1.0 %copy-start = (bf16[128,1024]{1,0:T(8,128)(2,1)S(1)}, bf16[128,1024]{1,0:T(8,128)(2,1)}, u32[]{:S(2)}) copy-start(bf16[128,1024]{1,0:T(8,128)(2,1)} %embed_ref.1) | copy-start | bytes 786436
  2.1 10.7 %collective-permute-start = (bf16[17,16,128]{2,1,0:T(8,128)(2,1)S(1)}, bf16[17,16,128]{2,1,0:T(8,128)(2,1)S(1)}, u32[]{:S(2)}, u32[]{:S(2)}) collective-permute-start(bf16[17,16,128]{2,1,0:T(8,128)(2,1)S(1)} %get-tuple-element.25), channel_id=1, source_target_pairs={{0,8},{2,10},{4,12},{6,14},{8,0},{10,2},{12,4},{14,6},{1,9},{3,11}... | collective-permute-start | bytes 208904 | tf_op jit(solution)/shard_map/ppermute | solution.py:237
  6.2 6.7 %collective-permute-start.1 = (bf16[34,16,128]{2,1,0:T(8,128)(2,1)S(1)}, bf16[34,16,128]{2,1,0:T(8,128)(2,1)S(1)}, u32[]{:S(2)}, u32[]{:S(2)}) collective-permute-start(bf16[34,16,128]{2,1,0:T(8,128)(2,1)S(1)} %get-tuple-element.26), channel_id=1, source_target_pairs={{0,4},{2,6},{4,0},{6,2},{8,12},{10,14},{12,8},{14,10},{1,5},{3,7},... | collective-permute-start | bytes 417800 | tf_op jit(solution)/shard_map/ppermute | solution.py:237
  7.8 10.9 %collective-permute-start.2 = (bf16[17,16,128]{2,1,0:T(8,128)(2,1)S(1)}, bf16[17,16,128]{2,1,0:T(8,128)(2,1)S(1)}, u32[]{:S(2)}, u32[]{:S(2)}) collective-permute-start(bf16[17,16,128]{2,1,0:T(8,128)(2,1)S(1)} %get-tuple-element.28), channel_id=1, source_target_pairs={{0,10},{2,8},{4,14},{6,12},{8,2},{10,0},{12,6},{14,4},{1,11},{3,9}... | collective-permute-start | bytes 208904 | tf_op jit(solution)/shard_map/ppermute | solution.py:237
  9.1 9.7 %collective-permute-start.3 = (bf16[17,16,128]{2,1,0:T(8,128)(2,1)S(1)}, bf16[17,16,128]{2,1,0:T(8,128)(2,1)S(1)}, u32[]{:S(2)}, u32[]{:S(2)}) collective-permute-start(bf16[17,16,128]{2,1,0:T(8,128)(2,1)S(1)} %get-tuple-element.29), channel_id=1, source_target_pairs={{0,14},{2,12},{4,10},{6,8},{8,6},{10,4},{12,2},{14,0},{1,15},{3,13... | collective-permute-start | bytes 208904 | tf_op jit(solution)/shard_map/ppermute | solution.py:237
  11.5 7.2 %collective-permute-start.4 = (bf16[17,16,128]{2,1,0:T(8,128)(2,1)S(1)}, bf16[17,16,128]{2,1,0:T(8,128)(2,1)S(1)}, u32[]{:S(2)}, u32[]{:S(2)}) collective-permute-start(bf16[17,16,128]{2,1,0:T(8,128)(2,1)S(1)} %get-tuple-element.30), channel_id=1, source_target_pairs={{0,12},{2,14},{4,8},{6,10},{8,4},{10,6},{12,0},{14,2},{1,13},{3,15... | collective-permute-start | bytes 208904 | tf_op jit(solution)/shard_map/ppermute | solution.py:237
  13.0 6.2 %collective-permute-start.5 = (bf16[34,16,128]{2,1,0:T(8,128)(2,1)S(1)}, bf16[34,16,128]{2,1,0:T(8,128)(2,1)S(1)}, u32[]{:S(2)}, u32[]{:S(2)}) collective-permute-start(bf16[34,16,128]{2,1,0:T(8,128)(2,1)S(1)} %pad_maximum_fusion.2), channel_id=1, source_target_pairs={{0,2},{2,0},{4,6},{6,4},{8,10},{10,8},{12,14},{14,12},{1,3},{3,1},... | collective-permute-start | bytes 417800 | tf_op jit(solution)/shard_map/ppermute | solution.py:237
  14.9 4.4 %collective-permute-start.7 = (bf16[51,16,128]{2,1,0:T(8,128)(2,1)S(1)}, bf16[51,16,128]{2,1,0:T(8,128)(2,1)S(1)}, u32[]{:S(2)}, u32[]{:S(2)}) collective-permute-start(bf16[51,16,128]{2,1,0:T(8,128)(2,1)S(1)} %pad_maximum_fusion.1), channel_id=1, source_target_pairs={{0,1},{1,0},{2,3},{3,2},{4,5},{5,4},{6,7},{7,6},{8,9},{9,8},{10,11... | collective-permute-start | bytes 626696 | tf_op jit(solution)/shard_map/ppermute | solution.py:237
  19.1 1.7 %collective-permute-start.6 = (bf16[85,16,128]{2,1,0:T(8,128)(2,1)S(1)}, bf16[85,16,128]{2,1,0:T(8,128)(2,1)S(1)}, u32[]{:S(2)}, u32[]{:S(2)}) collective-permute-start(bf16[85,16,128]{2,1,0:T(8,128)(2,1)S(1)} %pad_maximum_fusion), channel_id=1, source_target_pairs={{0,1},{1,0},{2,3},{3,2},{4,5},{5,4},{6,7},{7,6},{8,9},{9,8},{10,11... | collective-permute-start | bytes 1044488 | tf_op jit(solution)/shard_map/ppermute | solution.py:237

commit v29 on v23

--- a/solution.py
+++ b/solution.py
@@ -221,7 +221,7 @@
     place = iota((lines, slots), 1) % (slots // folds) // (slots // owners // folds)
     values = jnp.zeros((lines, slots), jnp.float32)
     for index, k in enumerate(order):
-        values = jnp.where(place == index, result_ref[me_ref[0] ^ k], values)
+        values = jnp.where(place == index, result_ref[owners - 1 - (me_ref[0] ^ k)], values)
     values = jnp.concatenate([values, jnp.zeros((8 - lines, slots), jnp.float32)], axis=0)
     at = (iota((slots, rows), 0) == slot_ref[...]).astype(jnp.float32)
     picked = jnp.dot(
@@ -338,7 +338,8 @@
         cost_estimate=compare_cost,
         name="far",
     )(query, other_second, *near)
-    results = lax.all_to_all(results, "shard", 0, 0, tiled=True)
+    members = [list(range(owners - 1, -1, -1))]
+    results = lax.all_to_all(results, "shard", 0, 0, axis_index_groups=members, tiled=True)
     best, distance, cohesion = pl.pallas_call(
         functools.partial(pick_kernel, order, parts),
         out_shape=[jax.ShapeDtypeStruct((1, local_rows), jnp.float32)] * 2

time: 33.6 us -> 31.5 us (0.938)
  blocking collectives: 10.3 us -> 8.28 us
    all_to_all x1, blocking collectives: 10.3 us -> 8.28 us  [local(): lax.all_to_all(results, 'shard', 0, 0, axis_index_groups=members, tiled=T...]
where the time goes in v29:
time: 31.5 us; the launch traced here: 31.4 us
  starting transfers between devices  13.1 us (42%)
  blocking collectives  8.28 us (26%)
  waiting for transfers between devices  4.91 us (16%)
  Pallas kernels  3.35 us (11%)
  other arithmetic  0.84 us (3%)
  between operations  0.76 us (2%)
    ppermute x8, starting transfers between devices, from_partner(): lax.ppermute(value, axis, [(i, i ^ k) for i in range(lax.axis_size(axis))])  13.1 us
    all_to_all x1, blocking collectives, local(): lax.all_to_all(results, 'shard', 0, 0, axis_index_groups=members, tiled=T...  8.28 us
    ppermute x8, waiting for transfers between devices, from_partner(): lax.ppermute(value, axis, [(i, i ^ k) for i in range(lax.axis_size(axis))])  4.91 us
    pallas_call x1, Pallas kernels, local(): pl.pallas_call(functools.partial(near_kernel, rows_all, owner_map.shape[0...  0.97 us
    pallas_call x1, Pallas kernels, local(): pl.pallas_call(functools.partial(far_kernel, rows_all, tiles), out_shape=...  0.97 us
    concatenate x1, other arithmetic, local(): ints = jnp.concatenate([owner_map, cluster_id, item_order]).reshape(1, -1)  0.76 us
    pallas_call x1, Pallas kernels, local(): pl.pallas_call(functools.partial(pick_kernel, order, parts), out_shape=[j...  0.72 us
  transfers between devices with their start and end apart: 8, of which 3 were waited for; matrix products, arithmetic and copies ran while one was open for 1% of the time, Pallas kernels for 3%

profile of v29, /device:TPU:0, one launch (start us, length us, event | category | flops | bytes accessed | tf_op | source)
XLA Modules:
  0.0 31.4 jit_solution(16418164872360722517)
XLA Ops:
  0.6 0.0 copy-start
  0.6 0.8 %pad_add_fusion = s32[512]{0:T(512)S(1)} fusion(s32[128]{0:T(128)} %param.6, s32[128]{0:T(128)} %param.5, s32[256]{0:T(256)} %param.7), kind=kLoop, calls=%fused_computation.10 | loop fusion | flops 1024 | bytes 4096 | tf_op jit(solution)/shard_map/concatenate | solution.py:279
  1.4 0.3 slots.1
  1.7 0.0 copy-done
  1.7 0.4 %pack.1 = (bf16[17,16,128]{2,1,0:T(8,128)(2,1)S(1)}, bf16[34,16,128]{2,1,0:T(8,128)(2,1)S(1)}, bf16[17,16,128]{2,1,0:T(8,128)(2,1)S(1)}, bf16[17,16,128]{2,1,0:T...) custom-call(s32[1,128]{1,0:T(1,128)S(1)} %get-tuple-element.23.slot_, ...), custom_call_target="tpu_custom_call" | custom-call | tf_op jit(solution)/shard_map/pack/pallas_call | solution.py:299
  2.1 4.1 %collective-permute-start = (bf16[17,16,128]{2,1,0:T(8,128)(2,1)S(1)}, bf16[17,16,128]{2,1,0:T(8,128)(2,1)S(1)}, u32[]{:S(2)}, u32[]{:S(2)}) collective-permute-start(bf16[17,16,128]{2,1,0:T(8,128)(2,1)S(1)} %get-tuple-element.25), channel_id=1, source_target_pairs={{0,8},{2,10},{4,12},{6,14},{8,0},{10,2},{12,4},{14,6},{1,9},{3,11}... | collective-permute-start | bytes 208904 | tf_op jit(solution)/shard_map/ppermute | solution.py:235
  6.2 1.6 %collective-permute-start.1 = (bf16[34,16,128]{2,1,0:T(8,128)(2,1)S(1)}, bf16[34,16,128]{2,1,0:T(8,128)(2,1)S(1)}, u32[]{:S(2)}, u32[]{:S(2)}) collective-permute-start(bf16[34,16,128]{2,1,0:T(8,128)(2,1)S(1)} %get-tuple-element.26), channel_id=1, source_target_pairs={{0,4},{2,6},{4,0},{6,2},{8,12},{10,14},{12,8},{14,10},{1,5},{3,7},... | collective-permute-start | bytes 417800 | tf_op jit(solution)/shard_map/ppermute | solution.py:235
  7.8 1.3 %collective-permute-start.2 = (bf16[17,16,128]{2,1,0:T(8,128)(2,1)S(1)}, bf16[17,16,128]{2,1,0:T(8,128)(2,1)S(1)}, u32[]{:S(2)}, u32[]{:S(2)}) collective-permute-start(bf16[17,16,128]{2,1,0:T(8,128)(2,1)S(1)} %get-tuple-element.28), channel_id=1, source_target_pairs={{0,10},{2,8},{4,14},{6,12},{8,2},{10,0},{12,6},{14,4},{1,11},{3,9}... | collective-permute-start | bytes 208904 | tf_op jit(solution)/shard_map/ppermute | solution.py:235
  9.1 2.4 %collective-permute-start.3 = (bf16[17,16,128]{2,1,0:T(8,128)(2,1)S(1)}, bf16[17,16,128]{2,1,0:T(8,128)(2,1)S(1)}, u32[]{:S(2)}, u32[]{:S(2)}) collective-permute-start(bf16[17,16,128]{2,1,0:T(8,128)(2,1)S(1)} %get-tuple-element.29), channel_id=1, source_target_pairs={{0,14},{2,12},{4,10},{6,8},{8,6},{10,4},{12,2},{14,0},{1,15},{3,13... | collective-permute-start | bytes 208904 | tf_op jit(solution)/shard_map/ppermute | solution.py:235
  11.5 1.4 %collective-permute-start.4 = (bf16[17,16,128]{2,1,0:T(8,128)(2,1)S(1)}, bf16[17,16,128]{2,1,0:T(8,128)(2,1)S(1)}, u32[]{:S(2)}, u32[]{:S(2)}) collective-permute-start(bf16[17,16,128]{2,1,0:T(8,128)(2,1)S(1)} %get-tuple-element.30), channel_id=1, source_target_pairs={{0,12},{2,14},{4,8},{6,10},{8,4},{10,6},{12,0},{14,2},{1,13},{3,15... | collective-permute-start | bytes 208904 | tf_op jit(solution)/shard_map/ppermute | solution.py:235
  12.9 0.0 collective-permute-done
  12.9 0.0 collective-permute-done.1
  13.0 1.9 %collective-permute-start.5 = (bf16[34,16,128]{2,1,0:T(8,128)(2,1)S(1)}, bf16[34,16,128]{2,1,0:T(8,128)(2,1)S(1)}, u32[]{:S(2)}, u32[]{:S(2)}) collective-permute-start(bf16[34,16,128]{2,1,0:T(8,128)(2,1)S(1)} %pad_maximum_fusion.2), channel_id=1, source_target_pairs={{0,2},{2,0},{4,6},{6,4},{8,10},{10,8},{12,14},{14,12},{1,3},{3,1},... | collective-permute-start | bytes 417800 | tf_op jit(solution)/shard_map/ppermute | solution.py:235
  14.9 3.9 %collective-permute-done.2 = bf16[17,16,128]{2,1,0:T(8,128)(2,1)S(1)} collective-permute-done((bf16[17,16,128]{2,1,0:T(8,128)(2,1)S(1)}, bf16[17,16,128]{2,1,0:T(8,128)(2,1)S(1)}, u32[]{:S(2)}, u32[]{:S(2)}) %collective-permute-start.2) | collective-permute-done | bytes 69664 | tf_op jit(solution)/shard_map/ppermute | solution.py:235
  18.8 0.1 collective-permute-start.7
  18.9 0.0 collective-permute-done.3
  18.9 0.0 collective-permute-done.4
  18.9 0.2 collective-permute-done.5
  19.1 0.4 %collective-permute-start.6 = (bf16[68,16,128]{2,1,0:T(8,128)(2,1)S(1)}, bf16[68,16,128]{2,1,0:T(8,128)(2,1)S(1)}, u32[]{:S(2)}, u32[]{:S(2)}) collective-permute-start(bf16[68,16,128]{2,1,0:T(8,128)(2,1)S(1)} %pad_maximum_fusion), channel_id=1, source_target_pairs={{0,1},{1,0},{2,3},{3,2},{4,5},{5,4},{6,7},{7,6},{8,9},{9,8},{10,11... | collective-permute-start | bytes 835592 | tf_op jit(solution)/shard_map/ppermute | solution.py:235
  19.6 0.8 %collective-permute-done.7.other_ref = bf16[68,16,128]{2,1,0:T(8,128)(2,1)S(1)} collective-permute-done((bf16[68,16,128]{2,1,0:T(8,128)(2,1)S(1)}, bf16[68,16,128]{2,1,0:T(8,128)(2,1)S(1)}, u32[]{:S(2)}, u32[]{:S(2)}) %collective-permute-start.7) | collective-permute-done | bytes 278560 | tf_op jit(solution)/shard_map/ppermute | solution.py:235
  20.4 1.0 %near.1 = (bf16[1024,256]{1,0:T(8,128)(2,1)S(1)}, s32[288,128]{1,0:T(8,128)S(1)}, s32[2,256]{1,0:T(2,128)S(1)}, f32[1,256]{1,0:T(1,128)S(1)}, f32[288,1024]{1,0:T(8,128)S(1)}, /*index=5*/f32[288,128]{1,0:T(8,128)S(1)}) custom-call(s32[1]{0:T(128)} %bitcast.me_ref, s32[1,512]{1,0:T(1,128)S(1)} %bitcast.6, ...), custom_call_target="tpu_custom_call" | custom-call | flops 268435456 | bytes 1048576 | tf_op jit(solution)/shard_map/near/pallas_call | solution.py:313
  21.4 0.0 collective-permute-done.6.other_ref
  21.4 1.0 %far.1 = (f32[8,2,256]{2,1,0:T(2,128)S(1)}, f32[1,32]{1,0:T(1,128)S(1)}) custom-call(bf16[136,16,128]{2,1,0:T(8,128)(2,1)S(1)} %constant_dynamic-update-slice_fusion.query_ref, bf16[68,16,128]{2,1,0:T(8,128)(2,1)S(1)} %collective-permute-done.6.other_ref, bf16[1024,256]{1,0:T(8,128)(2,1)S(1)} %get-tuple-element.32.query_t_ref, ...), custom_call_target="tpu_custom_call" | custom-call | flops 268435456 | bytes 1048576 | tf_op jit(solution)/shard_map/far/pallas_call | solution.py:329
  22.4 8.3 %all_to_all.5.result_ref = f32[8,2,256]{2,1,0:T(2,128)S(1)} all-to-all(f32[8,2,256]{2,1,0:T(2,128)S(1)} %get-tuple-element.38), channel_id=1, replica_groups={{14,12,10,8,6,4,2,0},{15,13,11,9,7,5,3,1},{30,28,26,24,22,20,18,16},{31..., dimensions={0} | all-to-all | bytes 32768 | tf_op jit(solution)/shard_map/all_to_all | solution.py:342
  30.6 0.7 %pick.1 = (f32[1,128]{1,0:T(1,128)}, f32[1,128]{1,0:T(1,128)}, f32[1,32]{1,0:T(1,128)}) custom-call(s32[1]{0:T(128)} %bitcast.me_ref, s32[1,128]{1,0:T(1,128)S(1)} %get-tuple-element.23.slot_ref, f32[8,2,256]{2,1,0:T(2,128)S(1)} %all_to_all.5.result_ref, f32[1,32]{1,0:T(1,128)S(1)} %get-tuple-element.39.norm_ref), custom_call_target="tpu_custom_call" | custom-call | tf_op jit(solution)/shard_map/pick/pallas_call | solution.py:343
  (10 shorter events, 0.2 us)
Async XLA Ops:
  0.6 1.0 %copy-start = (bf16[128,1024]{1,0:T(8,128)(2,1)S(1)}, bf16[128,1024]{1,0:T(8,128)(2,1)}, u32[]{:S(2)}) copy-start(bf16[128,1024]{1,0:T(8,128)(2,1)} %embed_ref.1) | copy-start | bytes 786436
  2.1 10.7 %collective-permute-start = (bf16[17,16,128]{2,1,0:T(8,128)(2,1)S(1)}, bf16[17,16,128]{2,1,0:T(8,128)(2,1)S(1)}, u32[]{:S(2)}, u32[]{:S(2)}) collective-permute-start(bf16[17,16,128]{2,1,0:T(8,128)(2,1)S(1)} %get-tuple-element.25), channel_id=1, source_target_pairs={{0,8},{2,10},{4,12},{6,14},{8,0},{10,2},{12,4},{14,6},{1,9},{3,11}... | collective-permute-start | bytes 208904 | tf_op jit(solution)/shard_map/ppermute | solution.py:235
  6.2 6.7 %collective-permute-start.1 = (bf16[34,16,128]{2,1,0:T(8,128)(2,1)S(1)}, bf16[34,16,128]{2,1,0:T(8,128)(2,1)S(1)}, u32[]{:S(2)}, u32[]{:S(2)}) collective-permute-start(bf16[34,16,128]{2,1,0:T(8,128)(2,1)S(1)} %get-tuple-element.26), channel_id=1, source_target_pairs={{0,4},{2,6},{4,0},{6,2},{8,12},{10,14},{12,8},{14,10},{1,5},{3,7},... | collective-permute-start | bytes 417800 | tf_op jit(solution)/shard_map/ppermute | solution.py:235
  7.8 10.9 %collective-permute-start.2 = (bf16[17,16,128]{2,1,0:T(8,128)(2,1)S(1)}, bf16[17,16,128]{2,1,0:T(8,128)(2,1)S(1)}, u32[]{:S(2)}, u32[]{:S(2)}) collective-permute-start(bf16[17,16,128]{2,1,0:T(8,128)(2,1)S(1)} %get-tuple-element.28), channel_id=1, source_target_pairs={{0,10},{2,8},{4,14},{6,12},{8,2},{10,0},{12,6},{14,4},{1,11},{3,9}... | collective-permute-start | bytes 208904 | tf_op jit(solution)/shard_map/ppermute | solution.py:235
  9.1 9.8 %collective-permute-start.3 = (bf16[17,16,128]{2,1,0:T(8,128)(2,1)S(1)}, bf16[17,16,128]{2,1,0:T(8,128)(2,1)S(1)}, u32[]{:S(2)}, u32[]{:S(2)}) collective-permute-start(bf16[17,16,128]{2,1,0:T(8,128)(2,1)S(1)} %get-tuple-element.29), channel_id=1, source_target_pairs={{0,14},{2,12},{4,10},{6,8},{8,6},{10,4},{12,2},{14,0},{1,15},{3,13... | collective-permute-start | bytes 208904 | tf_op jit(solution)/shard_map/ppermute | solution.py:235
  11.5 7.4 %collective-permute-start.4 = (bf16[17,16,128]{2,1,0:T(8,128)(2,1)S(1)}, bf16[17,16,128]{2,1,0:T(8,128)(2,1)S(1)}, u32[]{:S(2)}, u32[]{:S(2)}) collective-permute-start(bf16[17,16,128]{2,1,0:T(8,128)(2,1)S(1)} %get-tuple-element.30), channel_id=1, source_target_pairs={{0,12},{2,14},{4,8},{6,10},{8,4},{10,6},{12,0},{14,2},{1,13},{3,15... | collective-permute-start | bytes 208904 | tf_op jit(solution)/shard_map/ppermute | solution.py:235
  13.0 6.2 %collective-permute-start.5 = (bf16[34,16,128]{2,1,0:T(8,128)(2,1)S(1)}, bf16[34,16,128]{2,1,0:T(8,128)(2,1)S(1)}, u32[]{:S(2)}, u32[]{:S(2)}) collective-permute-start(bf16[34,16,128]{2,1,0:T(8,128)(2,1)S(1)} %pad_maximum_fusion.2), channel_id=1, source_target_pairs={{0,2},{2,0},{4,6},{6,4},{8,10},{10,8},{12,14},{14,12},{1,3},{3,1},... | collective-permute-start | bytes 417800 | tf_op jit(solution)/shard_map/ppermute | solution.py:235
  18.8 1.6 %collective-permute-start.7 = (bf16[68,16,128]{2,1,0:T(8,128)(2,1)S(1)}, bf16[68,16,128]{2,1,0:T(8,128)(2,1)S(1)}, u32[]{:S(2)}, u32[]{:S(2)}) collective-permute-start(bf16[68,16,128]{2,1,0:T(8,128)(2,1)S(1)} %pad_maximum_fusion.1), channel_id=1, source_target_pairs={{0,1},{1,0},{2,3},{3,2},{4,5},{5,4},{6,7},{7,6},{8,9},{9,8},{10,11... | collective-permute-start | bytes 835592 | tf_op jit(solution)/shard_map/ppermute | solution.py:235
  19.1 2.3 %collective-permute-start.6 = (bf16[68,16,128]{2,1,0:T(8,128)(2,1)S(1)}, bf16[68,16,128]{2,1,0:T(8,128)(2,1)S(1)}, u32[]{:S(2)}, u32[]{:S(2)}) collective-permute-start(bf16[68,16,128]{2,1,0:T(8,128)(2,1)S(1)} %pad_maximum_fusion), channel_id=1, source_target_pairs={{0,1},{1,0},{2,3},{3,2},{4,5},{5,4},{6,7},{7,6},{8,9},{9,8},{10,11... | collective-permute-start | bytes 835592 | tf_op jit(solution)/shard_map/ppermute | solution.py:235

commit v30 on v29

--- a/solution.py
+++ b/solution.py
@@ -221,7 +221,7 @@
     place = iota((lines, slots), 1) % (slots // folds) // (slots // owners // folds)
     values = jnp.zeros((lines, slots), jnp.float32)
     for index, k in enumerate(order):
-        values = jnp.where(place == index, result_ref[owners - 1 - (me_ref[0] ^ k)], values)
+        values = jnp.where(place == index, result_ref[((me_ref[0] ^ k) + owners - 1) % owners], values)
     values = jnp.concatenate([values, jnp.zeros((8 - lines, slots), jnp.float32)], axis=0)
     at = (iota((slots, rows), 0) == slot_ref[...]).astype(jnp.float32)
     picked = jnp.dot(
@@ -338,7 +338,7 @@
         cost_estimate=compare_cost,
         name="far",
     )(query, other_second, *near)
-    members = [list(range(owners - 1, -1, -1))]
+    members = [list(range(1, owners)) + [0]]
     results = lax.all_to_all(results, "shard", 0, 0, axis_index_groups=members, tiled=True)
     best, distance, cohesion = pl.pallas_call(
         functools.partial(pick_kernel, order, parts),

time: 31.5 us -> 32.7 us (1.038)
  blocking collectives: 8.28 us -> 9.43 us
    all_to_all x1, blocking collectives: 8.28 us -> 9.43 us  [local(): lax.all_to_all(results, 'shard', 0, 0, axis_index_groups=members, tiled=T...]
where the time goes in v30:
time: 32.7 us; the launch traced here: 32.5 us
  starting transfers between devices  13.1 us (40%)
  blocking collectives  9.43 us (29%)
  waiting for transfers between devices  4.91 us (15%)
  Pallas kernels  3.35 us (10%)
  other arithmetic  0.84 us (3%)
  between operations  0.76 us (2%)
    ppermute x8, starting transfers between devices, from_partner(): lax.ppermute(value, axis, [(i, i ^ k) for i in range(lax.axis_size(axis))])  13.1 us
    all_to_all x1, blocking collectives, local(): lax.all_to_all(results, 'shard', 0, 0, axis_index_groups=members, tiled=T...  9.43 us
    ppermute x8, waiting for transfers between devices, from_partner(): lax.ppermute(value, axis, [(i, i ^ k) for i in range(lax.axis_size(axis))])  4.91 us
    pallas_call x1, Pallas kernels, local(): pl.pallas_call(functools.partial(near_kernel, rows_all, owner_map.shape[0...  0.97 us
    pallas_call x1, Pallas kernels, local(): pl.pallas_call(functools.partial(far_kernel, rows_all, tiles), out_shape=...  0.97 us
    concatenate x1, other arithmetic, local(): ints = jnp.concatenate([owner_map, cluster_id, item_order]).reshape(1, -1)  0.76 us
    pallas_call x1, Pallas kernels, local(): pl.pallas_call(functools.partial(pick_kernel, order, parts), out_shape=[j...  0.72 us
  transfers between devices with their start and end apart: 8, of which 3 were waited for; matrix products, arithmetic and copies ran while one was open for 1% of the time, Pallas kernels for 3%

profile of v30, /device:TPU:0, one launch (start us, length us, event | category | flops | bytes accessed | tf_op | source)
XLA Modules:
  0.0 32.5 jit_solution(7165472470215271777)
XLA Ops:
  0.6 0.0 copy-start
  0.6 0.8 %pad_add_fusion = s32[512]{0:T(512)S(1)} fusion(s32[128]{0:T(128)} %param.6, s32[128]{0:T(128)} %param.5, s32[256]{0:T(256)} %param.7), kind=kLoop, calls=%fused_computation.10 | loop fusion | flops 1024 | bytes 4096 | tf_op jit(solution)/shard_map/concatenate | solution.py:279
  1.4 0.3 slots.1
  1.7 0.0 copy-done
  1.7 0.4 %pack.1 = (bf16[17,16,128]{2,1,0:T(8,128)(2,1)S(1)}, bf16[34,16,128]{2,1,0:T(8,128)(2,1)S(1)}, bf16[17,16,128]{2,1,0:T(8,128)(2,1)S(1)}, bf16[17,16,128]{2,1,0:T...) custom-call(s32[1,128]{1,0:T(1,128)S(1)} %get-tuple-element.23.slot_, ...), custom_call_target="tpu_custom_call" | custom-call | tf_op jit(solution)/shard_map/pack/pallas_call | solution.py:299
  2.1 4.1 %collective-permute-start = (bf16[17,16,128]{2,1,0:T(8,128)(2,1)S(1)}, bf16[17,16,128]{2,1,0:T(8,128)(2,1)S(1)}, u32[]{:S(2)}, u32[]{:S(2)}) collective-permute-start(bf16[17,16,128]{2,1,0:T(8,128)(2,1)S(1)} %get-tuple-element.25), channel_id=1, source_target_pairs={{0,8},{2,10},{4,12},{6,14},{8,0},{10,2},{12,4},{14,6},{1,9},{3,11}... | collective-permute-start | bytes 208904 | tf_op jit(solution)/shard_map/ppermute | solution.py:235
  6.2 1.6 %collective-permute-start.1 = (bf16[34,16,128]{2,1,0:T(8,128)(2,1)S(1)}, bf16[34,16,128]{2,1,0:T(8,128)(2,1)S(1)}, u32[]{:S(2)}, u32[]{:S(2)}) collective-permute-start(bf16[34,16,128]{2,1,0:T(8,128)(2,1)S(1)} %get-tuple-element.26), channel_id=1, source_target_pairs={{0,4},{2,6},{4,0},{6,2},{8,12},{10,14},{12,8},{14,10},{1,5},{3,7},... | collective-permute-start | bytes 417800 | tf_op jit(solution)/shard_map/ppermute | solution.py:235
  7.8 1.3 %collective-permute-start.2 = (bf16[17,16,128]{2,1,0:T(8,128)(2,1)S(1)}, bf16[17,16,128]{2,1,0:T(8,128)(2,1)S(1)}, u32[]{:S(2)}, u32[]{:S(2)}) collective-permute-start(bf16[17,16,128]{2,1,0:T(8,128)(2,1)S(1)} %get-tuple-element.28), channel_id=1, source_target_pairs={{0,10},{2,8},{4,14},{6,12},{8,2},{10,0},{12,6},{14,4},{1,11},{3,9}... | collective-permute-start | bytes 208904 | tf_op jit(solution)/shard_map/ppermute | solution.py:235
  9.1 2.4 %collective-permute-start.3 = (bf16[17,16,128]{2,1,0:T(8,128)(2,1)S(1)}, bf16[17,16,128]{2,1,0:T(8,128)(2,1)S(1)}, u32[]{:S(2)}, u32[]{:S(2)}) collective-permute-start(bf16[17,16,128]{2,1,0:T(8,128)(2,1)S(1)} %get-tuple-element.29), channel_id=1, source_target_pairs={{0,14},{2,12},{4,10},{6,8},{8,6},{10,4},{12,2},{14,0},{1,15},{3,13... | collective-permute-start | bytes 208904 | tf_op jit(solution)/shard_map/ppermute | solution.py:235
  11.5 1.4 %collective-permute-start.4 = (bf16[17,16,128]{2,1,0:T(8,128)(2,1)S(1)}, bf16[17,16,128]{2,1,0:T(8,128)(2,1)S(1)}, u32[]{:S(2)}, u32[]{:S(2)}) collective-permute-start(bf16[17,16,128]{2,1,0:T(8,128)(2,1)S(1)} %get-tuple-element.30), channel_id=1, source_target_pairs={{0,12},{2,14},{4,8},{6,10},{8,4},{10,6},{12,0},{14,2},{1,13},{3,15... | collective-permute-start | bytes 208904 | tf_op jit(solution)/shard_map/ppermute | solution.py:235
  12.9 0.0 collective-permute-done
  12.9 0.0 collective-permute-done.1
  13.0 1.9 %collective-permute-start.5 = (bf16[34,16,128]{2,1,0:T(8,128)(2,1)S(1)}, bf16[34,16,128]{2,1,0:T(8,128)(2,1)S(1)}, u32[]{:S(2)}, u32[]{:S(2)}) collective-permute-start(bf16[34,16,128]{2,1,0:T(8,128)(2,1)S(1)} %pad_maximum_fusion.2), channel_id=1, source_target_pairs={{0,2},{2,0},{4,6},{6,4},{8,10},{10,8},{12,14},{14,12},{1,3},{3,1},... | collective-permute-start | bytes 417800 | tf_op jit(solution)/shard_map/ppermute | solution.py:235
  14.9 3.9 %collective-permute-done.2 = bf16[17,16,128]{2,1,0:T(8,128)(2,1)S(1)} collective-permute-done((bf16[17,16,128]{2,1,0:T(8,128)(2,1)S(1)}, bf16[17,16,128]{2,1,0:T(8,128)(2,1)S(1)}, u32[]{:S(2)}, u32[]{:S(2)}) %collective-permute-start.2) | collective-permute-done | bytes 69664 | tf_op jit(solution)/shard_map/ppermute | solution.py:235
  18.8 0.1 collective-permute-start.7
  18.9 0.0 collective-permute-done.3
  18.9 0.0 collective-permute-done.4
  18.9 0.2 collective-permute-done.5
  19.1 0.4 %collective-permute-start.6 = (bf16[68,16,128]{2,1,0:T(8,128)(2,1)S(1)}, bf16[68,16,128]{2,1,0:T(8,128)(2,1)S(1)}, u32[]{:S(2)}, u32[]{:S(2)}) collective-permute-start(bf16[68,16,128]{2,1,0:T(8,128)(2,1)S(1)} %pad_maximum_fusion), channel_id=1, source_target_pairs={{0,1},{1,0},{2,3},{3,2},{4,5},{5,4},{6,7},{7,6},{8,9},{9,8},{10,11... | collective-permute-start | bytes 835592 | tf_op jit(solution)/shard_map/ppermute | solution.py:235
  19.6 0.8 %collective-permute-done.7.other_ref = bf16[68,16,128]{2,1,0:T(8,128)(2,1)S(1)} collective-permute-done((bf16[68,16,128]{2,1,0:T(8,128)(2,1)S(1)}, bf16[68,16,128]{2,1,0:T(8,128)(2,1)S(1)}, u32[]{:S(2)}, u32[]{:S(2)}) %collective-permute-start.7) | collective-permute-done | bytes 278560 | tf_op jit(solution)/shard_map/ppermute | solution.py:235
  20.4 1.0 %near.1 = (bf16[1024,256]{1,0:T(8,128)(2,1)S(1)}, s32[288,128]{1,0:T(8,128)S(1)}, s32[2,256]{1,0:T(2,128)S(1)}, f32[1,256]{1,0:T(1,128)S(1)}, f32[288,1024]{1,0:T(8,128)S(1)}, /*index=5*/f32[288,128]{1,0:T(8,128)S(1)}) custom-call(s32[1]{0:T(128)} %bitcast.me_ref, s32[1,512]{1,0:T(1,128)S(1)} %bitcast.6, ...), custom_call_target="tpu_custom_call" | custom-call | flops 268435456 | bytes 1048576 | tf_op jit(solution)/shard_map/near/pallas_call | solution.py:313
  21.4 0.0 collective-permute-done.6.other_ref
  21.4 1.0 %far.1 = (f32[8,2,256]{2,1,0:T(2,128)S(1)}, f32[1,32]{1,0:T(1,128)S(1)}) custom-call(bf16[136,16,128]{2,1,0:T(8,128)(2,1)S(1)} %constant_dynamic-update-slice_fusion.query_ref, bf16[68,16,128]{2,1,0:T(8,128)(2,1)S(1)} %collective-permute-done.6.other_ref, bf16[1024,256]{1,0:T(8,128)(2,1)S(1)} %get-tuple-element.32.query_t_ref, ...), custom_call_target="tpu_custom_call" | custom-call | flops 268435456 | bytes 1048576 | tf_op jit(solution)/shard_map/far/pallas_call | solution.py:329
  22.4 9.4 %all_to_all.5.result_ref = f32[8,2,256]{2,1,0:T(2,128)S(1)} all-to-all(f32[8,2,256]{2,1,0:T(2,128)S(1)} %get-tuple-element.38), channel_id=1, replica_groups={{2,4,6,8,10,12,14,0},{3,5,7,9,11,13,15,1},{18,20,22,24,26,28,30,16},{19..., dimensions={0} | all-to-all | bytes 32768 | tf_op jit(solution)/shard_map/all_to_all | solution.py:342
  31.8 0.7 %pick.1 = (f32[1,128]{1,0:T(1,128)}, f32[1,128]{1,0:T(1,128)}, f32[1,32]{1,0:T(1,128)}) custom-call(s32[1]{0:T(128)} %bitcast.me_ref, s32[1,128]{1,0:T(1,128)S(1)} %get-tuple-element.23.slot_ref, f32[8,2,256]{2,1,0:T(2,128)S(1)} %all_to_all.5.result_ref, f32[1,32]{1,0:T(1,128)S(1)} %get-tuple-element.39.norm_ref), custom_call_target="tpu_custom_call" | custom-call | tf_op jit(solution)/shard_map/pick/pallas_call | solution.py:343
  (10 shorter events, 0.2 us)
Async XLA Ops:
  0.6 1.0 %copy-start = (bf16[128,1024]{1,0:T(8,128)(2,1)S(1)}, bf16[128,1024]{1,0:T(8,128)(2,1)}, u32[]{:S(2)}) copy-start(bf16[128,1024]{1,0:T(8,128)(2,1)} %embed_ref.1) | copy-start | bytes 786436
  2.1 10.7 %collective-permute-start = (bf16[17,16,128]{2,1,0:T(8,128)(2,1)S(1)}, bf16[17,16,128]{2,1,0:T(8,128)(2,1)S(1)}, u32[]{:S(2)}, u32[]{:S(2)}) collective-permute-start(bf16[17,16,128]{2,1,0:T(8,128)(2,1)S(1)} %get-tuple-element.25), channel_id=1, source_target_pairs={{0,8},{2,10},{4,12},{6,14},{8,0},{10,2},{12,4},{14,6},{1,9},{3,11}... | collective-permute-start | bytes 208904 | tf_op jit(solution)/shard_map/ppermute | solution.py:235
  6.2 6.7 %collective-permute-start.1 = (bf16[34,16,128]{2,1,0:T(8,128)(2,1)S(1)}, bf16[34,16,128]{2,1,0:T(8,128)(2,1)S(1)}, u32[]{:S(2)}, u32[]{:S(2)}) collective-permute-start(bf16[34,16,128]{2,1,0:T(8,128)(2,1)S(1)} %get-tuple-element.26), channel_id=1, source_target_pairs={{0,4},{2,6},{4,0},{6,2},{8,12},{10,14},{12,8},{14,10},{1,5},{3,7},... | collective-permute-start | bytes 417800 | tf_op jit(solution)/shard_map/ppermute | solution.py:235
  7.8 10.9 %collective-permute-start.2 = (bf16[17,16,128]{2,1,0:T(8,128)(2,1)S(1)}, bf16[17,16,128]{2,1,0:T(8,128)(2,1)S(1)}, u32[]{:S(2)}, u32[]{:S(2)}) collective-permute-start(bf16[17,16,128]{2,1,0:T(8,128)(2,1)S(1)} %get-tuple-element.28), channel_id=1, source_target_pairs={{0,10},{2,8},{4,14},{6,12},{8,2},{10,0},{12,6},{14,4},{1,11},{3,9}... | collective-permute-start | bytes 208904 | tf_op jit(solution)/shard_map/ppermute | solution.py:235
  9.1 9.8 %collective-permute-start.3 = (bf16[17,16,128]{2,1,0:T(8,128)(2,1)S(1)}, bf16[17,16,128]{2,1,0:T(8,128)(2,1)S(1)}, u32[]{:S(2)}, u32[]{:S(2)}) collective-permute-start(bf16[17,16,128]{2,1,0:T(8,128)(2,1)S(1)} %get-tuple-element.29), channel_id=1, source_target_pairs={{0,14},{2,12},{4,10},{6,8},{8,6},{10,4},{12,2},{14,0},{1,15},{3,13... | collective-permute-start | bytes 208904 | tf_op jit(solution)/shard_map/ppermute | solution.py:235
  11.5 7.4 %collective-permute-start.4 = (bf16[17,16,128]{2,1,0:T(8,128)(2,1)S(1)}, bf16[17,16,128]{2,1,0:T(8,128)(2,1)S(1)}, u32[]{:S(2)}, u32[]{:S(2)}) collective-permute-start(bf16[17,16,128]{2,1,0:T(8,128)(2,1)S(1)} %get-tuple-element.30), channel_id=1, source_target_pairs={{0,12},{2,14},{4,8},{6,10},{8,4},{10,6},{12,0},{14,2},{1,13},{3,15... | collective-permute-start | bytes 208904 | tf_op jit(solution)/shard_map/ppermute | solution.py:235
  13.0 6.2 %collective-permute-start.5 = (bf16[34,16,128]{2,1,0:T(8,128)(2,1)S(1)}, bf16[34,16,128]{2,1,0:T(8,128)(2,1)S(1)}, u32[]{:S(2)}, u32[]{:S(2)}) collective-permute-start(bf16[34,16,128]{2,1,0:T(8,128)(2,1)S(1)} %pad_maximum_fusion.2), channel_id=1, source_target_pairs={{0,2},{2,0},{4,6},{6,4},{8,10},{10,8},{12,14},{14,12},{1,3},{3,1},... | collective-permute-start | bytes 417800 | tf_op jit(solution)/shard_map/ppermute | solution.py:235
  18.8 1.6 %collective-permute-start.7 = (bf16[68,16,128]{2,1,0:T(8,128)(2,1)S(1)}, bf16[68,16,128]{2,1,0:T(8,128)(2,1)S(1)}, u32[]{:S(2)}, u32[]{:S(2)}) collective-permute-start(bf16[68,16,128]{2,1,0:T(8,128)(2,1)S(1)} %pad_maximum_fusion.1), channel_id=1, source_target_pairs={{0,1},{1,0},{2,3},{3,2},{4,5},{5,4},{6,7},{7,6},{8,9},{9,8},{10,11... | collective-permute-start | bytes 835592 | tf_op jit(solution)/shard_map/ppermute | solution.py:235
  19.1 2.3 %collective-permute-start.6 = (bf16[68,16,128]{2,1,0:T(8,128)(2,1)S(1)}, bf16[68,16,128]{2,1,0:T(8,128)(2,1)S(1)}, u32[]{:S(2)}, u32[]{:S(2)}) collective-permute-start(bf16[68,16,128]{2,1,0:T(8,128)(2,1)S(1)} %pad_maximum_fusion), channel_id=1, source_target_pairs={{0,1},{1,0},{2,3},{3,2},{4,5},{5,4},{6,7},{7,6},{8,9},{9,8},{10,11... | collective-permute-start | bytes 835592 | tf_op jit(solution)/shard_map/ppermute | solution.py:235

commit v31 on v30

--- a/solution.py
+++ b/solution.py
@@ -221,7 +221,9 @@
     place = iota((lines, slots), 1) % (slots // folds) // (slots // owners // folds)
     values = jnp.zeros((lines, slots), jnp.float32)
     for index, k in enumerate(order):
-        values = jnp.where(place == index, result_ref[((me_ref[0] ^ k) + owners - 1) % owners], values)
+        owner = me_ref[0] ^ k
+        member = jnp.where(owner % 2 == 1, owner // 2, owners - 1 - owner // 2)
+        values = jnp.where(place == index, result_ref[member], values)
     values = jnp.concatenate([values, jnp.zeros((8 - lines, slots), jnp.float32)], axis=0)
     at = (iota((slots, rows), 0) == slot_ref[...]).astype(jnp.float32)
     picked = jnp.dot(
@@ -338,7 +340,7 @@
         cost_estimate=compare_cost,
         name="far",
     )(query, other_second, *near)
-    members = [list(range(1, owners)) + [0]]
+    members = [list(range(1, owners, 2)) + list(range(owners - 2, -1, -2))]
     results = lax.all_to_all(results, "shard", 0, 0, axis_index_groups=members, tiled=True)
     best, distance, cohesion = pl.pallas_call(
         functools.partial(pick_kernel, order, parts),

time: 32.7 us -> 32.7 us (level)
  no operation moved by 1% of the time
where the time goes in v31:
time: 32.7 us; the launch traced here: 32.6 us
  starting transfers between devices  13.1 us (40%)
  blocking collectives  9.45 us (29%)
  waiting for transfers between devices  4.91 us (15%)
  Pallas kernels  3.37 us (10%)
  other arithmetic  0.84 us (3%)
  between operations  0.76 us (2%)
    ppermute x8, starting transfers between devices, from_partner(): lax.ppermute(value, axis, [(i, i ^ k) for i in range(lax.axis_size(axis))])  13.1 us
    all_to_all x1, blocking collectives, local(): lax.all_to_all(results, 'shard', 0, 0, axis_index_groups=members, tiled=T...  9.45 us
    ppermute x8, waiting for transfers between devices, from_partner(): lax.ppermute(value, axis, [(i, i ^ k) for i in range(lax.axis_size(axis))])  4.91 us
    pallas_call x1, Pallas kernels, local(): pl.pallas_call(functools.partial(near_kernel, rows_all, owner_map.shape[0...  0.97 us
    pallas_call x1, Pallas kernels, local(): pl.pallas_call(functools.partial(far_kernel, rows_all, tiles), out_shape=...  0.97 us
    concatenate x1, other arithmetic, local(): ints = jnp.concatenate([owner_map, cluster_id, item_order]).reshape(1, -1)  0.76 us
    pallas_call x1, Pallas kernels, local(): pl.pallas_call(functools.partial(pick_kernel, order, parts), out_shape=[j...  0.73 us
  transfers between devices with their start and end apart: 8, of which 3 were waited for; matrix products, arithmetic and copies ran while one was open for 1% of the time, Pallas kernels for 3%

profile of v31, /device:TPU:0, one launch (start us, length us, event | category | flops | bytes accessed | tf_op | source)
XLA Modules:
  0.0 32.6 jit_solution(797478290982135430)
XLA Ops:
  0.6 0.0 copy-start
  0.6 0.8 %pad_add_fusion = s32[512]{0:T(512)S(1)} fusion(s32[128]{0:T(128)} %param.6, s32[128]{0:T(128)} %param.5, s32[256]{0:T(256)} %param.7), kind=kLoop, calls=%fused_computation.10 | loop fusion | flops 1024 | bytes 4096 | tf_op jit(solution)/shard_map/concatenate | solution.py:281
  1.4 0.3 slots.1
  1.7 0.0 copy-done
  1.7 0.4 %pack.1 = (bf16[17,16,128]{2,1,0:T(8,128)(2,1)S(1)}, bf16[34,16,128]{2,1,0:T(8,128)(2,1)S(1)}, bf16[17,16,128]{2,1,0:T(8,128)(2,1)S(1)}, bf16[17,16,128]{2,1,0:T...) custom-call(s32[1,128]{1,0:T(1,128)S(1)} %get-tuple-element.23.slot_, ...), custom_call_target="tpu_custom_call" | custom-call | tf_op jit(solution)/shard_map/pack/pallas_call | solution.py:301
  2.1 4.1 %collective-permute-start = (bf16[17,16,128]{2,1,0:T(8,128)(2,1)S(1)}, bf16[17,16,128]{2,1,0:T(8,128)(2,1)S(1)}, u32[]{:S(2)}, u32[]{:S(2)}) collective-permute-start(bf16[17,16,128]{2,1,0:T(8,128)(2,1)S(1)} %get-tuple-element.25), channel_id=1, source_target_pairs={{0,8},{2,10},{4,12},{6,14},{8,0},{10,2},{12,4},{14,6},{1,9},{3,11}... | collective-permute-start | bytes 208904 | tf_op jit(solution)/shard_map/ppermute | solution.py:237
  6.2 1.6 %collective-permute-start.1 = (bf16[34,16,128]{2,1,0:T(8,128)(2,1)S(1)}, bf16[34,16,128]{2,1,0:T(8,128)(2,1)S(1)}, u32[]{:S(2)}, u32[]{:S(2)}) collective-permute-start(bf16[34,16,128]{2,1,0:T(8,128)(2,1)S(1)} %get-tuple-element.26), channel_id=1, source_target_pairs={{0,4},{2,6},{4,0},{6,2},{8,12},{10,14},{12,8},{14,10},{1,5},{3,7},... | collective-permute-start | bytes 417800 | tf_op jit(solution)/shard_map/ppermute | solution.py:237
  7.8 1.3 %collective-permute-start.2 = (bf16[17,16,128]{2,1,0:T(8,128)(2,1)S(1)}, bf16[17,16,128]{2,1,0:T(8,128)(2,1)S(1)}, u32[]{:S(2)}, u32[]{:S(2)}) collective-permute-start(bf16[17,16,128]{2,1,0:T(8,128)(2,1)S(1)} %get-tuple-element.28), channel_id=1, source_target_pairs={{0,10},{2,8},{4,14},{6,12},{8,2},{10,0},{12,6},{14,4},{1,11},{3,9}... | collective-permute-start | bytes 208904 | tf_op jit(solution)/shard_map/ppermute | solution.py:237
  9.1 2.4 %collective-permute-start.3 = (bf16[17,16,128]{2,1,0:T(8,128)(2,1)S(1)}, bf16[17,16,128]{2,1,0:T(8,128)(2,1)S(1)}, u32[]{:S(2)}, u32[]{:S(2)}) collective-permute-start(bf16[17,16,128]{2,1,0:T(8,128)(2,1)S(1)} %get-tuple-element.29), channel_id=1, source_target_pairs={{0,14},{2,12},{4,10},{6,8},{8,6},{10,4},{12,2},{14,0},{1,15},{3,13... | collective-permute-start | bytes 208904 | tf_op jit(solution)/shard_map/ppermute | solution.py:237
  11.5 1.4 %collective-permute-start.4 = (bf16[17,16,128]{2,1,0:T(8,128)(2,1)S(1)}, bf16[17,16,128]{2,1,0:T(8,128)(2,1)S(1)}, u32[]{:S(2)}, u32[]{:S(2)}) collective-permute-start(bf16[17,16,128]{2,1,0:T(8,128)(2,1)S(1)} %get-tuple-element.30), channel_id=1, source_target_pairs={{0,12},{2,14},{4,8},{6,10},{8,4},{10,6},{12,0},{14,2},{1,13},{3,15... | collective-permute-start | bytes 208904 | tf_op jit(solution)/shard_map/ppermute | solution.py:237
  12.9 0.0 collective-permute-done
  12.9 0.0 collective-permute-done.1
  13.0 1.9 %collective-permute-start.5 = (bf16[34,16,128]{2,1,0:T(8,128)(2,1)S(1)}, bf16[34,16,128]{2,1,0:T(8,128)(2,1)S(1)}, u32[]{:S(2)}, u32[]{:S(2)}) collective-permute-start(bf16[34,16,128]{2,1,0:T(8,128)(2,1)S(1)} %pad_maximum_fusion.2), channel_id=1, source_target_pairs={{0,2},{2,0},{4,6},{6,4},{8,10},{10,8},{12,14},{14,12},{1,3},{3,1},... | collective-permute-start | bytes 417800 | tf_op jit(solution)/shard_map/ppermute | solution.py:237
  14.9 3.9 %collective-permute-done.2 = bf16[17,16,128]{2,1,0:T(8,128)(2,1)S(1)} collective-permute-done((bf16[17,16,128]{2,1,0:T(8,128)(2,1)S(1)}, bf16[17,16,128]{2,1,0:T(8,128)(2,1)S(1)}, u32[]{:S(2)}, u32[]{:S(2)}) %collective-permute-start.2) | collective-permute-done | bytes 69664 | tf_op jit(solution)/shard_map/ppermute | solution.py:237
  18.8 0.1 collective-permute-start.7
  18.9 0.0 collective-permute-done.3
  18.9 0.0 collective-permute-done.4
  18.9 0.2 collective-permute-done.5
  19.1 0.4 %collective-permute-start.6 = (bf16[68,16,128]{2,1,0:T(8,128)(2,1)S(1)}, bf16[68,16,128]{2,1,0:T(8,128)(2,1)S(1)}, u32[]{:S(2)}, u32[]{:S(2)}) collective-permute-start(bf16[68,16,128]{2,1,0:T(8,128)(2,1)S(1)} %pad_maximum_fusion), channel_id=1, source_target_pairs={{0,1},{1,0},{2,3},{3,2},{4,5},{5,4},{6,7},{7,6},{8,9},{9,8},{10,11... | collective-permute-start | bytes 835592 | tf_op jit(solution)/shard_map/ppermute | solution.py:237
  19.6 0.8 %collective-permute-done.7.other_ref = bf16[68,16,128]{2,1,0:T(8,128)(2,1)S(1)} collective-permute-done((bf16[68,16,128]{2,1,0:T(8,128)(2,1)S(1)}, bf16[68,16,128]{2,1,0:T(8,128)(2,1)S(1)}, u32[]{:S(2)}, u32[]{:S(2)}) %collective-permute-start.7) | collective-permute-done | bytes 278560 | tf_op jit(solution)/shard_map/ppermute | solution.py:237
  20.4 1.0 %near.1 = (bf16[1024,256]{1,0:T(8,128)(2,1)S(1)}, s32[288,128]{1,0:T(8,128)S(1)}, s32[2,256]{1,0:T(2,128)S(1)}, f32[1,256]{1,0:T(1,128)S(1)}, f32[288,1024]{1,0:T(8,128)S(1)}, /*index=5*/f32[288,128]{1,0:T(8,128)S(1)}) custom-call(s32[1]{0:T(128)} %bitcast.me_ref, s32[1,512]{1,0:T(1,128)S(1)} %bitcast.6, ...), custom_call_target="tpu_custom_call" | custom-call | flops 268435456 | bytes 1048576 | tf_op jit(solution)/shard_map/near/pallas_call | solution.py:315
  21.4 0.0 collective-permute-done.6.other_ref
  21.4 1.0 %far.1 = (f32[8,2,256]{2,1,0:T(2,128)S(1)}, f32[1,32]{1,0:T(1,128)S(1)}) custom-call(bf16[136,16,128]{2,1,0:T(8,128)(2,1)S(1)} %constant_dynamic-update-slice_fusion.query_ref, bf16[68,16,128]{2,1,0:T(8,128)(2,1)S(1)} %collective-permute-done.6.other_ref, bf16[1024,256]{1,0:T(8,128)(2,1)S(1)} %get-tuple-element.32.query_t_ref, ...), custom_call_target="tpu_custom_call" | custom-call | flops 268435456 | bytes 1048576 | tf_op jit(solution)/shard_map/far/pallas_call | solution.py:331
  22.4 9.5 %all_to_all.5.result_ref = f32[8,2,256]{2,1,0:T(2,128)S(1)} all-to-all(f32[8,2,256]{2,1,0:T(2,128)S(1)} %get-tuple-element.38), channel_id=1, replica_groups={{2,6,10,14,12,8,4,0},{3,7,11,15,13,9,5,1},{18,22,26,30,28,24,20,16},{19..., dimensions={0} | all-to-all | bytes 32768 | tf_op jit(solution)/shard_map/all_to_all | solution.py:344
  31.8 0.7 %pick.1 = (f32[1,128]{1,0:T(1,128)}, f32[1,128]{1,0:T(1,128)}, f32[1,32]{1,0:T(1,128)}) custom-call(s32[1]{0:T(128)} %bitcast.me_ref, s32[1,128]{1,0:T(1,128)S(1)} %get-tuple-element.23.slot_ref, f32[8,2,256]{2,1,0:T(2,128)S(1)} %all_to_all.5.result_ref, f32[1,32]{1,0:T(1,128)S(1)} %get-tuple-element.39.norm_ref), custom_call_target="tpu_custom_call" | custom-call | tf_op jit(solution)/shard_map/pick/pallas_call | solution.py:345
  (10 shorter events, 0.2 us)
Async XLA Ops:
  0.6 1.0 %copy-start = (bf16[128,1024]{1,0:T(8,128)(2,1)S(1)}, bf16[128,1024]{1,0:T(8,128)(2,1)}, u32[]{:S(2)}) copy-start(bf16[128,1024]{1,0:T(8,128)(2,1)} %embed_ref.1) | copy-start | bytes 786436
  2.1 10.7 %collective-permute-start = (bf16[17,16,128]{2,1,0:T(8,128)(2,1)S(1)}, bf16[17,16,128]{2,1,0:T(8,128)(2,1)S(1)}, u32[]{:S(2)}, u32[]{:S(2)}) collective-permute-start(bf16[17,16,128]{2,1,0:T(8,128)(2,1)S(1)} %get-tuple-element.25), channel_id=1, source_target_pairs={{0,8},{2,10},{4,12},{6,14},{8,0},{10,2},{12,4},{14,6},{1,9},{3,11}... | collective-permute-start | bytes 208904 | tf_op jit(solution)/shard_map/ppermute | solution.py:237
  6.2 6.7 %collective-permute-start.1 = (bf16[34,16,128]{2,1,0:T(8,128)(2,1)S(1)}, bf16[34,16,128]{2,1,0:T(8,128)(2,1)S(1)}, u32[]{:S(2)}, u32[]{:S(2)}) collective-permute-start(bf16[34,16,128]{2,1,0:T(8,128)(2,1)S(1)} %get-tuple-element.26), channel_id=1, source_target_pairs={{0,4},{2,6},{4,0},{6,2},{8,12},{10,14},{12,8},{14,10},{1,5},{3,7},... | collective-permute-start | bytes 417800 | tf_op jit(solution)/shard_map/ppermute | solution.py:237
  7.8 10.9 %collective-permute-start.2 = (bf16[17,16,128]{2,1,0:T(8,128)(2,1)S(1)}, bf16[17,16,128]{2,1,0:T(8,128)(2,1)S(1)}, u32[]{:S(2)}, u32[]{:S(2)}) collective-permute-start(bf16[17,16,128]{2,1,0:T(8,128)(2,1)S(1)} %get-tuple-element.28), channel_id=1, source_target_pairs={{0,10},{2,8},{4,14},{6,12},{8,2},{10,0},{12,6},{14,4},{1,11},{3,9}... | collective-permute-start | bytes 208904 | tf_op jit(solution)/shard_map/ppermute | solution.py:237
  9.1 9.8 %collective-permute-start.3 = (bf16[17,16,128]{2,1,0:T(8,128)(2,1)S(1)}, bf16[17,16,128]{2,1,0:T(8,128)(2,1)S(1)}, u32[]{:S(2)}, u32[]{:S(2)}) collective-permute-start(bf16[17,16,128]{2,1,0:T(8,128)(2,1)S(1)} %get-tuple-element.29), channel_id=1, source_target_pairs={{0,14},{2,12},{4,10},{6,8},{8,6},{10,4},{12,2},{14,0},{1,15},{3,13... | collective-permute-start | bytes 208904 | tf_op jit(solution)/shard_map/ppermute | solution.py:237
  11.5 7.4 %collective-permute-start.4 = (bf16[17,16,128]{2,1,0:T(8,128)(2,1)S(1)}, bf16[17,16,128]{2,1,0:T(8,128)(2,1)S(1)}, u32[]{:S(2)}, u32[]{:S(2)}) collective-permute-start(bf16[17,16,128]{2,1,0:T(8,128)(2,1)S(1)} %get-tuple-element.30), channel_id=1, source_target_pairs={{0,12},{2,14},{4,8},{6,10},{8,4},{10,6},{12,0},{14,2},{1,13},{3,15... | collective-permute-start | bytes 208904 | tf_op jit(solution)/shard_map/ppermute | solution.py:237
  13.0 6.2 %collective-permute-start.5 = (bf16[34,16,128]{2,1,0:T(8,128)(2,1)S(1)}, bf16[34,16,128]{2,1,0:T(8,128)(2,1)S(1)}, u32[]{:S(2)}, u32[]{:S(2)}) collective-permute-start(bf16[34,16,128]{2,1,0:T(8,128)(2,1)S(1)} %pad_maximum_fusion.2), channel_id=1, source_target_pairs={{0,2},{2,0},{4,6},{6,4},{8,10},{10,8},{12,14},{14,12},{1,3},{3,1},... | collective-permute-start | bytes 417800 | tf_op jit(solution)/shard_map/ppermute | solution.py:237
  18.8 1.6 %collective-permute-start.7 = (bf16[68,16,128]{2,1,0:T(8,128)(2,1)S(1)}, bf16[68,16,128]{2,1,0:T(8,128)(2,1)S(1)}, u32[]{:S(2)}, u32[]{:S(2)}) collective-permute-start(bf16[68,16,128]{2,1,0:T(8,128)(2,1)S(1)} %pad_maximum_fusion.1), channel_id=1, source_target_pairs={{0,1},{1,0},{2,3},{3,2},{4,5},{5,4},{6,7},{7,6},{8,9},{9,8},{10,11... | collective-permute-start | bytes 835592 | tf_op jit(solution)/shard_map/ppermute | solution.py:237
  19.1 2.3 %collective-permute-start.6 = (bf16[68,16,128]{2,1,0:T(8,128)(2,1)S(1)}, bf16[68,16,128]{2,1,0:T(8,128)(2,1)S(1)}, u32[]{:S(2)}, u32[]{:S(2)}) collective-permute-start(bf16[68,16,128]{2,1,0:T(8,128)(2,1)S(1)} %pad_maximum_fusion), channel_id=1, source_target_pairs={{0,1},{1,0},{2,3},{3,2},{4,5},{5,4},{6,7},{7,6},{8,9},{9,8},{10,11... | collective-permute-start | bytes 835592 | tf_op jit(solution)/shard_map/ppermute | solution.py:237

commit v32 on v31

--- a/solution.py
+++ b/solution.py
@@ -11,6 +11,7 @@
 DIGITS = 3
 SENDS = ((4,), (2, 3), (5,), (7,), (6,), (1,), (0,))
 PARTNERS = (4, 2, 0, 5, 7, 6, 1, 3)
+MEMBERS = (5, 7, 6, 4, 3, 2, 1, 0)
 WHOLE = pl.BlockSpec(memory_space=pltpu.VMEM)
 SCALAR = pl.BlockSpec(memory_space=pltpu.SMEM)
 
@@ -222,7 +223,9 @@
     values = jnp.zeros((lines, slots), jnp.float32)
     for index, k in enumerate(order):
         owner = me_ref[0] ^ k
-        member = jnp.where(owner % 2 == 1, owner // 2, owners - 1 - owner // 2)
+        member = owner
+        if owners == len(MEMBERS):
+            member = sum(jnp.where(owner == name, at, 0) for at, name in enumerate(MEMBERS))
         values = jnp.where(place == index, result_ref[member], values)
     values = jnp.concatenate([values, jnp.zeros((8 - lines, slots), jnp.float32)], axis=0)
     at = (iota((slots, rows), 0) == slot_ref[...]).astype(jnp.float32)
@@ -284,6 +287,7 @@
     order = PARTNERS if direct else tuple(range(owners))
     parts = owners if direct else 1
     tiles = 2 * (width // LANES) + 1
+    members = MEMBERS if direct else tuple(range(owners))
     sends = [[PARTNERS.index(k) for k in ks] for ks in SENDS] if direct else [[0]]
     half = slots // parts // 2
     slot, digit = pl.pallas_call(
@@ -340,8 +344,8 @@
         cost_estimate=compare_cost,
         name="far",
     )(query, other_second, *near)
-    members = [list(range(1, owners, 2)) + list(range(owners - 2, -1, -2))]
-    results = lax.all_to_all(results, "shard", 0, 0, axis_index_groups=members, tiled=True)
+    groups = [list(members)]
+    results = lax.all_to_all(results, "shard", 0, 0, axis_index_groups=groups, tiled=True)
     best, distance, cohesion = pl.pallas_call(
         functools.partial(pick_kernel, order, parts),
         out_shape=[jax.ShapeDtypeStruct((1, local_rows), jnp.float32)] * 2

time: 32.7 us -> 31.6 us (0.966)
  blocking collectives: 9.45 us -> 8.33 us
    all_to_all x1, blocking collectives: 9.45 us -> 8.33 us  [local(): lax.all_to_all(results, 'shard', 0, 0, axis_index_groups=groups, tiled=True)]
where the time goes in v32:
time: 31.6 us; the launch traced here: 31.4 us
  starting transfers between devices  13.1 us (41%)
  blocking collectives  8.33 us (26%)
  waiting for transfers between devices  4.91 us (16%)
  Pallas kernels  3.37 us (11%)
  other arithmetic  0.84 us (3%)
  between operations  0.76 us (2%)
    ppermute x8, starting transfers between devices, from_partner(): lax.ppermute(value, axis, [(i, i ^ k) for i in range(lax.axis_size(axis))])  13.1 us
    all_to_all x1, blocking collectives, local(): lax.all_to_all(results, 'shard', 0, 0, axis_index_groups=groups, tiled=True)  8.33 us
    ppermute x8, waiting for transfers between devices, from_partner(): lax.ppermute(value, axis, [(i, i ^ k) for i in range(lax.axis_size(axis))])  4.91 us
    pallas_call x1, Pallas kernels, local(): pl.pallas_call(functools.partial(near_kernel, rows_all, owner_map.shape[0...  0.97 us
    pallas_call x1, Pallas kernels, local(): pl.pallas_call(functools.partial(far_kernel, rows_all, tiles), out_shape=...  0.97 us
    concatenate x1, other arithmetic, local(): ints = jnp.concatenate([owner_map, cluster_id, item_order]).reshape(1, -1)  0.76 us
    pallas_call x1, Pallas kernels, local(): pl.pallas_call(functools.partial(pick_kernel, order, parts), out_shape=[j...  0.74 us
  transfers between devices with their start and end apart: 8, of which 3 were waited for; matrix products, arithmetic and copies ran while one was open for 1% of the time, Pallas kernels for 3%

profile of v32, /device:TPU:0, one launch (start us, length us, event | category | flops | bytes accessed | tf_op | source)
XLA Modules:
  0.0 31.4 jit_solution(1222922749761002135)
XLA Ops:
  0.6 0.0 copy-start
  0.6 0.8 %pad_add_fusion = s32[512]{0:T(512)S(1)} fusion(s32[128]{0:T(128)} %param.6, s32[128]{0:T(128)} %param.5, s32[256]{0:T(256)} %param.7), kind=kLoop, calls=%fused_computation.10 | loop fusion | flops 1024 | bytes 4096 | tf_op jit(solution)/shard_map/concatenate | solution.py:284
  1.4 0.3 slots.1
  1.7 0.0 copy-done
  1.7 0.4 %pack.1 = (bf16[17,16,128]{2,1,0:T(8,128)(2,1)S(1)}, bf16[34,16,128]{2,1,0:T(8,128)(2,1)S(1)}, bf16[17,16,128]{2,1,0:T(8,128)(2,1)S(1)}, bf16[17,16,128]{2,1,0:T...) custom-call(s32[1,128]{1,0:T(1,128)S(1)} %get-tuple-element.23.slot_, ...), custom_call_target="tpu_custom_call" | custom-call | tf_op jit(solution)/shard_map/pack/pallas_call | solution.py:305
  2.1 4.1 %collective-permute-start = (bf16[17,16,128]{2,1,0:T(8,128)(2,1)S(1)}, bf16[17,16,128]{2,1,0:T(8,128)(2,1)S(1)}, u32[]{:S(2)}, u32[]{:S(2)}) collective-permute-start(bf16[17,16,128]{2,1,0:T(8,128)(2,1)S(1)} %get-tuple-element.25), channel_id=1, source_target_pairs={{0,8},{2,10},{4,12},{6,14},{8,0},{10,2},{12,4},{14,6},{1,9},{3,11}... | collective-permute-start | bytes 208904 | tf_op jit(solution)/shard_map/ppermute | solution.py:240
  6.2 1.6 %collective-permute-start.1 = (bf16[34,16,128]{2,1,0:T(8,128)(2,1)S(1)}, bf16[34,16,128]{2,1,0:T(8,128)(2,1)S(1)}, u32[]{:S(2)}, u32[]{:S(2)}) collective-permute-start(bf16[34,16,128]{2,1,0:T(8,128)(2,1)S(1)} %get-tuple-element.26), channel_id=1, source_target_pairs={{0,4},{2,6},{4,0},{6,2},{8,12},{10,14},{12,8},{14,10},{1,5},{3,7},... | collective-permute-start | bytes 417800 | tf_op jit(solution)/shard_map/ppermute | solution.py:240
  7.8 1.3 %collective-permute-start.2 = (bf16[17,16,128]{2,1,0:T(8,128)(2,1)S(1)}, bf16[17,16,128]{2,1,0:T(8,128)(2,1)S(1)}, u32[]{:S(2)}, u32[]{:S(2)}) collective-permute-start(bf16[17,16,128]{2,1,0:T(8,128)(2,1)S(1)} %get-tuple-element.28), channel_id=1, source_target_pairs={{0,10},{2,8},{4,14},{6,12},{8,2},{10,0},{12,6},{14,4},{1,11},{3,9}... | collective-permute-start | bytes 208904 | tf_op jit(solution)/shard_map/ppermute | solution.py:240
  9.1 2.4 %collective-permute-start.3 = (bf16[17,16,128]{2,1,0:T(8,128)(2,1)S(1)}, bf16[17,16,128]{2,1,0:T(8,128)(2,1)S(1)}, u32[]{:S(2)}, u32[]{:S(2)}) collective-permute-start(bf16[17,16,128]{2,1,0:T(8,128)(2,1)S(1)} %get-tuple-element.29), channel_id=1, source_target_pairs={{0,14},{2,12},{4,10},{6,8},{8,6},{10,4},{12,2},{14,0},{1,15},{3,13... | collective-permute-start | bytes 208904 | tf_op jit(solution)/shard_map/ppermute | solution.py:240
  11.5 1.4 %collective-permute-start.4 = (bf16[17,16,128]{2,1,0:T(8,128)(2,1)S(1)}, bf16[17,16,128]{2,1,0:T(8,128)(2,1)S(1)}, u32[]{:S(2)}, u32[]{:S(2)}) collective-permute-start(bf16[17,16,128]{2,1,0:T(8,128)(2,1)S(1)} %get-tuple-element.30), channel_id=1, source_target_pairs={{0,12},{2,14},{4,8},{6,10},{8,4},{10,6},{12,0},{14,2},{1,13},{3,15... | collective-permute-start | bytes 208904 | tf_op jit(solution)/shard_map/ppermute | solution.py:240
  12.9 0.0 collective-permute-done
  12.9 0.0 collective-permute-done.1
  13.0 1.9 %collective-permute-start.5 = (bf16[34,16,128]{2,1,0:T(8,128)(2,1)S(1)}, bf16[34,16,128]{2,1,0:T(8,128)(2,1)S(1)}, u32[]{:S(2)}, u32[]{:S(2)}) collective-permute-start(bf16[34,16,128]{2,1,0:T(8,128)(2,1)S(1)} %pad_maximum_fusion.2), channel_id=1, source_target_pairs={{0,2},{2,0},{4,6},{6,4},{8,10},{10,8},{12,14},{14,12},{1,3},{3,1},... | collective-permute-start | bytes 417800 | tf_op jit(solution)/shard_map/ppermute | solution.py:240
  14.9 3.9 %collective-permute-done.2 = bf16[17,16,128]{2,1,0:T(8,128)(2,1)S(1)} collective-permute-done((bf16[17,16,128]{2,1,0:T(8,128)(2,1)S(1)}, bf16[17,16,128]{2,1,0:T(8,128)(2,1)S(1)}, u32[]{:S(2)}, u32[]{:S(2)}) %collective-permute-start.2) | collective-permute-done | bytes 69664 | tf_op jit(solution)/shard_map/ppermute | solution.py:240
  18.8 0.1 collective-permute-start.7
  18.9 0.0 collective-permute-done.3
  18.9 0.0 collective-permute-done.4
  18.9 0.2 collective-permute-done.5
  19.1 0.4 %collective-permute-start.6 = (bf16[68,16,128]{2,1,0:T(8,128)(2,1)S(1)}, bf16[68,16,128]{2,1,0:T(8,128)(2,1)S(1)}, u32[]{:S(2)}, u32[]{:S(2)}) collective-permute-start(bf16[68,16,128]{2,1,0:T(8,128)(2,1)S(1)} %pad_maximum_fusion), channel_id=1, source_target_pairs={{0,1},{1,0},{2,3},{3,2},{4,5},{5,4},{6,7},{7,6},{8,9},{9,8},{10,11... | collective-permute-start | bytes 835592 | tf_op jit(solution)/shard_map/ppermute | solution.py:240
  19.6 0.8 %collective-permute-done.7.other_ref = bf16[68,16,128]{2,1,0:T(8,128)(2,1)S(1)} collective-permute-done((bf16[68,16,128]{2,1,0:T(8,128)(2,1)S(1)}, bf16[68,16,128]{2,1,0:T(8,128)(2,1)S(1)}, u32[]{:S(2)}, u32[]{:S(2)}) %collective-permute-start.7) | collective-permute-done | bytes 278560 | tf_op jit(solution)/shard_map/ppermute | solution.py:240
  20.4 1.0 %near.1 = (bf16[1024,256]{1,0:T(8,128)(2,1)S(1)}, s32[288,128]{1,0:T(8,128)S(1)}, s32[2,256]{1,0:T(2,128)S(1)}, f32[1,256]{1,0:T(1,128)S(1)}, f32[288,1024]{1,0:T(8,128)S(1)}, /*index=5*/f32[288,128]{1,0:T(8,128)S(1)}) custom-call(s32[1]{0:T(128)} %bitcast.me_ref, s32[1,512]{1,0:T(1,128)S(1)} %bitcast.6, ...), custom_call_target="tpu_custom_call" | custom-call | flops 268435456 | bytes 1048576 | tf_op jit(solution)/shard_map/near/pallas_call | solution.py:319
  21.4 0.0 collective-permute-done.6.other_ref
  21.4 1.0 %far.1 = (f32[8,2,256]{2,1,0:T(2,128)S(1)}, f32[1,32]{1,0:T(1,128)S(1)}) custom-call(bf16[136,16,128]{2,1,0:T(8,128)(2,1)S(1)} %constant_dynamic-update-slice_fusion.query_ref, bf16[68,16,128]{2,1,0:T(8,128)(2,1)S(1)} %collective-permute-done.6.other_ref, bf16[1024,256]{1,0:T(8,128)(2,1)S(1)} %get-tuple-element.32.query_t_ref, ...), custom_call_target="tpu_custom_call" | custom-call | flops 268435456 | bytes 1048576 | tf_op jit(solution)/shard_map/far/pallas_call | solution.py:335
  22.4 8.3 %all_to_all.5.result_ref = f32[8,2,256]{2,1,0:T(2,128)S(1)} all-to-all(f32[8,2,256]{2,1,0:T(2,128)S(1)} %get-tuple-element.38), channel_id=1, replica_groups={{10,14,12,8,6,4,2,0},{11,15,13,9,7,5,3,1},{26,30,28,24,22,20,18,16},{27..., dimensions={0} | all-to-all | bytes 32768 | tf_op jit(solution)/shard_map/all_to_all | solution.py:348
  30.7 0.7 %pick.1 = (f32[1,128]{1,0:T(1,128)}, f32[1,128]{1,0:T(1,128)}, f32[1,32]{1,0:T(1,128)}) custom-call(s32[1]{0:T(128)} %bitcast.me_ref, s32[1,128]{1,0:T(1,128)S(1)} %get-tuple-element.23.slot_ref, f32[8,2,256]{2,1,0:T(2,128)S(1)} %all_to_all.5.result_ref, f32[1,32]{1,0:T(1,128)S(1)} %get-tuple-element.39.norm_ref), custom_call_target="tpu_custom_call" | custom-call | tf_op jit(solution)/shard_map/pick/pallas_call | solution.py:349
  (10 shorter events, 0.2 us)
Async XLA Ops:
  0.6 1.0 %copy-start = (bf16[128,1024]{1,0:T(8,128)(2,1)S(1)}, bf16[128,1024]{1,0:T(8,128)(2,1)}, u32[]{:S(2)}) copy-start(bf16[128,1024]{1,0:T(8,128)(2,1)} %embed_ref.1) | copy-start | bytes 786436
  2.1 10.7 %collective-permute-start = (bf16[17,16,128]{2,1,0:T(8,128)(2,1)S(1)}, bf16[17,16,128]{2,1,0:T(8,128)(2,1)S(1)}, u32[]{:S(2)}, u32[]{:S(2)}) collective-permute-start(bf16[17,16,128]{2,1,0:T(8,128)(2,1)S(1)} %get-tuple-element.25), channel_id=1, source_target_pairs={{0,8},{2,10},{4,12},{6,14},{8,0},{10,2},{12,4},{14,6},{1,9},{3,11}... | collective-permute-start | bytes 208904 | tf_op jit(solution)/shard_map/ppermute | solution.py:240
  6.2 6.7 %collective-permute-start.1 = (bf16[34,16,128]{2,1,0:T(8,128)(2,1)S(1)}, bf16[34,16,128]{2,1,0:T(8,128)(2,1)S(1)}, u32[]{:S(2)}, u32[]{:S(2)}) collective-permute-start(bf16[34,16,128]{2,1,0:T(8,128)(2,1)S(1)} %get-tuple-element.26), channel_id=1, source_target_pairs={{0,4},{2,6},{4,0},{6,2},{8,12},{10,14},{12,8},{14,10},{1,5},{3,7},... | collective-permute-start | bytes 417800 | tf_op jit(solution)/shard_map/ppermute | solution.py:240
  7.8 10.9 %collective-permute-start.2 = (bf16[17,16,128]{2,1,0:T(8,128)(2,1)S(1)}, bf16[17,16,128]{2,1,0:T(8,128)(2,1)S(1)}, u32[]{:S(2)}, u32[]{:S(2)}) collective-permute-start(bf16[17,16,128]{2,1,0:T(8,128)(2,1)S(1)} %get-tuple-element.28), channel_id=1, source_target_pairs={{0,10},{2,8},{4,14},{6,12},{8,2},{10,0},{12,6},{14,4},{1,11},{3,9}... | collective-permute-start | bytes 208904 | tf_op jit(solution)/shard_map/ppermute | solution.py:240
  9.1 9.8 %collective-permute-start.3 = (bf16[17,16,128]{2,1,0:T(8,128)(2,1)S(1)}, bf16[17,16,128]{2,1,0:T(8,128)(2,1)S(1)}, u32[]{:S(2)}, u32[]{:S(2)}) collective-permute-start(bf16[17,16,128]{2,1,0:T(8,128)(2,1)S(1)} %get-tuple-element.29), channel_id=1, source_target_pairs={{0,14},{2,12},{4,10},{6,8},{8,6},{10,4},{12,2},{14,0},{1,15},{3,13... | collective-permute-start | bytes 208904 | tf_op jit(solution)/shard_map/ppermute | solution.py:240
  11.5 7.4 %collective-permute-start.4 = (bf16[17,16,128]{2,1,0:T(8,128)(2,1)S(1)}, bf16[17,16,128]{2,1,0:T(8,128)(2,1)S(1)}, u32[]{:S(2)}, u32[]{:S(2)}) collective-permute-start(bf16[17,16,128]{2,1,0:T(8,128)(2,1)S(1)} %get-tuple-element.30), channel_id=1, source_target_pairs={{0,12},{2,14},{4,8},{6,10},{8,4},{10,6},{12,0},{14,2},{1,13},{3,15... | collective-permute-start | bytes 208904 | tf_op jit(solution)/shard_map/ppermute | solution.py:240
  13.0 6.2 %collective-permute-start.5 = (bf16[34,16,128]{2,1,0:T(8,128)(2,1)S(1)}, bf16[34,16,128]{2,1,0:T(8,128)(2,1)S(1)}, u32[]{:S(2)}, u32[]{:S(2)}) collective-permute-start(bf16[34,16,128]{2,1,0:T(8,128)(2,1)S(1)} %pad_maximum_fusion.2), channel_id=1, source_target_pairs={{0,2},{2,0},{4,6},{6,4},{8,10},{10,8},{12,14},{14,12},{1,3},{3,1},... | collective-permute-start | bytes 417800 | tf_op jit(solution)/shard_map/ppermute | solution.py:240
  18.8 1.6 %collective-permute-start.7 = (bf16[68,16,128]{2,1,0:T(8,128)(2,1)S(1)}, bf16[68,16,128]{2,1,0:T(8,128)(2,1)S(1)}, u32[]{:S(2)}, u32[]{:S(2)}) collective-permute-start(bf16[68,16,128]{2,1,0:T(8,128)(2,1)S(1)} %pad_maximum_fusion.1), channel_id=1, source_target_pairs={{0,1},{1,0},{2,3},{3,2},{4,5},{5,4},{6,7},{7,6},{8,9},{9,8},{10,11... | collective-permute-start | bytes 835592 | tf_op jit(solution)/shard_map/ppermute | solution.py:240
  19.1 2.3 %collective-permute-start.6 = (bf16[68,16,128]{2,1,0:T(8,128)(2,1)S(1)}, bf16[68,16,128]{2,1,0:T(8,128)(2,1)S(1)}, u32[]{:S(2)}, u32[]{:S(2)}) collective-permute-start(bf16[68,16,128]{2,1,0:T(8,128)(2,1)S(1)} %pad_maximum_fusion), channel_id=1, source_target_pairs={{0,1},{1,0},{2,3},{3,2},{4,5},{5,4},{6,7},{7,6},{8,9},{9,8},{10,11... | collective-permute-start | bytes 835592 | tf_op jit(solution)/shard_map/ppermute | solution.py:240

commit v33 on v32

--- a/solution.py
+++ b/solution.py
@@ -11,6 +11,7 @@
 DIGITS = 3
 SENDS = ((4,), (2, 3), (5,), (7,), (6,), (1,), (0,))
 PARTNERS = (4, 2, 0, 5, 7, 6, 1, 3)
+EARLY = 3
 MEMBERS = (5, 7, 6, 4, 3, 2, 1, 0)
 WHOLE = pl.BlockSpec(memory_space=pltpu.VMEM)
 SCALAR = pl.BlockSpec(memory_space=pltpu.SMEM)
@@ -102,11 +103,12 @@
 
 
 def unpacked(block_ref, tiles):
-    blocks = block_ref.shape[0] // tiles
+    blocks, half = block_ref.shape[0] // tiles, block_ref.shape[1]
     each = tiles // 2
+    empty = [jnp.zeros((half, LANES), block_ref.dtype)] * (-blocks % max(LANES // (2 * half), 1))
 
     def column(tile):
-        return jnp.concatenate([block_ref[i * tiles + tile] for i in range(blocks)], axis=0)
+        return jnp.concatenate([block_ref[i * tiles + tile] for i in range(blocks)] + empty, axis=0)
 
     halves = [
         jnp.concatenate([column(first + tile) for tile in range(each)], axis=1)
@@ -250,8 +252,7 @@
     pair = from_partner(jnp.concatenate([sent[1,], pair[tiles:]]), 1, "shard")
     got[1], got[3] = pair[:tiles], pair[tiles:]
     got = [got[k] for k in PARTNERS]
-    half = len(got) // 2
-    return jnp.concatenate(got[:half]), jnp.concatenate(got[half:])
+    return jnp.concatenate(got[:EARLY]), jnp.concatenate(got[EARLY:])
 
 
 def exchange_all(packed, me):

time: 31.6 us -> 31.8 us (level)
  blocking collectives: 8.33 us -> 8.97 us
    all_to_all x1, blocking collectives: 8.33 us -> 8.97 us  [local(): lax.all_to_all(results, 'shard', 0, 0, axis_index_groups=groups, tiled=True)]
where the time goes in v33:
time: 31.8 us; the launch traced here: 31.6 us
  starting transfers between devices  12.8 us (40%)
  blocking collectives  8.97 us (28%)
  waiting for transfers between devices  4.68 us (15%)
  Pallas kernels  3.41 us (11%)
  other arithmetic  0.84 us (3%)
  between operations  0.76 us (2%)
    ppermute x8, starting transfers between devices, from_partner(): lax.ppermute(value, axis, [(i, i ^ k) for i in range(lax.axis_size(axis))])  12.8 us
    all_to_all x1, blocking collectives, local(): lax.all_to_all(results, 'shard', 0, 0, axis_index_groups=groups, tiled=True)  8.97 us
    ppermute x8, waiting for transfers between devices, from_partner(): lax.ppermute(value, axis, [(i, i ^ k) for i in range(lax.axis_size(axis))])  4.68 us
    pallas_call x1, Pallas kernels, local(): pl.pallas_call(functools.partial(far_kernel, rows_all, tiles), out_shape=...  1 us
    pallas_call x1, Pallas kernels, local(): pl.pallas_call(functools.partial(near_kernel, rows_all, owner_map.shape[0...  0.97 us
    concatenate x1, other arithmetic, local(): ints = jnp.concatenate([owner_map, cluster_id, item_order]).reshape(1, -1)  0.76 us
    pallas_call x1, Pallas kernels, local(): pl.pallas_call(functools.partial(pick_kernel, order, parts), out_shape=[j...  0.74 us
  transfers between devices with their start and end apart: 8, of which 3 were waited for; matrix products, arithmetic and copies ran while one was open for 1% of the time, Pallas kernels for 3%

profile of v33, /device:TPU:0, one launch (start us, length us, event | category | flops | bytes accessed | tf_op | source)
XLA Modules:
  0.0 31.6 jit_solution(4998492073111889840)
XLA Ops:
  0.6 0.0 copy-start
  0.6 0.8 %pad_add_fusion = s32[512]{0:T(512)S(1)} fusion(s32[128]{0:T(128)} %param.6, s32[128]{0:T(128)} %param.5, s32[256]{0:T(256)} %param.7), kind=kLoop, calls=%fused_computation.10 | loop fusion | flops 1024 | bytes 4096 | tf_op jit(solution)/shard_map/concatenate | solution.py:285
  1.4 0.3 slots.1
  1.7 0.0 copy-done
  1.7 0.4 %pack.1 = (bf16[17,16,128]{2,1,0:T(8,128)(2,1)S(1)}, bf16[34,16,128]{2,1,0:T(8,128)(2,1)S(1)}, bf16[17,16,128]{2,1,0:T(8,128)(2,1)S(1)}, bf16[17,16,128]{2,1,0:T...) custom-call(s32[1,128]{1,0:T(1,128)S(1)} %get-tuple-element.23.slot_, ...), custom_call_target="tpu_custom_call" | custom-call | tf_op jit(solution)/shard_map/pack/pallas_call | solution.py:306
  2.1 4.1 %collective-permute-start = (bf16[17,16,128]{2,1,0:T(8,128)(2,1)S(1)}, bf16[17,16,128]{2,1,0:T(8,128)(2,1)S(1)}, u32[]{:S(2)}, u32[]{:S(2)}) collective-permute-start(bf16[17,16,128]{2,1,0:T(8,128)(2,1)S(1)} %get-tuple-element.25), channel_id=1, source_target_pairs={{0,8},{2,10},{4,12},{6,14},{8,0},{10,2},{12,4},{14,6},{1,9},{3,11}... | collective-permute-start | bytes 208904 | tf_op jit(solution)/shard_map/ppermute | solution.py:242
  6.2 1.6 %collective-permute-start.1 = (bf16[34,16,128]{2,1,0:T(8,128)(2,1)S(1)}, bf16[34,16,128]{2,1,0:T(8,128)(2,1)S(1)}, u32[]{:S(2)}, u32[]{:S(2)}) collective-permute-start(bf16[34,16,128]{2,1,0:T(8,128)(2,1)S(1)} %get-tuple-element.26), channel_id=1, source_target_pairs={{0,4},{2,6},{4,0},{6,2},{8,12},{10,14},{12,8},{14,10},{1,5},{3,7},... | collective-permute-start | bytes 417800 | tf_op jit(solution)/shard_map/ppermute | solution.py:242
  7.8 1.3 %collective-permute-start.2 = (bf16[17,16,128]{2,1,0:T(8,128)(2,1)S(1)}, bf16[17,16,128]{2,1,0:T(8,128)(2,1)S(1)}, u32[]{:S(2)}, u32[]{:S(2)}) collective-permute-start(bf16[17,16,128]{2,1,0:T(8,128)(2,1)S(1)} %get-tuple-element.28), channel_id=1, source_target_pairs={{0,10},{2,8},{4,14},{6,12},{8,2},{10,0},{12,6},{14,4},{1,11},{3,9}... | collective-permute-start | bytes 208904 | tf_op jit(solution)/shard_map/ppermute | solution.py:242
  9.1 2.4 %collective-permute-start.3 = (bf16[17,16,128]{2,1,0:T(8,128)(2,1)S(1)}, bf16[17,16,128]{2,1,0:T(8,128)(2,1)S(1)}, u32[]{:S(2)}, u32[]{:S(2)}) collective-permute-start(bf16[17,16,128]{2,1,0:T(8,128)(2,1)S(1)} %get-tuple-element.29), channel_id=1, source_target_pairs={{0,14},{2,12},{4,10},{6,8},{8,6},{10,4},{12,2},{14,0},{1,15},{3,13... | collective-permute-start | bytes 208904 | tf_op jit(solution)/shard_map/ppermute | solution.py:242
  11.5 1.4 %collective-permute-start.4 = (bf16[17,16,128]{2,1,0:T(8,128)(2,1)S(1)}, bf16[17,16,128]{2,1,0:T(8,128)(2,1)S(1)}, u32[]{:S(2)}, u32[]{:S(2)}) collective-permute-start(bf16[17,16,128]{2,1,0:T(8,128)(2,1)S(1)} %get-tuple-element.30), channel_id=1, source_target_pairs={{0,12},{2,14},{4,8},{6,10},{8,4},{10,6},{12,0},{14,2},{1,13},{3,15... | collective-permute-start | bytes 208904 | tf_op jit(solution)/shard_map/ppermute | solution.py:242
  12.9 0.0 collective-permute-done
  12.9 0.0 collective-permute-done.1
  13.0 1.9 %collective-permute-start.5 = (bf16[34,16,128]{2,1,0:T(8,128)(2,1)S(1)}, bf16[34,16,128]{2,1,0:T(8,128)(2,1)S(1)}, u32[]{:S(2)}, u32[]{:S(2)}) collective-permute-start(bf16[34,16,128]{2,1,0:T(8,128)(2,1)S(1)} %pad_maximum_fusion.2), channel_id=1, source_target_pairs={{0,2},{2,0},{4,6},{6,4},{8,10},{10,8},{12,14},{14,12},{1,3},{3,1},... | collective-permute-start | bytes 417800 | tf_op jit(solution)/shard_map/ppermute | solution.py:242
  14.9 0.1 collective-permute-start.7
  15.0 3.7 %collective-permute-done.2 = bf16[17,16,128]{2,1,0:T(8,128)(2,1)S(1)} collective-permute-done((bf16[17,16,128]{2,1,0:T(8,128)(2,1)S(1)}, bf16[17,16,128]{2,1,0:T(8,128)(2,1)S(1)}, u32[]{:S(2)}, u32[]{:S(2)}) %collective-permute-start.2) | collective-permute-done | bytes 69664 | tf_op jit(solution)/shard_map/ppermute | solution.py:242
  18.7 0.0 collective-permute-done.3
  18.8 0.0 collective-permute-done.4
  18.8 0.3 %collective-permute-done.5 = bf16[34,16,128]{2,1,0:T(8,128)(2,1)S(1)} collective-permute-done((bf16[34,16,128]{2,1,0:T(8,128)(2,1)S(1)}, bf16[34,16,128]{2,1,0:T(8,128)(2,1)S(1)}, u32[]{:S(2)}, u32[]{:S(2)}) %collective-permute-start.5) | collective-permute-done | bytes 139296 | tf_op jit(solution)/shard_map/ppermute | solution.py:242
  19.1 0.1 collective-permute-start.6
  19.3 0.0 collective-permute-done.7.other_ref
  19.3 1.0 %near.1 = (bf16[1024,256]{1,0:T(8,128)(2,1)S(1)}, s32[288,128]{1,0:T(8,128)S(1)}, s32[2,256]{1,0:T(2,128)S(1)}, f32[1,256]{1,0:T(1,128)S(1)}, f32[288,1024]{1,0:T(8,128)S(1)}, /*index=5*/f32[288,128]{1,0:T(8,128)S(1)}) custom-call(s32[1]{0:T(128)} %bitcast.me_ref, s32[1,512]{1,0:T(1,128)S(1)} %bitcast.6, ...), custom_call_target="tpu_custom_call" | custom-call | flops 268435456 | bytes 1048576 | tf_op jit(solution)/shard_map/near/pallas_call | solution.py:320
  20.3 0.6 %collective-permute-done.6.other_ref = bf16[85,16,128]{2,1,0:T(8,128)(2,1)S(1)} collective-permute-done((bf16[85,16,128]{2,1,0:T(8,128)(2,1)S(1)}, bf16[85,16,128]{2,1,0:T(8,128)(2,1)S(1)}, u32[]{:S(2)}, u32[]{:S(2)}) %collective-permute-start.6) | collective-permute-done | bytes 348192 | tf_op jit(solution)/shard_map/ppermute | solution.py:242
  20.9 1.0 %far.1 = (f32[8,2,256]{2,1,0:T(2,128)S(1)}, f32[1,32]{1,0:T(1,128)S(1)}) custom-call(bf16[136,16,128]{2,1,0:T(8,128)(2,1)S(1)} %constant_dynamic-update-slice_fusion.query_ref, bf16[85,16,128]{2,1,0:T(8,128)(2,1)S(1)} %collective-permute-done.6.other_ref, bf16[1024,256]{1,0:T(8,128)(2,1)S(1)} %get-tuple-element.32.query_t_ref, ...), custom_call_target="tpu_custom_call" | custom-call | flops 268435456 | bytes 1048576 | tf_op jit(solution)/shard_map/far/pallas_call | solution.py:336
  21.9 9.0 %all_to_all.5.result_ref = f32[8,2,256]{2,1,0:T(2,128)S(1)} all-to-all(f32[8,2,256]{2,1,0:T(2,128)S(1)} %get-tuple-element.38), channel_id=1, replica_groups={{10,14,12,8,6,4,2,0},{11,15,13,9,7,5,3,1},{26,30,28,24,22,20,18,16},{27..., dimensions={0} | all-to-all | bytes 32768 | tf_op jit(solution)/shard_map/all_to_all | solution.py:349
  30.8 0.7 %pick.1 = (f32[1,128]{1,0:T(1,128)}, f32[1,128]{1,0:T(1,128)}, f32[1,32]{1,0:T(1,128)}) custom-call(s32[1]{0:T(128)} %bitcast.me_ref, s32[1,128]{1,0:T(1,128)S(1)} %get-tuple-element.23.slot_ref, f32[8,2,256]{2,1,0:T(2,128)S(1)} %all_to_all.5.result_ref, f32[1,32]{1,0:T(1,128)S(1)} %get-tuple-element.39.norm_ref), custom_call_target="tpu_custom_call" | custom-call | tf_op jit(solution)/shard_map/pick/pallas_call | solution.py:350
  (10 shorter events, 0.2 us)
Async XLA Ops:
  0.6 1.0 %copy-start = (bf16[128,1024]{1,0:T(8,128)(2,1)S(1)}, bf16[128,1024]{1,0:T(8,128)(2,1)}, u32[]{:S(2)}) copy-start(bf16[128,1024]{1,0:T(8,128)(2,1)} %embed_ref.1) | copy-start | bytes 786436
  2.1 10.7 %collective-permute-start = (bf16[17,16,128]{2,1,0:T(8,128)(2,1)S(1)}, bf16[17,16,128]{2,1,0:T(8,128)(2,1)S(1)}, u32[]{:S(2)}, u32[]{:S(2)}) collective-permute-start(bf16[17,16,128]{2,1,0:T(8,128)(2,1)S(1)} %get-tuple-element.25), channel_id=1, source_target_pairs={{0,8},{2,10},{4,12},{6,14},{8,0},{10,2},{12,4},{14,6},{1,9},{3,11}... | collective-permute-start | bytes 208904 | tf_op jit(solution)/shard_map/ppermute | solution.py:242
  6.2 6.7 %collective-permute-start.1 = (bf16[34,16,128]{2,1,0:T(8,128)(2,1)S(1)}, bf16[34,16,128]{2,1,0:T(8,128)(2,1)S(1)}, u32[]{:S(2)}, u32[]{:S(2)}) collective-permute-start(bf16[34,16,128]{2,1,0:T(8,128)(2,1)S(1)} %get-tuple-element.26), channel_id=1, source_target_pairs={{0,4},{2,6},{4,0},{6,2},{8,12},{10,14},{12,8},{14,10},{1,5},{3,7},... | collective-permute-start | bytes 417800 | tf_op jit(solution)/shard_map/ppermute | solution.py:242
  7.8 10.9 %collective-permute-start.2 = (bf16[17,16,128]{2,1,0:T(8,128)(2,1)S(1)}, bf16[17,16,128]{2,1,0:T(8,128)(2,1)S(1)}, u32[]{:S(2)}, u32[]{:S(2)}) collective-permute-start(bf16[17,16,128]{2,1,0:T(8,128)(2,1)S(1)} %get-tuple-element.28), channel_id=1, source_target_pairs={{0,10},{2,8},{4,14},{6,12},{8,2},{10,0},{12,6},{14,4},{1,11},{3,9}... | collective-permute-start | bytes 208904 | tf_op jit(solution)/shard_map/ppermute | solution.py:242
  9.1 9.7 %collective-permute-start.3 = (bf16[17,16,128]{2,1,0:T(8,128)(2,1)S(1)}, bf16[17,16,128]{2,1,0:T(8,128)(2,1)S(1)}, u32[]{:S(2)}, u32[]{:S(2)}) collective-permute-start(bf16[17,16,128]{2,1,0:T(8,128)(2,1)S(1)} %get-tuple-element.29), channel_id=1, source_target_pairs={{0,14},{2,12},{4,10},{6,8},{8,6},{10,4},{12,2},{14,0},{1,15},{3,13... | collective-permute-start | bytes 208904 | tf_op jit(solution)/shard_map/ppermute | solution.py:242
  11.5 7.2 %collective-permute-start.4 = (bf16[17,16,128]{2,1,0:T(8,128)(2,1)S(1)}, bf16[17,16,128]{2,1,0:T(8,128)(2,1)S(1)}, u32[]{:S(2)}, u32[]{:S(2)}) collective-permute-start(bf16[17,16,128]{2,1,0:T(8,128)(2,1)S(1)} %get-tuple-element.30), channel_id=1, source_target_pairs={{0,12},{2,14},{4,8},{6,10},{8,4},{10,6},{12,0},{14,2},{1,13},{3,15... | collective-permute-start | bytes 208904 | tf_op jit(solution)/shard_map/ppermute | solution.py:242
  13.0 6.2 %collective-permute-start.5 = (bf16[34,16,128]{2,1,0:T(8,128)(2,1)S(1)}, bf16[34,16,128]{2,1,0:T(8,128)(2,1)S(1)}, u32[]{:S(2)}, u32[]{:S(2)}) collective-permute-start(bf16[34,16,128]{2,1,0:T(8,128)(2,1)S(1)} %pad_maximum_fusion.2), channel_id=1, source_target_pairs={{0,2},{2,0},{4,6},{6,4},{8,10},{10,8},{12,14},{14,12},{1,3},{3,1},... | collective-permute-start | bytes 417800 | tf_op jit(solution)/shard_map/ppermute | solution.py:242
  14.9 4.4 %collective-permute-start.7 = (bf16[51,16,128]{2,1,0:T(8,128)(2,1)S(1)}, bf16[51,16,128]{2,1,0:T(8,128)(2,1)S(1)}, u32[]{:S(2)}, u32[]{:S(2)}) collective-permute-start(bf16[51,16,128]{2,1,0:T(8,128)(2,1)S(1)} %pad_maximum_fusion.1), channel_id=1, source_target_pairs={{0,1},{1,0},{2,3},{3,2},{4,5},{5,4},{6,7},{7,6},{8,9},{9,8},{10,11... | collective-permute-start | bytes 626696 | tf_op jit(solution)/shard_map/ppermute | solution.py:242
  19.1 1.7 %collective-permute-start.6 = (bf16[85,16,128]{2,1,0:T(8,128)(2,1)S(1)}, bf16[85,16,128]{2,1,0:T(8,128)(2,1)S(1)}, u32[]{:S(2)}, u32[]{:S(2)}) collective-permute-start(bf16[85,16,128]{2,1,0:T(8,128)(2,1)S(1)} %pad_maximum_fusion), channel_id=1, source_target_pairs={{0,1},{1,0},{2,3},{3,2},{4,5},{5,4},{6,7},{7,6},{8,9},{9,8},{10,11... | collective-permute-start | bytes 1044488 | tf_op jit(solution)/shard_map/ppermute | solution.py:242

commit v34 on v32

--- a/solution.py
+++ b/solution.py
@@ -11,7 +11,7 @@
 DIGITS = 3
 SENDS = ((4,), (2, 3), (5,), (7,), (6,), (1,), (0,))
 PARTNERS = (4, 2, 0, 5, 7, 6, 1, 3)
-MEMBERS = (5, 7, 6, 4, 3, 2, 1, 0)
+MEMBERS = (7, 5, 6, 4, 3, 2, 1, 0)
 WHOLE = pl.BlockSpec(memory_space=pltpu.VMEM)
 SCALAR = pl.BlockSpec(memory_space=pltpu.SMEM)
 

time: 31.6 us -> 31.5 us (level)
  no operation moved by 1% of the time
where the time goes in v34:
time: 31.5 us; the launch traced here: 31.4 us
  starting transfers between devices  13.1 us (42%)
  blocking collectives  8.25 us (26%)
  waiting for transfers between devices  4.91 us (16%)
  Pallas kernels  3.37 us (11%)
  other arithmetic  0.84 us (3%)
  between operations  0.76 us (2%)
    ppermute x8, starting transfers between devices, from_partner(): lax.ppermute(value, axis, [(i, i ^ k) for i in range(lax.axis_size(axis))])  13.1 us
    all_to_all x1, blocking collectives, local(): lax.all_to_all(results, 'shard', 0, 0, axis_index_groups=groups, tiled=True)  8.25 us
    ppermute x8, waiting for transfers between devices, from_partner(): lax.ppermute(value, axis, [(i, i ^ k) for i in range(lax.axis_size(axis))])  4.91 us
    pallas_call x1, Pallas kernels, local(): pl.pallas_call(functools.partial(near_kernel, rows_all, owner_map.shape[0...  0.97 us
    pallas_call x1, Pallas kernels, local(): pl.pallas_call(functools.partial(far_kernel, rows_all, tiles), out_shape=...  0.97 us
    concatenate x1, other arithmetic, local(): ints = jnp.concatenate([owner_map, cluster_id, item_order]).reshape(1, -1)  0.76 us
    pallas_call x1, Pallas kernels, local(): pl.pallas_call(functools.partial(pick_kernel, order, parts), out_shape=[j...  0.74 us
  transfers between devices with their start and end apart: 8, of which 3 were waited for; matrix products, arithmetic and copies ran while one was open for 1% of the time, Pallas kernels for 3%

profile of v34, /device:TPU:0, one launch (start us, length us, event | category | flops | bytes accessed | tf_op | source)
XLA Modules:
  0.0 31.4 jit_solution(4972329324381892888)
XLA Ops:
  0.6 0.0 copy-start
  0.6 0.8 %pad_add_fusion = s32[512]{0:T(512)S(1)} fusion(s32[128]{0:T(128)} %param.6, s32[128]{0:T(128)} %param.5, s32[256]{0:T(256)} %param.7), kind=kLoop, calls=%fused_computation.10 | loop fusion | flops 1024 | bytes 4096 | tf_op jit(solution)/shard_map/concatenate | solution.py:284
  1.4 0.3 slots.1
  1.7 0.0 copy-done
  1.7 0.4 %pack.1 = (bf16[17,16,128]{2,1,0:T(8,128)(2,1)S(1)}, bf16[34,16,128]{2,1,0:T(8,128)(2,1)S(1)}, bf16[17,16,128]{2,1,0:T(8,128)(2,1)S(1)}, bf16[17,16,128]{2,1,0:T...) custom-call(s32[1,128]{1,0:T(1,128)S(1)} %get-tuple-element.23.slot_, ...), custom_call_target="tpu_custom_call" | custom-call | tf_op jit(solution)/shard_map/pack/pallas_call | solution.py:305
  2.1 4.1 %collective-permute-start = (bf16[17,16,128]{2,1,0:T(8,128)(2,1)S(1)}, bf16[17,16,128]{2,1,0:T(8,128)(2,1)S(1)}, u32[]{:S(2)}, u32[]{:S(2)}) collective-permute-start(bf16[17,16,128]{2,1,0:T(8,128)(2,1)S(1)} %get-tuple-element.25), channel_id=1, source_target_pairs={{0,8},{2,10},{4,12},{6,14},{8,0},{10,2},{12,4},{14,6},{1,9},{3,11}... | collective-permute-start | bytes 208904 | tf_op jit(solution)/shard_map/ppermute | solution.py:240
  6.2 1.6 %collective-permute-start.1 = (bf16[34,16,128]{2,1,0:T(8,128)(2,1)S(1)}, bf16[34,16,128]{2,1,0:T(8,128)(2,1)S(1)}, u32[]{:S(2)}, u32[]{:S(2)}) collective-permute-start(bf16[34,16,128]{2,1,0:T(8,128)(2,1)S(1)} %get-tuple-element.26), channel_id=1, source_target_pairs={{0,4},{2,6},{4,0},{6,2},{8,12},{10,14},{12,8},{14,10},{1,5},{3,7},... | collective-permute-start | bytes 417800 | tf_op jit(solution)/shard_map/ppermute | solution.py:240
  7.8 1.3 %collective-permute-start.2 = (bf16[17,16,128]{2,1,0:T(8,128)(2,1)S(1)}, bf16[17,16,128]{2,1,0:T(8,128)(2,1)S(1)}, u32[]{:S(2)}, u32[]{:S(2)}) collective-permute-start(bf16[17,16,128]{2,1,0:T(8,128)(2,1)S(1)} %get-tuple-element.28), channel_id=1, source_target_pairs={{0,10},{2,8},{4,14},{6,12},{8,2},{10,0},{12,6},{14,4},{1,11},{3,9}... | collective-permute-start | bytes 208904 | tf_op jit(solution)/shard_map/ppermute | solution.py:240
  9.1 2.4 %collective-permute-start.3 = (bf16[17,16,128]{2,1,0:T(8,128)(2,1)S(1)}, bf16[17,16,128]{2,1,0:T(8,128)(2,1)S(1)}, u32[]{:S(2)}, u32[]{:S(2)}) collective-permute-start(bf16[17,16,128]{2,1,0:T(8,128)(2,1)S(1)} %get-tuple-element.29), channel_id=1, source_target_pairs={{0,14},{2,12},{4,10},{6,8},{8,6},{10,4},{12,2},{14,0},{1,15},{3,13... | collective-permute-start | bytes 208904 | tf_op jit(solution)/shard_map/ppermute | solution.py:240
  11.5 1.4 %collective-permute-start.4 = (bf16[17,16,128]{2,1,0:T(8,128)(2,1)S(1)}, bf16[17,16,128]{2,1,0:T(8,128)(2,1)S(1)}, u32[]{:S(2)}, u32[]{:S(2)}) collective-permute-start(bf16[17,16,128]{2,1,0:T(8,128)(2,1)S(1)} %get-tuple-element.30), channel_id=1, source_target_pairs={{0,12},{2,14},{4,8},{6,10},{8,4},{10,6},{12,0},{14,2},{1,13},{3,15... | collective-permute-start | bytes 208904 | tf_op jit(solution)/shard_map/ppermute | solution.py:240
  12.9 0.0 collective-permute-done
  12.9 0.0 collective-permute-done.1
  13.0 1.9 %collective-permute-start.5 = (bf16[34,16,128]{2,1,0:T(8,128)(2,1)S(1)}, bf16[34,16,128]{2,1,0:T(8,128)(2,1)S(1)}, u32[]{:S(2)}, u32[]{:S(2)}) collective-permute-start(bf16[34,16,128]{2,1,0:T(8,128)(2,1)S(1)} %pad_maximum_fusion.2), channel_id=1, source_target_pairs={{0,2},{2,0},{4,6},{6,4},{8,10},{10,8},{12,14},{14,12},{1,3},{3,1},... | collective-permute-start | bytes 417800 | tf_op jit(solution)/shard_map/ppermute | solution.py:240
  14.9 3.9 %collective-permute-done.2 = bf16[17,16,128]{2,1,0:T(8,128)(2,1)S(1)} collective-permute-done((bf16[17,16,128]{2,1,0:T(8,128)(2,1)S(1)}, bf16[17,16,128]{2,1,0:T(8,128)(2,1)S(1)}, u32[]{:S(2)}, u32[]{:S(2)}) %collective-permute-start.2) | collective-permute-done | bytes 69664 | tf_op jit(solution)/shard_map/ppermute | solution.py:240
  18.8 0.1 collective-permute-start.7
  18.9 0.0 collective-permute-done.3
  18.9 0.0 collective-permute-done.4
  18.9 0.2 collective-permute-done.5
  19.1 0.4 %collective-permute-start.6 = (bf16[68,16,128]{2,1,0:T(8,128)(2,1)S(1)}, bf16[68,16,128]{2,1,0:T(8,128)(2,1)S(1)}, u32[]{:S(2)}, u32[]{:S(2)}) collective-permute-start(bf16[68,16,128]{2,1,0:T(8,128)(2,1)S(1)} %pad_maximum_fusion), channel_id=1, source_target_pairs={{0,1},{1,0},{2,3},{3,2},{4,5},{5,4},{6,7},{7,6},{8,9},{9,8},{10,11... | collective-permute-start | bytes 835592 | tf_op jit(solution)/shard_map/ppermute | solution.py:240
  19.6 0.8 %collective-permute-done.7.other_ref = bf16[68,16,128]{2,1,0:T(8,128)(2,1)S(1)} collective-permute-done((bf16[68,16,128]{2,1,0:T(8,128)(2,1)S(1)}, bf16[68,16,128]{2,1,0:T(8,128)(2,1)S(1)}, u32[]{:S(2)}, u32[]{:S(2)}) %collective-permute-start.7) | collective-permute-done | bytes 278560 | tf_op jit(solution)/shard_map/ppermute | solution.py:240
  20.4 1.0 %near.1 = (bf16[1024,256]{1,0:T(8,128)(2,1)S(1)}, s32[288,128]{1,0:T(8,128)S(1)}, s32[2,256]{1,0:T(2,128)S(1)}, f32[1,256]{1,0:T(1,128)S(1)}, f32[288,1024]{1,0:T(8,128)S(1)}, /*index=5*/f32[288,128]{1,0:T(8,128)S(1)}) custom-call(s32[1]{0:T(128)} %bitcast.me_ref, s32[1,512]{1,0:T(1,128)S(1)} %bitcast.6, ...), custom_call_target="tpu_custom_call" | custom-call | flops 268435456 | bytes 1048576 | tf_op jit(solution)/shard_map/near/pallas_call | solution.py:319
  21.4 0.0 collective-permute-done.6.other_ref
  21.4 1.0 %far.1 = (f32[8,2,256]{2,1,0:T(2,128)S(1)}, f32[1,32]{1,0:T(1,128)S(1)}) custom-call(bf16[136,16,128]{2,1,0:T(8,128)(2,1)S(1)} %constant_dynamic-update-slice_fusion.query_ref, bf16[68,16,128]{2,1,0:T(8,128)(2,1)S(1)} %collective-permute-done.6.other_ref, bf16[1024,256]{1,0:T(8,128)(2,1)S(1)} %get-tuple-element.32.query_t_ref, ...), custom_call_target="tpu_custom_call" | custom-call | flops 268435456 | bytes 1048576 | tf_op jit(solution)/shard_map/far/pallas_call | solution.py:335
  22.4 8.3 %all_to_all.5.result_ref = f32[8,2,256]{2,1,0:T(2,128)S(1)} all-to-all(f32[8,2,256]{2,1,0:T(2,128)S(1)} %get-tuple-element.38), channel_id=1, replica_groups={{14,10,12,8,6,4,2,0},{15,11,13,9,7,5,3,1},{30,26,28,24,22,20,18,16},{31..., dimensions={0} | all-to-all | bytes 32768 | tf_op jit(solution)/shard_map/all_to_all | solution.py:348
  30.6 0.7 %pick.1 = (f32[1,128]{1,0:T(1,128)}, f32[1,128]{1,0:T(1,128)}, f32[1,32]{1,0:T(1,128)}) custom-call(s32[1]{0:T(128)} %bitcast.me_ref, s32[1,128]{1,0:T(1,128)S(1)} %get-tuple-element.23.slot_ref, f32[8,2,256]{2,1,0:T(2,128)S(1)} %all_to_all.5.result_ref, f32[1,32]{1,0:T(1,128)S(1)} %get-tuple-element.39.norm_ref), custom_call_target="tpu_custom_call" | custom-call | tf_op jit(solution)/shard_map/pick/pallas_call | solution.py:349
  (10 shorter events, 0.2 us)
Async XLA Ops:
  0.6 1.0 %copy-start = (bf16[128,1024]{1,0:T(8,128)(2,1)S(1)}, bf16[128,1024]{1,0:T(8,128)(2,1)}, u32[]{:S(2)}) copy-start(bf16[128,1024]{1,0:T(8,128)(2,1)} %embed_ref.1) | copy-start | bytes 786436
  2.1 10.7 %collective-permute-start = (bf16[17,16,128]{2,1,0:T(8,128)(2,1)S(1)}, bf16[17,16,128]{2,1,0:T(8,128)(2,1)S(1)}, u32[]{:S(2)}, u32[]{:S(2)}) collective-permute-start(bf16[17,16,128]{2,1,0:T(8,128)(2,1)S(1)} %get-tuple-element.25), channel_id=1, source_target_pairs={{0,8},{2,10},{4,12},{6,14},{8,0},{10,2},{12,4},{14,6},{1,9},{3,11}... | collective-permute-start | bytes 208904 | tf_op jit(solution)/shard_map/ppermute | solution.py:240
  6.2 6.7 %collective-permute-start.1 = (bf16[34,16,128]{2,1,0:T(8,128)(2,1)S(1)}, bf16[34,16,128]{2,1,0:T(8,128)(2,1)S(1)}, u32[]{:S(2)}, u32[]{:S(2)}) collective-permute-start(bf16[34,16,128]{2,1,0:T(8,128)(2,1)S(1)} %get-tuple-element.26), channel_id=1, source_target_pairs={{0,4},{2,6},{4,0},{6,2},{8,12},{10,14},{12,8},{14,10},{1,5},{3,7},... | collective-permute-start | bytes 417800 | tf_op jit(solution)/shard_map/ppermute | solution.py:240
  7.8 10.9 %collective-permute-start.2 = (bf16[17,16,128]{2,1,0:T(8,128)(2,1)S(1)}, bf16[17,16,128]{2,1,0:T(8,128)(2,1)S(1)}, u32[]{:S(2)}, u32[]{:S(2)}) collective-permute-start(bf16[17,16,128]{2,1,0:T(8,128)(2,1)S(1)} %get-tuple-element.28), channel_id=1, source_target_pairs={{0,10},{2,8},{4,14},{6,12},{8,2},{10,0},{12,6},{14,4},{1,11},{3,9}... | collective-permute-start | bytes 208904 | tf_op jit(solution)/shard_map/ppermute | solution.py:240
  9.1 9.8 %collective-permute-start.3 = (bf16[17,16,128]{2,1,0:T(8,128)(2,1)S(1)}, bf16[17,16,128]{2,1,0:T(8,128)(2,1)S(1)}, u32[]{:S(2)}, u32[]{:S(2)}) collective-permute-start(bf16[17,16,128]{2,1,0:T(8,128)(2,1)S(1)} %get-tuple-element.29), channel_id=1, source_target_pairs={{0,14},{2,12},{4,10},{6,8},{8,6},{10,4},{12,2},{14,0},{1,15},{3,13... | collective-permute-start | bytes 208904 | tf_op jit(solution)/shard_map/ppermute | solution.py:240
  11.5 7.4 %collective-permute-start.4 = (bf16[17,16,128]{2,1,0:T(8,128)(2,1)S(1)}, bf16[17,16,128]{2,1,0:T(8,128)(2,1)S(1)}, u32[]{:S(2)}, u32[]{:S(2)}) collective-permute-start(bf16[17,16,128]{2,1,0:T(8,128)(2,1)S(1)} %get-tuple-element.30), channel_id=1, source_target_pairs={{0,12},{2,14},{4,8},{6,10},{8,4},{10,6},{12,0},{14,2},{1,13},{3,15... | collective-permute-start | bytes 208904 | tf_op jit(solution)/shard_map/ppermute | solution.py:240
  13.0 6.2 %collective-permute-start.5 = (bf16[34,16,128]{2,1,0:T(8,128)(2,1)S(1)}, bf16[34,16,128]{2,1,0:T(8,128)(2,1)S(1)}, u32[]{:S(2)}, u32[]{:S(2)}) collective-permute-start(bf16[34,16,128]{2,1,0:T(8,128)(2,1)S(1)} %pad_maximum_fusion.2), channel_id=1, source_target_pairs={{0,2},{2,0},{4,6},{6,4},{8,10},{10,8},{12,14},{14,12},{1,3},{3,1},... | collective-permute-start | bytes 417800 | tf_op jit(solution)/shard_map/ppermute | solution.py:240
  18.8 1.6 %collective-permute-start.7 = (bf16[68,16,128]{2,1,0:T(8,128)(2,1)S(1)}, bf16[68,16,128]{2,1,0:T(8,128)(2,1)S(1)}, u32[]{:S(2)}, u32[]{:S(2)}) collective-permute-start(bf16[68,16,128]{2,1,0:T(8,128)(2,1)S(1)} %pad_maximum_fusion.1), channel_id=1, source_target_pairs={{0,1},{1,0},{2,3},{3,2},{4,5},{5,4},{6,7},{7,6},{8,9},{9,8},{10,11... | collective-permute-start | bytes 835592 | tf_op jit(solution)/shard_map/ppermute | solution.py:240
  19.1 2.3 %collective-permute-start.6 = (bf16[68,16,128]{2,1,0:T(8,128)(2,1)S(1)}, bf16[68,16,128]{2,1,0:T(8,128)(2,1)S(1)}, u32[]{:S(2)}, u32[]{:S(2)}) collective-permute-start(bf16[68,16,128]{2,1,0:T(8,128)(2,1)S(1)} %pad_maximum_fusion), channel_id=1, source_target_pairs={{0,1},{1,0},{2,3},{3,2},{4,5},{5,4},{6,7},{7,6},{8,9},{9,8},{10,11... | collective-permute-start | bytes 835592 | tf_op jit(solution)/shard_map/ppermute | solution.py:240
